TPU v7x, 128 devices: a whole 4x4x4 slice. The times are simulated.
128 devices in a mesh: seq: 32 (over x, z, core), exp: 4 (over y).
Axes of the slice: x: 4, y: 4, z: 4, core: 2. Of those that a mesh axis runs over, the one named last changes fastest.
Arguments:
- candidate: bfloat16 [4096, 4096], P('seq'), may hold values from -2 to 2
- in_proj: bfloat16 [4096, 4096], P(None, 'exp'), may hold values from -0.09375 to 0.09375
- bc_proj: bfloat16 [4096, 256], replicated, may hold values from -0.0078125 to 0.0078125
- step_proj: bfloat16 [4096, 32], P(None, 'exp'), may hold values from -0.875 to 0.875
- step_bias: float32 [32], P('exp'), may hold values from -1 to 1
- decay_rate: float32 [32], P('exp'), may hold values from 2e-05 to 0.04
- skip_gain: float32 [32], P('exp'), may hold values from 0.5 to 1.5
- out_proj: bfloat16 [4096, 4096], P('exp'), may hold values from -0.09375 to 0.09375
- expert_ids: int32 [4096, 2], P('seq'), may hold values from 0 to 15, all different within a row; in each aligned block of 128 rows (0 to 127, 128 to 255, ...) at most 24 rows name the same one
- gate_weights: bfloat16 [4096, 2], P('seq'), may hold values from 0.099609375 to 0.8984375
- expert_gate: bfloat16 [4, 4096, 8192], P('exp', None, 'seq'), may hold values from -0.09375 to 0.09375
- expert_up: bfloat16 [4, 4096, 8192], P('exp', None, 'seq'), may hold values from -0.09375 to 0.09375
- expert_down: bfloat16 [4, 8192, 4096], P('exp', 'seq'), may hold values from -0.0625 to 0.0625
- energy_head: float32 [4096], replicated, may hold values from -6 to 6
Outputs:
- new_candidate: bfloat16 [4096, 4096], P('seq', 'exp')
Inputs may be any that keep to these rules, and one draw needn't show every extreme that they name: `expert_ids`: each row names 2 different experts. In the rows of one device no expert is named by more than 24 rows, a bound that some block reaches. Experts 4 and above are not computed in this layer and add nothing.
All inputs are finite; a program needn't handle non-finite values.
Results may differ from a plain program's by a relative error of at most 0.011.
Values may be sent and summed in bfloat16 or wider, within the bound.
No kernel may reach another device: no remote copies, remote signals or barrier semaphores. Data moves between devices by JAX's collectives and lax.ppermute only.
A program may use at most 128 MiB of HBM per device.

v0:
```python
import jax
import jax.numpy as jnp
from jax import lax
from jax.sharding import PartitionSpec as P

CAP = 24


EPS = 1e-05
DESCENT = 0.5
HIGH = lax.Precision.HIGHEST


def carried_in(part, axis, combine, identity, reverse):
    count = lax.axis_size(axis)
    place = lax.axis_index(axis)
    ahead = count - 1 - place if reverse else place
    gathered = jax.tree.map(lambda a: lax.all_gather(a, axis), part)
    state = jax.tree.map(lambda a, e: jnp.zeros_like(a) + jnp.asarray(e, a.dtype), part, identity)

    def one(lap, state):
        source = count - 1 - lap if reverse else lap
        return combine(
            state, jax.tree.map(lambda a: lax.dynamic_index_in_dim(a, source, 0, False), gathered)
        )

    return lax.fori_loop(0, ahead, one, state)


def chain_terms(b_rows, step, inner, rate):
    tlen = step.shape[0]
    rowpos = lax.broadcasted_iota(jnp.int32, (tlen, tlen), 0)
    colpos = lax.broadcasted_iota(jnp.int32, (tlen, tlen), 1)
    lower = (rowpos >= colpos).astype(jnp.float32)
    cum = jnp.dot(lower, -step * rate[None, :], precision=HIGH)
    last = cum[-1]
    tail = jnp.exp(last[None, :] - cum) * step
    fresh = jnp.einsum("th,thp,tn->hpn", tail, inner, b_rows, precision=HIGH)
    return (jnp.exp(last), fresh, jnp.exp(cum))


def block_mix(inner, b_rows, c_rows, step, rate, skip_gain, state):
    tlen = inner.shape[0]
    rowpos = lax.broadcasted_iota(jnp.int32, (tlen, tlen), 0)
    colpos = lax.broadcasted_iota(jnp.int32, (tlen, tlen), 1)
    lower = (rowpos >= colpos).astype(jnp.float32)
    cum = jnp.dot(lower, -step * rate[None, :], precision=HIGH)
    gaps = cum.T[:, :, None] - cum.T[:, None, :]
    weights = lower[None] * jnp.exp(jnp.minimum(gaps, 0.0))
    scores = jnp.dot(c_rows, b_rows.T, precision=HIGH)
    mixing = weights * scores[None] * step.T[:, None, :]
    result = jnp.einsum("hts,shp->thp", mixing, inner, precision=HIGH)
    growth = jnp.exp(cum)
    result = result + growth[:, :, None] * jnp.einsum("tn,hpn->thp", c_rows, state, precision=HIGH)
    result = result + skip_gain[None, :, None] * inner
    last = cum[-1]
    tail = jnp.exp(last[None, :] - cum) * step
    new_state = jnp.exp(last)[:, None, None] * state + jnp.einsum(
        "th,thp,tn->hpn", tail, inner, b_rows, precision=HIGH
    )
    return (result, new_state)


def chain_combine(earlier, later):
    return (earlier[0] * later[0], later[0][:, None, None] * earlier[1] + later[1])


def slot_table(ids_rows, gate_rows, expert, slots):
    tlen = ids_rows.shape[0]
    match = ids_rows == expert
    hits = jnp.sum(match.astype(jnp.float32), axis=1)
    weight = jnp.sum(jnp.where(match, gate_rows.astype(jnp.float32), 0.0), axis=1)
    rowpos = lax.broadcasted_iota(jnp.int32, (tlen, tlen), 0)
    colpos = lax.broadcasted_iota(jnp.int32, (tlen, tlen), 1)
    strict = (rowpos > colpos).astype(jnp.float32)
    places = jnp.dot(strict, hits, precision=HIGH)
    slot_pos = lax.broadcasted_iota(jnp.int32, (slots, tlen), 0).astype(jnp.float32)
    table = jnp.where((places[None, :] == slot_pos) & (hits[None, :] > 0.0), 1.0, 0.0).astype(
        jnp.float32
    )
    return (table, weight)


def expert_terms(rows, w_gate, w_up, head_vec):
    gate_val = jnp.dot(rows, w_gate, preferred_element_type=jnp.float32)
    up_val = jnp.dot(rows, w_up, preferred_element_type=jnp.float32)
    sig = jax.nn.sigmoid(gate_val)
    first = (head_vec * up_val * sig * (1.0 + gate_val * (1.0 - sig))).astype(jnp.bfloat16)
    second = (head_vec * gate_val * sig).astype(jnp.bfloat16)
    return jnp.dot(first, w_gate.T, preferred_element_type=jnp.float32) + jnp.dot(
        second, w_up.T, preferred_element_type=jnp.float32
    )


def shards(
    candidate,
    in_proj,
    bc_proj,
    step_proj,
    step_bias,
    decay_rate,
    skip_gain,
    out_proj,
    expert_ids,
    gate_weights,
    expert_gate,
    expert_up,
    expert_down,
    energy_head,
):
    tok_rows, width = candidate.shape
    heads_here = step_bias.shape[0]
    head_size = in_proj.shape[1] // heads_here
    state_size = bc_proj.shape[1] // 2
    column = lax.axis_index("exp")
    col_count = width // lax.axis_size("exp")
    col_start = column * col_count
    inner_b = jnp.dot(candidate, in_proj, preferred_element_type=jnp.float32).astype(jnp.bfloat16)
    bc_val = jnp.dot(candidate, bc_proj, preferred_element_type=jnp.float32)
    b_rows = bc_val[:, :state_size]
    c_rows = bc_val[:, state_size:]
    pre_step = (
        jnp.dot(candidate, step_proj, preferred_element_type=jnp.float32) + step_bias[None, :]
    )
    step = jax.nn.softplus(pre_step)
    inner = inner_b.astype(jnp.float32).reshape(tok_rows, heads_here, head_size)
    decay, fresh, growth = chain_terms(b_rows, step, inner, decay_rate)
    identity = (jnp.ones_like(decay), jnp.zeros_like(fresh))
    carried = carried_in((decay, fresh), "seq", chain_combine, identity, False)[1]

    def mixer(inner_v, b_v, c_v, step_v, state_v):
        return block_mix(inner_v, b_v, c_v, step_v, decay_rate, skip_gain, state_v)

    (mixed, _), pullback = jax.vjp(mixer, inner, b_rows, c_rows, step, carried)
    partial_mix = jnp.dot(
        mixed.reshape(tok_rows, heads_here * head_size).astype(jnp.bfloat16),
        out_proj,
        preferred_element_type=jnp.float32,
    )
    own_cand = lax.dynamic_slice_in_dim(candidate, col_start, col_count, 1).astype(jnp.float32)
    mix_sum = lax.psum(partial_mix, "exp")
    hidden = (candidate.astype(jnp.float32) + mix_sum).astype(jnp.bfloat16)
    hidden_f = hidden.astype(jnp.float32)
    scale = jnp.sqrt(jnp.mean(hidden_f * hidden_f, axis=-1, keepdims=True) + EPS)
    normed = hidden_f / scale
    own_expert = column * expert_gate.shape[0]
    table, weight = slot_table(expert_ids, gate_weights, own_expert, CAP)
    slot_rows = jnp.dot(
        table.astype(jnp.bfloat16), normed.astype(jnp.bfloat16), preferred_element_type=jnp.float32
    ).astype(jnp.bfloat16)
    gathered = lax.all_gather(slot_rows, "seq", axis=0, tiled=True)
    head_vec = jnp.dot(expert_down[0].astype(jnp.float32), energy_head, precision=HIGH)
    slot_grads = lax.psum_scatter(
        expert_terms(gathered, expert_gate[0], expert_up[0], head_vec),
        "seq",
        scatter_dimension=0,
        tiled=True,
    )
    token_part = weight[:, None] * jnp.dot(table.T, slot_grads, precision=HIGH)
    token_grad = lax.psum(token_part, "exp")
    along = jnp.mean(normed * token_grad, axis=-1, keepdims=True)
    hid_grad = energy_head[None, :] + (token_grad - normed * along) / scale
    hid_bf = hid_grad.astype(jnp.bfloat16)
    hid_cols = lax.dynamic_slice_in_dim(hid_grad, col_start, col_count, 1)
    out_grad = jnp.dot(hid_bf, out_proj.T, preferred_element_type=jnp.float32).reshape(
        tok_rows, heads_here, head_size
    )
    local_grad = jnp.einsum("th,tn,thp->hpn", growth, c_rows, out_grad, precision=HIGH)
    later = carried_in((decay, local_grad), "seq", chain_combine, identity, True)[1]
    g_inner, g_b, g_c, g_step, _ = pullback((out_grad, later))
    g_pre = g_step * jax.nn.sigmoid(pre_step)
    g_bc = jnp.concatenate([g_b, g_c], axis=1)
    partial_grad = jnp.dot(
        g_inner.reshape(tok_rows, heads_here * head_size).astype(jnp.bfloat16),
        in_proj.T,
        preferred_element_type=jnp.float32,
    )
    partial_grad = partial_grad + jnp.dot(
        g_bc.astype(jnp.bfloat16), bc_proj.T, preferred_element_type=jnp.float32
    )
    partial_grad = partial_grad + jnp.dot(
        g_pre.astype(jnp.bfloat16), step_proj.T, preferred_element_type=jnp.float32
    )
    summed = lax.psum_scatter(partial_grad, "exp", scatter_dimension=1, tiled=True)
    return (own_cand - DESCENT * (hid_cols + summed)).astype(jnp.bfloat16)


def solution(mesh):
    in_specs = (
        P("seq", None),
        P(None, "exp"),
        P(),
        P(None, "exp"),
        P("exp"),
        P("exp"),
        P("exp"),
        P("exp", None),
        P("seq", None),
        P("seq", None),
        P("exp", None, "seq"),
        P("exp", None, "seq"),
        P("exp", "seq", None),
        P(),
    )
    out_specs = P("seq", "exp")
    return jax.shard_map(shards, mesh=mesh, in_specs=in_specs, out_specs=out_specs, check_vma=False)
```

profile of v0, /device:TPU:1, one launch (start us, length us, event | category | flops | bytes accessed | tf_op | source)
XLA Modules:
  0.0 698.6 jit_solution(6986910636939789820)
XLA Ops:
  6.5 2.4 compare_select_fusion
  11.2 2.4 fusion.140
  13.6 4.7 fusion.29
  19.2 2.3 fusion.42
  21.6 25.5 %all-gather.2 = f32[32,1,8]{2,1,0:T(1,128)} all-gather(f32[1,1,8]{2,1,0:T(1,128)} %bitcast.164), channel_id=1, replica_groups=mesh['seq'=32,'exp'=4] {'seq'}, dimensions={0}, use_global_device_ids=true | all-gather | bytes 1056 | tf_op jit(solution)/shard_map/all_gather | solution.py:18
  48.7 49.3 %all-gather.9.cloned.1.call-done = f32[256,128,128]{2,1,0:T(8,128)} async-done(((f32[8,128,128]{2,1,0:T(8,128)}), f32[256,128,128]{2,1,0:T(8,128)}) %all-gather.9.cloned.1.call-update) | async-done | bytes 16777232 | tf_op jit(solution)/shard_map/all_gather | solution.py:18
  98.8 2.8 while.26
  99.5 2.1 bitcast_add_fusion.9
  101.7 1.6 fusion.85
  104.1 1.9 fusion.27
  106.0 6.0 fusion.141
  112.7 1.2 select_reduce_fusion
  115.2 138.2 %all-reduce.4.cloned.1.call-done = f32[128,4096]{1,0:T(8,128)} async-done(((f32[128,4096]{1,0:T(8,128)}), f32[128,4096]{1,0:T(8,128)}) %all-reduce.4.cloned.1.call-update) | async-done | bytes 2097168 | tf_op jit(solution)/shard_map/psum | solution.py:141
  253.4 2.1 fusion
  257.4 3.9 fusion.8
  261.3 45.5 %all-gather.7.cloned.1.call-done = bf16[768,4096]{1,0:T(8,128)(2,1)} async-done(((bf16[24,4096]{1,0:T(8,128)(2,1)}), bf16[768,4096]{1,0:T(8,128)(2,1)}) %all-gather.7.cloned.1.call-update) | async-done | bytes 6291472 | tf_op jit(solution)/shard_map/all_gather | solution.py:151
  306.8 6.1 fusion.3
  312.9 14.8 %fusion.1 = f32[768,4096]{1,0:T(8,128)} fusion(bf16[1,4096,256]{2,1,0:T(8,128)(2,1)} %param.28, bf16[768,4096]{1,0:T(8,128)(2,1)} %all-gather.7.cloned.1.call-done, bf16[1,4096,256]{2,1,0:T(8,128)(2,1)S(1)} %copy-done, f32[768,256]{1,0:T(8,128)} %fusion.3, f32[256]{0:T(256)} %bitcast.160), kind=kOutput, calls=%fused_computation.12 | convolution fusion | flops 3223191552 | bytes 23856128 | tf_op jit(solution)/shard_map/dot_general | solution.py:90
  327.7 11.2 %convolution_add_fusion = f32[768,4096]{1,0:T(8,128)} fusion(f32[768,4096]{1,0:T(8,128)} %fusion.1, bf16[1,4096,256]{2,1,0:T(8,128)(2,1)S(1)} %copy-done, f32[768,256]{1,0:T(8,128)} %fusion.3, f32[256]{0:T(256)} %bitcast.161), kind=kOutput, calls=%fused_computation.4 | convolution fusion | flops 1614938112 | bytes 28050432 | tf_op jit(solution)/shard_map/dot_general | solution.py:90
  339.0 101.9 %reduce-scatter.3.cloned.1.call-done = f32[24,4096]{1,0:T(8,128)} async-done(((f32[768,4096]{1,0:T(8,128)}), f32[24,4096]{1,0:T(8,128)}) %reduce-scatter.3.cloned.1.call-update) | async-done | bytes 393232 | tf_op jit(solution)/shard_map/reduce_scatter | solution.py:153
  440.9 4.4 convolution_multiply_fusion
  445.6 58.8 %all-reduce.6.cloned.1.call-done = f32[128,4096]{1,0:T(8,128)} async-done(((f32[128,4096]{1,0:T(8,128)}), f32[128,4096]{1,0:T(8,128)}) %all-reduce.6.cloned.1.call-update) | async-done | bytes 2097168 | tf_op jit(solution)/shard_map/psum | solution.py:160
  504.4 2.2 multiply_reduce_fusion
  507.7 7.1 %multiply_reduce_fusion.2 = (f32[128,8]{0,1:T(8,128)}, f32[128,1024]{0,1:T(8,128)S(1)}) fusion(f32[128,8,128]{0,2,1:T(8,128)S(1)} %copy-done.13, bf16[1024,4096]{1,0:T(8,128)(2,1)} %param.25, f32[128,4096]{1,0:T(8,128)S(1)} %divide_add_fusion), kind=kOutput, calls=%fused_computation.76 | convolution fusion | flops 1074527232 | bytes 11538432 | tf_op jit(solution)/shard_map/dot_general | solution.py:165
  514.8 1.5 fusion.56
  517.5 1.6 fusion.95
  520.0 69.3 %all-gather.11.cloned.1.call-done = f32[256,128,128]{2,1,0:T(8,128)} async-done(((f32[8,128,128]{2,1,0:T(8,128)}), f32[256,128,128]{2,1,0:T(8,128)}) %all-gather.11.cloned.1.call-update) | async-done | bytes 16777232 | tf_op jit(solution)/shard_map/all_gather | solution.py:18
  589.4 57.3 %while.27 = (s32[]{:T(128)}, f32[8,128,128]{2,1,0:T(8,128)S(1)}, s32[]{:T(128)}, f32[32,8]{1,0:T(8,128)}, f32[32,8,128,128]{3,2,1,0:T(8,128)}, /*index=5*/s32[]{:T(128)}, s32[]{:T(128)}, s32[]{:T(128)}, s32[]{:T(128)}) while((s32[]{:T(128)}, f32[8,128,128]{2,1,0:T(8,128)S(1)}, s32[]{:T(128)}, f32[32,8]{1,0:T(8,128)}, ...), condition=%wide.region_10.11_spmd, body=%wide.region_9.10_spmd.sunk | while | flops 262150 | bytes 1573107 | solution.py:27
  592.0 1.2 bitcast_add_fusion.10
  593.9 1.2 bitcast_add_fusion.10
  597.7 1.2 bitcast_add_fusion.10
  601.5 1.2 bitcast_add_fusion.10
  607.2 1.2 bitcast_add_fusion.10
  609.1 1.2 bitcast_add_fusion.10
  611.1 1.2 bitcast_add_fusion.10
  616.8 1.2 bitcast_add_fusion.10
  618.7 1.2 bitcast_add_fusion.10
  620.6 1.2 bitcast_add_fusion.10
  628.2 1.2 bitcast_add_fusion.10
  630.0 1.2 bitcast_add_fusion.10
  631.9 1.2 bitcast_add_fusion.10
  633.8 1.2 bitcast_add_fusion.10
  635.7 1.2 bitcast_add_fusion.10
  649.3 2.2 fusion.28
  652.5 6.5 fusion.142
  660.3 1.8 convolution_add_fusion.1
  662.1 27.6 %reduce-scatter.5.cloned.1.call-done = f32[128,1024]{1,0:T(8,128)} async-done(((f32[128,4096]{1,0:T(8,128)}), f32[128,1024]{1,0:T(8,128)}) %reduce-scatter.5.cloned.1.call-update) | async-done | bytes 524304 | tf_op jit(solution)/shard_map/reduce_scatter | solution.py:184
  689.8 2.0 subtract_convert_fusion
  (163 shorter events, 57.4 us)
Async XLA Ops:
  6.5 306.4 %copy-start = (bf16[1,4096,256]{2,1,0:T(8,128)(2,1)S(1)}, bf16[1,4096,256]{2,1,0:T(8,128)(2,1)}, u32[]{:S(2)}) copy-start(bf16[1,4096,256]{2,1,0:T(8,128)(2,1)} %param.29) | copy-start | bytes 6291460
  6.5 7.0 %copy-start.2 = (bf16[128,4096]{1,0:T(8,128)(2,1)S(1)}, bf16[128,4096]{1,0:T(8,128)(2,1)}, u32[]{:S(2)}) copy-start(bf16[128,4096]{1,0:T(8,128)(2,1)} %param.18) | copy-start | bytes 3145732
  6.5 91.4 %all-gather.9.cloned.1.call-start = ((), (), s32[]{:S(2)}) async-start(), calls=%async_computation.7 | async-start | bytes 17301504 | tf_op jit(solution)/shard_map/all_gather | solution.py:18
  10.5 0.6 copy-start.21
  13.6 432.0 %copy-start.9 = (f32[128,256]{1,0:T(8,128)}, f32[128,256]{1,0:T(8,128)S(1)}, u32[]{:S(2)}) copy-start(f32[128,256]{1,0:T(8,128)S(1)} %fusion.140) | copy-start | bytes 393220
  21.6 231.8 %all-reduce.4.cloned.1.call-start = ((), (), s32[]{:S(2)}) async-start(), calls=%async_computation.2 | async-start | bytes 4194304 | tf_op jit(solution)/shard_map/psum | solution.py:141
  103.3 0.8 copy-start.12
  112.1 194.7 %all-gather.7.cloned.1.call-start = ((), (), s32[]{:S(2)}) async-start(), calls=%async_computation.3 | async-start | bytes 6488064 | tf_op jit(solution)/shard_map/all_gather | solution.py:151
  253.4 2.7 copy-start.5
  253.4 2.7 copy-start.28
  253.4 2.7 copy-start.29
  253.4 2.7 copy-start.30
  255.5 0.5 copy-start.25
  257.2 183.7 %reduce-scatter.3.cloned.1.call-start = ((), (), s32[]{:S(2)}) async-start(), calls=%async_computation.4 | async-start | bytes 12976128 | tf_op jit(solution)/shard_map/reduce_scatter | solution.py:153
  338.9 165.5 %all-reduce.6.cloned.1.call-start = ((), (), s32[]{:S(2)}) async-start(), calls=%async_computation.5 | async-start | bytes 4194304 | tf_op jit(solution)/shard_map/psum | solution.py:160
  440.9 63.6 %copy-start.6 = (f32[128,4096]{1,0:T(8,128)S(1)}, f32[128,4096]{1,0:T(8,128)}, u32[]{:S(2)}) copy-start(f32[128,4096]{1,0:T(8,128)} %all-reduce.4.cloned.1.call-done) | copy-start | bytes 6291460
  445.3 144.1 %all-gather.11.cloned.1.call-start = ((), (), s32[]{:S(2)}) async-start(), calls=%async_computation.8 | async-start | bytes 17301504 | tf_op jit(solution)/shard_map/all_gather | solution.py:18
  445.6 61.1 %copy-start.18 = (f32[4096]{0:T(1024)S(1)}, f32[4096]{0:T(1024)}, u32[]{:S(2)}) copy-start(f32[4096]{0:T(1024)} %param.31) | copy-start | bytes 49156
  445.6 61.1 %copy-start.26 = (f32[128]{0:T(128)S(1)}, f32[128]{0:T(128)}, u32[]{:S(2)}) copy-start(f32[128]{0:T(128)} %copy-done.25) | copy-start | bytes 1540
  504.4 2.2 copy-start.8
  506.7 1.0 copy-start.13
  507.7 7.1 %copy-start.4 = (f32[128,4096]{1,0:T(8,128)}, f32[128,4096]{1,0:T(8,128)S(1)}, u32[]{:S(2)}) copy-start(f32[128,4096]{1,0:T(8,128)S(1)} %divide_add_fusion) | copy-start | bytes 6291460
  507.7 7.1 %slice-start = ((f32[128,256]{1,0:T(8,128)}), f32[128,128]{1,0:T(8,128)S(1)}, s32[]{:S(2)}) async-start(f32[128,256]{1,0:T(8,128)} %copy-done.9), calls=%async_computation.9 | async-start | bytes 131072 | tf_op jit(solution)/shard_map/slice | solution.py:121
  507.7 8.7 %copy-start.3 = (f32[8,128,128]{2,1,0:T(8,128)S(1)}, f32[8,128,128]{2,1,0:T(8,128)}, u32[]{:S(2)}) copy-start(f32[8,128,128]{2,1,0:T(8,128)} %get-tuple-element.133) | copy-start | bytes 1572868
  514.8 2.7 copy-start.11
  514.8 2.7 copy-start.15
  514.8 2.7 copy-start.16
  514.8 2.7 copy-start.19
  516.4 2.7 copy-start.10
  516.4 173.4 %reduce-scatter.5.cloned.1.call-start = ((), (), s32[]{:S(2)}) async-start(), calls=%async_computation.6 | async-start | bytes 2621440 | tf_op jit(solution)/shard_map/reduce_scatter | solution.py:184
  646.7 2.6 copy-start.20
  649.0 2.5 copy-start.27
  649.0 2.8 copy-start.22
  652.5 6.6 copy-start.7
  652.5 6.6 copy-start.17
  659.1 0.9 copy-start.23
  659.1 0.9 copy-start.24
  659.1 0.9 copy-start.31
  659.1 0.9 copy-start.32
  659.1 0.9 copy-start.33
  659.1 0.9 copy-start.34
  659.2 1.1 copy-start.14
  660.3 31.5 %copy-start.1 = (bf16[1,4096,256]{2,1,0:T(8,128)(2,1)S(1)}, bf16[1,4096,256]{2,1,0:T(8,128)(2,1)}, u32[]{:S(2)}) copy-start(bf16[1,4096,256]{2,1,0:T(8,128)(2,1)} %param.29) | copy-start | bytes 6291460
Sparse Core Ops, SparseCore 0:
  21.7 76.2 all-gather.8
  112.2 141.1 all-reduce.3
  257.3 49.4 all-gather.6
  339.1 101.7 reduce-scatter.2
  445.4 58.9 all-reduce.5
  516.5 72.7 all-gather.10
  662.2 27.4 reduce-scatter.4
where the time goes:
time: 702 us; the launch traced here: 699 us
  waiting for transfers between devices  491 us (70%)
  matrix products  90.9 us (13%)
  other arithmetic  48.7 us (7%)
  local copies, waits for them, and re-layouts  26.9 us (4%)
  blocking collectives  25.5 us (4%)
  between operations  14 us (2%)
    psum x1, waiting for transfers between devices, shards(): mix_sum = lax.psum(partial_mix, 'exp')  138 us
    all_gather x2, waiting for transfers between devices, carried_in(): gathered = jax.tree.map(lambda a: lax.all_gather(a, axis), part)  119 us
    reduce_scatter x1, waiting for transfers between devices, shards(): lax.psum_scatter(expert_terms(gathered, expert_gate[0], expert_up[0], hea...  102 us
    psum x1, waiting for transfers between devices, shards(): token_grad = lax.psum(token_part, 'exp')  58.8 us
    all_gather x1, waiting for transfers between devices, shards(): gathered = lax.all_gather(slot_rows, 'seq', axis=0, tiled=True)  45.5 us
    add x31, other arithmetic, chain_combine(): later[0][:, None, None] * earlier[1] + later[1]  37.6 us
    reduce_scatter x1, waiting for transfers between devices, shards(): lax.psum_scatter(partial_grad, 'exp', scatter_dimension=1, tiled=True)  27.6 us
    all_gather x1, blocking collectives, carried_in(): gathered = jax.tree.map(lambda a: lax.all_gather(a, axis), part)  25.5 us
  transfers between devices with their start and end apart: 7, of which 7 were waited for; matrix products, arithmetic and copies ran while one was open for 2% of the time, Pallas kernels for 0%

commit v1 on v0

v1 whole, which is shorter than its diff:
```python
import functools

import jax
import jax.numpy as jnp
import numpy as np
from jax import lax
from jax.experimental import pallas as pl
from jax.experimental.pallas import tpu as pltpu
from jax.sharding import Mesh
from jax.sharding import PartitionSpec as P

CAP = 24
EPS = 1e-05
DESCENT = 0.5
HIGH = lax.Precision.HIGHEST
BF = jnp.bfloat16
F32 = jnp.float32
SEQ = ("x", "z", "c")
PLANE = ("x", "z")
EXTRA = 8


def mm(a, b):
    return jnp.dot(a, b, preferred_element_type=F32)


def mm_t(a, b):
    return lax.dot_general(a, b, (((1,), (1,)), ((), ())), preferred_element_type=F32)


def t_mm(a, b):
    return lax.dot_general(a, b, (((0,), (0,)), ((), ())), preferred_element_type=F32)


def shift(value, axis, by):
    count = lax.axis_size(axis)
    return lax.ppermute(value, axis, [(i, (i + by) % count) for i in range(count)])


def lower_mask(tlen):
    rowpos = lax.broadcasted_iota(jnp.int32, (tlen, tlen), 0)
    colpos = lax.broadcasted_iota(jnp.int32, (tlen, tlen), 1)
    return rowpos >= colpos


def slot_table(ids_rows, gate_rows, expert):
    tlen = ids_rows.shape[0]
    match = ids_rows == expert
    hits = jnp.sum(match.astype(F32), axis=1)
    weight = jnp.sum(jnp.where(match, gate_rows.astype(F32), 0.0), axis=1)
    rowpos = lax.broadcasted_iota(jnp.int32, (tlen, tlen), 0)
    colpos = lax.broadcasted_iota(jnp.int32, (tlen, tlen), 1)
    places = jnp.sum(jnp.where(rowpos > colpos, hits[None, :], 0.0), axis=1)
    slot_pos = lax.broadcasted_iota(jnp.int32, (CAP, tlen), 0).astype(F32)
    table = (places[None, :] == slot_pos) & (hits[None, :] > 0.0)
    return table.astype(F32), weight


def expert_kernel(rows_ref, wg0, wg1, wu0, wu1, hv_ref, out_ref, first, second):
    half = wg0.shape[1]
    rows = rows_ref[...]
    for k, (wg, wu) in enumerate(((wg0, wu0), (wg1, wu1))):
        span = slice(k * half, (k + 1) * half)
        gate = mm(rows, wg[...])
        up = mm(rows, wu[...])
        sig = 1.0 / (1.0 + jnp.exp(-gate))
        hv = hv_ref[k : k + 1, :]
        first[:, span] = (hv * up * sig * (1.0 + gate * (1.0 - sig))).astype(BF)
        second[:, span] = (hv * gate * sig).astype(BF)
    width = rows.shape[1]
    step = min(width, 512)

    @pl.loop(0, width // step)
    def _(i):
        cols = pl.ds(pl.multiple_of(i * step, step), step)
        total = mm_t(first[:, :half], wg0[cols, :]) + mm_t(second[:, :half], wu0[cols, :])
        total += mm_t(first[:, half:], wg1[cols, :]) + mm_t(second[:, half:], wu1[cols, :])
        out_ref[:, cols] = total.astype(BF)


def expert_rows(rows, wg0, wg1, wu0, wu1, head_vec):
    count, width = rows.shape
    half = wg0.shape[1]
    return pl.pallas_call(
        expert_kernel,
        out_shape=jax.ShapeDtypeStruct((count, width), BF),
        in_specs=[pl.BlockSpec(memory_space=pltpu.VMEM)] * 6,
        out_specs=pl.BlockSpec(memory_space=pltpu.VMEM),
        scratch_shapes=[pltpu.VMEM((count, 2 * half), BF)] * 2,
        compiler_params=pltpu.CompilerParams(vmem_limit_bytes=48 << 20),
        cost_estimate=pl.CostEstimate(
            flops=16 * count * width * half,
            bytes_accessed=8 * width * half + 4 * count * width,
            transcendentals=2 * count * half,
        ),
        name="experts",
    )(rows, wg0, wg1, wu0, wu1, head_vec)


def shards(
    candidate,
    in_proj,
    bc_proj,
    step_proj,
    step_bias,
    decay_rate,
    skip_gain,
    out_proj,
    expert_ids,
    gate_weights,
    expert_gate,
    expert_up,
    expert_down,
    energy_head,
):
    tlen, width = candidate.shape
    heads = step_bias.shape[0]
    chan = in_proj.shape[1]
    size = chan // heads
    nstate = bc_proj.shape[1] // 2
    column = lax.axis_index("e")
    n_exp = lax.axis_size("e")
    n_seq = lax.axis_size(SEQ)
    n_plane = lax.axis_size(PLANE)
    col_count = width // n_exp
    slice_rows = chan // n_seq

    def spread(v):
        return jnp.repeat(v, size, axis=1)

    wg0, wu0 = expert_gate[0], expert_up[0]
    head_own = jnp.sum(expert_down[0].astype(F32) * energy_head[None, :], axis=1)
    wg1 = shift(wg0, "c", 1)
    wu1 = shift(wu0, "c", 1)
    head_other = shift(head_own[None, :], "c", 1)
    head_vec = jnp.concatenate([head_own[None, :], head_other], axis=0)

    inner_b = mm(candidate, in_proj).astype(BF)
    bc_val = mm(candidate, bc_proj)
    b_bf = bc_val[:, :nstate].astype(BF)
    c_bf = bc_val[:, nstate:].astype(BF)
    pre = mm(candidate, step_proj) + step_bias[None, :]
    step = jax.nn.softplus(pre)
    lower = lower_mask(tlen)
    cum = jnp.dot(lower.astype(F32), -step * decay_rate[None, :], precision=HIGH)
    last = cum[-1]
    growth = jnp.exp(cum)
    fade = jnp.exp(last[None, :] - cum)
    tail = fade * step
    inner = inner_b.astype(F32)
    fed = (spread(tail) * inner).astype(BF)
    fresh = t_mm(fed, b_bf).astype(BF)

    hi = lax.reduce_precision(last, 8, 7)
    mid = lax.reduce_precision(last - hi, 8, 7)
    low = last - hi - mid
    parts = jnp.stack([hi, mid, low] + [jnp.zeros_like(hi)] * (EXTRA - 3), axis=1)
    parts = jnp.repeat(parts, n_seq // heads, axis=0)[:, :, None]
    payload = jnp.concatenate(
        [
            fresh.reshape(n_seq, slice_rows, nstate),
            jnp.broadcast_to(parts, (n_seq, EXTRA, nstate)).astype(BF),
        ],
        axis=1,
    )
    got = lax.all_to_all(payload, SEQ, 0, 0, tiled=True)
    lasts = jnp.sum(got[:, slice_rows : slice_rows + 3, 0].astype(F32), axis=1)
    blk_row = lax.broadcasted_iota(jnp.int32, (n_seq, n_seq), 0)
    blk_col = lax.broadcasted_iota(jnp.int32, (n_seq, n_seq), 1)
    upto = jnp.sum(jnp.where(blk_row >= blk_col, lasts[None, :], 0.0), axis=1)
    before = jnp.sum(jnp.where(blk_row > blk_col, lasts[None, :], 0.0), axis=1)
    carry = jnp.where(
        blk_row > blk_col, jnp.exp(jnp.minimum(before[:, None] - upto[None, :], 0.0)), 0.0
    )
    entering = jnp.dot(
        carry, got[:, :slice_rows].reshape(n_seq, slice_rows * nstate).astype(F32), precision=HIGH
    )
    state = lax.all_to_all(
        entering.astype(BF).reshape(n_seq, slice_rows, nstate), SEQ, 0, 0, tiled=True
    ).reshape(chan, nstate)

    scores = mm_t(c_bf, b_bf)
    cum_t = cum.T
    weights = jnp.where(
        lower[None], jnp.exp(jnp.minimum(cum_t[:, :, None] - cum_t[:, None, :], 0.0)), 0.0
    )
    step_t = step.T
    mixing = (weights * scores[None] * step_t[:, None, :]).astype(BF)
    inner_h = inner_b.reshape(tlen, heads, size)
    within = jnp.einsum("hts,shp->thp", mixing, inner_h, preferred_element_type=F32)
    reads = mm_t(c_bf, state)
    growth_w = spread(growth)
    mixed = (
        within.reshape(tlen, chan) + growth_w * reads + spread(skip_gain[None, :]) * inner
    ).astype(BF)

    pairs = [
        slot_table(expert_ids, gate_weights, lax.rem(column + k, n_exp)) for k in range(n_exp)
    ]
    table = jnp.concatenate([p[0] for p in pairs], axis=0).astype(BF)
    own_table, own_weight = pairs[0]
    slot_weight = jnp.sum(own_table * own_weight[None, :], axis=1, keepdims=True)
    mixed_slots = mm(table, mixed).astype(BF)
    part = mm(mixed_slots, out_proj)
    mix_sum = part[:CAP]
    for k in range(1, n_exp):
        mix_sum = mix_sum + shift(part[k * CAP : (k + 1) * CAP].astype(BF), "e", k).astype(F32)
    own_rows = mm(own_table.astype(BF), candidate)
    hidden = (own_rows + mix_sum).astype(BF).astype(F32)
    scale = jnp.sqrt(jnp.mean(hidden * hidden, axis=-1, keepdims=True) + EPS)
    normed = hidden / scale
    routed = normed.astype(BF)

    rows = lax.all_to_all(
        jnp.broadcast_to(routed[None], (n_plane, CAP, width)), PLANE, 0, 0, tiled=True
    ).reshape(n_plane * CAP, width)
    terms = expert_rows(rows, wg0, wg1, wu0, wu1, head_vec)
    back = lax.all_to_all(terms.reshape(n_plane, CAP, width), PLANE, 0, 0, tiled=True)
    slot_grad = jnp.sum(back.astype(F32), axis=0)
    along = jnp.mean(normed * slot_grad, axis=-1, keepdims=True)
    slot_term = (slot_weight * (slot_grad - normed * along) / scale).astype(BF)
    all_terms = jnp.concatenate(
        [slot_term] + [shift(slot_term, "e", n_exp - k) for k in range(1, n_exp)], axis=0
    )
    hid_grad = energy_head[None, :] + t_mm(table, all_terms)
    hid_cols = lax.dynamic_slice_in_dim(hid_grad, column * col_count, col_count, 1)
    out_grad = mm_t(hid_grad.astype(BF), out_proj)
    grad_b = out_grad.astype(BF)

    grown = (growth_w * out_grad).astype(BF)
    local_grad = t_mm(grown, c_bf).astype(BF)
    got_grad = lax.all_to_all(
        local_grad.reshape(n_seq, slice_rows, nstate), SEQ, 0, 0, tiled=True
    ).reshape(n_seq, slice_rows * nstate)
    leaving = lax.dot_general(
        carry, got_grad.astype(F32), (((0,), (0,)), ((), ())), precision=HIGH
    )
    later = lax.all_to_all(
        leaving.astype(BF).reshape(n_seq, slice_rows, nstate), SEQ, 0, 0, tiled=True
    ).reshape(chan, nstate)

    def per_head(v):
        return jnp.sum(v.reshape(tlen, heads, size), axis=2)

    grad_h = grad_b.reshape(tlen, heads, size)
    d_mix = jnp.einsum("thp,shp->hts", grad_h, inner_h, preferred_element_type=F32)
    d_w = d_mix * weights
    d_scores = jnp.sum(d_w * step_t[:, None, :], axis=0).astype(BF)
    d_ws = d_w * scores[None]
    d_step_in = jnp.sum(d_ws, axis=1).T
    d_gap_rows = jnp.sum(d_ws * step_t[:, None, :], axis=2).T
    fed_back = mm_t(b_bf, later)
    g_within = jnp.einsum("hts,thp->shp", mixing, grad_h, preferred_element_type=F32)
    g_inner = (
        g_within.reshape(tlen, chan)
        + spread(skip_gain[None, :]) * out_grad
        + spread(tail) * fed_back
    ).astype(BF)
    g_c = mm(d_scores, b_bf) + mm(grown, state)
    g_b = t_mm(d_scores, c_bf) + mm(fed, later)
    d_tail = per_head(inner * fed_back)
    tail_term = d_tail * tail
    kept = jnp.sum(
        (state.astype(F32) * later.astype(F32)).reshape(heads, size * nstate), axis=1
    )
    d_last = jnp.exp(last) * kept + jnp.sum(tail_term, axis=0)
    d_cum = d_gap_rows - step * d_step_in + growth * per_head(out_grad * reads) - tail_term
    is_last = lax.broadcasted_iota(jnp.int32, (tlen, heads), 0) == tlen - 1
    d_cum = d_cum + jnp.where(is_last, d_last[None, :], 0.0)
    d_decay = lax.dot_general(
        lower.astype(F32), d_cum, (((0,), (0,)), ((), ())), precision=HIGH
    )
    g_step = d_step_in + fade * d_tail - decay_rate[None, :] * d_decay
    g_pre = (g_step * jax.nn.sigmoid(pre)).astype(BF)
    g_bc = jnp.concatenate([g_b, g_c], axis=1).astype(BF)
    partial_grad = mm_t(g_inner, in_proj) + mm_t(g_bc, bc_proj) + mm_t(g_pre, step_proj)

    def cols_of(k):
        start = lax.rem(column + k, n_exp) * col_count
        return lax.dynamic_slice_in_dim(partial_grad, start, col_count, 1)

    summed = hid_cols + cols_of(0)
    for k in range(1, n_exp):
        summed = summed + shift(cols_of(k).astype(BF), "e", k).astype(F32)
    own_cand = lax.dynamic_slice_in_dim(candidate, column * col_count, col_count, 1).astype(F32)
    return (own_cand - DESCENT * summed).astype(BF)


def solution(mesh):
    n_seq, n_exp = mesh.devices.shape
    side = int(round((n_seq // 2) ** 0.5))
    grid = Mesh(mesh.devices.reshape(side, side, 2, n_exp), ("x", "z", "c", "e"))
    in_specs = (
        P(SEQ, None),
        P(None, "e"),
        P(),
        P(None, "e"),
        P("e"),
        P("e"),
        P("e"),
        P("e", None),
        P(SEQ, None),
        P(SEQ, None),
        P("e", None, SEQ),
        P("e", None, SEQ),
        P("e", SEQ, None),
        P(),
    )
    return jax.shard_map(
        shards, mesh=grid, in_specs=in_specs, out_specs=P(SEQ, "e"), check_vma=False
    )
```

time: 702 us -> 300 us (0.43)
  waiting for transfers between devices: 491 us -> 114 us
  starting transfers between devices: 0.65 us -> 60.2 us
  matrix products: 90.9 us -> 54.5 us
  blocking collectives: 25.5 us -> 0 us
  other arithmetic: 48.7 us -> 26.2 us
  between operations: 14 us -> 0.66 us
  Pallas kernels: 0 us -> 13.2 us
    psum x2 -> x0, waiting for transfers between devices: 197 us -> none  [the longest x1 138 us: shards(): mix_sum = lax.psum(partial_mix, 'exp')]
    all_gather x3 -> x0, waiting for transfers between devices: 164 us -> none  [the longest x2 119 us: carried_in(): gathered = jax.tree.map(lambda a: lax.all_gather(a, axis), part)]
    reduce_scatter x2 -> x0, waiting for transfers between devices: 130 us -> none  [the longest x1 102 us: shards(): lax.psum_scatter(expert_terms(gathered, expert_gate[0], expert_up[0], hea...]
    all_to_all x0 -> x6, waiting for transfers between devices: none -> 81.4 us  [the longest x1 35.9 us: shards(): lax.all_to_all(terms.reshape(n_plane, CAP, width), PLANE, 0, 0, tiled=True)]
    all_to_all x0 -> x6, starting transfers between devices: none -> 41.2 us  [the longest x1 9.82 us: shards(): lax.all_to_all(local_grad.reshape(n_seq, slice_rows, nstate), SEQ, 0, 0,...]
    add x32 -> x1, other arithmetic: 38.2 us -> 0.19 us  [shards(): d_last = jnp.exp(last) * kept + jnp.sum(tail_term, axis=0)]
    dot_general x29 -> x26, matrix products: 90.9 us -> 54.5 us  [the longest x8 21.4 us: mm(): return jnp.dot(a, b, preferred_element_type=F32)]
    ppermute x0 -> x12, waiting for transfers between devices: none -> 32.4 us  [shift(): lax.ppermute(value, axis, [(i, (i + by) % count) for i in range(count)])]
  transfers between devices with their start and end apart: 7 -> 18, of which waited for: 7 -> 15; matrix products, arithmetic and copies ran while one was open for 2% -> 9% of each run, Pallas kernels for 0% -> 0%
where the time goes in v1:
time: 300 us; the launch traced here: 298 us
  waiting for transfers between devices  114 us (38%)
  starting transfers between devices  60.2 us (20%)
  matrix products  54.5 us (18%)
  local copies, waits for them, and re-layouts  29.5 us (10%)
  other arithmetic  26.2 us (9%)
  Pallas kernels  13.2 us (4%)
    all_to_all x1, waiting for transfers between devices, shards(): lax.all_to_all(terms.reshape(n_plane, CAP, width), PLANE, 0, 0, tiled=True)  35.9 us
    ppermute x12, waiting for transfers between devices, shift(): lax.ppermute(value, axis, [(i, (i + by) % count) for i in range(count)])  32.4 us
    all_to_all x1, waiting for transfers between devices, shards(): lax.all_to_all(jnp.broadcast_to(routed[None], (n_plane, CAP, width)), PLA...  31.9 us
    dot_general x8, matrix products, mm(): return jnp.dot(a, b, preferred_element_type=F32)  21.4 us
    dot_general x7, matrix products, mm_t(): lax.dot_general(a, b, (((1,), (1,)), ((), ())), preferred_element_type=F32)  19.4 us
    ppermute x12, starting transfers between devices, shift(): lax.ppermute(value, axis, [(i, (i + by) % count) for i in range(count)])  19 us
    pallas_call x1, Pallas kernels, expert_rows(): pl.pallas_call(expert_kernel, out_shape=jax.ShapeDtypeStruct((count, widt...  13.2 us
    unnamed x96, local copies, waits for them, and re-layouts  11.4 us
  transfers between devices with their start and end apart: 18, of which 15 were waited for; matrix products, arithmetic and copies ran while one was open for 9% of the time, Pallas kernels for 0%

profile of v1, /device:TPU:1, one launch (start us, length us, event | category | flops | bytes accessed | tf_op | source)
XLA Modules:
  0.0 298.0 jit_solution(15779058958471425618)
XLA Ops:
  0.0 2.4 compare_select_fusion
  4.2 1.7 convolution_convert_fusion.6
  5.9 4.6 %convolution_convert_fusion.4 = bf16[128,1024]{1,0:T(8,128)(2,1)S(1)} fusion(bf16[128,4096]{1,0:T(8,128)(2,1)S(1)} %copy-done.4, bf16[4096,1024]{1,0:T(8,128)(2,1)} %param.15), kind=kOutput, calls=%fused_computation.11 | convolution fusion | flops 1073872896 | bytes 9699328 | tf_op jit(solution)/shard_map/dot_general | solution.py:24
  15.4 1.7 pad_maximum_fusion
  17.1 9.5 %all-to-all-start = ((bf16[32,40,128]{2,1,0:T(8,128)(2,1)}), bf16[32,40,128]{2,1,0:T(8,128)(2,1)}, u32[]{:S(2)}, u32[]{:S(2)}) async-start(bf16[32,40,128]{2,1,0:T(8,128)(2,1)} %pad_maximum_fusion), calls=%async_computation | async-start | bytes 655360 | tf_op jit(solution)/shard_map/all_to_all | solution.py:166
  31.2 1.9 fusion.42
  33.1 3.2 %all-to-all-done = bf16[32,40,128]{2,1,0:T(8,128)(2,1)} async-done(((bf16[32,40,128]{2,1,0:T(8,128)(2,1)}), bf16[32,40,128]{2,1,0:T(8,128)(2,1)}, u32[]{:S(2)}, u32[]{:S(2)}) %all-to-all-start) | async-done | bytes 327712 | tf_op jit(solution)/shard_map/all_to_all | solution.py:166
  39.8 4.4 %all-to-all-start.1 = ((bf16[32,32,128]{2,1,0:T(8,128)(2,1)}), bf16[32,32,128]{2,1,0:T(8,128)(2,1)}, u32[]{:S(2)}, u32[]{:S(2)}) async-start(bf16[32,32,128]{2,1,0:T(8,128)(2,1)} %bitcast.163), calls=%async_computation.1 | async-start | bytes 524288 | tf_op jit(solution)/shard_map/all_to_all | solution.py:178
  44.7 2.0 copy.73
  48.2 4.9 %all-to-all-done.1 = bf16[32,32,128]{2,1,0:T(8,128)(2,1)} async-done(((bf16[32,32,128]{2,1,0:T(8,128)(2,1)}), bf16[32,32,128]{2,1,0:T(8,128)(2,1)}, u32[]{:S(2)}, u32[]{:S(2)}) %all-to-all-start.1) | async-done | bytes 262176 | tf_op jit(solution)/shard_map/all_to_all | solution.py:178
  53.1 2.0 fusion.64
  56.1 6.9 %fusion.116 = (bf16[96,4096]{1,0:T(8,128)(2,1)}, f32[96,4096]{1,0:T(8,128)}) fusion(bf16[1024,4096]{1,0:T(8,128)(2,1)} %param.21, bf16[128,1024]{1,0:T(8,128)(2,1)S(1)} %convolution_convert_fusion.4, f32[128,1024]{1,0:T(8,128)} %copy.73, f32[128,1024]{1,0:T(8,128)} %fusion.64, f32[16,8,8,128]{3,2,1,0:T(8,128)} %bitcast.158, ...), kind=kOutput, calls=%fused_computation.199 | convolution fusion | flops 831848448 | bytes 12611584 | tf_op jit(solution)/shard_map/dot_general | solution.py:24
  65.5 2.6 collective-permute-start.1
  69.2 2.7 collective-permute-done
  71.9 5.3 %collective-permute-done.1 = bf16[24,4096]{1,0:T(8,128)(2,1)S(1)} collective-permute-done((bf16[24,4096]{1,0:T(8,128)(2,1)S(1)}, bf16[24,4096]{1,0:T(8,128)(2,1)S(1)}, u32[]{:S(2)}, u32[]{:S(2)}) %collective-permute-start.1) | collective-permute-done | bytes 196640 | tf_op jit(solution)/shard_map/ppermute | solution.py:37
  79.5 2.0 broadcast_in_dim.156
  81.5 4.6 %all-to-all-start.2 = ((bf16[16,24,4096]{2,1,0:T(8,128)(2,1)}), bf16[16,24,4096]{2,1,0:T(8,128)(2,1)}, u32[]{:S(2)}, u32[]{:S(2)}) async-start(bf16[16,24,4096]{2,1,0:T(8,128)(2,1)} %broadcast_in_dim.156), calls=%async_computation.2 | async-start | bytes 6291456 | tf_op jit(solution)/shard_map/all_to_all | solution.py:214
  87.3 2.1 fusion
  90.1 3.0 collective-permute-done.5
  94.6 31.9 %all-to-all-done.2 = bf16[16,24,4096]{2,1,0:T(8,128)(2,1)} async-done(((bf16[16,24,4096]{2,1,0:T(8,128)(2,1)}), bf16[16,24,4096]{2,1,0:T(8,128)(2,1)}, u32[]{:S(2)}, u32[]{:S(2)}) %all-to-all-start.2) | async-done | bytes 3145760 | tf_op jit(solution)/shard_map/all_to_all | solution.py:214
  126.5 1.6 copy-done.1
  128.1 1.6 copy-done.3
  129.7 13.2 %experts.1 = bf16[384,4096]{1,0:T(8,128)(2,1)} custom-call(bf16[384,4096]{1,0:T(8,128)(2,1)} %bitcast.8.rows_ref, bf16[4096,256]{1,0:T(8,128)(2,1)S(1)} %bitcast.154, bf16[4096,256]{1,0:T(8,128)(2,1)S(1)} %copy-done.3, bf16[4096,256]{1,0:T(8,128)(2,1)} %bitcast.179, bf16[4096,256]{1,0:T(8,128)(2,1)} %collective-permute-done.4.wu1, ...), custom_call_target="tpu_custom_call" | custom-call | flops 6442450944 | bytes 14680064 | tf_op jit(solution)/shard_map/experts/pallas_call | solution.py:84
  142.8 8.4 %all-to-all-start.3 = ((bf16[16,24,4096]{2,1,0:T(8,128)(2,1)}), bf16[16,24,4096]{2,1,0:T(8,128)(2,1)}, u32[]{:S(2)}, u32[]{:S(2)}) async-start(bf16[16,24,4096]{2,1,0:T(8,128)(2,1)} %bitcast.160), calls=%async_computation.3 | async-start | bytes 6291456 | tf_op jit(solution)/shard_map/all_to_all | solution.py:218
  151.4 35.9 %all-to-all-done.3 = bf16[16,24,4096]{2,1,0:T(8,128)(2,1)} async-done(((bf16[16,24,4096]{2,1,0:T(8,128)(2,1)}), bf16[16,24,4096]{2,1,0:T(8,128)(2,1)}, u32[]{:S(2)}, u32[]{:S(2)}) %all-to-all-start.3) | async-done | bytes 3145760 | tf_op jit(solution)/shard_map/all_to_all | solution.py:218
  187.3 2.5 convert_reduce_fusion
  190.9 10.0 %collective-permute-start.6 = (bf16[24,4096]{1,0:T(8,128)(2,1)}, bf16[24,4096]{1,0:T(8,128)(2,1)}, u32[]{:S(2)}, u32[]{:S(2)}) collective-permute-start(bf16[24,4096]{1,0:T(8,128)(2,1)} %divide_convert_fusion), channel_id=1, source_target_pairs={{0,3},{1,0},{2,1},{3,2},{4,7},{5,4},{6,5},{7,6},{8,11},{9,8},{10,9... | collective-permute-start | bytes 589832 | tf_op jit(solution)/shard_map/ppermute | solution.py:37
  202.0 3.9 %collective-permute-done.6 = bf16[24,4096]{1,0:T(8,128)(2,1)} collective-permute-done((bf16[24,4096]{1,0:T(8,128)(2,1)}, bf16[24,4096]{1,0:T(8,128)(2,1)}, u32[]{:S(2)}, u32[]{:S(2)}) %collective-permute-start.6) | collective-permute-done | bytes 196640 | tf_op jit(solution)/shard_map/ppermute | solution.py:37
  207.4 1.7 collective-permute-done.8
  209.1 1.7 convolution_add_fusion.2
  210.8 7.0 %fusion.9 = f32[128,1024]{1,0:T(8,128)S(1)} fusion(bf16[1024,4096]{1,0:T(8,128)(2,1)} %param.21, f32[128,4096]{1,0:T(8,128)S(1)} %convolution_add_fusion.2), kind=kOutput, calls=%fused_computation.26 | convolution fusion | flops 1074266112 | bytes 11010048 | tf_op jit(solution)/shard_map/dot_general | solution.py:28
  220.7 9.8 %all-to-all-start.4 = ((bf16[32,32,128]{2,1,0:T(8,128)(2,1)}), bf16[32,32,128]{2,1,0:T(8,128)(2,1)}, u32[]{:S(2)}, u32[]{:S(2)}) async-start(bf16[32,32,128]{2,1,0:T(8,128)(2,1)} %bitcast.165), calls=%async_computation.4 | async-start | bytes 524288 | tf_op jit(solution)/shard_map/all_to_all | solution.py:232
  231.8 2.2 fusion.39
  234.1 5.6 %all-to-all-done.4 = bf16[32,32,128]{2,1,0:T(8,128)(2,1)} async-done(((bf16[32,32,128]{2,1,0:T(8,128)(2,1)}), bf16[32,32,128]{2,1,0:T(8,128)(2,1)}, u32[]{:S(2)}, u32[]{:S(2)}) %all-to-all-start.4) | async-done | bytes 262176 | tf_op jit(solution)/shard_map/all_to_all | solution.py:232
  239.6 1.4 fusion.2
  241.8 4.6 %all-to-all-start.5 = ((bf16[32,32,128]{2,1,0:T(8,128)(2,1)}), bf16[32,32,128]{2,1,0:T(8,128)(2,1)}, u32[]{:S(2)}, u32[]{:S(2)}) async-start(bf16[32,32,128]{2,1,0:T(8,128)(2,1)} %bitcast.164), calls=%async_computation.5 | async-start | bytes 524288 | tf_op jit(solution)/shard_map/all_to_all | solution.py:238
  246.4 2.1 multiply_reduce_fusion.3
  249.5 1.9 reduce_sum.248
  251.4 1.5 copy.69
  252.9 2.0 copy.74
  254.9 1.6 fusion.5
  256.5 2.0 fusion.57
  259.9 1.9 multiply_reduce_fusion
  269.0 6.9 %fusion.31 = f32[128,4096]{1,0:T(8,128)S(1)} fusion(bf16[4096,1024]{1,0:T(8,128)(2,1)} %param.15, f32[128,1024]{1,0:T(8,128)} %fusion.57, f32[128,1024]{1,0:T(8,128)} %copy.74, f32[128,1024]{1,0:T(8,128)} %copy-done.10, f32[16,8,8,128]{3,2,1,0:T(8,128)} %bitcast.157, f32[1024]{0:T(1024)S(1)} %broadcast_bitcast_fusion), kind=kOutput, calls=%fused_computation.71 | convolution fusion | flops 1074397184 | bytes 12587008 | tf_op jit(solution)/shard_map/dot_general | solution.py:28
  281.5 7.8 %collective-permute-done.10 = bf16[128,1024]{1,0:T(8,128)(2,1)} collective-permute-done((bf16[128,1024]{1,0:T(8,128)(2,1)}, bf16[128,1024]{1,0:T(8,128)(2,1)}, u32[]{:S(2)}, u32[]{:S(2)}) %collective-permute-start.10) | collective-permute-done | bytes 262176 | tf_op jit(solution)/shard_map/ppermute | solution.py:37
  289.3 3.9 %collective-permute-done.11 = bf16[128,1024]{1,0:T(8,128)(2,1)} collective-permute-done((bf16[128,1024]{1,0:T(8,128)(2,1)}, bf16[128,1024]{1,0:T(8,128)(2,1)}, u32[]{:S(2)}, u32[]{:S(2)}) %collective-permute-start.11) | collective-permute-done | bytes 262176 | tf_op jit(solution)/shard_map/ppermute | solution.py:37
  293.2 2.5 collective-permute-done.9
  295.7 2.4 subtract_convert_fusion
  (168 shorter events, 50.3 us)
Async XLA Ops:
  0.0 4.2 %copy-start = (bf16[4096,256]{1,0:T(8,128)(2,1)S(1)}, bf16[4096,256]{1,0:T(8,128)(2,1)}, u32[]{:S(2)}) copy-start(bf16[4096,256]{1,0:T(8,128)(2,1)} %param.16) | copy-start | bytes 6291460
  0.0 5.9 %copy-start.4 = (bf16[128,4096]{1,0:T(8,128)(2,1)S(1)}, bf16[128,4096]{1,0:T(8,128)(2,1)}, u32[]{:S(2)}) copy-start(bf16[128,4096]{1,0:T(8,128)(2,1)} %param.14) | copy-start | bytes 3145732
  2.4 1.7 copy-start.26
  3.2 28.0 %copy-start.22 = (f32[128,8]{0,1:T(8,128)}, f32[128,8]{0,1:T(8,128)S(1)}, u32[]{:S(2)}) copy-start(f32[128,8]{0,1:T(8,128)S(1)} %fusion.55) | copy-start | bytes 12292
  17.1 19.2 %all-to-all-start = ((bf16[32,40,128]{2,1,0:T(8,128)(2,1)}), bf16[32,40,128]{2,1,0:T(8,128)(2,1)}, u32[]{:S(2)}, u32[]{:S(2)}) async-start(bf16[32,40,128]{2,1,0:T(8,128)(2,1)} %pad_maximum_fusion), calls=%async_computation | async-start | bytes 655360 | tf_op jit(solution)/shard_map/all_to_all | solution.py:166
  31.2 15.5 %copy-start.29 = (pred[128,128]{1,0:T(8,128)(4,1)}, pred[128,128]{1,0:T(8,128)(4,1)S(1)}, u32[]{:S(2)}) copy-start(pred[128,128]{1,0:T(8,128)(4,1)S(1)} %iota_compare_fusion) | copy-start | bytes 49156
  33.1 13.7 %copy-start.30 = (f32[128]{0:T(128)S(1)}, f32[128]{0:T(128)}, u32[]{:S(2)}) copy-start(f32[128]{0:T(128)} %get-tuple-element.42) | copy-start | bytes 1540
  37.6 9.1 %copy-start.41 = (f32[32]{0:T(128)}, f32[32]{0:T(128)S(1)}, u32[]{:S(2)}) copy-start(f32[32]{0:T(128)S(1)} %get-tuple-element.14) | copy-start | bytes 388
  37.6 9.2 %copy-start.39 = (f32[32]{0:T(128)}, f32[32]{0:T(128)S(1)}, u32[]{:S(2)}) copy-start(f32[32]{0:T(128)S(1)} %get-tuple-element.13) | copy-start | bytes 388
  39.8 13.3 %all-to-all-start.1 = ((bf16[32,32,128]{2,1,0:T(8,128)(2,1)}), bf16[32,32,128]{2,1,0:T(8,128)(2,1)}, u32[]{:S(2)}, u32[]{:S(2)}) async-start(bf16[32,32,128]{2,1,0:T(8,128)(2,1)} %bitcast.163), calls=%async_computation.1 | async-start | bytes 524288 | tf_op jit(solution)/shard_map/all_to_all | solution.py:178
  56.1 21.2 %copy-start.32 = (pred[128]{0:T(512)(128)(4,1)S(1)}, pred[128]{0:T(512)(128)(4,1)}, u32[]{:S(2)}) copy-start(pred[128]{0:T(512)(128)(4,1)} %get-tuple-element.46) | copy-start | bytes 388
  56.1 21.2 %copy-start.33 = (f32[24]{0:T(128)S(1)}, f32[24]{0:T(128)}, u32[]{:S(2)}) copy-start(f32[24]{0:T(128)} %iota_convert_fusion) | copy-start | bytes 292
  64.2 7.7 %collective-permute-start = (bf16[24,4096]{1,0:T(8,128)(2,1)S(1)}, bf16[24,4096]{1,0:T(8,128)(2,1)S(1)}, u32[]{:S(2)}, u32[]{:S(2)}) collective-permute-start(bf16[24,4096]{1,0:T(8,128)(2,1)S(1)} %get-tuple-element.18), channel_id=1, source_target_pairs={{0,1},{1,2},{2,3},{3,0},{4,5},{5,6},{6,7},{7,4},{8,9},{9,10},{10,1... | collective-permute-start | bytes 589832 | tf_op jit(solution)/shard_map/ppermute | solution.py:37
  65.5 11.7 %collective-permute-start.1 = (bf16[24,4096]{1,0:T(8,128)(2,1)S(1)}, bf16[24,4096]{1,0:T(8,128)(2,1)S(1)}, u32[]{:S(2)}, u32[]{:S(2)}) collective-permute-start(bf16[24,4096]{1,0:T(8,128)(2,1)S(1)} %get-tuple-element.20), channel_id=1, source_target_pairs={{0,2},{1,3},{2,0},{3,1},{4,6},{5,7},{6,4},{7,5},{8,10},{9,11},{10,... | collective-permute-start | bytes 589832 | tf_op jit(solution)/shard_map/ppermute | solution.py:37
  68.2 9.1 %collective-permute-start.2 = (bf16[24,4096]{1,0:T(8,128)(2,1)S(1)}, bf16[24,4096]{1,0:T(8,128)(2,1)S(1)}, u32[]{:S(2)}, u32[]{:S(2)}) collective-permute-start(bf16[24,4096]{1,0:T(8,128)(2,1)S(1)} %get-tuple-element.19), channel_id=1, source_target_pairs={{0,3},{1,0},{2,1},{3,2},{4,7},{5,4},{6,5},{7,6},{8,11},{9,8},{10,9... | collective-permute-start | bytes 589832 | tf_op jit(solution)/shard_map/ppermute | solution.py:37
  81.5 5.8 %copy-start.17 = (f32[4096]{0:T(1024)S(1)}, f32[4096]{0:T(1024)}, u32[]{:S(2)}) copy-start(f32[4096]{0:T(1024)} %param.27) | copy-start | bytes 49156
  81.5 45.0 %all-to-all-start.2 = ((bf16[16,24,4096]{2,1,0:T(8,128)(2,1)}), bf16[16,24,4096]{2,1,0:T(8,128)(2,1)}, u32[]{:S(2)}, u32[]{:S(2)}) async-start(bf16[16,24,4096]{2,1,0:T(8,128)(2,1)} %broadcast_in_dim.156), calls=%async_computation.2 | async-start | bytes 6291456 | tf_op jit(solution)/shard_map/all_to_all | solution.py:214
  86.1 7.1 %collective-permute-start.3 = (bf16[4096,256]{1,0:T(8,128)(2,1)}, bf16[4096,256]{1,0:T(8,128)(2,1)S(1)}, u32[]{:S(2)}, u32[]{:S(2)}) collective-permute-start(bf16[4096,256]{1,0:T(8,128)(2,1)} %bitcast.153), channel_id=1, source_target_pairs={{0,4},{4,0},{1,5},{5,1},{2,6},{6,2},{3,7},{7,3},{8,12},{12,8},{9,1... | collective-permute-start | bytes 6291464 | tf_op jit(solution)/shard_map/ppermute | solution.py:37
  87.2 7.4 %collective-permute-start.4 = (bf16[4096,256]{1,0:T(8,128)(2,1)}, bf16[4096,256]{1,0:T(8,128)(2,1)}, u32[]{:S(2)}, u32[]{:S(2)}) collective-permute-start(bf16[4096,256]{1,0:T(8,128)(2,1)} %bitcast.178), channel_id=1, source_target_pairs={{0,4},{4,0},{1,5},{5,1},{2,6},{6,2},{3,7},{7,3},{8,12},{12,8},{9,1... | collective-permute-start | bytes 6291464 | tf_op jit(solution)/shard_map/ppermute | solution.py:37
  89.4 3.6 %collective-permute-start.5 = (f32[1,256]{1,0:T(1,128)S(1)}, f32[1,256]{1,0:T(1,128)S(1)}, u32[]{:S(2)}, u32[]{:S(2)}) collective-permute-start(f32[1,256]{1,0:T(1,128)S(1)} %bitcast.174), channel_id=1, source_target_pairs={{0,4},{4,0},{1,5},{5,1},{2,6},{6,2},{3,7},{7,3},{8,12},{12,8},{9,1... | collective-permute-start | bytes 3080 | tf_op jit(solution)/shard_map/ppermute | solution.py:37
  93.2 1.4 copy-start.2
  126.5 1.6 copy-start.1
  128.1 1.6 copy-start.3
  142.8 8.4 %copy-start.31 = (f32[128]{0:T(128)S(1)}, f32[128]{0:T(128)}, u32[]{:S(2)}) copy-start(f32[128]{0:T(128)} %get-tuple-element.42) | copy-start | bytes 1540
  142.8 8.4 %copy-start.38 = (f32[128]{0:T(128)S(1)}, f32[128]{0:T(128)}, u32[]{:S(2)}) copy-start(f32[128]{0:T(128)} %get-tuple-element.8) | copy-start | bytes 1540
  142.8 44.5 %all-to-all-start.3 = ((bf16[16,24,4096]{2,1,0:T(8,128)(2,1)}), bf16[16,24,4096]{2,1,0:T(8,128)(2,1)}, u32[]{:S(2)}, u32[]{:S(2)}) async-start(bf16[16,24,4096]{2,1,0:T(8,128)(2,1)} %bitcast.160), calls=%async_computation.3 | async-start | bytes 6291456 | tf_op jit(solution)/shard_map/all_to_all | solution.py:218
  151.4 57.6 %copy-start.19 = (bf16[24,128]{1,0:T(8,128)(2,1)S(1)}, bf16[24,128]{1,0:T(8,128)(2,1)}, u32[]{:S(2)}) copy-start(bf16[24,128]{1,0:T(8,128)(2,1)} %get-tuple-element.27) | copy-start | bytes 18436
  151.4 57.6 %copy-start.20 = (bf16[24,128]{1,0:T(8,128)(2,1)S(1)}, bf16[24,128]{1,0:T(8,128)(2,1)}, u32[]{:S(2)}) copy-start(bf16[24,128]{1,0:T(8,128)(2,1)} %get-tuple-element.28) | copy-start | bytes 18436
  151.4 57.6 %copy-start.21 = (bf16[24,128]{1,0:T(8,128)(2,1)S(1)}, bf16[24,128]{1,0:T(8,128)(2,1)}, u32[]{:S(2)}) copy-start(bf16[24,128]{1,0:T(8,128)(2,1)} %get-tuple-element.29) | copy-start | bytes 18436
  187.3 2.5 copy-start.12
  190.9 15.1 %collective-permute-start.6 = (bf16[24,4096]{1,0:T(8,128)(2,1)}, bf16[24,4096]{1,0:T(8,128)(2,1)}, u32[]{:S(2)}, u32[]{:S(2)}) collective-permute-start(bf16[24,4096]{1,0:T(8,128)(2,1)} %divide_convert_fusion), channel_id=1, source_target_pairs={{0,3},{1,0},{2,1},{3,2},{4,7},{5,4},{6,5},{7,6},{8,11},{9,8},{10,9... | collective-permute-start | bytes 589832 | tf_op jit(solution)/shard_map/ppermute | solution.py:37
  200.9 6.4 %collective-permute-start.7 = (bf16[24,4096]{1,0:T(8,128)(2,1)}, bf16[24,4096]{1,0:T(8,128)(2,1)}, u32[]{:S(2)}, u32[]{:S(2)}) collective-permute-start(bf16[24,4096]{1,0:T(8,128)(2,1)} %divide_convert_fusion), channel_id=1, source_target_pairs={{0,2},{1,3},{2,0},{3,1},{4,6},{5,7},{6,4},{7,5},{8,10},{9,11},{10,... | collective-permute-start | bytes 589832 | tf_op jit(solution)/shard_map/ppermute | solution.py:37
  200.9 8.2 %collective-permute-start.8 = (bf16[24,4096]{1,0:T(8,128)(2,1)}, bf16[24,4096]{1,0:T(8,128)(2,1)}, u32[]{:S(2)}, u32[]{:S(2)}) collective-permute-start(bf16[24,4096]{1,0:T(8,128)(2,1)} %divide_convert_fusion), channel_id=1, source_target_pairs={{0,1},{1,2},{2,3},{3,0},{4,5},{5,6},{6,7},{7,4},{8,9},{9,10},{10,1... | collective-permute-start | bytes 589832 | tf_op jit(solution)/shard_map/ppermute | solution.py:37
  210.8 7.1 %copy-start.5 = (f32[128,4096]{1,0:T(8,128)}, f32[128,4096]{1,0:T(8,128)S(1)}, u32[]{:S(2)}) copy-start(f32[128,4096]{1,0:T(8,128)S(1)} %convolution_add_fusion.2) | copy-start | bytes 6291460
  210.8 7.1 %copy-start.8 = (f32[128,1024]{1,0:T(8,128)S(1)}, f32[128,1024]{1,0:T(8,128)}, u32[]{:S(2)}) copy-start(f32[128,1024]{1,0:T(8,128)} %fusion.64) | copy-start | bytes 1572868
  210.8 7.1 %copy-start.9 = (f32[128,8,128]{2,1,0:T(8,128)S(1)}, f32[128,8,128]{2,1,0:T(8,128)}, u32[]{:S(2)}) copy-start(f32[128,8,128]{2,1,0:T(8,128)} %broadcast_in_dim.148) | copy-start | bytes 1572868
  217.9 13.9 %copy-start.23 = (f32[128,8]{0,1:T(8,128)S(1)}, f32[128,8]{0,1:T(8,128)}, u32[]{:S(2)}) copy-start(f32[128,8]{0,1:T(8,128)} %copy-done.22) | copy-start | bytes 12292
  217.9 13.9 %copy-start.36 = (f32[8,128]{1,0:T(8,128)S(1)}, f32[8,128]{1,0:T(8,128)}, u32[]{:S(2)}) copy-start(f32[8,128]{1,0:T(8,128)} %get-tuple-element.33) | copy-start | bytes 12292
  219.0 20.6 %copy-start.40 = (f32[32]{0:T(128)S(1)}, f32[32]{0:T(128)}, u32[]{:S(2)}) copy-start(f32[32]{0:T(128)} %copy-done.39) | copy-start | bytes 388
  220.7 19.0 %all-to-all-start.4 = ((bf16[32,32,128]{2,1,0:T(8,128)(2,1)}), bf16[32,32,128]{2,1,0:T(8,128)(2,1)}, u32[]{:S(2)}, u32[]{:S(2)}) async-start(bf16[32,32,128]{2,1,0:T(8,128)(2,1)} %bitcast.165), calls=%async_computation.4 | async-start | bytes 524288 | tf_op jit(solution)/shard_map/all_to_all | solution.py:232
  241.8 14.7 %all-to-all-start.5 = ((bf16[32,32,128]{2,1,0:T(8,128)(2,1)}), bf16[32,32,128]{2,1,0:T(8,128)(2,1)}, u32[]{:S(2)}, u32[]{:S(2)}) async-start(bf16[32,32,128]{2,1,0:T(8,128)(2,1)} %bitcast.164), calls=%async_computation.5 | async-start | bytes 524288 | tf_op jit(solution)/shard_map/all_to_all | solution.py:238
  246.4 2.1 copy-start.14
  258.5 9.3 %copy-start.25 = (f32[128,8]{0,1:T(8,128)S(1)}, f32[128,8]{0,1:T(8,128)}, u32[]{:S(2)}) copy-start(f32[128,8]{0,1:T(8,128)} %copy-done.24) | copy-start | bytes 12292
  268.9 7.0 %copy-start.28 = (f32[1,8]{0,1:T(8,128)S(1)}, f32[1,8]{0,1:T(8,128)}, u32[]{:S(2)}) copy-start(f32[1,8]{0,1:T(8,128)} %copy.71) | copy-start | bytes 100
  268.9 7.2 %copy-start.16 = (bf16[128,128]{0,1:T(8,128)(2,1)S(1)}, bf16[128,128]{0,1:T(8,128)(2,1)}, u32[]{:S(2)}) copy-start(bf16[128,128]{0,1:T(8,128)(2,1)} %fusion.5) | copy-start | bytes 98308
  280.0 9.4 %collective-permute-start.10 = (bf16[128,1024]{1,0:T(8,128)(2,1)}, bf16[128,1024]{1,0:T(8,128)(2,1)}, u32[]{:S(2)}, u32[]{:S(2)}) collective-permute-start(bf16[128,1024]{1,0:T(8,128)(2,1)} %get-tuple-element.17), channel_id=1, source_target_pairs={{0,2},{1,3},{2,0},{3,1},{4,6},{5,7},{6,4},{7,5},{8,10},{9,11},{10,... | collective-permute-start | bytes 786440 | tf_op jit(solution)/shard_map/ppermute | solution.py:37
  280.0 13.2 %collective-permute-start.11 = (bf16[128,1024]{1,0:T(8,128)(2,1)}, bf16[128,1024]{1,0:T(8,128)(2,1)}, u32[]{:S(2)}, u32[]{:S(2)}) collective-permute-start(bf16[128,1024]{1,0:T(8,128)(2,1)} %get-tuple-element.16), channel_id=1, source_target_pairs={{0,3},{1,0},{2,1},{3,2},{4,7},{5,4},{6,5},{7,6},{8,11},{9,8},{10,9... | collective-permute-start | bytes 786440 | tf_op jit(solution)/shard_map/ppermute | solution.py:37
  280.9 14.7 %collective-permute-start.9 = (bf16[128,1024]{1,0:T(8,128)(2,1)S(1)}, bf16[128,1024]{1,0:T(8,128)(2,1)}, u32[]{:S(2)}, u32[]{:S(2)}) collective-permute-start(bf16[128,1024]{1,0:T(8,128)(2,1)S(1)} %get-tuple-element.15), channel_id=1, source_target_pairs={{0,1},{1,2},{2,3},{3,0},{4,5},{5,6},{6,7},{7,4},{8,9},{9,10},{10,1... | collective-permute-start | bytes 786440 | tf_op jit(solution)/shard_map/ppermute | solution.py:37
  (16 other events, 14.3 us)

commit v2 on v1

v2 whole, which is shorter than its diff:
```python
import functools

import jax
import jax.numpy as jnp
import numpy as np
from jax import lax
from jax.experimental import pallas as pl
from jax.experimental.pallas import tpu as pltpu
from jax.sharding import Mesh
from jax.sharding import PartitionSpec as P

CAP = 24
EPS = 1e-05
DESCENT = 0.5
HIGH = lax.Precision.HIGHEST
BF = jnp.bfloat16
F32 = jnp.float32
SEQ = ("x", "z", "c")
PLANE = ("x", "z")
EXTRA = 16


def mm(a, b):
    return jnp.dot(a, b, preferred_element_type=F32)


def mm_t(a, b):
    return lax.dot_general(a, b, (((1,), (1,)), ((), ())), preferred_element_type=F32)


def t_mm(a, b):
    return lax.dot_general(a, b, (((0,), (0,)), ((), ())), preferred_element_type=F32)


def shift(value, axis, by):
    count = lax.axis_size(axis)
    return lax.ppermute(value, axis, [(i, (i + by) % count) for i in range(count)])


def slot_table(ids_rows, gate_rows, expert):
    tlen = ids_rows.shape[0]
    match = ids_rows == expert
    hits = jnp.sum(match.astype(F32), axis=1)
    weight = jnp.sum(jnp.where(match, gate_rows.astype(F32), 0.0), axis=1)
    rowpos = lax.broadcasted_iota(jnp.int32, (tlen, tlen), 0)
    colpos = lax.broadcasted_iota(jnp.int32, (tlen, tlen), 1)
    places = jnp.sum(jnp.where(rowpos > colpos, hits[None, :], 0.0), axis=1)
    slot_pos = lax.broadcasted_iota(jnp.int32, (CAP, tlen), 0).astype(F32)
    table = (places[None, :] == slot_pos) & (hits[None, :] > 0.0)
    return table.astype(F32), weight


def expert_kernel(rows_ref, wg0, wg1, wu0, wu1, hv_ref, out_ref, first, second):
    half = wg0.shape[1]
    rows = rows_ref[...]
    for k, (wg, wu) in enumerate(((wg0, wu0), (wg1, wu1))):
        span = slice(k * half, (k + 1) * half)
        gate = mm(rows, wg[...])
        up = mm(rows, wu[...])
        sig = 1.0 / (1.0 + jnp.exp(-gate))
        hv = hv_ref[k : k + 1, :]
        first[:, span] = (hv * up * sig * (1.0 + gate * (1.0 - sig))).astype(BF)
        second[:, span] = (hv * gate * sig).astype(BF)
    width = rows.shape[1]
    step = min(width, 512)

    @pl.loop(0, width // step)
    def _(i):
        cols = pl.ds(pl.multiple_of(i * step, step), step)
        total = mm_t(first[:, :half], wg0[cols, :]) + mm_t(second[:, :half], wu0[cols, :])
        total += mm_t(first[:, half:], wg1[cols, :]) + mm_t(second[:, half:], wu1[cols, :])
        out_ref[:, cols] = total.astype(BF)


def expert_rows(rows, wg0, wg1, wu0, wu1, head_vec):
    count, width = rows.shape
    half = wg0.shape[1]
    return pl.pallas_call(
        expert_kernel,
        out_shape=jax.ShapeDtypeStruct((count, width), BF),
        in_specs=[pl.BlockSpec(memory_space=pltpu.VMEM)] * 6,
        out_specs=pl.BlockSpec(memory_space=pltpu.VMEM),
        scratch_shapes=[pltpu.VMEM((count, 2 * half), BF)] * 2,
        compiler_params=pltpu.CompilerParams(vmem_limit_bytes=48 << 20),
        cost_estimate=pl.CostEstimate(
            flops=16 * count * width * half,
            bytes_accessed=8 * width * half + 4 * count * width,
            transcendentals=2 * count * half,
        ),
        name="experts",
    )(rows, wg0, wg1, wu0, wu1, head_vec)


def row_mask(tlen):
    rowpos = lax.broadcasted_iota(jnp.int32, (tlen, tlen), 0)
    colpos = lax.broadcasted_iota(jnp.int32, (tlen, tlen), 1)
    return rowpos >= colpos


def vmem(mib):
    return pltpu.CompilerParams(vmem_limit_bytes=mib << 20)


def whole(count):
    return [pl.BlockSpec(memory_space=pltpu.VMEM)] * count


def cost(flops, moved):
    return pl.CostEstimate(flops=flops, bytes_accessed=moved, transcendentals=0)


def proj_kernel(
    heads, slice_rows, cand, w_in, w_bc, w_step, bias, rate,
    inner_out, bc_out, pre_out, step_out, cum_out, step_t_out, cum_t_out, pay_out,
    acc, acc_bc, acc_pre,
):
    i = pl.program_id(0)

    @pl.when(i == 0)
    def _():
        acc[...] = jnp.zeros_like(acc)
        acc_bc[...] = jnp.zeros_like(acc_bc)
        acc_pre[...] = jnp.zeros_like(acc_pre)

    x = cand[...]
    acc[...] += mm(x, w_in[...])
    acc_bc[...] += mm(x, w_bc[...])
    acc_pre[:, :heads] += mm(x, w_step[...])

    @pl.when(i == pl.num_programs(0) - 1)
    def _():
        tlen, chan = acc.shape
        size = chan // heads
        nstate = acc_bc.shape[1] // 2
        pre = acc_pre[...] + bias[...]
        step = jnp.maximum(pre, 0.0) + jnp.log1p(jnp.exp(-jnp.abs(pre)))
        lower = row_mask(tlen).astype(F32)
        cum = jnp.dot(lower, -step * rate[...], precision=HIGH, preferred_element_type=F32)
        pre_out[...] = pre
        step_out[...] = step
        cum_out[...] = cum
        step_t_out[...] = step.T
        cum_t_out[...] = cum.T
        last = cum[tlen - 1 : tlen, :]
        tail = jnp.exp(last - cum) * step
        inner_b = acc[...].astype(BF)
        inner_out[...] = inner_b
        bc = acc_bc[...].astype(BF)
        bc_out[...] = bc
        b_rows = bc[:, :nstate]
        extra = pay_out.shape[1] - slice_rows
        place = lax.broadcasted_iota(jnp.int32, (extra, nstate), 0)
        per = size // slice_rows
        for h in range(heads):
            span = slice(h * size, (h + 1) * size)
            fed = (tail[:, h : h + 1] * inner_b[:, span].astype(F32)).astype(BF)
            fresh = t_mm(fed, b_rows).astype(BF)
            value = jnp.broadcast_to(last[:, h : h + 1], (extra, nstate))
            scaled = value * 65537.0
            hi = scaled - (scaled - value)
            rest = value - hi
            scaled = rest * 65537.0
            mid = scaled - (scaled - rest)
            low = rest - mid
            parts = jnp.where(place == 0, hi, jnp.where(place == 1, mid, low))
            parts = jnp.where(place < 3, parts, 0.0).astype(BF)
            for q in range(per):
                pay_out[h * per + q, :slice_rows, :] = fresh[q * slice_rows : (q + 1) * slice_rows]
                pay_out[h * per + q, slice_rows:, :] = parts


def project(candidate, in_proj, bc_proj, step_proj, bias, rate, heads, n_seq):
    tlen, width = candidate.shape
    chan = in_proj.shape[1]
    two = bc_proj.shape[1]
    slice_rows = chan // n_seq
    depth = min(width, 1024)
    small = jax.ShapeDtypeStruct((tlen, tlen), F32)
    fixed = lambda *shape: pl.BlockSpec(shape, lambda i: (0,) * len(shape))
    return pl.pallas_call(
        functools.partial(proj_kernel, heads, slice_rows),
        grid=(width // depth,),
        out_shape=(
            jax.ShapeDtypeStruct((tlen, chan), BF),
            jax.ShapeDtypeStruct((tlen, two), BF),
            small, small, small, small, small,
            jax.ShapeDtypeStruct((n_seq, slice_rows + EXTRA, two // 2), BF),
        ),
        in_specs=[
            pl.BlockSpec((tlen, depth), lambda i: (0, i)),
            pl.BlockSpec((depth, chan), lambda i: (i, 0)),
            pl.BlockSpec((depth, two), lambda i: (i, 0)),
            pl.BlockSpec((depth, heads), lambda i: (i, 0)),
            fixed(1, tlen), fixed(1, tlen),
        ],
        out_specs=(
            fixed(tlen, chan), fixed(tlen, two),
            fixed(tlen, tlen), fixed(tlen, tlen), fixed(tlen, tlen), fixed(tlen, tlen),
            fixed(tlen, tlen), fixed(n_seq, slice_rows + EXTRA, two // 2),
        ),
        scratch_shapes=[
            pltpu.VMEM((tlen, chan), F32), pltpu.VMEM((tlen, two), F32), pltpu.VMEM((tlen, tlen), F32)
        ],
        compiler_params=vmem(24),
        cost_estimate=cost(2 * tlen * width * (chan + two), 2 * width * (chan + two + 2 * tlen)),
        name="project",
    )(candidate, in_proj, bc_proj, step_proj, bias, rate)


def enter_kernel(got, out, decay):
    count, rows, nstate = out.shape
    out[0] = jnp.zeros((rows, nstate), BF)
    state = jnp.zeros((rows, nstate), F32)
    for s in range(count):
        tags = got[s, rows:, :].astype(F32)
        fade = jnp.exp(jnp.sum(tags, axis=0, keepdims=True))
        decay[s : s + 1, :] = fade
        if s < count - 1:
            state = fade * state + got[s, :rows, :].astype(F32)
            out[s + 1] = state.astype(BF)


def enter_states(got, slice_rows):
    count, _, nstate = got.shape
    return pl.pallas_call(
        enter_kernel,
        out_shape=(
            jax.ShapeDtypeStruct((count, slice_rows, nstate), BF),
            jax.ShapeDtypeStruct((count, nstate), F32),
        ),
        in_specs=whole(1),
        out_specs=tuple(whole(2)),
        compiler_params=vmem(8),
        name="enter",
    )(got)


def leave_kernel(got, decay, out):
    count, rows, nstate = out.shape
    out[count - 1] = jnp.zeros((rows, nstate), BF)
    state = jnp.zeros((rows, nstate), F32)
    for s in range(count - 1, 0, -1):
        state = decay[s : s + 1, :] * state + got[s].astype(F32)
        out[s - 1] = state.astype(BF)


def leave_states(got, decay):
    return pl.pallas_call(
        leave_kernel,
        out_shape=jax.ShapeDtypeStruct(got.shape, BF),
        in_specs=whole(2),
        out_specs=whole(1)[0],
        compiler_params=vmem(8),
        name="leave",
    )(got, decay)


def decay_weights(cum, cum_t, h):
    tlen = cum.shape[0]
    gaps = jnp.minimum(cum[:, h : h + 1] - cum_t[h : h + 1, :], 0.0)
    return jnp.where(row_mask(tlen), jnp.exp(gaps), 0.0)


def within_kernel(heads, inner_ref, bc_ref, cum_ref, cum_t_ref, step_t_ref, skip_ref, out):
    tlen, chan = out.shape
    size = chan // heads
    bc = bc_ref[...]
    nstate = bc.shape[1] // 2
    scores = mm_t(bc[:, nstate:], bc[:, :nstate])
    cum, cum_t, step_t = cum_ref[...], cum_t_ref[...], step_t_ref[...]
    for h in range(heads):
        span = slice(h * size, (h + 1) * size)
        mixing = (decay_weights(cum, cum_t, h) * scores * step_t[h : h + 1, :]).astype(BF)
        inner = inner_ref[:, span]
        out[:, span] = mm(mixing, inner) + skip_ref[:, span] * inner.astype(F32)


def mix_within(inner_b, bc_bf, cum, cum_t, step_t, skip, heads):
    tlen, chan = inner_b.shape
    return pl.pallas_call(
        functools.partial(within_kernel, heads),
        out_shape=jax.ShapeDtypeStruct((tlen, chan), F32),
        in_specs=whole(6),
        out_specs=whole(1)[0],
        compiler_params=vmem(12),
        cost_estimate=cost(2 * tlen * tlen * chan * 4, 8 * tlen * chan),
        name="mix_within",
    )(inner_b, bc_bf, cum, cum_t, step_t, skip)


def slots_kernel(
    heads, cap, within, bc_ref, cum_ref, state, table, own_table, cand, w_out,
    own_out, send1, send2, send3, reads_out, slots,
):
    @pl.when(pl.program_id(0) == 0)
    def _():
        chan = within.shape[1]
        size = chan // heads
        nstate = bc_ref.shape[1] // 2
        c_rows = bc_ref[:, nstate:]
        growth = jnp.exp(cum_ref[...])
        for h in range(heads):
            span = slice(h * size, (h + 1) * size)
            reads = mm_t(c_rows, state[span, :])
            reads_out[:, span] = reads
            mixed = (within[:, span] + growth[:, h : h + 1] * reads).astype(BF)
            slots[:, span] = mm(table[...], mixed).astype(BF)

    part = mm(slots[...], w_out[...])
    own_out[...] = part[:cap] + mm(own_table[...], cand[...])
    for k, send in enumerate((send1, send2, send3)):
        send[...] = part[(k + 1) * cap : (k + 2) * cap].astype(BF)


def mix_slots(within, bc_bf, cum, state, table, own_table, candidate, out_proj, heads):
    tlen, chan = within.shape
    width = out_proj.shape[1]
    rows = table.shape[0]
    block = min(width, 1024)
    fixed = lambda a: pl.BlockSpec(a.shape, lambda i: (0,) * a.ndim)
    cols = lambda n: pl.BlockSpec((n, block), lambda i: (0, i))
    sent = jax.ShapeDtypeStruct((CAP, width), BF)
    return pl.pallas_call(
        functools.partial(slots_kernel, heads, CAP),
        grid=(width // block,),
        out_shape=(
            jax.ShapeDtypeStruct((CAP, width), F32), sent, sent, sent,
            jax.ShapeDtypeStruct((tlen, chan), F32),
        ),
        in_specs=[fixed(a) for a in (within, bc_bf, cum, state, table, own_table)]
        + [cols(tlen), cols(chan)],
        out_specs=(cols(CAP), cols(CAP), cols(CAP), cols(CAP), fixed(within)),
        scratch_shapes=[pltpu.VMEM((rows, chan), BF)],
        compiler_params=vmem(24),
        cost_estimate=cost(2 * rows * chan * width, 2 * chan * width),
        name="mix_slots",
    )(within, bc_bf, cum, state, table, own_table, candidate, out_proj)


def outgrad_kernel(heads, table, terms, energy, w_out, bc_ref, cum_ref, hid_out, grad_out, local_out, acc):
    i = pl.program_id(0)

    @pl.when(i == 0)
    def _():
        acc[...] = jnp.zeros_like(acc)

    hid = energy[...] + t_mm(table[...], terms[...])
    hid_out[...] = hid
    acc[...] += mm_t(hid.astype(BF), w_out[...])

    @pl.when(i == pl.num_programs(0) - 1)
    def _():
        chan = acc.shape[1]
        size = chan // heads
        nstate = bc_ref.shape[1] // 2
        c_rows = bc_ref[:, nstate:]
        growth = jnp.exp(cum_ref[...])
        for h in range(heads):
            span = slice(h * size, (h + 1) * size)
            grad = acc[:, span]
            grad_out[:, span] = grad
            grown = (growth[:, h : h + 1] * grad).astype(BF)
            local_out[span, :] = t_mm(grown, c_rows).astype(BF)


def out_gradient(table, terms, energy, out_proj, bc_bf, cum, heads):
    tlen = table.shape[1]
    chan, width = out_proj.shape
    nstate = bc_bf.shape[1] // 2
    block = min(width, 1024)
    fixed = lambda *shape: pl.BlockSpec(shape, lambda i: (0,) * len(shape))
    cols = lambda n: pl.BlockSpec((n, block), lambda i: (0, i))
    return pl.pallas_call(
        functools.partial(outgrad_kernel, heads),
        grid=(width // block,),
        out_shape=(
            jax.ShapeDtypeStruct((tlen, width), F32),
            jax.ShapeDtypeStruct((tlen, chan), F32),
            jax.ShapeDtypeStruct((chan, nstate), BF),
        ),
        in_specs=[
            fixed(*table.shape), cols(terms.shape[0]), cols(1), cols(chan),
            fixed(*bc_bf.shape), fixed(*cum.shape),
        ],
        out_specs=(cols(tlen), fixed(tlen, chan), fixed(chan, nstate)),
        scratch_shapes=[pltpu.VMEM((tlen, chan), F32)],
        compiler_params=vmem(24),
        cost_estimate=cost(2 * tlen * chan * width, 2 * chan * width),
        name="out_gradient",
    )(table, terms, energy, out_proj, bc_bf, cum)


def near_kernel(
    heads, grad_ref, inner_ref, bc_ref, cum_ref, cum_t_ref, step_ref, step_t_ref, reads, state, skip_ref,
    g_out, gb_out, gc_out, dcum_out, dstep_out, rows, cols,
):
    tlen, chan = grad_ref.shape
    size = chan // heads
    nstate = bc_ref.shape[1] // 2
    b_rows, c_rows = bc_ref[:, :nstate], bc_ref[:, nstate:]
    scores = mm_t(c_rows, b_rows)
    cum, cum_t, step_t = cum_ref[...], cum_t_ref[...], step_t_ref[...]
    growth = jnp.exp(cum)
    rows[...] = jnp.zeros_like(rows)
    cols[...] = jnp.zeros_like(cols)
    d_scores = jnp.zeros((tlen, tlen), F32)
    g_c = jnp.zeros((tlen, nstate), F32)
    for h in range(heads):
        span = slice(h * size, (h + 1) * size)
        grad = grad_ref[:, span]
        grad_b = grad.astype(BF)
        inner = inner_ref[:, span]
        step_h = step_t[h : h + 1, :]
        weights = decay_weights(cum, cum_t, h)
        d_w = mm_t(grad_b, inner) * weights
        d_scores = d_scores + d_w * step_h
        d_ws = d_w * scores
        rows[h : h + 1, :] = jnp.sum(d_ws, axis=0, keepdims=True)
        grown = growth[:, h : h + 1] * grad
        cols[:, h : h + 1] = jnp.sum(d_ws * step_h, axis=1, keepdims=True) + jnp.sum(
            grown * reads[:, span], axis=1, keepdims=True
        )
        mixing = (weights * scores * step_h).astype(BF)
        g_out[:, span] = t_mm(mixing, grad_b) + skip_ref[:, span] * grad
        g_c = g_c + mm(grown.astype(BF), state[span, :])
    d_scores = d_scores.astype(BF)
    gc_out[...] = g_c + mm(d_scores, b_rows)
    gb_out[...] = t_mm(d_scores, c_rows)
    d_step = rows[...].T
    dstep_out[...] = d_step
    dcum_out[...] = cols[...] - step_ref[...] * d_step


def near_gradient(grad, inner_b, bc_bf, cum, cum_t, step, step_t, reads, state, skip, heads):
    tlen, chan = grad.shape
    small = jax.ShapeDtypeStruct((tlen, tlen), F32)
    return pl.pallas_call(
        functools.partial(near_kernel, heads),
        out_shape=(jax.ShapeDtypeStruct((tlen, chan), F32), small, small, small, small),
        in_specs=whole(10),
        out_specs=tuple(whole(5)),
        scratch_shapes=[pltpu.VMEM((tlen, tlen), F32)] * 2,
        compiler_params=vmem(16),
        cost_estimate=cost(2 * tlen * tlen * chan * 8, 20 * tlen * chan),
        name="near_gradient",
    )(grad, inner_b, bc_bf, cum, cum_t, step, step_t, reads, state, skip)


def far_kernel(
    heads, later, state, inner_ref, bc_ref, cum_ref, step_ref, pre_ref, rate, near, gb_ref, gc_ref,
    dcum_ref, dstep_ref, g_out, gbc_out, gpre_out, kept, cols,
):
    tlen, chan = near.shape
    size = chan // heads
    nstate = bc_ref.shape[1] // 2
    b_rows = bc_ref[:, :nstate]
    cum, step, pre = cum_ref[...], step_ref[...], pre_ref[...]
    last = cum[tlen - 1 : tlen, :]
    fade = jnp.exp(last - cum)
    tail = fade * step
    kept[...] = jnp.zeros_like(kept)
    cols[...] = jnp.zeros_like(cols)
    g_b = gb_ref[...]
    for h in range(heads):
        span = slice(h * size, (h + 1) * size)
        late = later[span, :]
        tail_h = tail[:, h : h + 1]
        fed_back = mm_t(b_rows, late)
        g_out[:, span] = (near[:, span] + tail_h * fed_back).astype(BF)
        inner = inner_ref[:, span].astype(F32)
        cols[:, h : h + 1] = jnp.sum(inner * fed_back, axis=1, keepdims=True)
        g_b = g_b + mm((tail_h * inner).astype(BF), late)
        kept[h : h + 1, :] = jnp.sum(
            state[span, :].astype(F32) * late.astype(F32), axis=0, keepdims=True
        )
    gbc_out[:, :nstate] = g_b.astype(BF)
    gbc_out[:, nstate:] = gc_ref[...].astype(BF)
    d_tail = cols[...]
    tail_term = d_tail * tail
    kept_row = jnp.sum(kept[...].T, axis=0, keepdims=True)
    d_last = jnp.exp(last) * kept_row + jnp.sum(tail_term, axis=0, keepdims=True)
    rowpos = lax.broadcasted_iota(jnp.int32, cum.shape, 0)
    d_cum = dcum_ref[...] - tail_term + jnp.where(rowpos == tlen - 1, d_last, 0.0)
    colpos = lax.broadcasted_iota(jnp.int32, cum.shape, 1)
    upper = (rowpos <= colpos).astype(F32)
    d_decay = jnp.dot(upper, d_cum, precision=HIGH, preferred_element_type=F32)
    g_step = dstep_ref[...] + fade * d_tail - rate[...] * d_decay
    gpre_out[...] = (g_step / (1.0 + jnp.exp(-pre))).astype(BF)


def far_gradient(later, state, inner_b, bc_bf, cum, step, pre, rate, near, gb, gc, dcum, dstep, heads):
    tlen, chan = near.shape
    return pl.pallas_call(
        functools.partial(far_kernel, heads),
        out_shape=(
            jax.ShapeDtypeStruct((tlen, chan), BF),
            jax.ShapeDtypeStruct(bc_bf.shape, BF),
            jax.ShapeDtypeStruct((tlen, tlen), BF),
        ),
        in_specs=whole(13),
        out_specs=tuple(whole(3)),
        scratch_shapes=[pltpu.VMEM((tlen, tlen), F32)] * 2,
        compiler_params=vmem(16),
        cost_estimate=cost(2 * tlen * tlen * chan * 4, 20 * tlen * chan),
        name="far_gradient",
    )(later, state, inner_b, bc_bf, cum, step, pre, rate, near, gb, gc, dcum, dstep)


def back_kernel(heads, which, g_ref, gbc, gpre, w_in, w_bc, w_step, out):
    total = mm_t(g_ref[...], w_in[...]) + mm_t(gbc[...], w_bc[...])
    total += mm_t(gpre[:, :heads], w_step[...])
    out[...] = total.astype(out.dtype)


def back_columns(which, g_inner, g_bc, g_pre, in_proj, bc_proj, step_proj, cols, dtype, heads):
    tlen, chan = g_inner.shape
    two = bc_proj.shape[1]
    block = min(cols, 512)
    per = cols // block
    fixed = lambda a: pl.BlockSpec(a.shape, lambda i, w: (0,) * a.ndim)
    rows = lambda n: pl.BlockSpec((block, n), lambda i, w: (w[0] * per + i, 0))
    return pl.pallas_call(
        functools.partial(back_kernel, heads),
        grid_spec=pltpu.PrefetchScalarGridSpec(
            num_scalar_prefetch=1,
            grid=(per,),
            in_specs=[fixed(g_inner), fixed(g_bc), fixed(g_pre), rows(chan), rows(two), rows(heads)],
            out_specs=pl.BlockSpec((tlen, block), lambda i, w: (0, i)),
        ),
        out_shape=jax.ShapeDtypeStruct((tlen, cols), dtype),
        compiler_params=vmem(12),
        cost_estimate=cost(2 * tlen * (chan + two) * cols, 2 * (chan + two) * cols),
        name="back_columns",
    )(which, g_inner, g_bc, g_pre, in_proj, bc_proj, step_proj)


def shards(
    candidate,
    in_proj,
    bc_proj,
    step_proj,
    step_bias,
    decay_rate,
    skip_gain,
    out_proj,
    expert_ids,
    gate_weights,
    expert_gate,
    expert_up,
    expert_down,
    energy_head,
):
    tlen, width = candidate.shape
    heads = step_bias.shape[0]
    chan = in_proj.shape[1]
    size = chan // heads
    nstate = bc_proj.shape[1] // 2
    column = lax.axis_index("e")
    n_exp = lax.axis_size("e")
    n_seq = lax.axis_size(SEQ)
    n_plane = lax.axis_size(PLANE)
    col_count = width // n_exp
    slice_rows = chan // n_seq
    lanes = lambda v: jnp.pad(v, (0, tlen - heads))[None, :]
    bias, rate = lanes(step_bias), lanes(decay_rate)
    skip = jnp.repeat(skip_gain, size)[None, :]
    energy = energy_head[None, :]

    wg0, wu0 = expert_gate[0], expert_up[0]
    head_own = jnp.sum(expert_down[0].astype(F32) * energy, axis=1)
    wg1 = shift(wg0, "c", 1)
    wu1 = shift(wu0, "c", 1)
    head_other = shift(head_own[None, :], "c", 1)
    head_vec = jnp.concatenate([head_own[None, :], head_other], axis=0)

    pairs = [
        slot_table(expert_ids, gate_weights, lax.rem(column + k, n_exp)) for k in range(n_exp)
    ]
    table = jnp.concatenate([p[0] for p in pairs], axis=0).astype(BF)
    own_table, own_weight = pairs[0]
    slot_weight = jnp.sum(own_table * own_weight[None, :], axis=1, keepdims=True)
    own_table = own_table.astype(BF)

    inner_b, bc_bf, pre, step, cum, step_t, cum_t, payload = project(
        candidate, in_proj, bc_proj, step_proj, bias, rate, heads, n_seq
    )
    payload, wg1, wu1, head_vec, table, own_table, slot_weight = lax.optimization_barrier(
        (payload, wg1, wu1, head_vec, table, own_table, slot_weight)
    )
    got = lax.all_to_all(payload, SEQ, 0, 0, tiled=True)
    within = mix_within(inner_b, bc_bf, cum, cum_t, step_t, skip, heads)
    entering, decay = enter_states(got, slice_rows)
    state = lax.all_to_all(entering, SEQ, 0, 0, tiled=True).reshape(chan, nstate)

    own, send1, send2, send3, reads = mix_slots(
        within, bc_bf, cum, state, table, own_table, candidate, out_proj, heads
    )
    for k, send in enumerate((send1, send2, send3)):
        own = own + shift(send, "e", k + 1).astype(F32)
    hidden = own.astype(BF).astype(F32)
    scale = jnp.sqrt(jnp.mean(hidden * hidden, axis=-1, keepdims=True) + EPS)
    normed = hidden / scale
    routed = normed.astype(BF)

    rows = lax.all_to_all(
        jnp.broadcast_to(routed[None], (n_plane, CAP, width)), PLANE, 0, 0, tiled=True
    ).reshape(n_plane * CAP, width)
    terms = expert_rows(rows, wg0, wg1, wu0, wu1, head_vec)
    back = lax.all_to_all(terms.reshape(n_plane, CAP, width), PLANE, 0, 0, tiled=True)
    slot_grad = jnp.sum(back.astype(F32), axis=0)
    along = jnp.mean(normed * slot_grad, axis=-1, keepdims=True)
    slot_term = (slot_weight * (slot_grad - normed * along) / scale).astype(BF)
    all_terms = jnp.concatenate(
        [slot_term] + [shift(slot_term, "e", n_exp - k) for k in range(1, n_exp)], axis=0
    )
    hid_grad, out_grad, local_grad = out_gradient(
        table, all_terms, energy, out_proj, bc_bf, cum, heads
    )

    got_grad = lax.all_to_all(
        local_grad.reshape(n_seq, slice_rows, nstate), SEQ, 0, 0, tiled=True
    )
    near, gb, gc, dcum, dstep = near_gradient(
        out_grad, inner_b, bc_bf, cum, cum_t, step, step_t, reads, state, skip, heads
    )
    leaving = leave_states(got_grad, decay)
    later = lax.all_to_all(leaving, SEQ, 0, 0, tiled=True).reshape(chan, nstate)
    g_inner, g_bc, g_pre = far_gradient(
        later, state, inner_b, bc_bf, cum, step, pre, rate, near, gb, gc, dcum, dstep, heads
    )

    def columns(k, dtype):
        which = lax.rem(column + k, n_exp)[None]
        return back_columns(
            which, g_inner, g_bc, g_pre, in_proj, bc_proj, step_proj, col_count, dtype, heads
        )

    arrived = [shift(columns(k, BF), "e", k) for k in (2, 1, 3)]
    summed = lax.dynamic_slice_in_dim(hid_grad, column * col_count, col_count, 1) + columns(0, F32)
    for value in arrived:
        summed = summed + value.astype(F32)
    own_cand = lax.dynamic_slice_in_dim(candidate, column * col_count, col_count, 1).astype(F32)
    return (own_cand - DESCENT * summed).astype(BF)


def solution(mesh):
    n_seq, n_exp = mesh.devices.shape
    side = int(round((n_seq // 2) ** 0.5))
    grid = Mesh(mesh.devices.reshape(side, side, 2, n_exp), ("x", "z", "c", "e"))
    in_specs = (
        P(SEQ, None),
        P(None, "e"),
        P(),
        P(None, "e"),
        P("e"),
        P("e"),
        P("e"),
        P("e", None),
        P(SEQ, None),
        P(SEQ, None),
        P("e", None, SEQ),
        P("e", None, SEQ),
        P("e", SEQ, None),
        P(),
    )
    return jax.shard_map(
        shards, mesh=grid, in_specs=in_specs, out_specs=P(SEQ, "e"), check_vma=False
    )
```

time: 300 us -> 258 us (0.86)
  blocking collectives: 0 us -> 118 us
  waiting for transfers between devices: 114 us -> 24.1 us
  matrix products: 54.5 us -> 0 us
  starting transfers between devices: 60.2 us -> 22.9 us
  Pallas kernels: 13.2 us -> 37.5 us
  other arithmetic: 26.2 us -> 7.93 us
  local copies, waits for them, and re-layouts: 29.5 us -> 45.4 us
    all_to_all x0 -> x4, blocking collectives: none -> 118 us  [the longest x1 41.3 us: shards(): lax.all_to_all(jnp.broadcast_to(routed[None], (n_plane, CAP, width)), PLA...]
    all_to_all x6 -> x2, waiting for transfers between devices: 81.4 us -> 4.32 us  [the longest x1 4.32 us: shards(): lax.all_to_all(entering, SEQ, 0, 0, tiled=True).reshape(chan, nstate)]
    dot_general x26 -> x0, matrix products: 54.5 us -> none  [the longest x8 21.4 us: mm(): return jnp.dot(a, b, preferred_element_type=F32)]
    all_to_all x6 -> x2, starting transfers between devices: 41.2 us -> 8.03 us  [the longest x1 4.38 us: shards(): later = lax.all_to_all(leaving, SEQ, 0, 0, tiled=True).reshape(chan, nstate)]
    unnamed x96 -> x125, local copies, waits for them, and re-layouts: 11.4 us -> 44.3 us
    pallas_call x0 -> x12, Pallas kernels: none -> 23.5 us  [the longest x4 6.89 us: back_columns(): pl.pallas_call(functools.partial(back_kernel, heads), grid_spec=pltpu.Pre...]
    ppermute x12, waiting for transfers between devices: 32.4 us -> 19.8 us  [shift(): lax.ppermute(value, axis, [(i, (i + by) % count) for i in range(count)])]
    reduce_sum x8 -> x2, other arithmetic: 9.19 us -> 2.31 us  [the longest x1 2.09 us: shards(): head_own = jnp.sum(expert_down[0].astype(F32) * energy, axis=1)]
  transfers between devices with their start and end apart: 18 -> 14, of which waited for: 15 -> 6; matrix products, arithmetic and copies ran while one was open for 9% -> 2% of each run, Pallas kernels for 0% -> 3%
where the time goes in v2:
time: 258 us; the launch traced here: 256 us
  blocking collectives  118 us (46%)
  local copies, waits for them, and re-layouts  45.4 us (18%)
  Pallas kernels  37.5 us (15%)
  waiting for transfers between devices  24.1 us (9%)
  starting transfers between devices  22.9 us (9%)
  other arithmetic  7.93 us (3%)
    unnamed x125, local copies, waits for them, and re-layouts  44.3 us
    all_to_all x1, blocking collectives, shards(): lax.all_to_all(jnp.broadcast_to(routed[None], (n_plane, CAP, width)), PLA...  41.3 us
    all_to_all x1, blocking collectives, shards(): lax.all_to_all(terms.reshape(n_plane, CAP, width), PLANE, 0, 0, tiled=True)  41.1 us
    ppermute x12, waiting for transfers between devices, shift(): lax.ppermute(value, axis, [(i, (i + by) % count) for i in range(count)])  19.8 us
    all_to_all x1, blocking collectives, shards(): got = lax.all_to_all(payload, SEQ, 0, 0, tiled=True)  18.2 us
    all_to_all x1, blocking collectives, shards(): lax.all_to_all(local_grad.reshape(n_seq, slice_rows, nstate), SEQ, 0, 0,...  17.4 us
    ppermute x12, starting transfers between devices, shift(): lax.ppermute(value, axis, [(i, (i + by) % count) for i in range(count)])  14.9 us
    pallas_call x1, Pallas kernels, expert_rows(): pl.pallas_call(expert_kernel, out_shape=jax.ShapeDtypeStruct((count, widt...  14 us
  transfers between devices with their start and end apart: 14, of which 6 were waited for; matrix products, arithmetic and copies ran while one was open for 2% of the time, Pallas kernels for 3%

profile of v2, /device:TPU:1, one launch (start us, length us, event | category | flops | bytes accessed | tf_op | source)
XLA Modules:
  0.0 256.4 jit_solution(6075803985219112027)
XLA Ops:
  0.0 1.5 collective-permute-start
  1.6 2.1 fusion
  5.8 3.4 %copy-done = bf16[4096,1024]{1,0:T(8,128)(2,1)S(1)} copy-done((bf16[4096,1024]{1,0:T(8,128)(2,1)S(1)}, bf16[4096,1024]{1,0:T(8,128)(2,1)}, u32[]{:S(2)}) %copy-start) | copy-done | bytes 8388632
  9.2 1.2 copy-done.5
  10.4 3.4 %project.1 = (bf16[128,1024]{1,0:T(8,128)(2,1)S(1)}, bf16[128,256]{1,0:T(8,128)(2,1)S(1)}, f32[128,128]{1,0:T(8,128)S(1)}, f32[128,128]{1,0:T(8,128)S(1)}, f32[1...) custom-call(bf16[128,4096]{1,0:T(8,128)(2,1)S(1)} %copy-done.5, ...), custom_call_target="tpu_custom_call" | custom-call | flops 1342177280 | bytes 12582912 | tf_op jit(solution)/shard_map/project/pallas_call | solution.py:180
  15.9 18.2 %all_to_all.30.got = bf16[32,48,128]{2,1,0:T(8,128)(2,1)S(1)} all-to-all(bf16[32,48,128]{2,1,0:T(8,128)(2,1)S(1)} %get-tuple-element.46), channel_id=1, replica_groups=mesh['x'=4,'z'=4,'c'=2,'e'=4] {'x','z','c'}, dimensions={0} | all-to-all | bytes 786432 | tf_op jit(solution)/shard_map/all_to_all | solution.py:590
  35.6 3.7 %all-to-all-start.1 = ((bf16[32,32,128]{2,1,0:T(8,128)(2,1)}), bf16[32,32,128]{2,1,0:T(8,128)(2,1)S(1)}, u32[]{:S(2)}, u32[]{:S(2)}) async-start(bf16[32,32,128]{2,1,0:T(8,128)(2,1)} %copy-done.26), calls=%async_computation.1 | async-start | bytes 524288 | tf_op jit(solution)/shard_map/all_to_all | solution.py:593
  40.0 0.9 copy-done.10
  43.8 4.3 %all-to-all-done.1 = bf16[32,32,128]{2,1,0:T(8,128)(2,1)S(1)} async-done(((bf16[32,32,128]{2,1,0:T(8,128)(2,1)}), bf16[32,32,128]{2,1,0:T(8,128)(2,1)S(1)}, u32[]{:S(2)}, u32[]{:S(2)}) %all-to-all-start.1) | async-done | bytes 262176 | tf_op jit(solution)/shard_map/all_to_all | solution.py:593
  48.1 3.5 %copy-done.4 = bf16[1024,4096]{1,0:T(8,128)(2,1)S(1)} copy-done((bf16[1024,4096]{1,0:T(8,128)(2,1)S(1)}, bf16[1024,4096]{1,0:T(8,128)(2,1)}, u32[]{:S(2)}) %copy-start.4) | copy-done | bytes 8388632
  51.6 1.2 copy-done.6
  52.8 1.0 copy-done.14
  54.6 4.3 %mix_slots.1 = (f32[24,4096]{1,0:T(8,128)S(1)}, bf16[24,4096]{1,0:T(8,128)(2,1)S(1)}, bf16[24,4096]{1,0:T(8,128)(2,1)S(1)}, bf16[24,4096]{1,0:T(8,128)(2,1)S(1)}, f32[128,1024]{1,0:T(8,128)S(1)}) custom-call(f32[128,1024]{1,0:T(8,128)S(1)} %copy-done.14, bf16[128,256]{1,0:T(8,128)(2,1)S(1)} %get-tuple-element.42.bc_ref, ...), custom_call_target="tpu_custom_call" | custom-call | flops 805306368 | bytes 8388608 | tf_op jit(solution)/shard_map/mix_slots/pallas_call | solution.py:323
  58.9 1.4 collective-permute-start.3
  60.3 2.6 %collective-permute-start.4 = (bf16[24,4096]{1,0:T(8,128)(2,1)S(1)}, bf16[24,4096]{1,0:T(8,128)(2,1)S(1)}, u32[]{:S(2)}, u32[]{:S(2)}) collective-permute-start(bf16[24,4096]{1,0:T(8,128)(2,1)S(1)} %get-tuple-element.51), channel_id=1, source_target_pairs={{0,2},{1,3},{2,0},{3,1},{4,6},{5,7},{6,4},{7,5},{8,10},{9,11},{10,... | collective-permute-start | bytes 589832 | tf_op jit(solution)/shard_map/ppermute | solution.py:37
  62.9 1.1 collective-permute-start.5
  63.9 2.7 %collective-permute-done.3 = bf16[24,4096]{1,0:T(8,128)(2,1)S(1)} collective-permute-done((bf16[24,4096]{1,0:T(8,128)(2,1)S(1)}, bf16[24,4096]{1,0:T(8,128)(2,1)S(1)}, u32[]{:S(2)}, u32[]{:S(2)}) %collective-permute-start.3) | collective-permute-done | bytes 196640 | tf_op jit(solution)/shard_map/ppermute | solution.py:37
  66.6 5.3 %collective-permute-done.4 = bf16[24,4096]{1,0:T(8,128)(2,1)S(1)} collective-permute-done((bf16[24,4096]{1,0:T(8,128)(2,1)S(1)}, bf16[24,4096]{1,0:T(8,128)(2,1)S(1)}, u32[]{:S(2)}, u32[]{:S(2)}) %collective-permute-start.4) | collective-permute-done | bytes 196640 | tf_op jit(solution)/shard_map/ppermute | solution.py:37
  72.7 41.3 %all_to_all.31 = bf16[16,24,4096]{2,1,0:T(8,128)(2,1)} all-to-all(bf16[16,24,4096]{2,1,0:T(8,128)(2,1)S(1)} %broadcast_in_dim.97), channel_id=1, replica_groups=mesh['x'=4,'z'=4,'c'=2,'e'=4] {'x','z'}, dimensions={0} | all-to-all | bytes 6291456 | tf_op jit(solution)/shard_map/all_to_all | solution.py:605
  114.0 14.0 %experts.1 = bf16[384,4096]{1,0:T(8,128)(2,1)} custom-call(bf16[384,4096]{1,0:T(8,128)(2,1)} %bitcast.34, bf16[4096,256]{1,0:T(8,128)(2,1)S(1)} %bitcast.33, bf16[4096,256]{1,0:T(8,128)(2,1)} %collective-permute-done.wg1, bf16[4096,256]{1,0:T(8,128)(2,1)} %bitcast.39, bf16[4096,256]{1,0:T(8,128)(2,1)} %collective-permute-done.1.wu1, f32[2,256]{1,0:T(2,128)S(1)} %copy-done.52), custom_call_target="tpu_custom_call" | custom-call | flops 6442450944 | bytes 14680064 | tf_op jit(solution)/shard_map/experts/pallas_call | solution.py:78
  128.0 41.1 %all_to_all.32 = bf16[16,24,4096]{2,1,0:T(8,128)(2,1)S(1)} all-to-all(bf16[16,24,4096]{2,1,0:T(8,128)(2,1)} %bitcast.35), channel_id=1, replica_groups=mesh['x'=4,'z'=4,'c'=2,'e'=4] {'x','z'}, dimensions={0} | all-to-all | bytes 6291456 | tf_op jit(solution)/shard_map/all_to_all | solution.py:609
  170.3 4.1 %collective-permute-start.7 = (bf16[24,4096]{1,0:T(8,128)(2,1)S(1)}, bf16[24,4096]{1,0:T(8,128)(2,1)S(1)}, u32[]{:S(2)}, u32[]{:S(2)}) collective-permute-start(bf16[24,4096]{1,0:T(8,128)(2,1)S(1)} %divide_convert_fusion), channel_id=1, source_target_pairs={{0,2},{1,3},{2,0},{3,1},{4,6},{5,7},{6,4},{7,5},{8,10},{9,11},{10,... | collective-permute-start | bytes 589832 | tf_op jit(solution)/shard_map/ppermute | solution.py:37
  174.4 1.9 collective-permute-done.8
  176.3 3.8 %collective-permute-done.7 = bf16[24,4096]{1,0:T(8,128)(2,1)S(1)} collective-permute-done((bf16[24,4096]{1,0:T(8,128)(2,1)S(1)}, bf16[24,4096]{1,0:T(8,128)(2,1)S(1)}, u32[]{:S(2)}, u32[]{:S(2)}) %collective-permute-start.7) | collective-permute-done | bytes 196640 | tf_op jit(solution)/shard_map/ppermute | solution.py:37
  180.2 5.2 %out_gradient.1 = (f32[128,4096]{1,0:T(8,128)S(1)}, f32[128,1024]{1,0:T(8,128)S(1)}, bf16[1024,128]{1,0:T(8,128)(2,1)S(1)}) custom-call(bf16[96,128]{1,0:T(8,128)(2,1)S(1)} %copy-done.37, bf16[96,4096]{1,0:T(8,128)(2,1)S(1)} %pad_maximum_fusion.terms, f32[1,4096]{1,0:T(1,128)S(1)} %bitcast.29, bf16[1024,4096]{1,0:T(8,128)(2,1)S(1)} %bitcast.24, ...), custom_call_target="tpu_custom_call" | custom-call | flops 1073741824 | bytes 8388608 | tf_op jit(solution)/shard_map/out_gradient/pallas_call | solution.py:373
  185.4 1.3 copy-done.38
  186.7 17.4 %all_to_all.33.got = bf16[32,32,128]{2,1,0:T(8,128)(2,1)S(1)} all-to-all(bf16[32,32,128]{2,1,0:T(8,128)(2,1)S(1)} %bitcast.28), channel_id=1, replica_groups=mesh['x'=4,'z'=4,'c'=2,'e'=4] {'x','z','c'}, dimensions={0} | all-to-all | bytes 524288 | tf_op jit(solution)/shard_map/all_to_all | solution.py:620
  204.9 4.4 %all-to-all-start.5 = ((bf16[32,32,128]{2,1,0:T(8,128)(2,1)}), bf16[32,32,128]{2,1,0:T(8,128)(2,1)}, u32[]{:S(2)}, u32[]{:S(2)}) async-start(bf16[32,32,128]{2,1,0:T(8,128)(2,1)} %copy-done.17), calls=%async_computation.5 | async-start | bytes 524288 | tf_op jit(solution)/shard_map/all_to_all | solution.py:627
  209.3 0.9 copy-done.11
  210.2 1.0 copy-done.21
  211.3 1.0 copy-done.25
  212.3 0.8 copy-done.28
  213.1 0.8 copy-done.32
  214.0 0.8 copy-done.35
  214.8 1.5 near_gradient.1
  219.6 0.9 copy-done.8
  220.6 0.9 copy-done.12
  221.5 1.0 copy-done.23
  227.6 1.7 far_gradient.1
  229.4 3.4 %copy-done.1 = bf16[4096,1024]{1,0:T(8,128)(2,1)S(1)} copy-done((bf16[4096,1024]{1,0:T(8,128)(2,1)S(1)}, bf16[4096,1024]{1,0:T(8,128)(2,1)}, u32[]{:S(2)}) %copy-start.1) | copy-done | bytes 8388632
  232.8 1.9 back_columns.7
  234.7 1.9 back_columns.6
  236.5 1.9 back_columns.5
  239.0 2.3 collective-permute-start.10
  241.7 3.4 %copy-done.2 = bf16[4096,1024]{1,0:T(8,128)(2,1)S(1)} copy-done((bf16[4096,1024]{1,0:T(8,128)(2,1)S(1)}, bf16[4096,1024]{1,0:T(8,128)(2,1)}, u32[]{:S(2)}) %copy-start.2) | copy-done | bytes 8388632
  246.7 1.3 back_columns.4
  247.9 6.1 %collective-permute-done.10 = bf16[128,1024]{1,0:T(8,128)(2,1)} collective-permute-done((bf16[128,1024]{1,0:T(8,128)(2,1)}, bf16[128,1024]{1,0:T(8,128)(2,1)}, u32[]{:S(2)}, u32[]{:S(2)}) %collective-permute-start.10) | collective-permute-done | bytes 262176 | tf_op jit(solution)/shard_map/ppermute | solution.py:37
  254.1 2.3 subtract_convert_fusion
  (146 shorter events, 23.6 us)
Async XLA Ops:
  0.0 4.3 %copy-start.54 = (bf16[4096,8]{0,1:T(8,128)(2,1)S(1)}, bf16[4096,8]{0,1:T(8,128)(2,1)}, u32[]{:S(2)}) copy-start(bf16[4096,8]{0,1:T(8,128)(2,1)} %param.17) | copy-start | bytes 196612
  0.0 4.8 %copy-start.58 = (f32[8]{0:T(128)S(1)}, f32[8]{0:T(128)}, u32[]{:S(2)}) copy-start(f32[8]{0:T(128)} %param.19) | copy-start | bytes 100
  0.0 4.8 %copy-start.59 = (f32[8]{0:T(128)S(1)}, f32[8]{0:T(128)}, u32[]{:S(2)}) copy-start(f32[8]{0:T(128)} %param.18) | copy-start | bytes 100
  0.0 4.8 %copy-start.57 = (bf16[128,2]{0,1:T(2,128)(2,1)S(1)}, bf16[128,2]{0,1:T(2,128)(2,1)}, u32[]{:S(2)}) copy-start(bf16[128,2]{0,1:T(2,128)(2,1)} %param.23) | copy-start | bytes 1540
  0.0 4.8 %copy-start.56 = (s32[128,2]{0,1:T(2,128)S(1)}, s32[128,2]{0,1:T(2,128)}, u32[]{:S(2)}) copy-start(s32[128,2]{0,1:T(2,128)} %param.22) | copy-start | bytes 3076
  0.0 5.8 %copy-start.3 = (bf16[4096,256]{1,0:T(8,128)(2,1)S(1)}, bf16[4096,256]{1,0:T(8,128)(2,1)}, u32[]{:S(2)}) copy-start(bf16[4096,256]{1,0:T(8,128)(2,1)} %w_bc.9) | copy-start | bytes 6291460
  0.0 15.8 %collective-permute-start = (bf16[4096,256]{1,0:T(8,128)(2,1)}, bf16[4096,256]{1,0:T(8,128)(2,1)}, u32[]{:S(2)}, u32[]{:S(2)}) collective-permute-start(bf16[4096,256]{1,0:T(8,128)(2,1)} %bitcast.32), channel_id=1, source_target_pairs={{0,4},{4,0},{1,5},{5,1},{2,6},{6,2},{3,7},{7,3},{8,12},{12,8},{9,1... | collective-permute-start | bytes 6291464 | tf_op jit(solution)/shard_map/ppermute | solution.py:37
  1.5 14.4 %collective-permute-start.1 = (bf16[4096,256]{1,0:T(8,128)(2,1)}, bf16[4096,256]{1,0:T(8,128)(2,1)}, u32[]{:S(2)}, u32[]{:S(2)}) collective-permute-start(bf16[4096,256]{1,0:T(8,128)(2,1)} %bitcast.38), channel_id=1, source_target_pairs={{0,4},{4,0},{1,5},{5,1},{2,6},{6,2},{3,7},{7,3},{8,12},{12,8},{9,1... | collective-permute-start | bytes 6291464 | tf_op jit(solution)/shard_map/ppermute | solution.py:37
  3.7 11.6 %collective-permute-start.2 = (f32[1,256]{1,0:T(1,128)S(1)}, f32[1,256]{1,0:T(1,128)S(1)}, u32[]{:S(2)}, u32[]{:S(2)}) collective-permute-start(f32[1,256]{1,0:T(1,128)S(1)} %bitcast.36), channel_id=1, source_target_pairs={{0,4},{4,0},{1,5},{5,1},{2,6},{6,2},{3,7},{7,3},{8,12},{12,8},{9,1... | collective-permute-start | bytes 3080 | tf_op jit(solution)/shard_map/ppermute | solution.py:37
  5.8 3.4 %copy-start = (bf16[4096,1024]{1,0:T(8,128)(2,1)S(1)}, bf16[4096,1024]{1,0:T(8,128)(2,1)}, u32[]{:S(2)}) copy-start(bf16[4096,1024]{1,0:T(8,128)(2,1)} %w_in.9) | copy-start | bytes 25165828
  9.2 1.2 copy-start.5
  14.6 19.7 %copy-start.27 = (f32[128,128]{1,0:T(8,128)}, f32[128,128]{1,0:T(8,128)S(1)}, u32[]{:S(2)}) copy-start(f32[128,128]{1,0:T(8,128)S(1)} %get-tuple-element.59.step_ref) | copy-start | bytes 196612
  14.6 19.7 %copy-start.30 = (f32[128,128]{1,0:T(8,128)}, f32[128,128]{1,0:T(8,128)S(1)}, u32[]{:S(2)}) copy-start(f32[128,128]{1,0:T(8,128)S(1)} %get-tuple-element.45.step_t_ref) | copy-start | bytes 196612
  14.6 19.7 %copy-start.33 = (f32[128,128]{1,0:T(8,128)}, f32[128,128]{1,0:T(8,128)S(1)}, u32[]{:S(2)}) copy-start(f32[128,128]{1,0:T(8,128)S(1)} %get-tuple-element.44.cum_t_ref) | copy-start | bytes 196612
  14.6 19.7 %copy-start.40 = (f32[128,128]{1,0:T(8,128)}, f32[128,128]{1,0:T(8,128)S(1)}, u32[]{:S(2)}) copy-start(f32[128,128]{1,0:T(8,128)S(1)} %get-tuple-element.60.pre_ref) | copy-start | bytes 196612
  35.6 12.5 %all-to-all-start.1 = ((bf16[32,32,128]{2,1,0:T(8,128)(2,1)}), bf16[32,32,128]{2,1,0:T(8,128)(2,1)S(1)}, u32[]{:S(2)}, u32[]{:S(2)}) async-start(bf16[32,32,128]{2,1,0:T(8,128)(2,1)} %copy-done.26), calls=%async_computation.1 | async-start | bytes 524288 | tf_op jit(solution)/shard_map/all_to_all | solution.py:593
  48.1 161.1 %copy-start.7 = (bf16[32,32,128]{2,1,0:T(8,128)(2,1)}, bf16[32,32,128]{2,1,0:T(8,128)(2,1)S(1)}, u32[]{:S(2)}) copy-start(bf16[32,32,128]{2,1,0:T(8,128)(2,1)S(1)} %all-to-all-done.1) | copy-start | bytes 786436
  48.1 3.5 %copy-start.4 = (bf16[1024,4096]{1,0:T(8,128)(2,1)S(1)}, bf16[1024,4096]{1,0:T(8,128)(2,1)}, u32[]{:S(2)}) copy-start(bf16[1024,4096]{1,0:T(8,128)(2,1)} %w_out.3) | copy-start | bytes 25165828
  51.6 1.2 copy-start.6
  52.8 1.0 copy-start.14
  58.9 13.8 %copy-start.20 = (f32[128,1024]{1,0:T(8,128)}, f32[128,1024]{1,0:T(8,128)S(1)}, u32[]{:S(2)}) copy-start(f32[128,1024]{1,0:T(8,128)S(1)} %get-tuple-element.62.reads) | copy-start | bytes 1572868
  58.9 7.7 %collective-permute-start.3 = (bf16[24,4096]{1,0:T(8,128)(2,1)S(1)}, bf16[24,4096]{1,0:T(8,128)(2,1)S(1)}, u32[]{:S(2)}, u32[]{:S(2)}) collective-permute-start(bf16[24,4096]{1,0:T(8,128)(2,1)S(1)} %get-tuple-element.50), channel_id=1, source_target_pairs={{0,1},{1,2},{2,3},{3,0},{4,5},{5,6},{6,7},{7,4},{8,9},{9,10},{10,1... | collective-permute-start | bytes 589832 | tf_op jit(solution)/shard_map/ppermute | solution.py:37
  60.3 11.7 %collective-permute-start.4 = (bf16[24,4096]{1,0:T(8,128)(2,1)S(1)}, bf16[24,4096]{1,0:T(8,128)(2,1)S(1)}, u32[]{:S(2)}, u32[]{:S(2)}) collective-permute-start(bf16[24,4096]{1,0:T(8,128)(2,1)S(1)} %get-tuple-element.51), channel_id=1, source_target_pairs={{0,2},{1,3},{2,0},{3,1},{4,6},{5,7},{6,4},{7,5},{8,10},{9,11},{10,... | collective-permute-start | bytes 589832 | tf_op jit(solution)/shard_map/ppermute | solution.py:37
  62.9 9.1 %collective-permute-start.5 = (bf16[24,4096]{1,0:T(8,128)(2,1)S(1)}, bf16[24,4096]{1,0:T(8,128)(2,1)S(1)}, u32[]{:S(2)}, u32[]{:S(2)}) collective-permute-start(bf16[24,4096]{1,0:T(8,128)(2,1)S(1)} %get-tuple-element.52), channel_id=1, source_target_pairs={{0,3},{1,0},{2,1},{3,2},{4,7},{5,4},{6,5},{7,6},{8,11},{9,8},{10,9... | collective-permute-start | bytes 589832 | tf_op jit(solution)/shard_map/ppermute | solution.py:37
  72.7 41.3 %copy-start.52 = (f32[2,256]{1,0:T(2,128)S(1)}, f32[2,256]{1,0:T(2,128)}, u32[]{:S(2)}) copy-start(f32[2,256]{1,0:T(2,128)} %pad_maximum_fusion.2.hv_ref) | copy-start | bytes 6148
  72.7 41.3 %copy-start.53 = (bf16[1,4096,256]{2,1,0:T(8,128)(2,1)S(1)}, bf16[1,4096,256]{2,1,0:T(8,128)(2,1)}, u32[]{:S(2)}) copy-start(bf16[1,4096,256]{2,1,0:T(8,128)(2,1)} %param.24) | copy-start | bytes 6291460
  114.0 66.1 %slice-start = ((s8[8388608]{0:T(1024)(128)(4,1)}), s8[4194304]{0:T(1024)(128)(4,1)S(1)}, s32[]{:S(2)}) async-start(s8[8388608]{0:T(1024)(128)(4,1)} %bitcast.23), calls=%async_computation.6 | async-start | bytes 8388608
  114.0 66.1 %slice-start.1 = ((s8[8388608]{0:T(1024)(128)(4,1)}), s8[4194304]{0:T(1024)(128)(4,1)S(1)}, s32[]{:S(2)}) async-start(s8[8388608]{0:T(1024)(128)(4,1)} %bitcast.23), calls=%async_computation.7 | async-start | bytes 8388608
  169.6 10.6 %copy-start.37 = (bf16[96,128]{1,0:T(8,128)(2,1)S(1)}, bf16[96,128]{1,0:T(8,128)(2,1)}, u32[]{:S(2)}) copy-start(bf16[96,128]{1,0:T(8,128)(2,1)} %pad_maximum_fusion.1.table) | copy-start | bytes 73732
  169.6 10.6 %copy-start.39 = (f32[4096]{0:T(1024)S(1)}, f32[4096]{0:T(1024)}, u32[]{:S(2)}) copy-start(f32[4096]{0:T(1024)} %param.27) | copy-start | bytes 49156
  170.0 6.3 %collective-permute-start.8 = (bf16[24,4096]{1,0:T(8,128)(2,1)S(1)}, bf16[24,4096]{1,0:T(8,128)(2,1)S(1)}, u32[]{:S(2)}, u32[]{:S(2)}) collective-permute-start(bf16[24,4096]{1,0:T(8,128)(2,1)S(1)} %divide_convert_fusion), channel_id=1, source_target_pairs={{0,1},{1,2},{2,3},{3,0},{4,5},{5,6},{6,7},{7,4},{8,9},{9,10},{10,1... | collective-permute-start | bytes 589832 | tf_op jit(solution)/shard_map/ppermute | solution.py:37
  170.3 9.7 %collective-permute-start.7 = (bf16[24,4096]{1,0:T(8,128)(2,1)S(1)}, bf16[24,4096]{1,0:T(8,128)(2,1)S(1)}, u32[]{:S(2)}, u32[]{:S(2)}) collective-permute-start(bf16[24,4096]{1,0:T(8,128)(2,1)S(1)} %divide_convert_fusion), channel_id=1, source_target_pairs={{0,2},{1,3},{2,0},{3,1},{4,6},{5,7},{6,4},{7,5},{8,10},{9,11},{10,... | collective-permute-start | bytes 589832 | tf_op jit(solution)/shard_map/ppermute | solution.py:37
  174.4 5.6 %collective-permute-start.6 = (bf16[24,4096]{1,0:T(8,128)(2,1)S(1)}, bf16[24,4096]{1,0:T(8,128)(2,1)S(1)}, u32[]{:S(2)}, u32[]{:S(2)}) collective-permute-start(bf16[24,4096]{1,0:T(8,128)(2,1)S(1)} %divide_convert_fusion), channel_id=1, source_target_pairs={{0,3},{1,0},{2,1},{3,2},{4,7},{5,4},{6,5},{7,6},{8,11},{9,8},{10,9... | collective-permute-start | bytes 589832 | tf_op jit(solution)/shard_map/ppermute | solution.py:37
  180.2 23.9 %copy-start.51 = (f32[32,128]{1,0:T(8,128)S(1)}, f32[32,128]{1,0:T(8,128)}, u32[]{:S(2)}) copy-start(f32[32,128]{1,0:T(8,128)} %copy-done.50) | copy-start | bytes 49156
  185.3 1.3 copy-start.38
  186.7 17.4 %copy-start.24 = (f32[128,1024]{1,0:T(8,128)}, f32[128,1024]{1,0:T(8,128)S(1)}, u32[]{:S(2)}) copy-start(f32[128,1024]{1,0:T(8,128)S(1)} %get-tuple-element.61.grad_ref) | copy-start | bytes 1572868
  204.9 14.7 %all-to-all-start.5 = ((bf16[32,32,128]{2,1,0:T(8,128)(2,1)}), bf16[32,32,128]{2,1,0:T(8,128)(2,1)}, u32[]{:S(2)}, u32[]{:S(2)}) async-start(bf16[32,32,128]{2,1,0:T(8,128)(2,1)} %copy-done.17), calls=%async_computation.5 | async-start | bytes 524288 | tf_op jit(solution)/shard_map/all_to_all | solution.py:627
  209.3 1.0 copy-start.11
  210.2 1.0 copy-start.21
  211.3 1.0 copy-start.25
  221.5 1.0 copy-start.23
  229.3 7.2 %copy-start.15 = (bf16[128,256]{1,0:T(8,128)(2,1)}, bf16[128,256]{1,0:T(8,128)(2,1)S(1)}, u32[]{:S(2)}) copy-start(bf16[128,256]{1,0:T(8,128)(2,1)S(1)} %get-tuple-element.69.gbc) | copy-start | bytes 196612
  229.3 7.2 %copy-start.18 = (bf16[128,128]{1,0:T(8,128)(2,1)}, bf16[128,128]{1,0:T(8,128)(2,1)S(1)}, u32[]{:S(2)}) copy-start(bf16[128,128]{1,0:T(8,128)(2,1)S(1)} %get-tuple-element.70.gpre) | copy-start | bytes 98308
  229.3 3.4 %copy-start.1 = (bf16[4096,1024]{1,0:T(8,128)(2,1)S(1)}, bf16[4096,1024]{1,0:T(8,128)(2,1)}, u32[]{:S(2)}) copy-start(bf16[4096,1024]{1,0:T(8,128)(2,1)} %w_in.9) | copy-start | bytes 25165828
  238.4 9.5 %collective-permute-start.9 = (bf16[128,1024]{1,0:T(8,128)(2,1)}, bf16[128,1024]{1,0:T(8,128)(2,1)}, u32[]{:S(2)}, u32[]{:S(2)}) collective-permute-start(bf16[128,1024]{1,0:T(8,128)(2,1)} %back_columns.5), channel_id=1, source_target_pairs={{0,2},{1,3},{2,0},{3,1},{4,6},{5,7},{6,4},{7,5},{8,10},{9,11},{10,... | collective-permute-start | bytes 786440 | tf_op jit(solution)/shard_map/ppermute | solution.py:37
  239.0 15.1 %collective-permute-start.10 = (bf16[128,1024]{1,0:T(8,128)(2,1)}, bf16[128,1024]{1,0:T(8,128)(2,1)}, u32[]{:S(2)}, u32[]{:S(2)}) collective-permute-start(bf16[128,1024]{1,0:T(8,128)(2,1)} %back_columns.6), channel_id=1, source_target_pairs={{0,1},{1,2},{2,3},{3,0},{4,5},{5,6},{6,7},{7,4},{8,9},{9,10},{10,1... | collective-permute-start | bytes 786440 | tf_op jit(solution)/shard_map/ppermute | solution.py:37
  241.3 12.8 %collective-permute-start.11 = (bf16[128,1024]{1,0:T(8,128)(2,1)}, bf16[128,1024]{1,0:T(8,128)(2,1)}, u32[]{:S(2)}, u32[]{:S(2)}) collective-permute-start(bf16[128,1024]{1,0:T(8,128)(2,1)} %back_columns.7), channel_id=1, source_target_pairs={{0,3},{1,0},{2,1},{3,2},{4,7},{5,4},{6,5},{7,6},{8,11},{9,8},{10,9... | collective-permute-start | bytes 786440 | tf_op jit(solution)/shard_map/ppermute | solution.py:37
  241.7 3.4 %copy-start.2 = (bf16[4096,1024]{1,0:T(8,128)(2,1)S(1)}, bf16[4096,1024]{1,0:T(8,128)(2,1)}, u32[]{:S(2)}) copy-start(bf16[4096,1024]{1,0:T(8,128)(2,1)} %w_in.9) | copy-start | bytes 25165828
  (28 other events, 22.0 us)

commit v3 on v2

--- a/solution.py
+++ b/solution.py
@@ -16,7 +16,6 @@
 BF = jnp.bfloat16
 F32 = jnp.float32
 SEQ = ("x", "z", "c")
-PLANE = ("x", "z")
 EXTRA = 16
 
 
@@ -50,45 +49,113 @@
     return table.astype(F32), weight
 
 
-def expert_kernel(rows_ref, wg0, wg1, wu0, wu1, hv_ref, out_ref, first, second):
+def swap_blocks(value, side, rows):
+    return jnp.concatenate(
+        [
+            value[(b * side + a) * rows : (b * side + a + 1) * rows]
+            for a in range(side)
+            for b in range(side)
+        ],
+        axis=0,
+    )
+
+
+def expert_kernel(side, *refs):
+    near, far = refs[:side], refs[side : 2 * side]
+    wg0, wg1, wu0, wu1, hv_ref = refs[2 * side : 2 * side + 5]
+    out_near, out_far, first, second = refs[2 * side + 5 :]
     half = wg0.shape[1]
-    rows = rows_ref[...]
+    depth = out_near.shape[1]
+    slot = out_near.shape[0] // (side * side)
+    near_rows = jnp.concatenate([r[...] for r in near], axis=0)
+    far_rows = jnp.concatenate([r[...] for r in far], axis=0)
+
+    def product(w):
+        return mm(near_rows, w[:depth, :]) + swap_blocks(mm(far_rows, w[depth:, :]), side, slot)
+
     for k, (wg, wu) in enumerate(((wg0, wu0), (wg1, wu1))):
         span = slice(k * half, (k + 1) * half)
-        gate = mm(rows, wg[...])
-        up = mm(rows, wu[...])
+        gate = product(wg)
+        up = product(wu)
         sig = 1.0 / (1.0 + jnp.exp(-gate))
         hv = hv_ref[k : k + 1, :]
         first[:, span] = (hv * up * sig * (1.0 + gate * (1.0 - sig))).astype(BF)
         second[:, span] = (hv * gate * sig).astype(BF)
-    width = rows.shape[1]
-    step = min(width, 512)
-
-    @pl.loop(0, width // step)
+    step = min(depth, 512)
+
+    def terms(cols):
+        total = mm_t(first[:, :half], wg0[cols, :]) + mm_t(second[:, :half], wu0[cols, :])
+        return total + mm_t(first[:, half:], wg1[cols, :]) + mm_t(second[:, half:], wu1[cols, :])
+
+    @pl.loop(0, depth // step)
     def _(i):
-        cols = pl.ds(pl.multiple_of(i * step, step), step)
-        total = mm_t(first[:, :half], wg0[cols, :]) + mm_t(second[:, :half], wu0[cols, :])
-        total += mm_t(first[:, half:], wg1[cols, :]) + mm_t(second[:, half:], wu1[cols, :])
-        out_ref[:, cols] = total.astype(BF)
-
-
-def expert_rows(rows, wg0, wg1, wu0, wu1, head_vec):
-    count, width = rows.shape
+        start = pl.multiple_of(i * step, step)
+        cols = pl.ds(start, step)
+        out_near[:, cols] = terms(cols).astype(BF)
+        more = pl.ds(pl.multiple_of(depth + start, step), step)
+        out_far[:, cols] = swap_blocks(terms(more), side, slot).astype(BF)
+
+
+def expert_rows(near, far, wg0, wg1, wu0, wu1, head_vec):
+    side = len(near)
+    count = side * near[0].shape[0]
+    depth = near[0].shape[1]
     half = wg0.shape[1]
-    return pl.pallas_call(
-        expert_kernel,
-        out_shape=jax.ShapeDtypeStruct((count, width), BF),
-        in_specs=[pl.BlockSpec(memory_space=pltpu.VMEM)] * 6,
-        out_specs=pl.BlockSpec(memory_space=pltpu.VMEM),
+    out = jax.ShapeDtypeStruct((count, depth), BF)
+    return single(
+        functools.partial(expert_kernel, side),
+        out_shape=(out, out),
+        args=(*near, *far, wg0, wg1, wu0, wu1, head_vec),
         scratch_shapes=[pltpu.VMEM((count, 2 * half), BF)] * 2,
-        compiler_params=pltpu.CompilerParams(vmem_limit_bytes=48 << 20),
-        cost_estimate=pl.CostEstimate(
-            flops=16 * count * width * half,
-            bytes_accessed=8 * width * half + 4 * count * width,
-            transcendentals=2 * count * half,
-        ),
+        compiler_params=vmem(56),
+        cost_estimate=cost(32 * count * depth * half, 16 * depth * half + 8 * count * depth),
         name="experts",
-    )(rows, wg0, wg1, wu0, wu1, head_vec)
+    )
+
+
+def gather_around(value, axis):
+    count = lax.axis_size(axis)
+    if count != 4:
+        return [value] + [shift(value, axis, count - k) for k in range(1, count)]
+    left, right = shift(value, axis, 1), shift(value, axis, 3)
+    cut = value.shape[0] // 2
+    across = jnp.concatenate(
+        [shift(left[:cut], axis, 1), shift(right[cut:], axis, 3)], axis=0
+    )
+    return [value, right, across, left]
+
+
+def gather_direct(value, axis):
+    count = lax.axis_size(axis)
+    return [value] + [shift(value, axis, count - k) for k in range(1, count)]
+
+
+def scatter_direct(pieces, axis):
+    total = pieces[0].astype(F32)
+    for k in range(1, len(pieces)):
+        total = total + shift(pieces[k], axis, k).astype(F32)
+    return total
+
+
+def scatter_around(pieces, axis):
+    if len(pieces) != 4:
+        return scatter_direct(pieces, axis)
+    own, right, across, left = pieces
+    cut = across.shape[0] // 2
+    top = shift(across[:cut], axis, 1)
+    bottom = shift(across[cut:], axis, 3)
+    right = jnp.concatenate(
+        [(right[:cut].astype(F32) + top.astype(F32)).astype(BF), right[cut:]], axis=0
+    )
+    left = jnp.concatenate(
+        [left[:cut], (left[cut:].astype(F32) + bottom.astype(F32)).astype(BF)], axis=0
+    )
+    return own.astype(F32) + shift(right, axis, 1).astype(F32) + shift(left, axis, 3).astype(F32)
+
+
+def split_rows(value, count):
+    rows = value.shape[0] // count
+    return [value[k * rows : (k + 1) * rows] for k in range(count)]
 
 
 def row_mask(tlen):
@@ -101,8 +168,20 @@
     return pltpu.CompilerParams(vmem_limit_bytes=mib << 20)
 
 
-def whole(count):
-    return [pl.BlockSpec(memory_space=pltpu.VMEM)] * count
+def whole(arrays):
+    return [pl.BlockSpec(a.shape, lambda i, n=len(a.shape): (0,) * n) for a in arrays]
+
+
+def single(kernel, out_shape, args, **options):
+    outs = whole(out_shape) if isinstance(out_shape, tuple) else whole((out_shape,))[0]
+    return pl.pallas_call(
+        kernel,
+        grid=(1,),
+        out_shape=out_shape,
+        in_specs=whole(args),
+        out_specs=tuple(outs) if isinstance(outs, list) else outs,
+        **options,
+    )(*args)
 
 
 def cost(flops, moved):
@@ -201,7 +280,7 @@
         scratch_shapes=[
             pltpu.VMEM((tlen, chan), F32), pltpu.VMEM((tlen, two), F32), pltpu.VMEM((tlen, tlen), F32)
         ],
-        compiler_params=vmem(24),
+        compiler_params=vmem(56),
         cost_estimate=cost(2 * tlen * width * (chan + two), 2 * width * (chan + two + 2 * tlen)),
         name="project",
     )(candidate, in_proj, bc_proj, step_proj, bias, rate)
@@ -222,17 +301,16 @@
 
 def enter_states(got, slice_rows):
     count, _, nstate = got.shape
-    return pl.pallas_call(
+    return single(
         enter_kernel,
         out_shape=(
             jax.ShapeDtypeStruct((count, slice_rows, nstate), BF),
             jax.ShapeDtypeStruct((count, nstate), F32),
         ),
-        in_specs=whole(1),
-        out_specs=tuple(whole(2)),
-        compiler_params=vmem(8),
+        args=(got,),
+        compiler_params=vmem(56),
         name="enter",
-    )(got)
+    )
 
 
 def leave_kernel(got, decay, out):
@@ -245,14 +323,13 @@
 
 
 def leave_states(got, decay):
-    return pl.pallas_call(
+    return single(
         leave_kernel,
         out_shape=jax.ShapeDtypeStruct(got.shape, BF),
-        in_specs=whole(2),
-        out_specs=whole(1)[0],
-        compiler_params=vmem(8),
+        args=(got, decay,),
+        compiler_params=vmem(56),
         name="leave",
-    )(got, decay)
+    )
 
 
 def decay_weights(cum, cum_t, h):
@@ -277,15 +354,14 @@
 
 def mix_within(inner_b, bc_bf, cum, cum_t, step_t, skip, heads):
     tlen, chan = inner_b.shape
-    return pl.pallas_call(
+    return single(
         functools.partial(within_kernel, heads),
         out_shape=jax.ShapeDtypeStruct((tlen, chan), F32),
-        in_specs=whole(6),
-        out_specs=whole(1)[0],
-        compiler_params=vmem(12),
+        args=(inner_b, bc_bf, cum, cum_t, step_t, skip,),
+        compiler_params=vmem(56),
         cost_estimate=cost(2 * tlen * tlen * chan * 4, 8 * tlen * chan),
         name="mix_within",
-    )(inner_b, bc_bf, cum, cum_t, step_t, skip)
+    )
 
 
 def slots_kernel(
@@ -331,7 +407,7 @@
         + [cols(tlen), cols(chan)],
         out_specs=(cols(CAP), cols(CAP), cols(CAP), cols(CAP), fixed(within)),
         scratch_shapes=[pltpu.VMEM((rows, chan), BF)],
-        compiler_params=vmem(24),
+        compiler_params=vmem(56),
         cost_estimate=cost(2 * rows * chan * width, 2 * chan * width),
         name="mix_slots",
     )(within, bc_bf, cum, state, table, own_table, candidate, out_proj)
@@ -384,7 +460,7 @@
         ],
         out_specs=(cols(tlen), fixed(tlen, chan), fixed(chan, nstate)),
         scratch_shapes=[pltpu.VMEM((tlen, chan), F32)],
-        compiler_params=vmem(24),
+        compiler_params=vmem(56),
         cost_estimate=cost(2 * tlen * chan * width, 2 * chan * width),
         name="out_gradient",
     )(table, terms, energy, out_proj, bc_bf, cum)
@@ -434,16 +510,15 @@
 def near_gradient(grad, inner_b, bc_bf, cum, cum_t, step, step_t, reads, state, skip, heads):
     tlen, chan = grad.shape
     small = jax.ShapeDtypeStruct((tlen, tlen), F32)
-    return pl.pallas_call(
+    return single(
         functools.partial(near_kernel, heads),
         out_shape=(jax.ShapeDtypeStruct((tlen, chan), F32), small, small, small, small),
-        in_specs=whole(10),
-        out_specs=tuple(whole(5)),
+        args=(grad, inner_b, bc_bf, cum, cum_t, step, step_t, reads, state, skip,),
         scratch_shapes=[pltpu.VMEM((tlen, tlen), F32)] * 2,
-        compiler_params=vmem(16),
+        compiler_params=vmem(56),
         cost_estimate=cost(2 * tlen * tlen * chan * 8, 20 * tlen * chan),
         name="near_gradient",
-    )(grad, inner_b, bc_bf, cum, cum_t, step, step_t, reads, state, skip)
+    )
 
 
 def far_kernel(
@@ -490,20 +565,19 @@
 
 def far_gradient(later, state, inner_b, bc_bf, cum, step, pre, rate, near, gb, gc, dcum, dstep, heads):
     tlen, chan = near.shape
-    return pl.pallas_call(
+    return single(
         functools.partial(far_kernel, heads),
         out_shape=(
             jax.ShapeDtypeStruct((tlen, chan), BF),
             jax.ShapeDtypeStruct(bc_bf.shape, BF),
             jax.ShapeDtypeStruct((tlen, tlen), BF),
         ),
-        in_specs=whole(13),
-        out_specs=tuple(whole(3)),
+        args=(later, state, inner_b, bc_bf, cum, step, pre, rate, near, gb, gc, dcum, dstep,),
         scratch_shapes=[pltpu.VMEM((tlen, tlen), F32)] * 2,
-        compiler_params=vmem(16),
+        compiler_params=vmem(56),
         cost_estimate=cost(2 * tlen * tlen * chan * 4, 20 * tlen * chan),
         name="far_gradient",
-    )(later, state, inner_b, bc_bf, cum, step, pre, rate, near, gb, gc, dcum, dstep)
+    )
 
 
 def back_kernel(heads, which, g_ref, gbc, gpre, w_in, w_bc, w_step, out):
@@ -528,7 +602,7 @@
             out_specs=pl.BlockSpec((tlen, block), lambda i, w: (0, i)),
         ),
         out_shape=jax.ShapeDtypeStruct((tlen, cols), dtype),
-        compiler_params=vmem(12),
+        compiler_params=vmem(56),
         cost_estimate=cost(2 * tlen * (chan + two) * cols, 2 * (chan + two) * cols),
         name="back_columns",
     )(which, g_inner, g_bc, g_pre, in_proj, bc_proj, step_proj)
@@ -558,7 +632,6 @@
     column = lax.axis_index("e")
     n_exp = lax.axis_size("e")
     n_seq = lax.axis_size(SEQ)
-    n_plane = lax.axis_size(PLANE)
     col_count = width // n_exp
     slice_rows = chan // n_seq
     lanes = lambda v: jnp.pad(v, (0, tlen - heads))[None, :]
@@ -602,12 +675,22 @@
     normed = hidden / scale
     routed = normed.astype(BF)
 
-    rows = lax.all_to_all(
-        jnp.broadcast_to(routed[None], (n_plane, CAP, width)), PLANE, 0, 0, tiled=True
-    ).reshape(n_plane * CAP, width)
-    terms = expert_rows(rows, wg0, wg1, wu0, wu1, head_vec)
-    back = lax.all_to_all(terms.reshape(n_plane, CAP, width), PLANE, 0, 0, tiled=True)
-    slot_grad = jnp.sum(back.astype(F32), axis=0)
+    side = lax.axis_size("x")
+    cut = width // 2
+    near_own = jnp.concatenate(gather_direct(routed[:, :cut], "z"), axis=0)
+    far_own = jnp.concatenate(gather_direct(routed[:, cut:], "x"), axis=0)
+    near_rows = gather_around(near_own, "x")
+    far_rows = gather_around(far_own, "z")
+    out_near, out_far = expert_rows(near_rows, far_rows, wg0, wg1, wu0, wu1, head_vec)
+    near_sum = scatter_around(split_rows(out_near, side), "x").astype(BF)
+    far_sum = scatter_around(split_rows(out_far, side), "z").astype(BF)
+    slot_grad = jnp.concatenate(
+        [
+            scatter_direct(split_rows(near_sum, side), "z"),
+            scatter_direct(split_rows(far_sum, side), "x"),
+        ],
+        axis=1,
+    )
     along = jnp.mean(normed * slot_grad, axis=-1, keepdims=True)
     slot_term = (slot_weight * (slot_grad - normed * along) / scale).astype(BF)
     all_terms = jnp.concatenate(

time: 258 us -> 235 us (0.911)
  blocking collectives: 118 us -> 42.6 us
  starting transfers between devices: 22.9 us -> 63.2 us
  local copies, waits for them, and re-layouts: 45.4 us -> 5.72 us
  Pallas kernels: 37.5 us -> 63.7 us
  waiting for transfers between devices: 24.1 us -> 47.6 us
  other arithmetic: 7.93 us -> 11 us
    all_to_all x2 -> x0, blocking collectives: 82.4 us -> none  [the longest x1 41.3 us: shards(): lax.all_to_all(jnp.broadcast_to(routed[None], (n_plane, CAP, width)), PLA...]
    unnamed x125 -> x41, local copies, waits for them, and re-layouts: 44.3 us -> 2.87 us
    ppermute x12 -> x40, starting transfers between devices: 14.9 us -> 55.9 us  [shift(): lax.ppermute(value, axis, [(i, (i + by) % count) for i in range(count)])]
    ppermute x12 -> x40, waiting for transfers between devices: 19.8 us -> 36.3 us  [shift(): lax.ppermute(value, axis, [(i, (i + by) % count) for i in range(count)])]
    pallas_call x6, Pallas kernels: 17.7 us -> 25.6 us  [single(): pl.pallas_call(kernel, grid=(1,), out_shape=out_shape, in_specs=whole(arg...]
    pallas_call x4, Pallas kernels: 6.89 us -> 13.9 us  [back_columns(): pl.pallas_call(functools.partial(back_kernel, heads), grid_spec=pltpu.Pre...]
    all_to_all x1, blocking collectives: 17.4 us -> 24 us  [shards(): lax.all_to_all(local_grad.reshape(n_seq, slice_rows, nstate), SEQ, 0, 0,...]
    all_to_all x1, waiting for transfers between devices: 0.01 us -> 5.34 us  [shards(): later = lax.all_to_all(leaving, SEQ, 0, 0, tiled=True).reshape(chan, nstate)]
  transfers between devices with their start and end apart: 14 -> 42, of which waited for: 6 -> 20; matrix products, arithmetic and copies ran while one was open for 2% -> 3% of each run, Pallas kernels for 3% -> 8%
where the time goes in v3:
time: 235 us; the launch traced here: 234 us
  Pallas kernels  63.7 us (27%)
  starting transfers between devices  63.2 us (27%)
  waiting for transfers between devices  47.6 us (20%)
  blocking collectives  42.6 us (18%)
  other arithmetic  11 us (5%)
  local copies, waits for them, and re-layouts  5.72 us (2%)
    ppermute x40, starting transfers between devices, shift(): lax.ppermute(value, axis, [(i, (i + by) % count) for i in range(count)])  55.9 us
    ppermute x40, waiting for transfers between devices, shift(): lax.ppermute(value, axis, [(i, (i + by) % count) for i in range(count)])  36.3 us
    pallas_call x6, Pallas kernels, single(): pl.pallas_call(kernel, grid=(1,), out_shape=out_shape, in_specs=whole(arg...  25.6 us
    all_to_all x1, blocking collectives, shards(): lax.all_to_all(local_grad.reshape(n_seq, slice_rows, nstate), SEQ, 0, 0,...  24 us
    all_to_all x1, blocking collectives, shards(): got = lax.all_to_all(payload, SEQ, 0, 0, tiled=True)  18.5 us
    pallas_call x4, Pallas kernels, back_columns(): pl.pallas_call(functools.partial(back_kernel, heads), grid_spec=pltpu.Pre...  13.9 us
    pallas_call x1, Pallas kernels, out_gradient(): pl.pallas_call(functools.partial(outgrad_kernel, heads), grid=(width // b...  8.25 us
    pallas_call x1, Pallas kernels, project(): pl.pallas_call(functools.partial(proj_kernel, heads, slice_rows), grid=(w...  8.22 us
  transfers between devices with their start and end apart: 42, of which 20 were waited for; matrix products, arithmetic and copies ran while one was open for 3% of the time, Pallas kernels for 8%

profile of v3, /device:TPU:1, one launch (start us, length us, event | category | flops | bytes accessed | tf_op | source)
XLA Modules:
  0.0 234.1 jit_solution(3340615884854039885)
XLA Ops:
  1.5 2.1 fusion
  6.6 8.2 %project.1 = (bf16[128,1024]{1,0:T(8,128)(2,1)}, bf16[128,256]{1,0:T(8,128)(2,1)}, f32[128,128]{1,0:T(8,128)}, f32[128,128]{1,0:T(8,128)}, f32[128,128]{1,0:T(8,...) custom-call(bf16[128,4096]{1,0:T(8,128)(2,1)} %cand.3, bf16[4096,1024]{1,0:T(8,128)(2,1)} %w_in.9, ...), custom_call_target="tpu_custom_call" | custom-call | flops 1342177280 | bytes 12582912 | tf_op jit(solution)/shard_map/project/pallas_call | solution.py:259
  16.2 18.5 %all_to_all.20.got = bf16[32,48,128]{2,1,0:T(8,128)(2,1)} all-to-all(bf16[32,48,128]{2,1,0:T(8,128)(2,1)} %get-tuple-element.48), channel_id=1, replica_groups=mesh['x'=4,'z'=4,'c'=2,'e'=4] {'x','z','c'}, dimensions={0} | all-to-all | bytes 786432 | tf_op jit(solution)/shard_map/all_to_all | solution.py:663
  34.7 1.8 enter.1
  36.6 3.7 %all-to-all-start.1 = ((bf16[32,32,128]{2,1,0:T(8,128)(2,1)}), bf16[32,32,128]{2,1,0:T(8,128)(2,1)S(1)}, u32[]{:S(2)}, u32[]{:S(2)}) async-start(bf16[32,32,128]{2,1,0:T(8,128)(2,1)} %get-tuple-element.49), calls=%async_computation.1 | async-start | bytes 524288 | tf_op jit(solution)/shard_map/all_to_all | solution.py:666
  40.9 2.2 mix_within.1.within
  43.1 6.0 %all-to-all-done.1 = bf16[32,32,128]{2,1,0:T(8,128)(2,1)S(1)} async-done(((bf16[32,32,128]{2,1,0:T(8,128)(2,1)}), bf16[32,32,128]{2,1,0:T(8,128)(2,1)S(1)}, u32[]{:S(2)}, u32[]{:S(2)}) %all-to-all-start.1) | async-done | bytes 262176 | tf_op jit(solution)/shard_map/all_to_all | solution.py:666
  49.8 7.7 %mix_slots.1 = (f32[24,4096]{1,0:T(8,128)}, bf16[24,4096]{1,0:T(8,128)(2,1)}, bf16[24,4096]{1,0:T(8,128)(2,1)}, bf16[24,4096]{1,0:T(8,128)(2,1)}, f32[128,1024]{1,0:T(8,128)}) custom-call(f32[128,1024]{1,0:T(8,128)} %mix_within.1.within, bf16[128,256]{1,0:T(8,128)(2,1)} %get-tuple-element.44.bc_ref, f32[128,128]{1,0:T(8,128)} %get-tuple-element.45.cum_ref, ...), custom_call_target="tpu_custom_call" | custom-call | flops 805306368 | bytes 8388608 | tf_op jit(solution)/shard_map/mix_slots/pallas_call | solution.py:399
  58.9 2.6 %collective-permute-start.4 = (bf16[24,4096]{1,0:T(8,128)(2,1)}, bf16[24,4096]{1,0:T(8,128)(2,1)S(1)}, u32[]{:S(2)}, u32[]{:S(2)}) collective-permute-start(bf16[24,4096]{1,0:T(8,128)(2,1)} %get-tuple-element.53), channel_id=1, source_target_pairs={{0,2},{1,3},{2,0},{3,1},{4,6},{5,7},{6,4},{7,5},{8,10},{9,11},{10,... | collective-permute-start | bytes 589832 | tf_op jit(solution)/shard_map/ppermute | solution.py:36
  62.6 2.9 %collective-permute-done.3 = bf16[24,4096]{1,0:T(8,128)(2,1)S(1)} collective-permute-done((bf16[24,4096]{1,0:T(8,128)(2,1)}, bf16[24,4096]{1,0:T(8,128)(2,1)S(1)}, u32[]{:S(2)}, u32[]{:S(2)}) %collective-permute-start.3) | collective-permute-done | bytes 196640 | tf_op jit(solution)/shard_map/ppermute | solution.py:36
  65.5 5.3 %collective-permute-done.4 = bf16[24,4096]{1,0:T(8,128)(2,1)S(1)} collective-permute-done((bf16[24,4096]{1,0:T(8,128)(2,1)}, bf16[24,4096]{1,0:T(8,128)(2,1)S(1)}, u32[]{:S(2)}, u32[]{:S(2)}) %collective-permute-start.4) | collective-permute-done | bytes 196640 | tf_op jit(solution)/shard_map/ppermute | solution.py:36
  72.8 1.8 collective-permute-start.7
  75.8 1.7 collective-permute-start.14
  79.7 2.3 collective-permute-start.9
  83.0 2.8 %collective-permute-start.16 = (bf16[96,2048]{1,0:T(8,128)(2,1)S(1)}, bf16[96,2048]{1,0:T(8,128)(2,1)S(1)}, u32[]{:S(2)}, u32[]{:S(2)}) collective-permute-start(bf16[96,2048]{1,0:T(8,128)(2,1)S(1)} %pad_maximum_fusion.3.refs_4_), channel_id=1, source_target_pairs={{0,24},{8,0},{16,8},{24,16},{1,25},{9,1},{17,9},{25,17},{2,26},{10... | collective-permute-start | bytes 1179656 | tf_op jit(solution)/shard_map/ppermute | solution.py:36
  85.7 3.0 %collective-permute-done.10.refs_3_ = bf16[96,2048]{1,0:T(8,128)(2,1)S(1)} collective-permute-done((bf16[96,2048]{1,0:T(8,128)(2,1)S(1)}, bf16[96,2048]{1,0:T(8,128)(2,1)S(1)}, u32[]{:S(2)}, u32[]{:S(2)}) %collective-permute-start.10) | collective-permute-done | bytes 393248 | tf_op jit(solution)/shard_map/ppermute | solution.py:36
  90.3 2.6 %collective-permute-start.12 = (bf16[48,2048]{1,0:T(8,128)(2,1)S(1)}, bf16[48,2048]{1,0:T(8,128)(2,1)S(1)}, u32[]{:S(2)}, u32[]{:S(2)}) collective-permute-start(bf16[48,2048]{1,0:T(8,128)(2,1)S(1)} %slice.132), channel_id=1, source_target_pairs={{0,96},{32,0},{64,32},{96,64},{1,97},{33,1},{65,33},{97,65},{2,98}... | collective-permute-start | bytes 589832 | tf_op jit(solution)/shard_map/ppermute | solution.py:36
  93.8 3.1 %collective-permute-start.19 = (bf16[48,2048]{1,0:T(8,128)(2,1)S(1)}, bf16[48,2048]{1,0:T(8,128)(2,1)S(1)}, u32[]{:S(2)}, u32[]{:S(2)}) collective-permute-start(bf16[48,2048]{1,0:T(8,128)(2,1)S(1)} %slice.135), channel_id=1, source_target_pairs={{0,24},{8,0},{16,8},{24,16},{1,25},{9,1},{17,9},{25,17},{2,26},{10... | collective-permute-start | bytes 589832 | tf_op jit(solution)/shard_map/ppermute | solution.py:36
  97.7 1.9 collective-permute-done.18
  100.4 13.2 %experts.1 = (bf16[384,2048]{1,0:T(8,128)(2,1)}, bf16[384,2048]{1,0:T(8,128)(2,1)}) custom-call(bf16[96,2048]{1,0:T(8,128)(2,1)} %copy-done.4, bf16[96,2048]{1,0:T(8,128)(2,1)} %copy-done.9, bf16[96,2048]{1,0:T(8,128)(2,1)} %pad_maximum_fusion.2.refs_2_, bf16[96,2048]{1,0:T(8,128)(2,1)} %copy-done.8, bf16[96,2048]{1,0:T(8,128)(2,1)} %copy-done.5, ...), custom_call_target="tpu_custom_call" | custom-call | flops 6442450944 | bytes 14680064 | tf_op jit(solution)/shard_map/experts/pallas_call | solution.py:177
  115.2 2.7 %collective-permute-start.22 = (bf16[48,2048]{1,0:T(8,128)(2,1)S(1)}, bf16[48,2048]{1,0:T(8,128)(2,1)S(1)}, u32[]{:S(2)}, u32[]{:S(2)}) collective-permute-start(bf16[48,2048]{1,0:T(8,128)(2,1)S(1)} %get-tuple-element.85), channel_id=1, source_target_pairs={{0,96},{32,0},{64,32},{96,64},{1,97},{33,1},{65,33},{97,65},{2,98}... | collective-permute-start | bytes 589832 | tf_op jit(solution)/shard_map/ppermute | solution.py:36
  119.4 1.6 collective-permute-start.29
  121.2 2.6 %collective-permute-start.23 = (bf16[96,2048]{1,0:T(8,128)(2,1)S(1)}, bf16[96,2048]{1,0:T(8,128)(2,1)S(1)}, u32[]{:S(2)}, u32[]{:S(2)}) collective-permute-start(bf16[96,2048]{1,0:T(8,128)(2,1)S(1)} %pad_maximum_fusion.6), channel_id=1, source_target_pairs={{0,96},{32,0},{64,32},{96,64},{1,97},{33,1},{65,33},{97,65},{2,98}... | collective-permute-start | bytes 1179656 | tf_op jit(solution)/shard_map/ppermute | solution.py:36
  124.5 2.8 %collective-permute-start.30 = (bf16[96,2048]{1,0:T(8,128)(2,1)S(1)}, bf16[96,2048]{1,0:T(8,128)(2,1)S(1)}, u32[]{:S(2)}, u32[]{:S(2)}) collective-permute-start(bf16[96,2048]{1,0:T(8,128)(2,1)S(1)} %pad_maximum_fusion.8), channel_id=1, source_target_pairs={{0,24},{8,0},{16,8},{24,16},{1,25},{9,1},{17,9},{25,17},{2,26},{10... | collective-permute-start | bytes 1179656 | tf_op jit(solution)/shard_map/ppermute | solution.py:36
  127.4 1.5 collective-permute-done.23
  128.9 2.8 %collective-permute-done.21 = bf16[96,2048]{1,0:T(8,128)(2,1)S(1)} collective-permute-done((bf16[96,2048]{1,0:T(8,128)(2,1)S(1)}, bf16[96,2048]{1,0:T(8,128)(2,1)S(1)}, u32[]{:S(2)}, u32[]{:S(2)}) %collective-permute-start.21) | collective-permute-done | bytes 393248 | tf_op jit(solution)/shard_map/ppermute | solution.py:36
  133.4 1.6 collective-permute-start.26
  135.0 1.6 collective-permute-start.25
  136.9 2.7 %collective-permute-start.33 = (bf16[24,2048]{1,0:T(8,128)(2,1)S(1)}, bf16[24,2048]{1,0:T(8,128)(2,1)S(1)}, u32[]{:S(2)}, u32[]{:S(2)}) collective-permute-start(bf16[24,2048]{1,0:T(8,128)(2,1)S(1)} %get-tuple-element.98), channel_id=1, source_target_pairs={{0,96},{32,0},{64,32},{96,64},{1,97},{33,1},{65,33},{97,65},{2,98}... | collective-permute-start | bytes 294920 | tf_op jit(solution)/shard_map/ppermute | solution.py:36
  142.2 2.4 %collective-permute-done.32 = bf16[24,2048]{1,0:T(8,128)(2,1)S(1)} collective-permute-done((bf16[24,2048]{1,0:T(8,128)(2,1)S(1)}, bf16[24,2048]{1,0:T(8,128)(2,1)S(1)}, u32[]{:S(2)}, u32[]{:S(2)}) %collective-permute-start.32) | collective-permute-done | bytes 98336 | tf_op jit(solution)/shard_map/ppermute | solution.py:36
  145.1 3.7 %collective-permute-start.35 = (bf16[24,4096]{1,0:T(8,128)(2,1)S(1)}, bf16[24,4096]{1,0:T(8,128)(2,1)S(1)}, u32[]{:S(2)}, u32[]{:S(2)}) collective-permute-start(bf16[24,4096]{1,0:T(8,128)(2,1)S(1)} %divide_convert_fusion), channel_id=1, source_target_pairs={{0,2},{1,3},{2,0},{3,1},{4,6},{5,7},{6,4},{7,5},{8,10},{9,11},{10,... | collective-permute-start | bytes 589832 | tf_op jit(solution)/shard_map/ppermute | solution.py:36
  148.8 2.0 collective-permute-done.36
  150.8 3.1 %collective-permute-done.35 = bf16[24,4096]{1,0:T(8,128)(2,1)S(1)} collective-permute-done((bf16[24,4096]{1,0:T(8,128)(2,1)S(1)}, bf16[24,4096]{1,0:T(8,128)(2,1)S(1)}, u32[]{:S(2)}, u32[]{:S(2)}) %collective-permute-start.35) | collective-permute-done | bytes 196640 | tf_op jit(solution)/shard_map/ppermute | solution.py:36
  154.9 8.3 %out_gradient.1 = (f32[128,4096]{1,0:T(8,128)}, f32[128,1024]{1,0:T(8,128)}, bf16[1024,128]{1,0:T(8,128)(2,1)}) custom-call(bf16[96,128]{1,0:T(8,128)(2,1)} %pad_maximum_fusion.10.table, bf16[96,4096]{1,0:T(8,128)(2,1)} %pad_maximum_fusion.terms, f32[1,4096]{1,0:T(1,128)} %bitcast.26, bf16[1024,4096]{1,0:T(8,128)(2,1)} %w_out.3, ...), custom_call_target="tpu_custom_call" | custom-call | flops 1073741824 | bytes 8388608 | tf_op jit(solution)/shard_map/out_gradient/pallas_call | solution.py:449
  163.2 24.0 %all_to_all.21.got = bf16[32,32,128]{2,1,0:T(8,128)(2,1)} all-to-all(bf16[32,32,128]{2,1,0:T(8,128)(2,1)} %bitcast.25), channel_id=1, replica_groups=mesh['x'=4,'z'=4,'c'=2,'e'=4] {'x','z','c'}, dimensions={0} | all-to-all | bytes 524288 | tf_op jit(solution)/shard_map/all_to_all | solution.py:703
  187.2 1.7 leave.1
  188.9 3.7 %all-to-all-start.3 = ((bf16[32,32,128]{2,1,0:T(8,128)(2,1)}), bf16[32,32,128]{2,1,0:T(8,128)(2,1)S(1)}, u32[]{:S(2)}, u32[]{:S(2)}) async-start(bf16[32,32,128]{2,1,0:T(8,128)(2,1)} %leave.1), calls=%async_computation.3 | async-start | bytes 524288 | tf_op jit(solution)/shard_map/all_to_all | solution.py:710
  192.6 3.8 %near_gradient.1 = (f32[128,1024]{1,0:T(8,128)}, f32[128,128]{1,0:T(8,128)}, f32[128,128]{1,0:T(8,128)}, f32[128,128]{1,0:T(8,128)}, f32[128,128]{1,0:T(8,128)}) custom-call(f32[128,1024]{1,0:T(8,128)} %get-tuple-element.65.grad_ref, bf16[128,1024]{1,0:T(8,128)(2,1)} %get-tuple-element.43.inner_ref, bf16[128,256]{1,0:T(8,128)(2,1)} %get-tuple-element.44.bc_ref, ...), custom_call_target="tpu_custom_call" | custom-call | flops 268435456 | bytes 2621440 | tf_op jit(solution)/shard_map/near_gradient/pallas_call | solution.py:177
  196.4 5.3 %all-to-all-done.3 = bf16[32,32,128]{2,1,0:T(8,128)(2,1)S(1)} async-done(((bf16[32,32,128]{2,1,0:T(8,128)(2,1)}), bf16[32,32,128]{2,1,0:T(8,128)(2,1)S(1)}, u32[]{:S(2)}, u32[]{:S(2)}) %all-to-all-start.3) | async-done | bytes 262176 | tf_op jit(solution)/shard_map/all_to_all | solution.py:710
  202.4 2.8 %far_gradient.1 = (bf16[128,1024]{1,0:T(8,128)(2,1)}, bf16[128,256]{1,0:T(8,128)(2,1)}, bf16[128,128]{1,0:T(8,128)(2,1)}) custom-call(bf16[1024,128]{1,0:T(8,128)(2,1)} %bitcast.24, bf16[1024,128]{1,0:T(8,128)(2,1)} %bitcast.23, bf16[128,1024]{1,0:T(8,128)(2,1)} %get-tuple-element.43.inner_ref, bf16[128,256]{1,0:T(8,128)(2,1)} %get-tuple-element.44.bc_ref, ...), custom_call_target="tpu_custom_call" | custom-call | flops 134217728 | bytes 2621440 | tf_op jit(solution)/shard_map/far_gradient/pallas_call | solution.py:177
  205.2 3.4 %back_columns.7 = bf16[128,1024]{1,0:T(8,128)(2,1)} custom-call(s32[1]{0:T(128)} %bitcast.16.which, bf16[128,1024]{1,0:T(8,128)(2,1)} %get-tuple-element.72.g_ref, bf16[128,256]{1,0:T(8,128)(2,1)} %get-tuple-element.73.gbc, bf16[128,128]{1,0:T(8,128)(2,1)} %get-tuple-element.74.gpre, bf16[4096,1024]{1,0:T(8,128)(2,1)} %w_in.9, bf16[4096,256]{1,0:T(8,128)(2,1)} %w_bc.9, ...), custom_call_target="tpu_custom_call" | custom-call | flops 335544320 | bytes 2621440 | tf_op jit(solution)/shard_map/back_columns/pallas_call | solution.py:596
  208.7 3.4 %back_columns.6 = bf16[128,1024]{1,0:T(8,128)(2,1)} custom-call(s32[1]{0:T(128)} %bitcast.15.which, bf16[128,1024]{1,0:T(8,128)(2,1)} %get-tuple-element.72.g_ref, bf16[128,256]{1,0:T(8,128)(2,1)} %get-tuple-element.73.gbc, bf16[128,128]{1,0:T(8,128)(2,1)} %get-tuple-element.74.gpre, bf16[4096,1024]{1,0:T(8,128)(2,1)} %w_in.9, bf16[4096,256]{1,0:T(8,128)(2,1)} %w_bc.9, ...), custom_call_target="tpu_custom_call" | custom-call | flops 335544320 | bytes 2621440 | tf_op jit(solution)/shard_map/back_columns/pallas_call | solution.py:596
  212.1 3.5 %back_columns.5 = bf16[128,1024]{1,0:T(8,128)(2,1)} custom-call(s32[1]{0:T(128)} %bitcast.14.which, bf16[128,1024]{1,0:T(8,128)(2,1)} %get-tuple-element.72.g_ref, bf16[128,256]{1,0:T(8,128)(2,1)} %get-tuple-element.73.gbc, bf16[128,128]{1,0:T(8,128)(2,1)} %get-tuple-element.74.gpre, bf16[4096,1024]{1,0:T(8,128)(2,1)} %w_in.9, bf16[4096,256]{1,0:T(8,128)(2,1)} %w_bc.9, ...), custom_call_target="tpu_custom_call" | custom-call | flops 335544320 | bytes 2621440 | tf_op jit(solution)/shard_map/back_columns/pallas_call | solution.py:596
  215.7 3.7 %collective-permute-start.37 = (bf16[128,1024]{1,0:T(8,128)(2,1)}, bf16[128,1024]{1,0:T(8,128)(2,1)S(1)}, u32[]{:S(2)}, u32[]{:S(2)}) collective-permute-start(bf16[128,1024]{1,0:T(8,128)(2,1)} %back_columns.5), channel_id=1, source_target_pairs={{0,2},{1,3},{2,0},{3,1},{4,6},{5,7},{6,4},{7,5},{8,10},{9,11},{10,... | collective-permute-start | bytes 786440 | tf_op jit(solution)/shard_map/ppermute | solution.py:36
  219.6 2.5 %collective-permute-start.39 = (bf16[128,1024]{1,0:T(8,128)(2,1)S(1)}, bf16[128,1024]{1,0:T(8,128)(2,1)S(1)}, u32[]{:S(2)}, u32[]{:S(2)}) collective-permute-start(bf16[128,1024]{1,0:T(8,128)(2,1)S(1)} %copy-done.6), channel_id=1, source_target_pairs={{0,3},{1,0},{2,1},{3,2},{4,7},{5,4},{6,5},{7,6},{8,11},{9,8},{10,9... | collective-permute-start | bytes 786440 | tf_op jit(solution)/shard_map/ppermute | solution.py:36
  222.0 3.5 %back_columns.4 = f32[128,1024]{1,0:T(8,128)} custom-call(s32[1]{0:T(128)} %bitcast.11.which, bf16[128,1024]{1,0:T(8,128)(2,1)} %get-tuple-element.72.g_ref, bf16[128,256]{1,0:T(8,128)(2,1)} %get-tuple-element.73.gbc, bf16[128,128]{1,0:T(8,128)(2,1)} %get-tuple-element.74.gpre, bf16[4096,1024]{1,0:T(8,128)(2,1)} %w_in.9, bf16[4096,256]{1,0:T(8,128)(2,1)} %w_bc.9, ...), custom_call_target="tpu_custom_call" | custom-call | flops 335544320 | bytes 2621440 | tf_op jit(solution)/shard_map/back_columns/pallas_call | solution.py:596
  226.2 5.8 %collective-permute-done.38 = bf16[128,1024]{1,0:T(8,128)(2,1)S(1)} collective-permute-done((bf16[128,1024]{1,0:T(8,128)(2,1)S(1)}, bf16[128,1024]{1,0:T(8,128)(2,1)S(1)}, u32[]{:S(2)}, u32[]{:S(2)}) %collective-permute-start.38) | collective-permute-done | bytes 262176 | tf_op jit(solution)/shard_map/ppermute | solution.py:36
  231.9 2.2 subtract_convert_fusion
  (136 shorter events, 31.4 us)
Async XLA Ops:
  0.0 16.2 %collective-permute-start = (bf16[4096,256]{1,0:T(8,128)(2,1)}, bf16[4096,256]{1,0:T(8,128)(2,1)S(1)}, u32[]{:S(2)}, u32[]{:S(2)}) collective-permute-start(bf16[4096,256]{1,0:T(8,128)(2,1)} %bitcast.31), channel_id=1, source_target_pairs={{0,4},{4,0},{1,5},{5,1},{2,6},{6,2},{3,7},{7,3},{8,12},{12,8},{9,1... | collective-permute-start | bytes 6291464 | tf_op jit(solution)/shard_map/ppermute | solution.py:36
  1.4 14.7 %collective-permute-start.1 = (bf16[4096,256]{1,0:T(8,128)(2,1)}, bf16[4096,256]{1,0:T(8,128)(2,1)}, u32[]{:S(2)}, u32[]{:S(2)}) collective-permute-start(bf16[4096,256]{1,0:T(8,128)(2,1)} %bitcast.33), channel_id=1, source_target_pairs={{0,4},{4,0},{1,5},{5,1},{2,6},{6,2},{3,7},{7,3},{8,12},{12,8},{9,1... | collective-permute-start | bytes 6291464 | tf_op jit(solution)/shard_map/ppermute | solution.py:36
  3.6 12.0 %collective-permute-start.2 = (f32[1,256]{1,0:T(1,128)S(1)}, f32[1,256]{1,0:T(1,128)S(1)}, u32[]{:S(2)}, u32[]{:S(2)}) collective-permute-start(f32[1,256]{1,0:T(1,128)S(1)} %bitcast.29), channel_id=1, source_target_pairs={{0,4},{4,0},{1,5},{5,1},{2,6},{6,2},{3,7},{7,3},{8,12},{12,8},{9,1... | collective-permute-start | bytes 3080 | tf_op jit(solution)/shard_map/ppermute | solution.py:36
  14.9 25.4 %copy-start.16 = (f32[8]{0:T(128)S(1)}, f32[8]{0:T(128)}, u32[]{:S(2)}) copy-start(f32[8]{0:T(128)} %param.20) | copy-start | bytes 100
  15.0 34.1 %copy-start.13 = (bf16[24,128]{1,0:T(8,128)(2,1)}, bf16[24,128]{1,0:T(8,128)(2,1)S(1)}, u32[]{:S(2)}) copy-start(bf16[24,128]{1,0:T(8,128)(2,1)S(1)} %get-tuple-element.50.own_table) | copy-start | bytes 18436
  16.2 41.4 %copy-start.19 = (bf16[4096,256]{1,0:T(8,128)(2,1)}, bf16[4096,256]{1,0:T(8,128)(2,1)S(1)}, u32[]{:S(2)}) copy-start(bf16[4096,256]{1,0:T(8,128)(2,1)S(1)} %collective-permute-done.refs_9_) | copy-start | bytes 6291460
  36.6 12.5 %all-to-all-start.1 = ((bf16[32,32,128]{2,1,0:T(8,128)(2,1)}), bf16[32,32,128]{2,1,0:T(8,128)(2,1)S(1)}, u32[]{:S(2)}, u32[]{:S(2)}) async-start(bf16[32,32,128]{2,1,0:T(8,128)(2,1)} %get-tuple-element.49), calls=%async_computation.1 | async-start | bytes 524288 | tf_op jit(solution)/shard_map/all_to_all | solution.py:666
  57.6 8.0 %collective-permute-start.3 = (bf16[24,4096]{1,0:T(8,128)(2,1)}, bf16[24,4096]{1,0:T(8,128)(2,1)S(1)}, u32[]{:S(2)}, u32[]{:S(2)}) collective-permute-start(bf16[24,4096]{1,0:T(8,128)(2,1)} %get-tuple-element.52), channel_id=1, source_target_pairs={{0,1},{1,2},{2,3},{3,0},{4,5},{5,6},{6,7},{7,4},{8,9},{9,10},{10,1... | collective-permute-start | bytes 589832 | tf_op jit(solution)/shard_map/ppermute | solution.py:36
  58.9 11.9 %collective-permute-start.4 = (bf16[24,4096]{1,0:T(8,128)(2,1)}, bf16[24,4096]{1,0:T(8,128)(2,1)S(1)}, u32[]{:S(2)}, u32[]{:S(2)}) collective-permute-start(bf16[24,4096]{1,0:T(8,128)(2,1)} %get-tuple-element.53), channel_id=1, source_target_pairs={{0,2},{1,3},{2,0},{3,1},{4,6},{5,7},{6,4},{7,5},{8,10},{9,11},{10,... | collective-permute-start | bytes 589832 | tf_op jit(solution)/shard_map/ppermute | solution.py:36
  61.5 9.3 %collective-permute-start.5 = (bf16[24,4096]{1,0:T(8,128)(2,1)}, bf16[24,4096]{1,0:T(8,128)(2,1)S(1)}, u32[]{:S(2)}, u32[]{:S(2)}) collective-permute-start(bf16[24,4096]{1,0:T(8,128)(2,1)} %get-tuple-element.54), channel_id=1, source_target_pairs={{0,3},{1,0},{2,1},{3,2},{4,7},{5,4},{6,5},{7,6},{8,11},{9,8},{10,9... | collective-permute-start | bytes 589832 | tf_op jit(solution)/shard_map/ppermute | solution.py:36
  72.2 5.3 %collective-permute-start.8 = (bf16[24,2048]{1,0:T(8,128)(2,1)S(1)}, bf16[24,2048]{1,0:T(8,128)(2,1)S(1)}, u32[]{:S(2)}, u32[]{:S(2)}) collective-permute-start(bf16[24,2048]{1,0:T(8,128)(2,1)S(1)} %get-tuple-element.101), channel_id=1, source_target_pairs={{0,8},{8,16},{16,24},{24,0},{1,9},{9,17},{17,25},{25,1},{2,10},{10... | collective-permute-start | bytes 294920 | tf_op jit(solution)/shard_map/ppermute | solution.py:36
  72.8 5.9 %collective-permute-start.7 = (bf16[24,2048]{1,0:T(8,128)(2,1)S(1)}, bf16[24,2048]{1,0:T(8,128)(2,1)S(1)}, u32[]{:S(2)}, u32[]{:S(2)}) collective-permute-start(bf16[24,2048]{1,0:T(8,128)(2,1)S(1)} %get-tuple-element.101), channel_id=1, source_target_pairs={{0,16},{8,24},{16,0},{24,8},{1,17},{9,25},{17,1},{25,9},{2,18},{10... | collective-permute-start | bytes 294920 | tf_op jit(solution)/shard_map/ppermute | solution.py:36
  74.6 4.6 %collective-permute-start.6 = (bf16[24,2048]{1,0:T(8,128)(2,1)S(1)}, bf16[24,2048]{1,0:T(8,128)(2,1)S(1)}, u32[]{:S(2)}, u32[]{:S(2)}) collective-permute-start(bf16[24,2048]{1,0:T(8,128)(2,1)S(1)} %get-tuple-element.101), channel_id=1, source_target_pairs={{0,24},{8,0},{16,8},{24,16},{1,25},{9,1},{17,9},{25,17},{2,26},{10... | collective-permute-start | bytes 294920 | tf_op jit(solution)/shard_map/ppermute | solution.py:36
  75.3 6.7 %collective-permute-start.15 = (bf16[24,2048]{1,0:T(8,128)(2,1)S(1)}, bf16[24,2048]{1,0:T(8,128)(2,1)S(1)}, u32[]{:S(2)}, u32[]{:S(2)}) collective-permute-start(bf16[24,2048]{1,0:T(8,128)(2,1)S(1)} %get-tuple-element.100), channel_id=1, source_target_pairs={{0,32},{32,64},{64,96},{96,0},{1,33},{33,65},{65,97},{97,1},{2,34}... | collective-permute-start | bytes 294920 | tf_op jit(solution)/shard_map/ppermute | solution.py:36
  75.8 6.2 %collective-permute-start.14 = (bf16[24,2048]{1,0:T(8,128)(2,1)S(1)}, bf16[24,2048]{1,0:T(8,128)(2,1)S(1)}, u32[]{:S(2)}, u32[]{:S(2)}) collective-permute-start(bf16[24,2048]{1,0:T(8,128)(2,1)S(1)} %get-tuple-element.100), channel_id=1, source_target_pairs={{0,64},{32,96},{64,0},{96,32},{1,65},{33,97},{65,1},{97,33},{2,66}... | collective-permute-start | bytes 294920 | tf_op jit(solution)/shard_map/ppermute | solution.py:36
  77.5 4.5 %collective-permute-start.13 = (bf16[24,2048]{1,0:T(8,128)(2,1)S(1)}, bf16[24,2048]{1,0:T(8,128)(2,1)S(1)}, u32[]{:S(2)}, u32[]{:S(2)}) collective-permute-start(bf16[24,2048]{1,0:T(8,128)(2,1)S(1)} %get-tuple-element.100), channel_id=1, source_target_pairs={{0,96},{32,0},{64,32},{96,64},{1,97},{33,1},{65,33},{97,65},{2,98}... | collective-permute-start | bytes 294920 | tf_op jit(solution)/shard_map/ppermute | solution.py:36
  79.2 18.5 %copy-start.4 = (bf16[96,2048]{1,0:T(8,128)(2,1)}, bf16[96,2048]{1,0:T(8,128)(2,1)S(1)}, u32[]{:S(2)}) copy-start(bf16[96,2048]{1,0:T(8,128)(2,1)S(1)} %pad_maximum_fusion.1.refs_0_) | copy-start | bytes 1179652
  79.2 9.5 %collective-permute-start.10 = (bf16[96,2048]{1,0:T(8,128)(2,1)S(1)}, bf16[96,2048]{1,0:T(8,128)(2,1)S(1)}, u32[]{:S(2)}, u32[]{:S(2)}) collective-permute-start(bf16[96,2048]{1,0:T(8,128)(2,1)S(1)} %pad_maximum_fusion.1.refs_0_), channel_id=1, source_target_pairs={{0,32},{32,64},{64,96},{96,0},{1,33},{33,65},{65,97},{97,1},{2,34}... | collective-permute-start | bytes 1179656 | tf_op jit(solution)/shard_map/ppermute | solution.py:36
  79.7 10.6 %collective-permute-start.9 = (bf16[96,2048]{1,0:T(8,128)(2,1)S(1)}, bf16[96,2048]{1,0:T(8,128)(2,1)S(1)}, u32[]{:S(2)}, u32[]{:S(2)}) collective-permute-start(bf16[96,2048]{1,0:T(8,128)(2,1)S(1)} %pad_maximum_fusion.1.refs_0_), channel_id=1, source_target_pairs={{0,96},{32,0},{64,32},{96,64},{1,97},{33,1},{65,33},{97,65},{2,98}... | collective-permute-start | bytes 1179656 | tf_op jit(solution)/shard_map/ppermute | solution.py:36
  82.0 18.4 %copy-start.5 = (bf16[96,2048]{1,0:T(8,128)(2,1)}, bf16[96,2048]{1,0:T(8,128)(2,1)S(1)}, u32[]{:S(2)}) copy-start(bf16[96,2048]{1,0:T(8,128)(2,1)S(1)} %pad_maximum_fusion.3.refs_4_) | copy-start | bytes 1179652
  82.0 10.9 %collective-permute-start.17 = (bf16[96,2048]{1,0:T(8,128)(2,1)S(1)}, bf16[96,2048]{1,0:T(8,128)(2,1)S(1)}, u32[]{:S(2)}, u32[]{:S(2)}) collective-permute-start(bf16[96,2048]{1,0:T(8,128)(2,1)S(1)} %pad_maximum_fusion.3.refs_4_), channel_id=1, source_target_pairs={{0,8},{8,16},{16,24},{24,0},{1,9},{9,17},{17,25},{25,1},{2,10},{10... | collective-permute-start | bytes 1179656 | tf_op jit(solution)/shard_map/ppermute | solution.py:36
  83.0 10.8 %collective-permute-start.16 = (bf16[96,2048]{1,0:T(8,128)(2,1)S(1)}, bf16[96,2048]{1,0:T(8,128)(2,1)S(1)}, u32[]{:S(2)}, u32[]{:S(2)}) collective-permute-start(bf16[96,2048]{1,0:T(8,128)(2,1)S(1)} %pad_maximum_fusion.3.refs_4_), channel_id=1, source_target_pairs={{0,24},{8,0},{16,8},{24,16},{1,25},{9,1},{17,9},{25,17},{2,26},{10... | collective-permute-start | bytes 1179656 | tf_op jit(solution)/shard_map/ppermute | solution.py:36
  88.7 11.7 %copy-start.8 = (bf16[96,2048]{1,0:T(8,128)(2,1)}, bf16[96,2048]{1,0:T(8,128)(2,1)S(1)}, u32[]{:S(2)}) copy-start(bf16[96,2048]{1,0:T(8,128)(2,1)S(1)} %collective-permute-done.10.refs_3_) | copy-start | bytes 1179652
  88.7 8.2 %collective-permute-start.11 = (bf16[48,2048]{1,0:T(8,128)(2,1)S(1)}, bf16[48,2048]{1,0:T(8,128)(2,1)S(1)}, u32[]{:S(2)}, u32[]{:S(2)}) collective-permute-start(bf16[48,2048]{1,0:T(8,128)(2,1)S(1)} %slice.131), channel_id=1, source_target_pairs={{0,32},{32,64},{64,96},{96,0},{1,33},{33,65},{65,97},{97,1},{2,34}... | collective-permute-start | bytes 589832 | tf_op jit(solution)/shard_map/ppermute | solution.py:36
  90.3 6.6 %collective-permute-start.12 = (bf16[48,2048]{1,0:T(8,128)(2,1)S(1)}, bf16[48,2048]{1,0:T(8,128)(2,1)S(1)}, u32[]{:S(2)}, u32[]{:S(2)}) collective-permute-start(bf16[48,2048]{1,0:T(8,128)(2,1)S(1)} %slice.132), channel_id=1, source_target_pairs={{0,96},{32,0},{64,32},{96,64},{1,97},{33,1},{65,33},{97,65},{2,98}... | collective-permute-start | bytes 589832 | tf_op jit(solution)/shard_map/ppermute | solution.py:36
  92.9 6.7 %collective-permute-start.18 = (bf16[48,2048]{1,0:T(8,128)(2,1)S(1)}, bf16[48,2048]{1,0:T(8,128)(2,1)S(1)}, u32[]{:S(2)}, u32[]{:S(2)}) collective-permute-start(bf16[48,2048]{1,0:T(8,128)(2,1)S(1)} %slice.134), channel_id=1, source_target_pairs={{0,8},{8,16},{16,24},{24,0},{1,9},{9,17},{17,25},{25,1},{2,10},{10... | collective-permute-start | bytes 589832 | tf_op jit(solution)/shard_map/ppermute | solution.py:36
  93.8 5.9 %collective-permute-start.19 = (bf16[48,2048]{1,0:T(8,128)(2,1)S(1)}, bf16[48,2048]{1,0:T(8,128)(2,1)S(1)}, u32[]{:S(2)}, u32[]{:S(2)}) collective-permute-start(bf16[48,2048]{1,0:T(8,128)(2,1)S(1)} %slice.135), channel_id=1, source_target_pairs={{0,24},{8,0},{16,8},{24,16},{1,25},{9,1},{17,9},{25,17},{2,26},{10... | collective-permute-start | bytes 589832 | tf_op jit(solution)/shard_map/ppermute | solution.py:36
  115.1 6.0 %collective-permute-start.20 = (bf16[48,2048]{1,0:T(8,128)(2,1)S(1)}, bf16[48,2048]{1,0:T(8,128)(2,1)S(1)}, u32[]{:S(2)}, u32[]{:S(2)}) collective-permute-start(bf16[48,2048]{1,0:T(8,128)(2,1)S(1)} %get-tuple-element.84), channel_id=1, source_target_pairs={{0,32},{32,64},{64,96},{96,0},{1,33},{33,65},{65,97},{97,1},{2,34}... | collective-permute-start | bytes 589832 | tf_op jit(solution)/shard_map/ppermute | solution.py:36
  115.2 5.9 %collective-permute-start.22 = (bf16[48,2048]{1,0:T(8,128)(2,1)S(1)}, bf16[48,2048]{1,0:T(8,128)(2,1)S(1)}, u32[]{:S(2)}, u32[]{:S(2)}) collective-permute-start(bf16[48,2048]{1,0:T(8,128)(2,1)S(1)} %get-tuple-element.85), channel_id=1, source_target_pairs={{0,96},{32,0},{64,32},{96,64},{1,97},{33,1},{65,33},{97,65},{2,98}... | collective-permute-start | bytes 589832 | tf_op jit(solution)/shard_map/ppermute | solution.py:36
  117.9 6.4 %collective-permute-start.27 = (bf16[48,2048]{1,0:T(8,128)(2,1)S(1)}, bf16[48,2048]{1,0:T(8,128)(2,1)S(1)}, u32[]{:S(2)}, u32[]{:S(2)}) collective-permute-start(bf16[48,2048]{1,0:T(8,128)(2,1)S(1)} %get-tuple-element.90), channel_id=1, source_target_pairs={{0,8},{8,16},{16,24},{24,0},{1,9},{9,17},{17,25},{25,1},{2,10},{10... | collective-permute-start | bytes 589832 | tf_op jit(solution)/shard_map/ppermute | solution.py:36
  119.4 4.9 %collective-permute-start.29 = (bf16[48,2048]{1,0:T(8,128)(2,1)S(1)}, bf16[48,2048]{1,0:T(8,128)(2,1)S(1)}, u32[]{:S(2)}, u32[]{:S(2)}) collective-permute-start(bf16[48,2048]{1,0:T(8,128)(2,1)S(1)} %get-tuple-element.91), channel_id=1, source_target_pairs={{0,24},{8,0},{16,8},{24,16},{1,25},{9,1},{17,9},{25,17},{2,26},{10... | collective-permute-start | bytes 589832 | tf_op jit(solution)/shard_map/ppermute | solution.py:36
  121.2 7.7 %collective-permute-start.23 = (bf16[96,2048]{1,0:T(8,128)(2,1)S(1)}, bf16[96,2048]{1,0:T(8,128)(2,1)S(1)}, u32[]{:S(2)}, u32[]{:S(2)}) collective-permute-start(bf16[96,2048]{1,0:T(8,128)(2,1)S(1)} %pad_maximum_fusion.6), channel_id=1, source_target_pairs={{0,96},{32,0},{64,32},{96,64},{1,97},{33,1},{65,33},{97,65},{2,98}... | collective-permute-start | bytes 1179656 | tf_op jit(solution)/shard_map/ppermute | solution.py:36
  123.8 7.9 %collective-permute-start.21 = (bf16[96,2048]{1,0:T(8,128)(2,1)S(1)}, bf16[96,2048]{1,0:T(8,128)(2,1)S(1)}, u32[]{:S(2)}, u32[]{:S(2)}) collective-permute-start(bf16[96,2048]{1,0:T(8,128)(2,1)S(1)} %pad_maximum_fusion.5), channel_id=1, source_target_pairs={{0,32},{32,64},{64,96},{96,0},{1,33},{33,65},{65,97},{97,1},{2,34}... | collective-permute-start | bytes 1179656 | tf_op jit(solution)/shard_map/ppermute | solution.py:36
  124.5 12.2 %collective-permute-start.30 = (bf16[96,2048]{1,0:T(8,128)(2,1)S(1)}, bf16[96,2048]{1,0:T(8,128)(2,1)S(1)}, u32[]{:S(2)}, u32[]{:S(2)}) collective-permute-start(bf16[96,2048]{1,0:T(8,128)(2,1)S(1)} %pad_maximum_fusion.8), channel_id=1, source_target_pairs={{0,24},{8,0},{16,8},{24,16},{1,25},{9,1},{17,9},{25,17},{2,26},{10... | collective-permute-start | bytes 1179656 | tf_op jit(solution)/shard_map/ppermute | solution.py:36
  127.3 9.4 %collective-permute-start.28 = (bf16[96,2048]{1,0:T(8,128)(2,1)S(1)}, bf16[96,2048]{1,0:T(8,128)(2,1)S(1)}, u32[]{:S(2)}, u32[]{:S(2)}) collective-permute-start(bf16[96,2048]{1,0:T(8,128)(2,1)S(1)} %pad_maximum_fusion.7), channel_id=1, source_target_pairs={{0,8},{8,16},{16,24},{24,0},{1,9},{9,17},{17,25},{25,1},{2,10},{10... | collective-permute-start | bytes 1179656 | tf_op jit(solution)/shard_map/ppermute | solution.py:36
  131.9 7.7 %collective-permute-start.24 = (bf16[24,2048]{1,0:T(8,128)(2,1)S(1)}, bf16[24,2048]{1,0:T(8,128)(2,1)S(1)}, u32[]{:S(2)}, u32[]{:S(2)}) collective-permute-start(bf16[24,2048]{1,0:T(8,128)(2,1)S(1)} %get-tuple-element.94), channel_id=1, source_target_pairs={{0,8},{8,16},{16,24},{24,0},{1,9},{9,17},{17,25},{25,1},{2,10},{10... | collective-permute-start | bytes 294920 | tf_op jit(solution)/shard_map/ppermute | solution.py:36
  133.4 6.2 %collective-permute-start.26 = (bf16[24,2048]{1,0:T(8,128)(2,1)S(1)}, bf16[24,2048]{1,0:T(8,128)(2,1)S(1)}, u32[]{:S(2)}, u32[]{:S(2)}) collective-permute-start(bf16[24,2048]{1,0:T(8,128)(2,1)S(1)} %get-tuple-element.95), channel_id=1, source_target_pairs={{0,24},{8,0},{16,8},{24,16},{1,25},{9,1},{17,9},{25,17},{2,26},{10... | collective-permute-start | bytes 294920 | tf_op jit(solution)/shard_map/ppermute | solution.py:36
  135.0 6.0 %collective-permute-start.25 = (bf16[24,2048]{1,0:T(8,128)(2,1)S(1)}, bf16[24,2048]{1,0:T(8,128)(2,1)S(1)}, u32[]{:S(2)}, u32[]{:S(2)}) collective-permute-start(bf16[24,2048]{1,0:T(8,128)(2,1)S(1)} %get-tuple-element.96), channel_id=1, source_target_pairs={{0,16},{8,24},{16,0},{24,8},{1,17},{9,25},{17,1},{25,9},{2,18},{10... | collective-permute-start | bytes 294920 | tf_op jit(solution)/shard_map/ppermute | solution.py:36
  136.8 5.0 %collective-permute-start.31 = (bf16[24,2048]{1,0:T(8,128)(2,1)S(1)}, bf16[24,2048]{1,0:T(8,128)(2,1)S(1)}, u32[]{:S(2)}, u32[]{:S(2)}) collective-permute-start(bf16[24,2048]{1,0:T(8,128)(2,1)S(1)} %get-tuple-element.97), channel_id=1, source_target_pairs={{0,32},{32,64},{64,96},{96,0},{1,33},{33,65},{65,97},{97,1},{2,34}... | collective-permute-start | bytes 294920 | tf_op jit(solution)/shard_map/ppermute | solution.py:36
  136.9 5.3 %collective-permute-start.33 = (bf16[24,2048]{1,0:T(8,128)(2,1)S(1)}, bf16[24,2048]{1,0:T(8,128)(2,1)S(1)}, u32[]{:S(2)}, u32[]{:S(2)}) collective-permute-start(bf16[24,2048]{1,0:T(8,128)(2,1)S(1)} %get-tuple-element.98), channel_id=1, source_target_pairs={{0,96},{32,0},{64,32},{96,64},{1,97},{33,1},{65,33},{97,65},{2,98}... | collective-permute-start | bytes 294920 | tf_op jit(solution)/shard_map/ppermute | solution.py:36
  139.6 5.0 %collective-permute-start.32 = (bf16[24,2048]{1,0:T(8,128)(2,1)S(1)}, bf16[24,2048]{1,0:T(8,128)(2,1)S(1)}, u32[]{:S(2)}, u32[]{:S(2)}) collective-permute-start(bf16[24,2048]{1,0:T(8,128)(2,1)S(1)} %get-tuple-element.99), channel_id=1, source_target_pairs={{0,64},{32,96},{64,0},{96,32},{1,65},{33,97},{65,1},{97,33},{2,66}... | collective-permute-start | bytes 294920 | tf_op jit(solution)/shard_map/ppermute | solution.py:36
  145.0 5.8 %collective-permute-start.36 = (bf16[24,4096]{1,0:T(8,128)(2,1)S(1)}, bf16[24,4096]{1,0:T(8,128)(2,1)S(1)}, u32[]{:S(2)}, u32[]{:S(2)}) collective-permute-start(bf16[24,4096]{1,0:T(8,128)(2,1)S(1)} %divide_convert_fusion), channel_id=1, source_target_pairs={{0,1},{1,2},{2,3},{3,0},{4,5},{5,6},{6,7},{7,4},{8,9},{9,10},{10,1... | collective-permute-start | bytes 589832 | tf_op jit(solution)/shard_map/ppermute | solution.py:36
  145.1 8.9 %collective-permute-start.35 = (bf16[24,4096]{1,0:T(8,128)(2,1)S(1)}, bf16[24,4096]{1,0:T(8,128)(2,1)S(1)}, u32[]{:S(2)}, u32[]{:S(2)}) collective-permute-start(bf16[24,4096]{1,0:T(8,128)(2,1)S(1)} %divide_convert_fusion), channel_id=1, source_target_pairs={{0,2},{1,3},{2,0},{3,1},{4,6},{5,7},{6,4},{7,5},{8,10},{9,11},{10,... | collective-permute-start | bytes 589832 | tf_op jit(solution)/shard_map/ppermute | solution.py:36
  148.8 5.2 %collective-permute-start.34 = (bf16[24,4096]{1,0:T(8,128)(2,1)S(1)}, bf16[24,4096]{1,0:T(8,128)(2,1)S(1)}, u32[]{:S(2)}, u32[]{:S(2)}) collective-permute-start(bf16[24,4096]{1,0:T(8,128)(2,1)S(1)} %divide_convert_fusion), channel_id=1, source_target_pairs={{0,3},{1,0},{2,1},{3,2},{4,7},{5,4},{6,5},{7,6},{8,11},{9,8},{10,9... | collective-permute-start | bytes 589832 | tf_op jit(solution)/shard_map/ppermute | solution.py:36
  188.9 12.8 %all-to-all-start.3 = ((bf16[32,32,128]{2,1,0:T(8,128)(2,1)}), bf16[32,32,128]{2,1,0:T(8,128)(2,1)S(1)}, u32[]{:S(2)}, u32[]{:S(2)}) async-start(bf16[32,32,128]{2,1,0:T(8,128)(2,1)} %leave.1), calls=%async_computation.3 | async-start | bytes 524288 | tf_op jit(solution)/shard_map/all_to_all | solution.py:710
  215.7 10.5 %collective-permute-start.37 = (bf16[128,1024]{1,0:T(8,128)(2,1)}, bf16[128,1024]{1,0:T(8,128)(2,1)S(1)}, u32[]{:S(2)}, u32[]{:S(2)}) collective-permute-start(bf16[128,1024]{1,0:T(8,128)(2,1)} %back_columns.5), channel_id=1, source_target_pairs={{0,2},{1,3},{2,0},{3,1},{4,6},{5,7},{6,4},{7,5},{8,10},{9,11},{10,... | collective-permute-start | bytes 786440 | tf_op jit(solution)/shard_map/ppermute | solution.py:36
  219.3 12.6 %collective-permute-start.38 = (bf16[128,1024]{1,0:T(8,128)(2,1)S(1)}, bf16[128,1024]{1,0:T(8,128)(2,1)S(1)}, u32[]{:S(2)}, u32[]{:S(2)}) collective-permute-start(bf16[128,1024]{1,0:T(8,128)(2,1)S(1)} %copy-done.7), channel_id=1, source_target_pairs={{0,1},{1,2},{2,3},{3,0},{4,5},{5,6},{6,7},{7,4},{8,9},{9,10},{10,1... | collective-permute-start | bytes 786440 | tf_op jit(solution)/shard_map/ppermute | solution.py:36
  219.6 12.4 %collective-permute-start.39 = (bf16[128,1024]{1,0:T(8,128)(2,1)S(1)}, bf16[128,1024]{1,0:T(8,128)(2,1)S(1)}, u32[]{:S(2)}, u32[]{:S(2)}) collective-permute-start(bf16[128,1024]{1,0:T(8,128)(2,1)S(1)} %copy-done.6), channel_id=1, source_target_pairs={{0,3},{1,0},{2,1},{3,2},{4,7},{5,4},{6,5},{7,6},{8,11},{9,8},{10,9... | collective-permute-start | bytes 786440 | tf_op jit(solution)/shard_map/ppermute | solution.py:36
  (14 other events, 74.0 us)

commit v4 on v3

--- a/solution.py
+++ b/solution.py
@@ -49,108 +49,92 @@
     return table.astype(F32), weight
 
 
-def swap_blocks(value, side, rows):
-    return jnp.concatenate(
-        [
-            value[(b * side + a) * rows : (b * side + a + 1) * rows]
-            for a in range(side)
-            for b in range(side)
-        ],
-        axis=0,
-    )
-
-
-def expert_kernel(side, *refs):
-    near, far = refs[:side], refs[side : 2 * side]
-    wg0, wg1, wu0, wu1, hv_ref = refs[2 * side : 2 * side + 5]
-    out_near, out_far, first, second = refs[2 * side + 5 :]
+def expert_kernel(pieces, *refs):
+    wg0, wg1, wu0, wu1, hv_ref, out, first, second = refs[pieces:]
     half = wg0.shape[1]
-    depth = out_near.shape[1]
-    slot = out_near.shape[0] // (side * side)
-    near_rows = jnp.concatenate([r[...] for r in near], axis=0)
-    far_rows = jnp.concatenate([r[...] for r in far], axis=0)
-
-    def product(w):
-        return mm(near_rows, w[:depth, :]) + swap_blocks(mm(far_rows, w[depth:, :]), side, slot)
-
+    width = out.shape[1]
+    rows = jnp.concatenate([r[...] for r in refs[:pieces]], axis=0)
     for k, (wg, wu) in enumerate(((wg0, wu0), (wg1, wu1))):
         span = slice(k * half, (k + 1) * half)
-        gate = product(wg)
-        up = product(wu)
+        gate = mm(rows, wg[...])
+        up = mm(rows, wu[...])
         sig = 1.0 / (1.0 + jnp.exp(-gate))
         hv = hv_ref[k : k + 1, :]
         first[:, span] = (hv * up * sig * (1.0 + gate * (1.0 - sig))).astype(BF)
         second[:, span] = (hv * gate * sig).astype(BF)
-    step = min(depth, 512)
-
-    def terms(cols):
+    step = min(width, 512)
+
+    @pl.loop(0, width // step)
+    def _(i):
+        cols = pl.ds(pl.multiple_of(i * step, step), step)
         total = mm_t(first[:, :half], wg0[cols, :]) + mm_t(second[:, :half], wu0[cols, :])
-        return total + mm_t(first[:, half:], wg1[cols, :]) + mm_t(second[:, half:], wu1[cols, :])
-
-    @pl.loop(0, depth // step)
-    def _(i):
-        start = pl.multiple_of(i * step, step)
-        cols = pl.ds(start, step)
-        out_near[:, cols] = terms(cols).astype(BF)
-        more = pl.ds(pl.multiple_of(depth + start, step), step)
-        out_far[:, cols] = swap_blocks(terms(more), side, slot).astype(BF)
-
-
-def expert_rows(near, far, wg0, wg1, wu0, wu1, head_vec):
-    side = len(near)
-    count = side * near[0].shape[0]
-    depth = near[0].shape[1]
+        total += mm_t(first[:, half:], wg1[cols, :]) + mm_t(second[:, half:], wu1[cols, :])
+        out[:, cols] = total.astype(BF)
+
+
+def expert_rows(rows, wg0, wg1, wu0, wu1, head_vec):
+    count = len(rows) * rows[0].shape[0]
+    width = rows[0].shape[1]
     half = wg0.shape[1]
-    out = jax.ShapeDtypeStruct((count, depth), BF)
     return single(
-        functools.partial(expert_kernel, side),
-        out_shape=(out, out),
-        args=(*near, *far, wg0, wg1, wu0, wu1, head_vec),
+        functools.partial(expert_kernel, len(rows)),
+        out_shape=jax.ShapeDtypeStruct((count, width), BF),
+        args=(*rows, wg0, wg1, wu0, wu1, head_vec),
         scratch_shapes=[pltpu.VMEM((count, 2 * half), BF)] * 2,
         compiler_params=vmem(56),
-        cost_estimate=cost(32 * count * depth * half, 16 * depth * half + 8 * count * depth),
+        cost_estimate=cost(16 * count * width * half, 8 * width * half + 4 * count * width),
         name="experts",
     )
 
 
-def gather_around(value, axis):
-    count = lax.axis_size(axis)
+def turn(value, outer, by):
+    side = lax.axis_size("x")
+    cores = lax.axis_size("c")
+    pairs = []
+    for x in range(side):
+        for z in range(side):
+            for c in range(cores):
+                along_x = (c == 0) == outer
+                to_x = (x + by) % side if along_x else x
+                to_z = z if along_x else (z + by) % side
+                pairs.append(((x * side + z) * cores + c, (to_x * side + to_z) * cores + c))
+    return lax.ppermute(value, SEQ, pairs)
+
+
+def gather_outer(value, count):
     if count != 4:
-        return [value] + [shift(value, axis, count - k) for k in range(1, count)]
-    left, right = shift(value, axis, 1), shift(value, axis, 3)
+        return [value] + [turn(value, True, count - k) for k in range(1, count)]
+    left, right = turn(value, True, 1), turn(value, True, 3)
     cut = value.shape[0] // 2
-    across = jnp.concatenate(
-        [shift(left[:cut], axis, 1), shift(right[cut:], axis, 3)], axis=0
-    )
+    across = jnp.concatenate([turn(left[:cut], True, 1), turn(right[cut:], True, 3)], axis=0)
     return [value, right, across, left]
 
 
-def gather_direct(value, axis):
-    count = lax.axis_size(axis)
-    return [value] + [shift(value, axis, count - k) for k in range(1, count)]
-
-
-def scatter_direct(pieces, axis):
+def gather_inner(value, count):
+    return [value] + [turn(value, False, count - k) for k in range(1, count)]
+
+
+def scatter_direct(pieces, outer):
     total = pieces[0].astype(F32)
     for k in range(1, len(pieces)):
-        total = total + shift(pieces[k], axis, k).astype(F32)
+        total = total + turn(pieces[k], outer, k).astype(F32)
     return total
 
 
-def scatter_around(pieces, axis):
+def scatter_outer(pieces):
     if len(pieces) != 4:
-        return scatter_direct(pieces, axis)
+        return scatter_direct(pieces, True)
     own, right, across, left = pieces
     cut = across.shape[0] // 2
-    top = shift(across[:cut], axis, 1)
-    bottom = shift(across[cut:], axis, 3)
+    top = turn(across[:cut], True, 1)
+    bottom = turn(across[cut:], True, 3)
     right = jnp.concatenate(
         [(right[:cut].astype(F32) + top.astype(F32)).astype(BF), right[cut:]], axis=0
     )
     left = jnp.concatenate(
         [left[:cut], (left[cut:].astype(F32) + bottom.astype(F32)).astype(BF)], axis=0
     )
-    return own.astype(F32) + shift(right, axis, 1).astype(F32) + shift(left, axis, 3).astype(F32)
+    return own.astype(F32) + turn(right, True, 1).astype(F32) + turn(left, True, 3).astype(F32)
 
 
 def split_rows(value, count):
@@ -204,7 +188,7 @@
     x = cand[...]
     acc[...] += mm(x, w_in[...])
     acc_bc[...] += mm(x, w_bc[...])
-    acc_pre[:, :heads] += mm(x, w_step[...])
+    acc_pre[:, :heads] += mm_t(x, w_step[...])
 
     @pl.when(i == pl.num_programs(0) - 1)
     def _():
@@ -253,7 +237,7 @@
     chan = in_proj.shape[1]
     two = bc_proj.shape[1]
     slice_rows = chan // n_seq
-    depth = min(width, 1024)
+    depth = min(width, 512)
     small = jax.ShapeDtypeStruct((tlen, tlen), F32)
     fixed = lambda *shape: pl.BlockSpec(shape, lambda i: (0,) * len(shape))
     return pl.pallas_call(
@@ -269,7 +253,7 @@
             pl.BlockSpec((tlen, depth), lambda i: (0, i)),
             pl.BlockSpec((depth, chan), lambda i: (i, 0)),
             pl.BlockSpec((depth, two), lambda i: (i, 0)),
-            pl.BlockSpec((depth, heads), lambda i: (i, 0)),
+            pl.BlockSpec((heads, depth), lambda i: (0, i)),
             fixed(1, tlen), fixed(1, tlen),
         ],
         out_specs=(
@@ -392,7 +376,7 @@
     tlen, chan = within.shape
     width = out_proj.shape[1]
     rows = table.shape[0]
-    block = min(width, 1024)
+    block = min(width, 512)
     fixed = lambda a: pl.BlockSpec(a.shape, lambda i: (0,) * a.ndim)
     cols = lambda n: pl.BlockSpec((n, block), lambda i: (0, i))
     sent = jax.ShapeDtypeStruct((CAP, width), BF)
@@ -443,7 +427,7 @@
     tlen = table.shape[1]
     chan, width = out_proj.shape
     nstate = bc_bf.shape[1] // 2
-    block = min(width, 1024)
+    block = min(width, 512)
     fixed = lambda *shape: pl.BlockSpec(shape, lambda i: (0,) * len(shape))
     cols = lambda n: pl.BlockSpec((n, block), lambda i: (0, i))
     return pl.pallas_call(
@@ -580,32 +564,44 @@
     )
 
 
-def back_kernel(heads, which, g_ref, gbc, gpre, w_in, w_bc, w_step, out):
+def back_kernel(heads, per, which, g_ref, gbc, gpre, w_in, w_bc, w_step, *outs):
     total = mm_t(g_ref[...], w_in[...]) + mm_t(gbc[...], w_bc[...])
-    total += mm_t(gpre[:, :heads], w_step[...])
-    out[...] = total.astype(out.dtype)
-
-
-def back_columns(which, g_inner, g_bc, g_pre, in_proj, bc_proj, step_proj, cols, dtype, heads):
+    total += mm(gpre[:, :heads], w_step[...])
+    for k, out in enumerate(outs):
+
+        @pl.when(pl.program_id(0) // per == k)
+        def _():
+            out[...] = total.astype(out.dtype)
+
+
+def back_columns(which, g_inner, g_bc, g_pre, in_proj, bc_proj, step_w, cols, dtype, heads):
     tlen, chan = g_inner.shape
     two = bc_proj.shape[1]
+    count = which.shape[0]
     block = min(cols, 512)
     per = cols // block
     fixed = lambda a: pl.BlockSpec(a.shape, lambda i, w: (0,) * a.ndim)
-    rows = lambda n: pl.BlockSpec((block, n), lambda i, w: (w[0] * per + i, 0))
+    place = lambda i, w: w[i // per] * per + i % per
+    rows = lambda n: pl.BlockSpec((block, n), lambda i, w: (place(i, w), 0))
     return pl.pallas_call(
-        functools.partial(back_kernel, heads),
+        functools.partial(back_kernel, heads, per),
         grid_spec=pltpu.PrefetchScalarGridSpec(
             num_scalar_prefetch=1,
-            grid=(per,),
-            in_specs=[fixed(g_inner), fixed(g_bc), fixed(g_pre), rows(chan), rows(two), rows(heads)],
-            out_specs=pl.BlockSpec((tlen, block), lambda i, w: (0, i)),
+            grid=(count * per,),
+            in_specs=[
+                fixed(g_inner), fixed(g_bc), fixed(g_pre), rows(chan), rows(two),
+                pl.BlockSpec((heads, block), lambda i, w: (0, place(i, w))),
+            ],
+            out_specs=tuple(
+                pl.BlockSpec((tlen, block), lambda i, w, k=k: (0, jnp.clip(i - k * per, 0, per - 1)))
+                for k in range(count)
+            ),
         ),
-        out_shape=jax.ShapeDtypeStruct((tlen, cols), dtype),
-        compiler_params=vmem(56),
-        cost_estimate=cost(2 * tlen * (chan + two) * cols, 2 * (chan + two) * cols),
+        out_shape=tuple(jax.ShapeDtypeStruct((tlen, cols), dtype) for _ in range(count)),
+        compiler_params=vmem(56),
+        cost_estimate=cost(2 * tlen * (chan + two) * cols * count, 2 * (chan + two) * cols * count),
         name="back_columns",
-    )(which, g_inner, g_bc, g_pre, in_proj, bc_proj, step_proj)
+    )(which, g_inner, g_bc, g_pre, in_proj, bc_proj, step_w)
 
 
 def shards(
@@ -626,6 +622,7 @@
 ):
     tlen, width = candidate.shape
     heads = step_bias.shape[0]
+    step_w = step_proj.T
     chan = in_proj.shape[1]
     size = chan // heads
     nstate = bc_proj.shape[1] // 2
@@ -640,11 +637,8 @@
     energy = energy_head[None, :]
 
     wg0, wu0 = expert_gate[0], expert_up[0]
-    head_own = jnp.sum(expert_down[0].astype(F32) * energy, axis=1)
     wg1 = shift(wg0, "c", 1)
     wu1 = shift(wu0, "c", 1)
-    head_other = shift(head_own[None, :], "c", 1)
-    head_vec = jnp.concatenate([head_own[None, :], head_other], axis=0)
 
     pairs = [
         slot_table(expert_ids, gate_weights, lax.rem(column + k, n_exp)) for k in range(n_exp)
@@ -655,14 +649,18 @@
     own_table = own_table.astype(BF)
 
     inner_b, bc_bf, pre, step, cum, step_t, cum_t, payload = project(
-        candidate, in_proj, bc_proj, step_proj, bias, rate, heads, n_seq
-    )
-    payload, wg1, wu1, head_vec, table, own_table, slot_weight = lax.optimization_barrier(
-        (payload, wg1, wu1, head_vec, table, own_table, slot_weight)
+        candidate, in_proj, bc_proj, step_w, bias, rate, heads, n_seq
+    )
+    payload, wg1, wu1, table, own_table, slot_weight = lax.optimization_barrier(
+        (payload, wg1, wu1, table, own_table, slot_weight)
     )
     got = lax.all_to_all(payload, SEQ, 0, 0, tiled=True)
     within = mix_within(inner_b, bc_bf, cum, cum_t, step_t, skip, heads)
     entering, decay = enter_states(got, slice_rows)
+    entering, down = lax.optimization_barrier((entering, expert_down[0]))
+    head_own = jnp.sum(down.astype(F32) * energy, axis=1)
+    head_other = shift(head_own[None, :], "c", 1)
+    head_vec = jnp.concatenate([head_own[None, :], head_other], axis=0)
     state = lax.all_to_all(entering, SEQ, 0, 0, tiled=True).reshape(chan, nstate)
 
     own, send1, send2, send3, reads = mix_slots(
@@ -676,21 +674,10 @@
     routed = normed.astype(BF)
 
     side = lax.axis_size("x")
-    cut = width // 2
-    near_own = jnp.concatenate(gather_direct(routed[:, :cut], "z"), axis=0)
-    far_own = jnp.concatenate(gather_direct(routed[:, cut:], "x"), axis=0)
-    near_rows = gather_around(near_own, "x")
-    far_rows = gather_around(far_own, "z")
-    out_near, out_far = expert_rows(near_rows, far_rows, wg0, wg1, wu0, wu1, head_vec)
-    near_sum = scatter_around(split_rows(out_near, side), "x").astype(BF)
-    far_sum = scatter_around(split_rows(out_far, side), "z").astype(BF)
-    slot_grad = jnp.concatenate(
-        [
-            scatter_direct(split_rows(near_sum, side), "z"),
-            scatter_direct(split_rows(far_sum, side), "x"),
-        ],
-        axis=1,
-    )
+    rows = gather_outer(jnp.concatenate(gather_inner(routed, side), axis=0), side)
+    terms = expert_rows(rows, wg0, wg1, wu0, wu1, head_vec)
+    line_sum = scatter_outer(split_rows(terms, side)).astype(BF)
+    slot_grad = scatter_direct(split_rows(line_sum, side), False)
     along = jnp.mean(normed * slot_grad, axis=-1, keepdims=True)
     slot_term = (slot_weight * (slot_grad - normed * along) / scale).astype(BF)
     all_terms = jnp.concatenate(
@@ -712,14 +699,16 @@
         later, state, inner_b, bc_bf, cum, step, pre, rate, near, gb, gc, dcum, dstep, heads
     )
 
-    def columns(k, dtype):
-        which = lax.rem(column + k, n_exp)[None]
+    def columns(places, dtype):
+        which = jnp.stack([lax.rem(column + k, n_exp) for k in places])
         return back_columns(
-            which, g_inner, g_bc, g_pre, in_proj, bc_proj, step_proj, col_count, dtype, heads
+            which, g_inner, g_bc, g_pre, in_proj, bc_proj, step_w, col_count, dtype, heads
         )
 
-    arrived = [shift(columns(k, BF), "e", k) for k in (2, 1, 3)]
-    summed = lax.dynamic_slice_in_dim(hid_grad, column * col_count, col_count, 1) + columns(0, F32)
+    order = (2, 1, 3)
+    arrived = [shift(part, "e", k) for k, part in zip(order, columns(order, BF))]
+    (own_part,) = columns((0,), F32)
+    summed = lax.dynamic_slice_in_dim(hid_grad, column * col_count, col_count, 1) + own_part
     for value in arrived:
         summed = summed + value.astype(F32)
     own_cand = lax.dynamic_slice_in_dim(candidate, column * col_count, col_count, 1).astype(F32)

time: 235 us -> 244 us (1.038)
  waiting for transfers between devices: 47.6 us -> 70.7 us
  starting transfers between devices: 63.2 us -> 44.3 us
  Pallas kernels: 63.7 us -> 68.2 us
    ppermute x0 -> x14, waiting for transfers between devices: none -> 39.4 us  [turn(): return lax.ppermute(value, SEQ, pairs)]
    ppermute x40 -> x12, starting transfers between devices: 55.9 us -> 19.5 us  [shift(): lax.ppermute(value, axis, [(i, (i + by) % count) for i in range(count)])]
    ppermute x0 -> x14, starting transfers between devices: none -> 17.4 us  [turn(): return lax.ppermute(value, SEQ, pairs)]
    ppermute x40 -> x12, waiting for transfers between devices: 36.3 us -> 20.5 us  [shift(): lax.ppermute(value, axis, [(i, (i + by) % count) for i in range(count)])]
    pallas_call x4 -> x2, Pallas kernels: 13.9 us -> 11.9 us  [back_columns(): pl.pallas_call(functools.partial(back_kernel, heads, per), grid_spec=pltp...]
  transfers between devices with their start and end apart: 42 -> 28, of which waited for: 20 -> 17; matrix products, arithmetic and copies ran while one was open for 3% -> 2% of each run, Pallas kernels for 8% -> 8%
where the time goes in v4:
time: 244 us; the launch traced here: 243 us
  waiting for transfers between devices  70.7 us (29%)
  Pallas kernels  68.2 us (28%)
  starting transfers between devices  44.3 us (18%)
  blocking collectives  44.2 us (18%)
  other arithmetic  10.1 us (4%)
  local copies, waits for them, and re-layouts  5.09 us (2%)
    ppermute x14, waiting for transfers between devices, turn(): return lax.ppermute(value, SEQ, pairs)  39.4 us
    pallas_call x6, Pallas kernels, single(): pl.pallas_call(kernel, grid=(1,), out_shape=out_shape, in_specs=whole(arg...  26.7 us
    all_to_all x1, blocking collectives, shards(): lax.all_to_all(local_grad.reshape(n_seq, slice_rows, nstate), SEQ, 0, 0,...  25.3 us
    ppermute x12, waiting for transfers between devices, shift(): lax.ppermute(value, axis, [(i, (i + by) % count) for i in range(count)])  20.5 us
    ppermute x12, starting transfers between devices, shift(): lax.ppermute(value, axis, [(i, (i + by) % count) for i in range(count)])  19.5 us
    all_to_all x1, blocking collectives, shards(): got = lax.all_to_all(payload, SEQ, 0, 0, tiled=True)  18.9 us
    ppermute x14, starting transfers between devices, turn(): return lax.ppermute(value, SEQ, pairs)  17.4 us
    pallas_call x2, Pallas kernels, back_columns(): pl.pallas_call(functools.partial(back_kernel, heads, per), grid_spec=pltp...  11.9 us
  transfers between devices with their start and end apart: 28, of which 17 were waited for; matrix products, arithmetic and copies ran while one was open for 2% of the time, Pallas kernels for 8%

profile of v4, /device:TPU:1, one launch (start us, length us, event | category | flops | bytes accessed | tf_op | source)
XLA Modules:
  0.0 242.9 jit_solution(18087439613245426812)
XLA Ops:
  0.0 1.4 collective-permute-start
  1.4 1.3 pad_bitcast_fusion
  4.5 9.6 %project.1 = (bf16[128,1024]{1,0:T(8,128)(2,1)}, bf16[128,256]{1,0:T(8,128)(2,1)}, f32[128,128]{1,0:T(8,128)}, f32[128,128]{1,0:T(8,128)}, f32[128,128]{1,0:T(8,...) custom-call(bf16[128,4096]{1,0:T(8,128)(2,1)} %cand.3, bf16[4096,1024]{1,0:T(8,128)(2,1)} %w_in.5, ...), custom_call_target="tpu_custom_call" | custom-call | flops 1342177280 | bytes 12582912 | tf_op jit(solution)/shard_map/project/pallas_call | solution.py:243
  14.2 18.9 %all_to_all.20.got = bf16[32,48,128]{2,1,0:T(8,128)(2,1)} all-to-all(bf16[32,48,128]{2,1,0:T(8,128)(2,1)} %get-tuple-element.50), channel_id=1, replica_groups=mesh['x'=4,'z'=4,'c'=2,'e'=4] {'x','z','c'}, dimensions={0} | all-to-all | bytes 786432 | tf_op jit(solution)/shard_map/all_to_all | solution.py:657
  33.2 1.8 enter.1
  35.0 3.7 %all-to-all-start.1 = ((bf16[32,32,128]{2,1,0:T(8,128)(2,1)}), bf16[32,32,128]{2,1,0:T(8,128)(2,1)S(1)}, u32[]{:S(2)}, u32[]{:S(2)}) async-start(bf16[32,32,128]{2,1,0:T(8,128)(2,1)} %get-tuple-element.52), calls=%async_computation.1 | async-start | bytes 524288 | tf_op jit(solution)/shard_map/all_to_all | solution.py:664
  39.3 2.2 mix_within.1.within
  41.5 6.0 %all-to-all-done.1 = bf16[32,32,128]{2,1,0:T(8,128)(2,1)S(1)} async-done(((bf16[32,32,128]{2,1,0:T(8,128)(2,1)}), bf16[32,32,128]{2,1,0:T(8,128)(2,1)S(1)}, u32[]{:S(2)}, u32[]{:S(2)}) %all-to-all-start.1) | async-done | bytes 262176 | tf_op jit(solution)/shard_map/all_to_all | solution.py:664
  48.2 9.8 %mix_slots.1 = (f32[24,4096]{1,0:T(8,128)}, bf16[24,4096]{1,0:T(8,128)(2,1)}, bf16[24,4096]{1,0:T(8,128)(2,1)}, bf16[24,4096]{1,0:T(8,128)(2,1)}, f32[128,1024]{1,0:T(8,128)}) custom-call(f32[128,1024]{1,0:T(8,128)} %mix_within.1.within, bf16[128,256]{1,0:T(8,128)(2,1)} %get-tuple-element.46.bc_ref, f32[128,128]{1,0:T(8,128)} %get-tuple-element.47.cum_ref, ...), custom_call_target="tpu_custom_call" | custom-call | flops 805306368 | bytes 8388608 | tf_op jit(solution)/shard_map/mix_slots/pallas_call | solution.py:383
  58.0 1.4 collective-permute-start.2
  59.3 2.6 %collective-permute-start.3 = (bf16[24,4096]{1,0:T(8,128)(2,1)}, bf16[24,4096]{1,0:T(8,128)(2,1)S(1)}, u32[]{:S(2)}, u32[]{:S(2)}) collective-permute-start(bf16[24,4096]{1,0:T(8,128)(2,1)} %get-tuple-element.56), channel_id=1, source_target_pairs={{0,2},{1,3},{2,0},{3,1},{4,6},{5,7},{6,4},{7,5},{8,10},{9,11},{10,... | collective-permute-start | bytes 589832 | tf_op jit(solution)/shard_map/ppermute | solution.py:36
  63.0 2.9 %collective-permute-done.2 = bf16[24,4096]{1,0:T(8,128)(2,1)S(1)} collective-permute-done((bf16[24,4096]{1,0:T(8,128)(2,1)}, bf16[24,4096]{1,0:T(8,128)(2,1)S(1)}, u32[]{:S(2)}, u32[]{:S(2)}) %collective-permute-start.2) | collective-permute-done | bytes 196640 | tf_op jit(solution)/shard_map/ppermute | solution.py:36
  65.9 5.3 %collective-permute-done.3 = bf16[24,4096]{1,0:T(8,128)(2,1)S(1)} collective-permute-done((bf16[24,4096]{1,0:T(8,128)(2,1)}, bf16[24,4096]{1,0:T(8,128)(2,1)S(1)}, u32[]{:S(2)}, u32[]{:S(2)}) %collective-permute-start.3) | collective-permute-done | bytes 196640 | tf_op jit(solution)/shard_map/ppermute | solution.py:36
  71.3 1.2 fusion
  72.9 1.7 collective-permute-start.6
  74.6 1.1 collective-permute-start.5
  75.7 5.1 %collective-permute-done.7 = bf16[24,4096]{1,0:T(8,128)(2,1)S(1)} collective-permute-done((bf16[24,4096]{1,0:T(8,128)(2,1)S(1)}, bf16[24,4096]{1,0:T(8,128)(2,1)S(1)}, u32[]{:S(2)}, u32[]{:S(2)}) %collective-permute-start.7) | collective-permute-done | bytes 196640 | tf_op jit(solution)/shard_map/ppermute | solution.py:101
  82.1 2.1 collective-permute-start.8
  84.3 9.7 %collective-permute-done.9.refs_3_ = bf16[96,4096]{1,0:T(8,128)(2,1)S(1)} collective-permute-done((bf16[96,4096]{1,0:T(8,128)(2,1)S(1)}, bf16[96,4096]{1,0:T(8,128)(2,1)S(1)}, u32[]{:S(2)}, u32[]{:S(2)}) %collective-permute-start.9) | collective-permute-done | bytes 786464 | tf_op jit(solution)/shard_map/ppermute | solution.py:101
  94.1 2.7 %collective-permute-start.11 = (bf16[48,4096]{1,0:T(8,128)(2,1)S(1)}, bf16[48,4096]{1,0:T(8,128)(2,1)S(1)}, u32[]{:S(2)}, u32[]{:S(2)}) collective-permute-start(bf16[48,4096]{1,0:T(8,128)(2,1)S(1)} %slice.62), channel_id=1, source_target_pairs={{0,96},{4,28},{8,104},{12,4},{16,112},{20,12},{24,120},{28,20},{32... | collective-permute-start | bytes 1179656 | tf_op jit(solution)/shard_map/ppermute | solution.py:101
  97.4 3.6 %collective-permute-start.12 = (f32[1,256]{1,0:T(1,128)S(1)}, f32[1,256]{1,0:T(1,128)S(1)}, u32[]{:S(2)}, u32[]{:S(2)}) collective-permute-start(f32[1,256]{1,0:T(1,128)S(1)} %bitcast.32), channel_id=1, source_target_pairs={{0,4},{4,0},{1,5},{5,1},{2,6},{6,2},{3,7},{7,3},{8,12},{12,8},{9,1... | collective-permute-start | bytes 3080 | tf_op jit(solution)/shard_map/ppermute | solution.py:36
  103.3 14.4 %experts.1 = bf16[384,4096]{1,0:T(8,128)(2,1)} custom-call(bf16[96,4096]{1,0:T(8,128)(2,1)} %copy-done.4, bf16[96,4096]{1,0:T(8,128)(2,1)} %copy-done.6, bf16[96,4096]{1,0:T(8,128)(2,1)} %pad_maximum_fusion.1.refs_2_, bf16[96,4096]{1,0:T(8,128)(2,1)} %copy-done.5, bf16[4096,256]{1,0:T(8,128)(2,1)} %bitcast.35, bf16[4096,256]{1,0:T(8,128)(2,1)} %copy-done.10, ...), custom_call_target="tpu_custom_call" | custom-call | flops 6442450944 | bytes 14680064 | tf_op jit(solution)/shard_map/experts/pallas_call | solution.py:161
  117.7 1.6 fusion.5
  119.6 2.7 %collective-permute-start.15 = (bf16[48,4096]{1,0:T(8,128)(2,1)S(1)}, bf16[48,4096]{1,0:T(8,128)(2,1)S(1)}, u32[]{:S(2)}, u32[]{:S(2)}) collective-permute-start(bf16[48,4096]{1,0:T(8,128)(2,1)S(1)} %get-tuple-element.89), channel_id=1, source_target_pairs={{0,96},{4,28},{8,104},{12,4},{16,112},{20,12},{24,120},{28,20},{32... | collective-permute-start | bytes 1179656 | tf_op jit(solution)/shard_map/ppermute | solution.py:101
  122.3 5.5 %collective-permute-done.13 = bf16[48,4096]{1,0:T(8,128)(2,1)S(1)} collective-permute-done((bf16[48,4096]{1,0:T(8,128)(2,1)S(1)}, bf16[48,4096]{1,0:T(8,128)(2,1)S(1)}, u32[]{:S(2)}, u32[]{:S(2)}) %collective-permute-start.13) | collective-permute-done | bytes 393248 | tf_op jit(solution)/shard_map/ppermute | solution.py:101
  128.0 2.7 %collective-permute-start.16 = (bf16[96,4096]{1,0:T(8,128)(2,1)S(1)}, bf16[96,4096]{1,0:T(8,128)(2,1)S(1)}, u32[]{:S(2)}, u32[]{:S(2)}) collective-permute-start(bf16[96,4096]{1,0:T(8,128)(2,1)S(1)} %pad_maximum_fusion.3), channel_id=1, source_target_pairs={{0,96},{4,28},{8,104},{12,4},{16,112},{20,12},{24,120},{28,20},{32... | collective-permute-start | bytes 2359304 | tf_op jit(solution)/shard_map/ppermute | solution.py:101
  130.9 8.8 %collective-permute-done.16 = bf16[96,4096]{1,0:T(8,128)(2,1)S(1)} collective-permute-done((bf16[96,4096]{1,0:T(8,128)(2,1)S(1)}, bf16[96,4096]{1,0:T(8,128)(2,1)S(1)}, u32[]{:S(2)}, u32[]{:S(2)}) %collective-permute-start.16) | collective-permute-done | bytes 786464 | tf_op jit(solution)/shard_map/ppermute | solution.py:101
  139.7 3.5 %collective-permute-done.14 = bf16[96,4096]{1,0:T(8,128)(2,1)S(1)} collective-permute-done((bf16[96,4096]{1,0:T(8,128)(2,1)S(1)}, bf16[96,4096]{1,0:T(8,128)(2,1)S(1)}, u32[]{:S(2)}, u32[]{:S(2)}) %collective-permute-start.14) | collective-permute-done | bytes 786464 | tf_op jit(solution)/shard_map/ppermute | solution.py:101
  143.7 2.7 %collective-permute-start.19 = (bf16[24,4096]{1,0:T(8,128)(2,1)S(1)}, bf16[24,4096]{1,0:T(8,128)(2,1)S(1)}, u32[]{:S(2)}, u32[]{:S(2)}) collective-permute-start(bf16[24,4096]{1,0:T(8,128)(2,1)S(1)} %get-tuple-element.93), channel_id=1, source_target_pairs={{0,24},{4,100},{8,0},{12,108},{16,8},{20,116},{24,16},{28,124},{32... | collective-permute-start | bytes 589832 | tf_op jit(solution)/shard_map/ppermute | solution.py:101
  146.6 6.3 %collective-permute-done.17 = bf16[24,4096]{1,0:T(8,128)(2,1)S(1)} collective-permute-done((bf16[24,4096]{1,0:T(8,128)(2,1)S(1)}, bf16[24,4096]{1,0:T(8,128)(2,1)S(1)}, u32[]{:S(2)}, u32[]{:S(2)}) %collective-permute-start.17) | collective-permute-done | bytes 196640 | tf_op jit(solution)/shard_map/ppermute | solution.py:101
  154.3 2.1 collective-permute-start.21
  156.4 1.3 collective-permute-start.20
  157.8 1.7 collective-permute-done.22
  159.4 2.5 %collective-permute-done.21 = bf16[24,4096]{1,0:T(8,128)(2,1)S(1)} collective-permute-done((bf16[24,4096]{1,0:T(8,128)(2,1)S(1)}, bf16[24,4096]{1,0:T(8,128)(2,1)S(1)}, u32[]{:S(2)}, u32[]{:S(2)}) %collective-permute-start.21) | collective-permute-done | bytes 196640 | tf_op jit(solution)/shard_map/ppermute | solution.py:36
  163.1 10.3 %out_gradient.1 = (f32[128,4096]{1,0:T(8,128)}, f32[128,1024]{1,0:T(8,128)}, bf16[1024,128]{1,0:T(8,128)(2,1)}) custom-call(bf16[96,128]{1,0:T(8,128)(2,1)} %pad_maximum_fusion.5.table, bf16[96,4096]{1,0:T(8,128)(2,1)} %pad_maximum_fusion.4.terms, f32[1,4096]{1,0:T(1,128)} %bitcast.29, bf16[1024,4096]{1,0:T(8,128)(2,1)} %w_out.3, ...), custom_call_target="tpu_custom_call" | custom-call | flops 1073741824 | bytes 8388608 | tf_op jit(solution)/shard_map/out_gradient/pallas_call | solution.py:433
  173.3 25.3 %all_to_all.21.got = bf16[32,32,128]{2,1,0:T(8,128)(2,1)} all-to-all(bf16[32,32,128]{2,1,0:T(8,128)(2,1)} %bitcast.28), channel_id=1, replica_groups=mesh['x'=4,'z'=4,'c'=2,'e'=4] {'x','z','c'}, dimensions={0} | all-to-all | bytes 524288 | tf_op jit(solution)/shard_map/all_to_all | solution.py:690
  198.6 1.7 leave.1
  200.4 3.7 %all-to-all-start.3 = ((bf16[32,32,128]{2,1,0:T(8,128)(2,1)}), bf16[32,32,128]{2,1,0:T(8,128)(2,1)S(1)}, u32[]{:S(2)}, u32[]{:S(2)}) async-start(bf16[32,32,128]{2,1,0:T(8,128)(2,1)} %leave.1), calls=%async_computation.3 | async-start | bytes 524288 | tf_op jit(solution)/shard_map/all_to_all | solution.py:697
  204.7 3.7 %near_gradient.1 = (f32[128,1024]{1,0:T(8,128)}, f32[128,128]{1,0:T(8,128)}, f32[128,128]{1,0:T(8,128)}, f32[128,128]{1,0:T(8,128)}, f32[128,128]{1,0:T(8,128)}) custom-call(f32[128,1024]{1,0:T(8,128)} %get-tuple-element.66.grad_ref, bf16[128,1024]{1,0:T(8,128)(2,1)} %get-tuple-element.45.inner_ref, bf16[128,256]{1,0:T(8,128)(2,1)} %get-tuple-element.46.bc_ref, ...), custom_call_target="tpu_custom_call" | custom-call | flops 268435456 | bytes 2621440 | tf_op jit(solution)/shard_map/near_gradient/pallas_call | solution.py:161
  208.4 4.7 %all-to-all-done.3 = bf16[32,32,128]{2,1,0:T(8,128)(2,1)S(1)} async-done(((bf16[32,32,128]{2,1,0:T(8,128)(2,1)}), bf16[32,32,128]{2,1,0:T(8,128)(2,1)S(1)}, u32[]{:S(2)}, u32[]{:S(2)}) %all-to-all-start.3) | async-done | bytes 262176 | tf_op jit(solution)/shard_map/all_to_all | solution.py:697
  213.9 2.8 %far_gradient.1 = (bf16[128,1024]{1,0:T(8,128)(2,1)}, bf16[128,256]{1,0:T(8,128)(2,1)}, bf16[128,128]{1,0:T(8,128)(2,1)}) custom-call(bf16[1024,128]{1,0:T(8,128)(2,1)} %bitcast.24, bf16[1024,128]{1,0:T(8,128)(2,1)} %bitcast.22, bf16[128,1024]{1,0:T(8,128)(2,1)} %get-tuple-element.45.inner_ref, bf16[128,256]{1,0:T(8,128)(2,1)} %get-tuple-element.46.bc_ref, ...), custom_call_target="tpu_custom_call" | custom-call | flops 134217728 | bytes 2621440 | tf_op jit(solution)/shard_map/far_gradient/pallas_call | solution.py:161
  216.7 8.5 %back_columns.3 = (bf16[128,1024]{1,0:T(8,128)(2,1)}, bf16[128,1024]{1,0:T(8,128)(2,1)}, bf16[128,1024]{1,0:T(8,128)(2,1)}) custom-call(s32[3]{0:T(128)} %pad_add_fusion.which, bf16[128,1024]{1,0:T(8,128)(2,1)} %get-tuple-element.73.g_ref, bf16[128,256]{1,0:T(8,128)(2,1)} %get-tuple-element.74.gbc, bf16[128,128]{1,0:T(8,128)(2,1)} %get-tuple-element.75.gpre, ...), custom_call_target="tpu_custom_call" | custom-call | flops 1006632960 | bytes 7864320 | tf_op jit(solution)/shard_map/back_columns/pallas_call | solution.py:586
  225.2 2.3 collective-permute-start.23
  228.1 2.0 collective-permute-start.25
  230.2 3.4 %back_columns.2 = f32[128,1024]{1,0:T(8,128)} custom-call(s32[1]{0:T(128)} %bitcast.12.which, bf16[128,1024]{1,0:T(8,128)(2,1)} %get-tuple-element.73.g_ref, bf16[128,256]{1,0:T(8,128)(2,1)} %get-tuple-element.74.gbc, bf16[128,128]{1,0:T(8,128)(2,1)} %get-tuple-element.75.gpre, bf16[4096,1024]{1,0:T(8,128)(2,1)} %w_in.5, bf16[4096,256]{1,0:T(8,128)(2,1)} %w_bc.5, ...), custom_call_target="tpu_custom_call" | custom-call | flops 335544320 | bytes 2621440 | tf_op jit(solution)/shard_map/back_columns/pallas_call | solution.py:586
  233.6 1.1 collective-permute-done.23
  234.6 6.1 %collective-permute-done.24 = bf16[128,1024]{1,0:T(8,128)(2,1)S(1)} collective-permute-done((bf16[128,1024]{1,0:T(8,128)(2,1)}, bf16[128,1024]{1,0:T(8,128)(2,1)S(1)}, u32[]{:S(2)}, u32[]{:S(2)}) %collective-permute-start.24) | collective-permute-done | bytes 262176 | tf_op jit(solution)/shard_map/ppermute | solution.py:36
  240.7 2.2 subtract_convert_fusion
  (75 shorter events, 14.9 us)
Async XLA Ops:
  0.0 14.2 %collective-permute-start = (bf16[4096,256]{1,0:T(8,128)(2,1)}, bf16[4096,256]{1,0:T(8,128)(2,1)S(1)}, u32[]{:S(2)}, u32[]{:S(2)}) collective-permute-start(bf16[4096,256]{1,0:T(8,128)(2,1)} %bitcast.34), channel_id=1, source_target_pairs={{0,4},{4,0},{1,5},{5,1},{2,6},{6,2},{3,7},{7,3},{8,12},{12,8},{9,1... | collective-permute-start | bytes 6291464 | tf_op jit(solution)/shard_map/ppermute | solution.py:36
  1.4 12.8 %collective-permute-start.1 = (bf16[4096,256]{1,0:T(8,128)(2,1)}, bf16[4096,256]{1,0:T(8,128)(2,1)}, u32[]{:S(2)}, u32[]{:S(2)}) collective-permute-start(bf16[4096,256]{1,0:T(8,128)(2,1)} %bitcast.36), channel_id=1, source_target_pairs={{0,4},{4,0},{1,5},{5,1},{2,6},{6,2},{3,7},{7,3},{8,12},{12,8},{9,1... | collective-permute-start | bytes 6291464 | tf_op jit(solution)/shard_map/ppermute | solution.py:36
  3.7 10.4 %copy-start.8 = (bf16[24,128]{1,0:T(8,128)(2,1)}, bf16[24,128]{1,0:T(8,128)(2,1)S(1)}, u32[]{:S(2)}) copy-start(bf16[24,128]{1,0:T(8,128)(2,1)S(1)} %get-tuple-element.53.own_table) | copy-start | bytes 18436
  14.2 24.5 %copy-start.9 = (f32[8]{0:T(128)S(1)}, f32[8]{0:T(128)}, u32[]{:S(2)}) copy-start(f32[8]{0:T(128)} %param.20) | copy-start | bytes 100
  14.2 43.8 %copy-start.10 = (bf16[4096,256]{1,0:T(8,128)(2,1)}, bf16[4096,256]{1,0:T(8,128)(2,1)S(1)}, u32[]{:S(2)}) copy-start(bf16[4096,256]{1,0:T(8,128)(2,1)S(1)} %collective-permute-done.refs_5_) | copy-start | bytes 6291460
  35.0 12.5 %all-to-all-start.1 = ((bf16[32,32,128]{2,1,0:T(8,128)(2,1)}), bf16[32,32,128]{2,1,0:T(8,128)(2,1)S(1)}, u32[]{:S(2)}, u32[]{:S(2)}) async-start(bf16[32,32,128]{2,1,0:T(8,128)(2,1)} %get-tuple-element.52), calls=%async_computation.1 | async-start | bytes 524288 | tf_op jit(solution)/shard_map/all_to_all | solution.py:664
  47.5 0.7 copy-start
  58.0 7.9 %collective-permute-start.2 = (bf16[24,4096]{1,0:T(8,128)(2,1)}, bf16[24,4096]{1,0:T(8,128)(2,1)S(1)}, u32[]{:S(2)}, u32[]{:S(2)}) collective-permute-start(bf16[24,4096]{1,0:T(8,128)(2,1)} %get-tuple-element.55), channel_id=1, source_target_pairs={{0,1},{1,2},{2,3},{3,0},{4,5},{5,6},{6,7},{7,4},{8,9},{9,10},{10,1... | collective-permute-start | bytes 589832 | tf_op jit(solution)/shard_map/ppermute | solution.py:36
  59.3 11.9 %collective-permute-start.3 = (bf16[24,4096]{1,0:T(8,128)(2,1)}, bf16[24,4096]{1,0:T(8,128)(2,1)S(1)}, u32[]{:S(2)}, u32[]{:S(2)}) collective-permute-start(bf16[24,4096]{1,0:T(8,128)(2,1)} %get-tuple-element.56), channel_id=1, source_target_pairs={{0,2},{1,3},{2,0},{3,1},{4,6},{5,7},{6,4},{7,5},{8,10},{9,11},{10,... | collective-permute-start | bytes 589832 | tf_op jit(solution)/shard_map/ppermute | solution.py:36
  62.0 9.3 %collective-permute-start.4 = (bf16[24,4096]{1,0:T(8,128)(2,1)}, bf16[24,4096]{1,0:T(8,128)(2,1)S(1)}, u32[]{:S(2)}, u32[]{:S(2)}) collective-permute-start(bf16[24,4096]{1,0:T(8,128)(2,1)} %get-tuple-element.57), channel_id=1, source_target_pairs={{0,3},{1,0},{2,1},{3,2},{4,7},{5,4},{6,5},{7,6},{8,11},{9,8},{10,9... | collective-permute-start | bytes 589832 | tf_op jit(solution)/shard_map/ppermute | solution.py:36
  72.6 24.2 %copy-start.2 = (bf16[1,256,4096]{2,1,0:T(8,128)(2,1)S(1)}, bf16[1,256,4096]{2,1,0:T(8,128)(2,1)}, u32[]{:S(2)}) copy-start(bf16[1,256,4096]{2,1,0:T(8,128)(2,1)} %param.26) | copy-start | bytes 6291460
  72.6 24.2 %copy-start.7 = (f32[4096]{0:T(1024)S(1)}, f32[4096]{0:T(1024)}, u32[]{:S(2)}) copy-start(f32[4096]{0:T(1024)} %param.27) | copy-start | bytes 49156
  72.6 8.2 %collective-permute-start.7 = (bf16[24,4096]{1,0:T(8,128)(2,1)S(1)}, bf16[24,4096]{1,0:T(8,128)(2,1)S(1)}, u32[]{:S(2)}, u32[]{:S(2)}) collective-permute-start(bf16[24,4096]{1,0:T(8,128)(2,1)S(1)} %fusion.4), channel_id=1, source_target_pairs={{0,8},{4,36},{8,16},{12,44},{16,24},{20,52},{24,0},{28,60},{32,40}... | collective-permute-start | bytes 589832 | tf_op jit(solution)/shard_map/ppermute | solution.py:101
  72.9 7.9 %collective-permute-start.6 = (bf16[24,4096]{1,0:T(8,128)(2,1)S(1)}, bf16[24,4096]{1,0:T(8,128)(2,1)S(1)}, u32[]{:S(2)}, u32[]{:S(2)}) collective-permute-start(bf16[24,4096]{1,0:T(8,128)(2,1)S(1)} %fusion.4), channel_id=1, source_target_pairs={{0,16},{4,68},{8,24},{12,76},{16,0},{20,84},{24,8},{28,92},{32,48}... | collective-permute-start | bytes 589832 | tf_op jit(solution)/shard_map/ppermute | solution.py:101
  74.6 6.8 %collective-permute-start.5 = (bf16[24,4096]{1,0:T(8,128)(2,1)S(1)}, bf16[24,4096]{1,0:T(8,128)(2,1)S(1)}, u32[]{:S(2)}, u32[]{:S(2)}) collective-permute-start(bf16[24,4096]{1,0:T(8,128)(2,1)S(1)} %fusion.4), channel_id=1, source_target_pairs={{0,24},{4,100},{8,0},{12,108},{16,8},{20,116},{24,16},{28,124},{32... | collective-permute-start | bytes 589832 | tf_op jit(solution)/shard_map/ppermute | solution.py:101
  81.5 15.8 %copy-start.4 = (bf16[96,4096]{1,0:T(8,128)(2,1)}, bf16[96,4096]{1,0:T(8,128)(2,1)S(1)}, u32[]{:S(2)}) copy-start(bf16[96,4096]{1,0:T(8,128)(2,1)S(1)} %pad_maximum_fusion.refs_0_) | copy-start | bytes 2359300
  81.5 12.4 %collective-permute-start.9 = (bf16[96,4096]{1,0:T(8,128)(2,1)S(1)}, bf16[96,4096]{1,0:T(8,128)(2,1)S(1)}, u32[]{:S(2)}, u32[]{:S(2)}) collective-permute-start(bf16[96,4096]{1,0:T(8,128)(2,1)S(1)} %pad_maximum_fusion.refs_0_), channel_id=1, source_target_pairs={{0,32},{4,12},{8,40},{12,20},{16,48},{20,28},{24,56},{28,4},{32,64... | collective-permute-start | bytes 2359304 | tf_op jit(solution)/shard_map/ppermute | solution.py:101
  82.1 11.9 %collective-permute-start.8 = (bf16[96,4096]{1,0:T(8,128)(2,1)S(1)}, bf16[96,4096]{1,0:T(8,128)(2,1)S(1)}, u32[]{:S(2)}, u32[]{:S(2)}) collective-permute-start(bf16[96,4096]{1,0:T(8,128)(2,1)S(1)} %pad_maximum_fusion.refs_0_), channel_id=1, source_target_pairs={{0,96},{4,28},{8,104},{12,4},{16,112},{20,12},{24,120},{28,20},{32... | collective-permute-start | bytes 2359304 | tf_op jit(solution)/shard_map/ppermute | solution.py:101
  93.9 3.4 %copy-start.5 = (bf16[96,4096]{1,0:T(8,128)(2,1)}, bf16[96,4096]{1,0:T(8,128)(2,1)S(1)}, u32[]{:S(2)}) copy-start(bf16[96,4096]{1,0:T(8,128)(2,1)S(1)} %collective-permute-done.9.refs_3_) | copy-start | bytes 2359300
  94.0 8.4 %collective-permute-start.10 = (bf16[48,4096]{1,0:T(8,128)(2,1)S(1)}, bf16[48,4096]{1,0:T(8,128)(2,1)S(1)}, u32[]{:S(2)}, u32[]{:S(2)}) collective-permute-start(bf16[48,4096]{1,0:T(8,128)(2,1)S(1)} %slice.61), channel_id=1, source_target_pairs={{0,32},{4,12},{8,40},{12,20},{16,48},{20,28},{24,56},{28,4},{32,64... | collective-permute-start | bytes 1179656 | tf_op jit(solution)/shard_map/ppermute | solution.py:101
  94.1 9.3 %copy-start.6 = (bf16[96,4096]{1,0:T(8,128)(2,1)}, bf16[96,4096]{1,0:T(8,128)(2,1)S(1)}, u32[]{:S(2)}) copy-start(bf16[96,4096]{1,0:T(8,128)(2,1)S(1)} %collective-permute-done.8.refs_1_) | copy-start | bytes 2359300
  94.1 8.3 %collective-permute-start.11 = (bf16[48,4096]{1,0:T(8,128)(2,1)S(1)}, bf16[48,4096]{1,0:T(8,128)(2,1)S(1)}, u32[]{:S(2)}, u32[]{:S(2)}) collective-permute-start(bf16[48,4096]{1,0:T(8,128)(2,1)S(1)} %slice.62), channel_id=1, source_target_pairs={{0,96},{4,28},{8,104},{12,4},{16,112},{20,12},{24,120},{28,20},{32... | collective-permute-start | bytes 1179656 | tf_op jit(solution)/shard_map/ppermute | solution.py:101
  97.4 4.4 %collective-permute-start.12 = (f32[1,256]{1,0:T(1,128)S(1)}, f32[1,256]{1,0:T(1,128)S(1)}, u32[]{:S(2)}, u32[]{:S(2)}) collective-permute-start(f32[1,256]{1,0:T(1,128)S(1)} %bitcast.32), channel_id=1, source_target_pairs={{0,4},{4,0},{1,5},{5,1},{2,6},{6,2},{3,7},{7,3},{8,12},{12,8},{9,1... | collective-permute-start | bytes 3080 | tf_op jit(solution)/shard_map/ppermute | solution.py:36
  117.7 10.0 %copy-start.1 = (bf16[384,4096]{1,0:T(8,128)(2,1)S(1)}, bf16[384,4096]{1,0:T(8,128)(2,1)}, u32[]{:S(2)}) copy-start(bf16[384,4096]{1,0:T(8,128)(2,1)} %experts.1) | copy-start | bytes 9437188
  119.4 8.4 %collective-permute-start.13 = (bf16[48,4096]{1,0:T(8,128)(2,1)S(1)}, bf16[48,4096]{1,0:T(8,128)(2,1)S(1)}, u32[]{:S(2)}, u32[]{:S(2)}) collective-permute-start(bf16[48,4096]{1,0:T(8,128)(2,1)S(1)} %get-tuple-element.88), channel_id=1, source_target_pairs={{0,32},{4,12},{8,40},{12,20},{16,48},{20,28},{24,56},{28,4},{32,64... | collective-permute-start | bytes 1179656 | tf_op jit(solution)/shard_map/ppermute | solution.py:101
  119.6 8.1 %collective-permute-start.15 = (bf16[48,4096]{1,0:T(8,128)(2,1)S(1)}, bf16[48,4096]{1,0:T(8,128)(2,1)S(1)}, u32[]{:S(2)}, u32[]{:S(2)}) collective-permute-start(bf16[48,4096]{1,0:T(8,128)(2,1)S(1)} %get-tuple-element.89), channel_id=1, source_target_pairs={{0,96},{4,28},{8,104},{12,4},{16,112},{20,12},{24,120},{28,20},{32... | collective-permute-start | bytes 1179656 | tf_op jit(solution)/shard_map/ppermute | solution.py:101
  128.0 11.7 %collective-permute-start.16 = (bf16[96,4096]{1,0:T(8,128)(2,1)S(1)}, bf16[96,4096]{1,0:T(8,128)(2,1)S(1)}, u32[]{:S(2)}, u32[]{:S(2)}) collective-permute-start(bf16[96,4096]{1,0:T(8,128)(2,1)S(1)} %pad_maximum_fusion.3), channel_id=1, source_target_pairs={{0,96},{4,28},{8,104},{12,4},{16,112},{20,12},{24,120},{28,20},{32... | collective-permute-start | bytes 2359304 | tf_op jit(solution)/shard_map/ppermute | solution.py:101
  130.8 12.4 %collective-permute-start.14 = (bf16[96,4096]{1,0:T(8,128)(2,1)S(1)}, bf16[96,4096]{1,0:T(8,128)(2,1)S(1)}, u32[]{:S(2)}, u32[]{:S(2)}) collective-permute-start(bf16[96,4096]{1,0:T(8,128)(2,1)S(1)} %pad_maximum_fusion.2), channel_id=1, source_target_pairs={{0,32},{4,12},{8,40},{12,20},{16,48},{20,28},{24,56},{28,4},{32,64... | collective-permute-start | bytes 2359304 | tf_op jit(solution)/shard_map/ppermute | solution.py:101
  143.6 9.3 %collective-permute-start.17 = (bf16[24,4096]{1,0:T(8,128)(2,1)S(1)}, bf16[24,4096]{1,0:T(8,128)(2,1)S(1)}, u32[]{:S(2)}, u32[]{:S(2)}) collective-permute-start(bf16[24,4096]{1,0:T(8,128)(2,1)S(1)} %get-tuple-element.92), channel_id=1, source_target_pairs={{0,8},{4,36},{8,16},{12,44},{16,24},{20,52},{24,0},{28,60},{32,40}... | collective-permute-start | bytes 589832 | tf_op jit(solution)/shard_map/ppermute | solution.py:101
  143.7 9.2 %collective-permute-start.19 = (bf16[24,4096]{1,0:T(8,128)(2,1)S(1)}, bf16[24,4096]{1,0:T(8,128)(2,1)S(1)}, u32[]{:S(2)}, u32[]{:S(2)}) collective-permute-start(bf16[24,4096]{1,0:T(8,128)(2,1)S(1)} %get-tuple-element.93), channel_id=1, source_target_pairs={{0,24},{4,100},{8,0},{12,108},{16,8},{20,116},{24,16},{28,124},{32... | collective-permute-start | bytes 589832 | tf_op jit(solution)/shard_map/ppermute | solution.py:101
  146.3 6.5 %collective-permute-start.18 = (bf16[24,4096]{1,0:T(8,128)(2,1)S(1)}, bf16[24,4096]{1,0:T(8,128)(2,1)S(1)}, u32[]{:S(2)}, u32[]{:S(2)}) collective-permute-start(bf16[24,4096]{1,0:T(8,128)(2,1)S(1)} %get-tuple-element.94), channel_id=1, source_target_pairs={{0,16},{4,68},{8,24},{12,76},{16,0},{20,84},{24,8},{28,92},{32,48}... | collective-permute-start | bytes 589832 | tf_op jit(solution)/shard_map/ppermute | solution.py:101
  153.3 6.1 %collective-permute-start.22 = (bf16[24,4096]{1,0:T(8,128)(2,1)S(1)}, bf16[24,4096]{1,0:T(8,128)(2,1)S(1)}, u32[]{:S(2)}, u32[]{:S(2)}) collective-permute-start(bf16[24,4096]{1,0:T(8,128)(2,1)S(1)} %divide_convert_fusion), channel_id=1, source_target_pairs={{0,1},{1,2},{2,3},{3,0},{4,5},{5,6},{6,7},{7,4},{8,9},{9,10},{10,1... | collective-permute-start | bytes 589832 | tf_op jit(solution)/shard_map/ppermute | solution.py:36
  154.3 7.6 %collective-permute-start.21 = (bf16[24,4096]{1,0:T(8,128)(2,1)S(1)}, bf16[24,4096]{1,0:T(8,128)(2,1)S(1)}, u32[]{:S(2)}, u32[]{:S(2)}) collective-permute-start(bf16[24,4096]{1,0:T(8,128)(2,1)S(1)} %divide_convert_fusion), channel_id=1, source_target_pairs={{0,2},{1,3},{2,0},{3,1},{4,6},{5,7},{6,4},{7,5},{8,10},{9,11},{10,... | collective-permute-start | bytes 589832 | tf_op jit(solution)/shard_map/ppermute | solution.py:36
  156.4 5.7 %collective-permute-start.20 = (bf16[24,4096]{1,0:T(8,128)(2,1)S(1)}, bf16[24,4096]{1,0:T(8,128)(2,1)S(1)}, u32[]{:S(2)}, u32[]{:S(2)}) collective-permute-start(bf16[24,4096]{1,0:T(8,128)(2,1)S(1)} %divide_convert_fusion), channel_id=1, source_target_pairs={{0,3},{1,0},{2,1},{3,2},{4,7},{5,4},{6,5},{7,6},{8,11},{9,8},{10,9... | collective-permute-start | bytes 589832 | tf_op jit(solution)/shard_map/ppermute | solution.py:36
  200.4 12.8 %all-to-all-start.3 = ((bf16[32,32,128]{2,1,0:T(8,128)(2,1)}), bf16[32,32,128]{2,1,0:T(8,128)(2,1)S(1)}, u32[]{:S(2)}, u32[]{:S(2)}) async-start(bf16[32,32,128]{2,1,0:T(8,128)(2,1)} %leave.1), calls=%async_computation.3 | async-start | bytes 524288 | tf_op jit(solution)/shard_map/all_to_all | solution.py:697
  213.2 0.7 copy-start.3
  225.2 9.5 %collective-permute-start.23 = (bf16[128,1024]{1,0:T(8,128)(2,1)}, bf16[128,1024]{1,0:T(8,128)(2,1)S(1)}, u32[]{:S(2)}, u32[]{:S(2)}) collective-permute-start(bf16[128,1024]{1,0:T(8,128)(2,1)} %get-tuple-element.76), channel_id=1, source_target_pairs={{0,2},{1,3},{2,0},{3,1},{4,6},{5,7},{6,4},{7,5},{8,10},{9,11},{10,... | collective-permute-start | bytes 786440 | tf_op jit(solution)/shard_map/ppermute | solution.py:36
  227.5 13.2 %collective-permute-start.24 = (bf16[128,1024]{1,0:T(8,128)(2,1)}, bf16[128,1024]{1,0:T(8,128)(2,1)S(1)}, u32[]{:S(2)}, u32[]{:S(2)}) collective-permute-start(bf16[128,1024]{1,0:T(8,128)(2,1)} %get-tuple-element.77), channel_id=1, source_target_pairs={{0,1},{1,2},{2,3},{3,0},{4,5},{5,6},{6,7},{7,4},{8,9},{9,10},{10,1... | collective-permute-start | bytes 786440 | tf_op jit(solution)/shard_map/ppermute | solution.py:36
  228.1 12.6 %collective-permute-start.25 = (bf16[128,1024]{1,0:T(8,128)(2,1)}, bf16[128,1024]{1,0:T(8,128)(2,1)S(1)}, u32[]{:S(2)}, u32[]{:S(2)}) collective-permute-start(bf16[128,1024]{1,0:T(8,128)(2,1)} %get-tuple-element.78), channel_id=1, source_target_pairs={{0,3},{1,0},{2,1},{3,2},{4,7},{5,4},{6,5},{7,6},{8,11},{9,8},{10,9... | collective-permute-start | bytes 786440 | tf_op jit(solution)/shard_map/ppermute | solution.py:36

commit v5 on v3

--- a/solution.py
+++ b/solution.py
@@ -102,15 +102,18 @@
     depth = near[0].shape[1]
     half = wg0.shape[1]
     out = jax.ShapeDtypeStruct((count, depth), BF)
-    return single(
+    args = (*near, *far, wg0, wg1, wu0, wu1, head_vec)
+    held = pl.BlockSpec(memory_space=pltpu.VMEM)
+    return pl.pallas_call(
         functools.partial(expert_kernel, side),
         out_shape=(out, out),
-        args=(*near, *far, wg0, wg1, wu0, wu1, head_vec),
+        in_specs=[held] * len(args),
+        out_specs=(held, held),
         scratch_shapes=[pltpu.VMEM((count, 2 * half), BF)] * 2,
-        compiler_params=vmem(56),
+        compiler_params=vmem(26),
         cost_estimate=cost(32 * count * depth * half, 16 * depth * half + 8 * count * depth),
         name="experts",
-    )
+    )(*args)
 
 
 def gather_around(value, axis):
@@ -204,7 +207,7 @@
     x = cand[...]
     acc[...] += mm(x, w_in[...])
     acc_bc[...] += mm(x, w_bc[...])
-    acc_pre[:, :heads] += mm(x, w_step[...])
+    acc_pre[:, :heads] += mm_t(x, w_step[...])
 
     @pl.when(i == pl.num_programs(0) - 1)
     def _():
@@ -269,7 +272,7 @@
             pl.BlockSpec((tlen, depth), lambda i: (0, i)),
             pl.BlockSpec((depth, chan), lambda i: (i, 0)),
             pl.BlockSpec((depth, two), lambda i: (i, 0)),
-            pl.BlockSpec((depth, heads), lambda i: (i, 0)),
+            pl.BlockSpec((heads, depth), lambda i: (0, i)),
             fixed(1, tlen), fixed(1, tlen),
         ],
         out_specs=(
@@ -392,7 +395,7 @@
     tlen, chan = within.shape
     width = out_proj.shape[1]
     rows = table.shape[0]
-    block = min(width, 1024)
+    block = min(width, 2048)
     fixed = lambda a: pl.BlockSpec(a.shape, lambda i: (0,) * a.ndim)
     cols = lambda n: pl.BlockSpec((n, block), lambda i: (0, i))
     sent = jax.ShapeDtypeStruct((CAP, width), BF)
@@ -443,7 +446,7 @@
     tlen = table.shape[1]
     chan, width = out_proj.shape
     nstate = bc_bf.shape[1] // 2
-    block = min(width, 1024)
+    block = min(width, 2048)
     fixed = lambda *shape: pl.BlockSpec(shape, lambda i: (0,) * len(shape))
     cols = lambda n: pl.BlockSpec((n, block), lambda i: (0, i))
     return pl.pallas_call(
@@ -580,32 +583,44 @@
     )
 
 
-def back_kernel(heads, which, g_ref, gbc, gpre, w_in, w_bc, w_step, out):
+def back_kernel(heads, per, which, g_ref, gbc, gpre, w_in, w_bc, w_step, *outs):
     total = mm_t(g_ref[...], w_in[...]) + mm_t(gbc[...], w_bc[...])
-    total += mm_t(gpre[:, :heads], w_step[...])
-    out[...] = total.astype(out.dtype)
-
-
-def back_columns(which, g_inner, g_bc, g_pre, in_proj, bc_proj, step_proj, cols, dtype, heads):
+    total += mm(gpre[:, :heads], w_step[...])
+    for k, out in enumerate(outs):
+
+        @pl.when(pl.program_id(0) // per == k)
+        def _():
+            out[...] = total.astype(out.dtype)
+
+
+def back_columns(which, g_inner, g_bc, g_pre, in_proj, bc_proj, step_w, cols, dtype, heads):
     tlen, chan = g_inner.shape
     two = bc_proj.shape[1]
-    block = min(cols, 512)
+    count = which.shape[0]
+    block = min(cols, 1024)
     per = cols // block
     fixed = lambda a: pl.BlockSpec(a.shape, lambda i, w: (0,) * a.ndim)
-    rows = lambda n: pl.BlockSpec((block, n), lambda i, w: (w[0] * per + i, 0))
+    place = lambda i, w: w[i // per] * per + i % per
+    rows = lambda n: pl.BlockSpec((block, n), lambda i, w: (place(i, w), 0))
     return pl.pallas_call(
-        functools.partial(back_kernel, heads),
+        functools.partial(back_kernel, heads, per),
         grid_spec=pltpu.PrefetchScalarGridSpec(
             num_scalar_prefetch=1,
-            grid=(per,),
-            in_specs=[fixed(g_inner), fixed(g_bc), fixed(g_pre), rows(chan), rows(two), rows(heads)],
-            out_specs=pl.BlockSpec((tlen, block), lambda i, w: (0, i)),
+            grid=(count * per,),
+            in_specs=[
+                fixed(g_inner), fixed(g_bc), fixed(g_pre), rows(chan), rows(two),
+                pl.BlockSpec((heads, block), lambda i, w: (0, place(i, w))),
+            ],
+            out_specs=tuple(
+                pl.BlockSpec((tlen, block), lambda i, w, k=k: (0, jnp.clip(i - k * per, 0, per - 1)))
+                for k in range(count)
+            ),
         ),
-        out_shape=jax.ShapeDtypeStruct((tlen, cols), dtype),
-        compiler_params=vmem(56),
-        cost_estimate=cost(2 * tlen * (chan + two) * cols, 2 * (chan + two) * cols),
+        out_shape=tuple(jax.ShapeDtypeStruct((tlen, cols), dtype) for _ in range(count)),
+        compiler_params=vmem(56),
+        cost_estimate=cost(2 * tlen * (chan + two) * cols * count, 2 * (chan + two) * cols * count),
         name="back_columns",
-    )(which, g_inner, g_bc, g_pre, in_proj, bc_proj, step_proj)
+    )(which, g_inner, g_bc, g_pre, in_proj, bc_proj, step_w)
 
 
 def shards(
@@ -626,6 +641,7 @@
 ):
     tlen, width = candidate.shape
     heads = step_bias.shape[0]
+    step_w = step_proj.T
     chan = in_proj.shape[1]
     size = chan // heads
     nstate = bc_proj.shape[1] // 2
@@ -640,11 +656,8 @@
     energy = energy_head[None, :]
 
     wg0, wu0 = expert_gate[0], expert_up[0]
-    head_own = jnp.sum(expert_down[0].astype(F32) * energy, axis=1)
     wg1 = shift(wg0, "c", 1)
     wu1 = shift(wu0, "c", 1)
-    head_other = shift(head_own[None, :], "c", 1)
-    head_vec = jnp.concatenate([head_own[None, :], head_other], axis=0)
 
     pairs = [
         slot_table(expert_ids, gate_weights, lax.rem(column + k, n_exp)) for k in range(n_exp)
@@ -655,14 +668,18 @@
     own_table = own_table.astype(BF)
 
     inner_b, bc_bf, pre, step, cum, step_t, cum_t, payload = project(
-        candidate, in_proj, bc_proj, step_proj, bias, rate, heads, n_seq
-    )
-    payload, wg1, wu1, head_vec, table, own_table, slot_weight = lax.optimization_barrier(
-        (payload, wg1, wu1, head_vec, table, own_table, slot_weight)
+        candidate, in_proj, bc_proj, step_w, bias, rate, heads, n_seq
+    )
+    payload, wg1, wu1, table, own_table, slot_weight = lax.optimization_barrier(
+        (payload, wg1, wu1, table, own_table, slot_weight)
     )
     got = lax.all_to_all(payload, SEQ, 0, 0, tiled=True)
     within = mix_within(inner_b, bc_bf, cum, cum_t, step_t, skip, heads)
     entering, decay = enter_states(got, slice_rows)
+    entering, down = lax.optimization_barrier((entering, expert_down[0]))
+    head_own = jnp.sum(down.astype(F32) * energy, axis=1)
+    head_other = shift(head_own[None, :], "c", 1)
+    head_vec = jnp.concatenate([head_own[None, :], head_other], axis=0)
     state = lax.all_to_all(entering, SEQ, 0, 0, tiled=True).reshape(chan, nstate)
 
     own, send1, send2, send3, reads = mix_slots(
@@ -712,14 +729,16 @@
         later, state, inner_b, bc_bf, cum, step, pre, rate, near, gb, gc, dcum, dstep, heads
     )
 
-    def columns(k, dtype):
-        which = lax.rem(column + k, n_exp)[None]
+    def columns(places, dtype):
+        which = jnp.stack([lax.rem(column + k, n_exp) for k in places])
         return back_columns(
-            which, g_inner, g_bc, g_pre, in_proj, bc_proj, step_proj, col_count, dtype, heads
+            which, g_inner, g_bc, g_pre, in_proj, bc_proj, step_w, col_count, dtype, heads
         )
 
-    arrived = [shift(columns(k, BF), "e", k) for k in (2, 1, 3)]
-    summed = lax.dynamic_slice_in_dim(hid_grad, column * col_count, col_count, 1) + columns(0, F32)
+    order = (2, 1, 3)
+    arrived = [shift(part, "e", k) for k, part in zip(order, columns(order, BF))]
+    (own_part,) = columns((0,), F32)
+    summed = lax.dynamic_slice_in_dim(hid_grad, column * col_count, col_count, 1) + own_part
     for value in arrived:
         summed = summed + value.astype(F32)
     own_cand = lax.dynamic_slice_in_dim(candidate, column * col_count, col_count, 1).astype(F32)

time: 235 us -> 232 us (0.987)
  waiting for transfers between devices: 47.6 us -> 56.5 us
  Pallas kernels: 63.7 us -> 54.9 us
    pallas_call x6 -> x5, Pallas kernels: 25.6 us -> 12.3 us  [single(): pl.pallas_call(kernel, grid=(1,), out_shape=out_shape, in_specs=whole(arg...]
    ppermute x40, waiting for transfers between devices: 36.3 us -> 45.9 us  [shift(): lax.ppermute(value, axis, [(i, (i + by) % count) for i in range(count)])]
    pallas_call x4 -> x3, Pallas kernels: 13.9 us -> 20.2 us  [the longest x2 11 us: back_columns(): pl.pallas_call(functools.partial(back_kernel, heads, per), grid_spec=pltp...]
  transfers between devices with their start and end apart: 42 -> 42, of which waited for: 20 -> 21; matrix products, arithmetic and copies ran while one was open for 3% -> 2% of each run, Pallas kernels for 8% -> 8%
where the time goes in v5:
time: 232 us; the launch traced here: 231 us
  starting transfers between devices  63.3 us (27%)
  waiting for transfers between devices  56.5 us (24%)
  Pallas kernels  54.9 us (24%)
  blocking collectives  43.9 us (19%)
  other arithmetic  8.67 us (4%)
  local copies, waits for them, and re-layouts  3.62 us (2%)
    ppermute x40, starting transfers between devices, shift(): lax.ppermute(value, axis, [(i, (i + by) % count) for i in range(count)])  56 us
    ppermute x40, waiting for transfers between devices, shift(): lax.ppermute(value, axis, [(i, (i + by) % count) for i in range(count)])  45.9 us
    all_to_all x1, blocking collectives, shards(): lax.all_to_all(local_grad.reshape(n_seq, slice_rows, nstate), SEQ, 0, 0,...  25 us
    all_to_all x1, blocking collectives, shards(): got = lax.all_to_all(payload, SEQ, 0, 0, tiled=True)  18.9 us
    pallas_call x5, Pallas kernels, single(): pl.pallas_call(kernel, grid=(1,), out_shape=out_shape, in_specs=whole(arg...  12.3 us
    pallas_call x2, Pallas kernels, back_columns(): pl.pallas_call(functools.partial(back_kernel, heads, per), grid_spec=pltp...  11 us
    pallas_call x1, Pallas kernels, expert_rows(): pl.pallas_call(functools.partial(expert_kernel, side), out_shape=(out, ou...  9.18 us
    pallas_call x1, Pallas kernels, project(): pl.pallas_call(functools.partial(proj_kernel, heads, slice_rows), grid=(w...  8.07 us
  transfers between devices with their start and end apart: 42, of which 21 were waited for; matrix products, arithmetic and copies ran while one was open for 2% of the time, Pallas kernels for 8%

profile of v5, /device:TPU:1, one launch (start us, length us, event | category | flops | bytes accessed | tf_op | source)
XLA Modules:
  0.0 231.4 jit_solution(1639330930583731129)
XLA Ops:
  4.6 8.1 %project.1 = (bf16[128,1024]{1,0:T(8,128)(2,1)}, bf16[128,256]{1,0:T(8,128)(2,1)}, f32[128,128]{1,0:T(8,128)}, f32[128,128]{1,0:T(8,128)}, f32[128,128]{1,0:T(8,...) custom-call(bf16[128,4096]{1,0:T(8,128)(2,1)} %cand.3, bf16[4096,1024]{1,0:T(8,128)(2,1)} %w_in.5, ...), custom_call_target="tpu_custom_call" | custom-call | flops 1342177280 | bytes 12582912 | tf_op jit(solution)/shard_map/project/pallas_call | solution.py:262
  12.7 18.9 %all_to_all.20.got = bf16[32,48,128]{2,1,0:T(8,128)(2,1)} all-to-all(bf16[32,48,128]{2,1,0:T(8,128)(2,1)} %get-tuple-element.52), channel_id=1, replica_groups=mesh['x'=4,'z'=4,'c'=2,'e'=4] {'x','z','c'}, dimensions={0} | all-to-all | bytes 786432 | tf_op jit(solution)/shard_map/all_to_all | solution.py:676
  31.6 1.8 enter.1
  33.4 3.7 %all-to-all-start.1 = ((bf16[32,32,128]{2,1,0:T(8,128)(2,1)}), bf16[32,32,128]{2,1,0:T(8,128)(2,1)S(1)}, u32[]{:S(2)}, u32[]{:S(2)}) async-start(bf16[32,32,128]{2,1,0:T(8,128)(2,1)} %get-tuple-element.54), calls=%async_computation.1 | async-start | bytes 524288 | tf_op jit(solution)/shard_map/all_to_all | solution.py:683
  37.8 2.2 mix_within.1.within
  40.0 6.0 %all-to-all-done.1 = bf16[32,32,128]{2,1,0:T(8,128)(2,1)S(1)} async-done(((bf16[32,32,128]{2,1,0:T(8,128)(2,1)}), bf16[32,32,128]{2,1,0:T(8,128)(2,1)S(1)}, u32[]{:S(2)}, u32[]{:S(2)}) %all-to-all-start.1) | async-done | bytes 262176 | tf_op jit(solution)/shard_map/all_to_all | solution.py:683
  46.7 6.6 %mix_slots.1 = (f32[24,4096]{1,0:T(8,128)}, bf16[24,4096]{1,0:T(8,128)(2,1)}, bf16[24,4096]{1,0:T(8,128)(2,1)}, bf16[24,4096]{1,0:T(8,128)(2,1)}, f32[128,1024]{1,0:T(8,128)}) custom-call(f32[128,1024]{1,0:T(8,128)} %mix_within.1.within, bf16[128,256]{1,0:T(8,128)(2,1)} %get-tuple-element.48.bc_ref, f32[128,128]{1,0:T(8,128)} %get-tuple-element.49.cum_ref, ...), custom_call_target="tpu_custom_call" | custom-call | flops 805306368 | bytes 8388608 | tf_op jit(solution)/shard_map/mix_slots/pallas_call | solution.py:402
  54.7 2.6 %collective-permute-start.3 = (bf16[24,4096]{1,0:T(8,128)(2,1)}, bf16[24,4096]{1,0:T(8,128)(2,1)S(1)}, u32[]{:S(2)}, u32[]{:S(2)}) collective-permute-start(bf16[24,4096]{1,0:T(8,128)(2,1)} %get-tuple-element.58), channel_id=1, source_target_pairs={{0,2},{1,3},{2,0},{3,1},{4,6},{5,7},{6,4},{7,5},{8,10},{9,11},{10,... | collective-permute-start | bytes 589832 | tf_op jit(solution)/shard_map/ppermute | solution.py:36
  58.3 2.9 %collective-permute-done.2 = bf16[24,4096]{1,0:T(8,128)(2,1)S(1)} collective-permute-done((bf16[24,4096]{1,0:T(8,128)(2,1)}, bf16[24,4096]{1,0:T(8,128)(2,1)S(1)}, u32[]{:S(2)}, u32[]{:S(2)}) %collective-permute-start.2) | collective-permute-done | bytes 196640 | tf_op jit(solution)/shard_map/ppermute | solution.py:36
  61.2 5.3 %collective-permute-done.3 = bf16[24,4096]{1,0:T(8,128)(2,1)S(1)} collective-permute-done((bf16[24,4096]{1,0:T(8,128)(2,1)}, bf16[24,4096]{1,0:T(8,128)(2,1)S(1)}, u32[]{:S(2)}, u32[]{:S(2)}) %collective-permute-start.3) | collective-permute-done | bytes 196640 | tf_op jit(solution)/shard_map/ppermute | solution.py:36
  68.5 1.8 collective-permute-start.6
  71.0 2.0 collective-permute-done.7
  73.0 1.5 collective-permute-done.6
  75.4 2.3 collective-permute-start.8
  78.9 1.5 collective-permute-start.12
  80.4 6.7 %collective-permute-done.14 = bf16[24,2048]{1,0:T(8,128)(2,1)S(1)} collective-permute-done((bf16[24,2048]{1,0:T(8,128)(2,1)S(1)}, bf16[24,2048]{1,0:T(8,128)(2,1)S(1)}, u32[]{:S(2)}, u32[]{:S(2)}) %collective-permute-start.14) | collective-permute-done | bytes 98336 | tf_op jit(solution)/shard_map/ppermute | solution.py:36
  89.7 3.0 %collective-permute-start.15 = (bf16[96,2048]{1,0:T(8,128)(2,1)S(1)}, bf16[96,2048]{1,0:T(8,128)(2,1)S(1)}, u32[]{:S(2)}, u32[]{:S(2)}) collective-permute-start(bf16[96,2048]{1,0:T(8,128)(2,1)S(1)} %pad_maximum_fusion.3.refs_4_), channel_id=1, source_target_pairs={{0,24},{8,0},{16,8},{24,16},{1,25},{9,1},{17,9},{25,17},{2,26},{10... | collective-permute-start | bytes 1179656 | tf_op jit(solution)/shard_map/ppermute | solution.py:36
  92.9 3.5 %collective-permute-start.11 = (bf16[48,2048]{1,0:T(8,128)(2,1)S(1)}, bf16[48,2048]{1,0:T(8,128)(2,1)S(1)}, u32[]{:S(2)}, u32[]{:S(2)}) collective-permute-start(bf16[48,2048]{1,0:T(8,128)(2,1)S(1)} %slice.132), channel_id=1, source_target_pairs={{0,96},{32,0},{64,32},{96,64},{1,97},{33,1},{65,33},{97,65},{2,98}... | collective-permute-start | bytes 589832 | tf_op jit(solution)/shard_map/ppermute | solution.py:36
  96.9 3.1 %collective-permute-start.19 = (f32[1,256]{1,0:T(1,128)S(1)}, f32[1,256]{1,0:T(1,128)S(1)}, u32[]{:S(2)}, u32[]{:S(2)}) collective-permute-start(f32[1,256]{1,0:T(1,128)S(1)} %bitcast.36), channel_id=1, source_target_pairs={{0,4},{4,0},{1,5},{5,1},{2,6},{6,2},{3,7},{7,3},{8,12},{12,8},{9,1... | collective-permute-start | bytes 3080 | tf_op jit(solution)/shard_map/ppermute | solution.py:36
  101.0 2.9 %collective-permute-start.18 = (bf16[48,2048]{1,0:T(8,128)(2,1)S(1)}, bf16[48,2048]{1,0:T(8,128)(2,1)S(1)}, u32[]{:S(2)}, u32[]{:S(2)}) collective-permute-start(bf16[48,2048]{1,0:T(8,128)(2,1)S(1)} %slice.135), channel_id=1, source_target_pairs={{0,24},{8,0},{16,8},{24,16},{1,25},{9,1},{17,9},{25,17},{2,26},{10... | collective-permute-start | bytes 589832 | tf_op jit(solution)/shard_map/ppermute | solution.py:36
  103.9 2.7 %collective-permute-done.17 = bf16[48,2048]{1,0:T(8,128)(2,1)S(1)} collective-permute-done((bf16[48,2048]{1,0:T(8,128)(2,1)S(1)}, bf16[48,2048]{1,0:T(8,128)(2,1)S(1)}, u32[]{:S(2)}, u32[]{:S(2)}) %collective-permute-start.17) | collective-permute-done | bytes 196640 | tf_op jit(solution)/shard_map/ppermute | solution.py:36
  106.7 9.2 %experts.1 = (bf16[384,2048]{1,0:T(8,128)(2,1)S(1)}, bf16[384,2048]{1,0:T(8,128)(2,1)S(1)}) custom-call(bf16[96,2048]{1,0:T(8,128)(2,1)S(1)} %pad_maximum_fusion.1.refs_0_, bf16[96,2048]{1,0:T(8,128)(2,1)S(1)} %collective-permute-done.8.refs_1_, bf16[96,2048]{1,0:T(8,128)(2,1)S(1)} %pad_maximum_fusion.2.refs_2_, ...), custom_call_target="tpu_custom_call" | custom-call | flops 6442450944 | bytes 14680064 | tf_op jit(solution)/shard_map/experts/pallas_call | solution.py:107
  116.1 2.7 %collective-permute-start.22 = (bf16[48,2048]{1,0:T(8,128)(2,1)S(1)}, bf16[48,2048]{1,0:T(8,128)(2,1)S(1)}, u32[]{:S(2)}, u32[]{:S(2)}) collective-permute-start(bf16[48,2048]{1,0:T(8,128)(2,1)S(1)} %get-tuple-element.93), channel_id=1, source_target_pairs={{0,96},{32,0},{64,32},{96,64},{1,97},{33,1},{65,33},{97,65},{2,98}... | collective-permute-start | bytes 589832 | tf_op jit(solution)/shard_map/ppermute | solution.py:36
  119.3 2.6 %collective-permute-start.29 = (bf16[48,2048]{1,0:T(8,128)(2,1)S(1)}, bf16[48,2048]{1,0:T(8,128)(2,1)S(1)}, u32[]{:S(2)}, u32[]{:S(2)}) collective-permute-start(bf16[48,2048]{1,0:T(8,128)(2,1)S(1)} %get-tuple-element.99), channel_id=1, source_target_pairs={{0,24},{8,0},{16,8},{24,16},{1,25},{9,1},{17,9},{25,17},{2,26},{10... | collective-permute-start | bytes 589832 | tf_op jit(solution)/shard_map/ppermute | solution.py:36
  122.1 2.6 %collective-permute-start.23 = (bf16[96,2048]{1,0:T(8,128)(2,1)S(1)}, bf16[96,2048]{1,0:T(8,128)(2,1)S(1)}, u32[]{:S(2)}, u32[]{:S(2)}) collective-permute-start(bf16[96,2048]{1,0:T(8,128)(2,1)S(1)} %pad_maximum_fusion.6), channel_id=1, source_target_pairs={{0,96},{32,0},{64,32},{96,64},{1,97},{33,1},{65,33},{97,65},{2,98}... | collective-permute-start | bytes 1179656 | tf_op jit(solution)/shard_map/ppermute | solution.py:36
  125.3 2.8 %collective-permute-start.30 = (bf16[96,2048]{1,0:T(8,128)(2,1)S(1)}, bf16[96,2048]{1,0:T(8,128)(2,1)S(1)}, u32[]{:S(2)}, u32[]{:S(2)}) collective-permute-start(bf16[96,2048]{1,0:T(8,128)(2,1)S(1)} %pad_maximum_fusion.8), channel_id=1, source_target_pairs={{0,24},{8,0},{16,8},{24,16},{1,25},{9,1},{17,9},{25,17},{2,26},{10... | collective-permute-start | bytes 1179656 | tf_op jit(solution)/shard_map/ppermute | solution.py:36
  128.3 1.6 collective-permute-done.23
  129.9 2.7 %collective-permute-done.21 = bf16[96,2048]{1,0:T(8,128)(2,1)S(1)} collective-permute-done((bf16[96,2048]{1,0:T(8,128)(2,1)S(1)}, bf16[96,2048]{1,0:T(8,128)(2,1)S(1)}, u32[]{:S(2)}, u32[]{:S(2)}) %collective-permute-start.21) | collective-permute-done | bytes 393248 | tf_op jit(solution)/shard_map/ppermute | solution.py:36
  133.3 2.6 %collective-permute-start.26 = (bf16[24,2048]{1,0:T(8,128)(2,1)S(1)}, bf16[24,2048]{1,0:T(8,128)(2,1)S(1)}, u32[]{:S(2)}, u32[]{:S(2)}) collective-permute-start(bf16[24,2048]{1,0:T(8,128)(2,1)S(1)} %get-tuple-element.103), channel_id=1, source_target_pairs={{0,24},{8,0},{16,8},{24,16},{1,25},{9,1},{17,9},{25,17},{2,26},{10... | collective-permute-start | bytes 294920 | tf_op jit(solution)/shard_map/ppermute | solution.py:36
  137.3 2.7 %collective-permute-start.33 = (bf16[24,2048]{1,0:T(8,128)(2,1)S(1)}, bf16[24,2048]{1,0:T(8,128)(2,1)S(1)}, u32[]{:S(2)}, u32[]{:S(2)}) collective-permute-start(bf16[24,2048]{1,0:T(8,128)(2,1)S(1)} %get-tuple-element.106), channel_id=1, source_target_pairs={{0,96},{32,0},{64,32},{96,64},{1,97},{33,1},{65,33},{97,65},{2,98}... | collective-permute-start | bytes 294920 | tf_op jit(solution)/shard_map/ppermute | solution.py:36
  140.1 1.8 collective-permute-done.25
  142.2 2.7 %collective-permute-done.32 = bf16[24,2048]{1,0:T(8,128)(2,1)S(1)} collective-permute-done((bf16[24,2048]{1,0:T(8,128)(2,1)S(1)}, bf16[24,2048]{1,0:T(8,128)(2,1)S(1)}, u32[]{:S(2)}, u32[]{:S(2)}) %collective-permute-start.32) | collective-permute-done | bytes 98336 | tf_op jit(solution)/shard_map/ppermute | solution.py:36
  145.5 3.6 %collective-permute-start.35 = (bf16[24,4096]{1,0:T(8,128)(2,1)S(1)}, bf16[24,4096]{1,0:T(8,128)(2,1)S(1)}, u32[]{:S(2)}, u32[]{:S(2)}) collective-permute-start(bf16[24,4096]{1,0:T(8,128)(2,1)S(1)} %divide_convert_fusion), channel_id=1, source_target_pairs={{0,2},{1,3},{2,0},{3,1},{4,6},{5,7},{6,4},{7,5},{8,10},{9,11},{10,... | collective-permute-start | bytes 589832 | tf_op jit(solution)/shard_map/ppermute | solution.py:36
  149.2 2.3 collective-permute-done.36
  151.5 3.1 %collective-permute-done.35 = bf16[24,4096]{1,0:T(8,128)(2,1)S(1)} collective-permute-done((bf16[24,4096]{1,0:T(8,128)(2,1)S(1)}, bf16[24,4096]{1,0:T(8,128)(2,1)S(1)}, u32[]{:S(2)}, u32[]{:S(2)}) %collective-permute-start.35) | collective-permute-done | bytes 196640 | tf_op jit(solution)/shard_map/ppermute | solution.py:36
  155.5 7.7 %out_gradient.1 = (f32[128,4096]{1,0:T(8,128)}, f32[128,1024]{1,0:T(8,128)}, bf16[1024,128]{1,0:T(8,128)(2,1)}) custom-call(bf16[96,128]{1,0:T(8,128)(2,1)} %pad_maximum_fusion.10.table, bf16[96,4096]{1,0:T(8,128)(2,1)} %pad_maximum_fusion.terms, f32[1,4096]{1,0:T(1,128)} %bitcast.33, bf16[1024,4096]{1,0:T(8,128)(2,1)} %w_out.3, ...), custom_call_target="tpu_custom_call" | custom-call | flops 1073741824 | bytes 8388608 | tf_op jit(solution)/shard_map/out_gradient/pallas_call | solution.py:452
  163.2 25.0 %all_to_all.21.got = bf16[32,32,128]{2,1,0:T(8,128)(2,1)} all-to-all(bf16[32,32,128]{2,1,0:T(8,128)(2,1)} %bitcast.32), channel_id=1, replica_groups=mesh['x'=4,'z'=4,'c'=2,'e'=4] {'x','z','c'}, dimensions={0} | all-to-all | bytes 524288 | tf_op jit(solution)/shard_map/all_to_all | solution.py:720
  188.2 1.7 leave.1
  189.9 3.7 %all-to-all-start.3 = ((bf16[32,32,128]{2,1,0:T(8,128)(2,1)}), bf16[32,32,128]{2,1,0:T(8,128)(2,1)S(1)}, u32[]{:S(2)}, u32[]{:S(2)}) async-start(bf16[32,32,128]{2,1,0:T(8,128)(2,1)} %leave.1), calls=%async_computation.3 | async-start | bytes 524288 | tf_op jit(solution)/shard_map/all_to_all | solution.py:727
  194.3 3.7 %near_gradient.1 = (f32[128,1024]{1,0:T(8,128)}, f32[128,128]{1,0:T(8,128)}, f32[128,128]{1,0:T(8,128)}, f32[128,128]{1,0:T(8,128)}, f32[128,128]{1,0:T(8,128)}) custom-call(f32[128,1024]{1,0:T(8,128)} %get-tuple-element.70.grad_ref, bf16[128,1024]{1,0:T(8,128)(2,1)} %get-tuple-element.47.inner_ref, bf16[128,256]{1,0:T(8,128)(2,1)} %get-tuple-element.48.bc_ref, ...), custom_call_target="tpu_custom_call" | custom-call | flops 268435456 | bytes 2621440 | tf_op jit(solution)/shard_map/near_gradient/pallas_call | solution.py:180
  198.0 4.7 %all-to-all-done.3 = bf16[32,32,128]{2,1,0:T(8,128)(2,1)S(1)} async-done(((bf16[32,32,128]{2,1,0:T(8,128)(2,1)}), bf16[32,32,128]{2,1,0:T(8,128)(2,1)S(1)}, u32[]{:S(2)}, u32[]{:S(2)}) %all-to-all-start.3) | async-done | bytes 262176 | tf_op jit(solution)/shard_map/all_to_all | solution.py:727
  203.5 2.8 %far_gradient.1 = (bf16[128,1024]{1,0:T(8,128)(2,1)}, bf16[128,256]{1,0:T(8,128)(2,1)}, bf16[128,128]{1,0:T(8,128)(2,1)}) custom-call(bf16[1024,128]{1,0:T(8,128)(2,1)} %bitcast.28, bf16[1024,128]{1,0:T(8,128)(2,1)} %bitcast.26, bf16[128,1024]{1,0:T(8,128)(2,1)} %get-tuple-element.47.inner_ref, bf16[128,256]{1,0:T(8,128)(2,1)} %get-tuple-element.48.bc_ref, ...), custom_call_target="tpu_custom_call" | custom-call | flops 134217728 | bytes 2621440 | tf_op jit(solution)/shard_map/far_gradient/pallas_call | solution.py:180
  206.3 7.3 %back_columns.3 = (bf16[128,1024]{1,0:T(8,128)(2,1)}, bf16[128,1024]{1,0:T(8,128)(2,1)}, bf16[128,1024]{1,0:T(8,128)(2,1)}) custom-call(s32[3]{0:T(128)} %pad_add_fusion.which, bf16[128,1024]{1,0:T(8,128)(2,1)} %get-tuple-element.77.g_ref, bf16[128,256]{1,0:T(8,128)(2,1)} %get-tuple-element.78.gbc, bf16[128,128]{1,0:T(8,128)(2,1)} %get-tuple-element.79.gpre, ...), custom_call_target="tpu_custom_call" | custom-call | flops 1006632960 | bytes 7864320 | tf_op jit(solution)/shard_map/back_columns/pallas_call | solution.py:605
  213.6 1.8 collective-permute-start.37
  216.3 1.8 collective-permute-start.39
  218.1 3.7 %back_columns.2 = f32[128,1024]{1,0:T(8,128)} custom-call(s32[1]{0:T(128)} %bitcast.12.which, bf16[128,1024]{1,0:T(8,128)(2,1)} %get-tuple-element.77.g_ref, bf16[128,256]{1,0:T(8,128)(2,1)} %get-tuple-element.78.gbc, bf16[128,128]{1,0:T(8,128)(2,1)} %get-tuple-element.79.gpre, bf16[4096,1024]{1,0:T(8,128)(2,1)} %w_in.5, bf16[4096,256]{1,0:T(8,128)(2,1)} %w_bc.5, ...), custom_call_target="tpu_custom_call" | custom-call | flops 335544320 | bytes 2621440 | tf_op jit(solution)/shard_map/back_columns/pallas_call | solution.py:605
  223.1 6.1 %collective-permute-done.38 = bf16[128,1024]{1,0:T(8,128)(2,1)S(1)} collective-permute-done((bf16[128,1024]{1,0:T(8,128)(2,1)}, bf16[128,1024]{1,0:T(8,128)(2,1)S(1)}, u32[]{:S(2)}, u32[]{:S(2)}) %collective-permute-start.38) | collective-permute-done | bytes 262176 | tf_op jit(solution)/shard_map/ppermute | solution.py:36
  229.2 2.2 subtract_convert_fusion
  (110 shorter events, 26.5 us)
Async XLA Ops:
  0.0 12.7 %collective-permute-start = (bf16[4096,256]{1,0:T(8,128)(2,1)}, bf16[4096,256]{1,0:T(8,128)(2,1)S(1)}, u32[]{:S(2)}, u32[]{:S(2)}) collective-permute-start(bf16[4096,256]{1,0:T(8,128)(2,1)} %bitcast.20), channel_id=1, source_target_pairs={{0,4},{4,0},{1,5},{5,1},{2,6},{6,2},{3,7},{7,3},{8,12},{12,8},{9,1... | collective-permute-start | bytes 6291464 | tf_op jit(solution)/shard_map/ppermute | solution.py:36
  1.4 11.2 %collective-permute-start.1 = (bf16[4096,256]{1,0:T(8,128)(2,1)}, bf16[4096,256]{1,0:T(8,128)(2,1)}, u32[]{:S(2)}, u32[]{:S(2)}) collective-permute-start(bf16[4096,256]{1,0:T(8,128)(2,1)} %bitcast.22), channel_id=1, source_target_pairs={{0,4},{4,0},{1,5},{5,1},{2,6},{6,2},{3,7},{7,3},{8,12},{12,8},{9,1... | collective-permute-start | bytes 6291464 | tf_op jit(solution)/shard_map/ppermute | solution.py:36
  3.8 8.9 %copy-start.6 = (bf16[24,128]{1,0:T(8,128)(2,1)}, bf16[24,128]{1,0:T(8,128)(2,1)S(1)}, u32[]{:S(2)}) copy-start(bf16[24,128]{1,0:T(8,128)(2,1)S(1)} %get-tuple-element.55.own_table) | copy-start | bytes 18436
  12.6 24.5 %copy-start.7 = (f32[8]{0:T(128)S(1)}, f32[8]{0:T(128)}, u32[]{:S(2)}) copy-start(f32[8]{0:T(128)} %param.20) | copy-start | bytes 100
  33.4 12.5 %all-to-all-start.1 = ((bf16[32,32,128]{2,1,0:T(8,128)(2,1)}), bf16[32,32,128]{2,1,0:T(8,128)(2,1)S(1)}, u32[]{:S(2)}, u32[]{:S(2)}) async-start(bf16[32,32,128]{2,1,0:T(8,128)(2,1)} %get-tuple-element.54), calls=%async_computation.1 | async-start | bytes 524288 | tf_op jit(solution)/shard_map/all_to_all | solution.py:683
  53.3 8.0 %collective-permute-start.2 = (bf16[24,4096]{1,0:T(8,128)(2,1)}, bf16[24,4096]{1,0:T(8,128)(2,1)S(1)}, u32[]{:S(2)}, u32[]{:S(2)}) collective-permute-start(bf16[24,4096]{1,0:T(8,128)(2,1)} %get-tuple-element.57), channel_id=1, source_target_pairs={{0,1},{1,2},{2,3},{3,0},{4,5},{5,6},{6,7},{7,4},{8,9},{9,10},{10,1... | collective-permute-start | bytes 589832 | tf_op jit(solution)/shard_map/ppermute | solution.py:36
  54.7 11.9 %collective-permute-start.3 = (bf16[24,4096]{1,0:T(8,128)(2,1)}, bf16[24,4096]{1,0:T(8,128)(2,1)S(1)}, u32[]{:S(2)}, u32[]{:S(2)}) collective-permute-start(bf16[24,4096]{1,0:T(8,128)(2,1)} %get-tuple-element.58), channel_id=1, source_target_pairs={{0,2},{1,3},{2,0},{3,1},{4,6},{5,7},{6,4},{7,5},{8,10},{9,11},{10,... | collective-permute-start | bytes 589832 | tf_op jit(solution)/shard_map/ppermute | solution.py:36
  57.3 9.3 %collective-permute-start.4 = (bf16[24,4096]{1,0:T(8,128)(2,1)}, bf16[24,4096]{1,0:T(8,128)(2,1)S(1)}, u32[]{:S(2)}, u32[]{:S(2)}) collective-permute-start(bf16[24,4096]{1,0:T(8,128)(2,1)} %get-tuple-element.59), channel_id=1, source_target_pairs={{0,3},{1,0},{2,1},{3,2},{4,7},{5,4},{6,5},{7,6},{8,11},{9,8},{10,9... | collective-permute-start | bytes 589832 | tf_op jit(solution)/shard_map/ppermute | solution.py:36
  67.8 28.6 %copy-start.3 = (bf16[1,256,4096]{2,1,0:T(8,128)(2,1)S(1)}, bf16[1,256,4096]{2,1,0:T(8,128)(2,1)}, u32[]{:S(2)}) copy-start(bf16[1,256,4096]{2,1,0:T(8,128)(2,1)} %param.26) | copy-start | bytes 6291460
  67.8 28.6 %copy-start.5 = (f32[4096]{0:T(1024)S(1)}, f32[4096]{0:T(1024)}, u32[]{:S(2)}) copy-start(f32[4096]{0:T(1024)} %param.27) | copy-start | bytes 49156
  67.9 5.1 %collective-permute-start.7 = (bf16[24,2048]{1,0:T(8,128)(2,1)S(1)}, bf16[24,2048]{1,0:T(8,128)(2,1)S(1)}, u32[]{:S(2)}, u32[]{:S(2)}) collective-permute-start(bf16[24,2048]{1,0:T(8,128)(2,1)S(1)} %get-tuple-element.109), channel_id=1, source_target_pairs={{0,8},{8,16},{16,24},{24,0},{1,9},{9,17},{17,25},{25,1},{2,10},{10... | collective-permute-start | bytes 294920 | tf_op jit(solution)/shard_map/ppermute | solution.py:36
  68.5 5.9 %collective-permute-start.6 = (bf16[24,2048]{1,0:T(8,128)(2,1)S(1)}, bf16[24,2048]{1,0:T(8,128)(2,1)S(1)}, u32[]{:S(2)}, u32[]{:S(2)}) collective-permute-start(bf16[24,2048]{1,0:T(8,128)(2,1)S(1)} %get-tuple-element.109), channel_id=1, source_target_pairs={{0,16},{8,24},{16,0},{24,8},{1,17},{9,25},{17,1},{25,9},{2,18},{10... | collective-permute-start | bytes 294920 | tf_op jit(solution)/shard_map/ppermute | solution.py:36
  70.4 4.6 %collective-permute-start.5 = (bf16[24,2048]{1,0:T(8,128)(2,1)S(1)}, bf16[24,2048]{1,0:T(8,128)(2,1)S(1)}, u32[]{:S(2)}, u32[]{:S(2)}) collective-permute-start(bf16[24,2048]{1,0:T(8,128)(2,1)S(1)} %get-tuple-element.109), channel_id=1, source_target_pairs={{0,24},{8,0},{16,8},{24,16},{1,25},{9,1},{17,9},{25,17},{2,26},{10... | collective-permute-start | bytes 294920 | tf_op jit(solution)/shard_map/ppermute | solution.py:36
  75.0 17.8 %collective-permute-start.9 = (bf16[96,2048]{1,0:T(8,128)(2,1)S(1)}, bf16[96,2048]{1,0:T(8,128)(2,1)S(1)}, u32[]{:S(2)}, u32[]{:S(2)}) collective-permute-start(bf16[96,2048]{1,0:T(8,128)(2,1)S(1)} %pad_maximum_fusion.1.refs_0_), channel_id=1, source_target_pairs={{0,32},{32,64},{64,96},{96,0},{1,33},{33,65},{65,97},{97,1},{2,34}... | collective-permute-start | bytes 1179656 | tf_op jit(solution)/shard_map/ppermute | solution.py:36
  75.4 17.4 %collective-permute-start.8 = (bf16[96,2048]{1,0:T(8,128)(2,1)S(1)}, bf16[96,2048]{1,0:T(8,128)(2,1)S(1)}, u32[]{:S(2)}, u32[]{:S(2)}) collective-permute-start(bf16[96,2048]{1,0:T(8,128)(2,1)S(1)} %pad_maximum_fusion.1.refs_0_), channel_id=1, source_target_pairs={{0,96},{32,0},{64,32},{96,64},{1,97},{33,1},{65,33},{97,65},{2,98}... | collective-permute-start | bytes 1179656 | tf_op jit(solution)/shard_map/ppermute | solution.py:36
  77.7 9.4 %collective-permute-start.14 = (bf16[24,2048]{1,0:T(8,128)(2,1)S(1)}, bf16[24,2048]{1,0:T(8,128)(2,1)S(1)}, u32[]{:S(2)}, u32[]{:S(2)}) collective-permute-start(bf16[24,2048]{1,0:T(8,128)(2,1)S(1)} %get-tuple-element.108), channel_id=1, source_target_pairs={{0,32},{32,64},{64,96},{96,0},{1,33},{33,65},{65,97},{97,1},{2,34}... | collective-permute-start | bytes 294920 | tf_op jit(solution)/shard_map/ppermute | solution.py:36
  77.7 10.5 %collective-permute-start.13 = (bf16[24,2048]{1,0:T(8,128)(2,1)S(1)}, bf16[24,2048]{1,0:T(8,128)(2,1)S(1)}, u32[]{:S(2)}, u32[]{:S(2)}) collective-permute-start(bf16[24,2048]{1,0:T(8,128)(2,1)S(1)} %get-tuple-element.108), channel_id=1, source_target_pairs={{0,64},{32,96},{64,0},{96,32},{1,65},{33,97},{65,1},{97,33},{2,66}... | collective-permute-start | bytes 294920 | tf_op jit(solution)/shard_map/ppermute | solution.py:36
  78.9 9.3 %collective-permute-start.12 = (bf16[24,2048]{1,0:T(8,128)(2,1)S(1)}, bf16[24,2048]{1,0:T(8,128)(2,1)S(1)}, u32[]{:S(2)}, u32[]{:S(2)}) collective-permute-start(bf16[24,2048]{1,0:T(8,128)(2,1)S(1)} %get-tuple-element.108), channel_id=1, source_target_pairs={{0,96},{32,0},{64,32},{96,64},{1,97},{33,1},{65,33},{97,65},{2,98}... | collective-permute-start | bytes 294920 | tf_op jit(solution)/shard_map/ppermute | solution.py:36
  88.3 12.6 %collective-permute-start.16 = (bf16[96,2048]{1,0:T(8,128)(2,1)S(1)}, bf16[96,2048]{1,0:T(8,128)(2,1)S(1)}, u32[]{:S(2)}, u32[]{:S(2)}) collective-permute-start(bf16[96,2048]{1,0:T(8,128)(2,1)S(1)} %pad_maximum_fusion.3.refs_4_), channel_id=1, source_target_pairs={{0,8},{8,16},{16,24},{24,0},{1,9},{9,17},{17,25},{25,1},{2,10},{10... | collective-permute-start | bytes 1179656 | tf_op jit(solution)/shard_map/ppermute | solution.py:36
  89.7 11.3 %collective-permute-start.15 = (bf16[96,2048]{1,0:T(8,128)(2,1)S(1)}, bf16[96,2048]{1,0:T(8,128)(2,1)S(1)}, u32[]{:S(2)}, u32[]{:S(2)}) collective-permute-start(bf16[96,2048]{1,0:T(8,128)(2,1)S(1)} %pad_maximum_fusion.3.refs_4_), channel_id=1, source_target_pairs={{0,24},{8,0},{16,8},{24,16},{1,25},{9,1},{17,9},{25,17},{2,26},{10... | collective-permute-start | bytes 1179656 | tf_op jit(solution)/shard_map/ppermute | solution.py:36
  92.7 11.2 %collective-permute-start.10 = (bf16[48,2048]{1,0:T(8,128)(2,1)S(1)}, bf16[48,2048]{1,0:T(8,128)(2,1)S(1)}, u32[]{:S(2)}, u32[]{:S(2)}) collective-permute-start(bf16[48,2048]{1,0:T(8,128)(2,1)S(1)} %slice.131), channel_id=1, source_target_pairs={{0,32},{32,64},{64,96},{96,0},{1,33},{33,65},{65,97},{97,1},{2,34}... | collective-permute-start | bytes 589832 | tf_op jit(solution)/shard_map/ppermute | solution.py:36
  92.9 11.0 %collective-permute-start.11 = (bf16[48,2048]{1,0:T(8,128)(2,1)S(1)}, bf16[48,2048]{1,0:T(8,128)(2,1)S(1)}, u32[]{:S(2)}, u32[]{:S(2)}) collective-permute-start(bf16[48,2048]{1,0:T(8,128)(2,1)S(1)} %slice.132), channel_id=1, source_target_pairs={{0,96},{32,0},{64,32},{96,64},{1,97},{33,1},{65,33},{97,65},{2,98}... | collective-permute-start | bytes 589832 | tf_op jit(solution)/shard_map/ppermute | solution.py:36
  96.4 10.3 %copy-start.1 = (bf16[1,4096,256]{2,1,0:T(8,128)(2,1)S(1)}, bf16[1,4096,256]{2,1,0:T(8,128)(2,1)}, u32[]{:S(2)}) copy-start(bf16[1,4096,256]{2,1,0:T(8,128)(2,1)} %param.25) | copy-start | bytes 6291460
  96.9 9.8 %copy-start = (bf16[1,4096,256]{2,1,0:T(8,128)(2,1)S(1)}, bf16[1,4096,256]{2,1,0:T(8,128)(2,1)}, u32[]{:S(2)}) copy-start(bf16[1,4096,256]{2,1,0:T(8,128)(2,1)} %param.24) | copy-start | bytes 6291460
  96.9 3.9 %collective-permute-start.19 = (f32[1,256]{1,0:T(1,128)S(1)}, f32[1,256]{1,0:T(1,128)S(1)}, u32[]{:S(2)}, u32[]{:S(2)}) collective-permute-start(f32[1,256]{1,0:T(1,128)S(1)} %bitcast.36), channel_id=1, source_target_pairs={{0,4},{4,0},{1,5},{5,1},{2,6},{6,2},{3,7},{7,3},{8,12},{12,8},{9,1... | collective-permute-start | bytes 3080 | tf_op jit(solution)/shard_map/ppermute | solution.py:36
  100.9 5.8 %collective-permute-start.17 = (bf16[48,2048]{1,0:T(8,128)(2,1)S(1)}, bf16[48,2048]{1,0:T(8,128)(2,1)S(1)}, u32[]{:S(2)}, u32[]{:S(2)}) collective-permute-start(bf16[48,2048]{1,0:T(8,128)(2,1)S(1)} %slice.134), channel_id=1, source_target_pairs={{0,8},{8,16},{16,24},{24,0},{1,9},{9,17},{17,25},{25,1},{2,10},{10... | collective-permute-start | bytes 589832 | tf_op jit(solution)/shard_map/ppermute | solution.py:36
  101.0 5.7 %collective-permute-start.18 = (bf16[48,2048]{1,0:T(8,128)(2,1)S(1)}, bf16[48,2048]{1,0:T(8,128)(2,1)S(1)}, u32[]{:S(2)}, u32[]{:S(2)}) collective-permute-start(bf16[48,2048]{1,0:T(8,128)(2,1)S(1)} %slice.135), channel_id=1, source_target_pairs={{0,24},{8,0},{16,8},{24,16},{1,25},{9,1},{17,9},{25,17},{2,26},{10... | collective-permute-start | bytes 589832 | tf_op jit(solution)/shard_map/ppermute | solution.py:36
  116.0 5.9 %collective-permute-start.20 = (bf16[48,2048]{1,0:T(8,128)(2,1)S(1)}, bf16[48,2048]{1,0:T(8,128)(2,1)S(1)}, u32[]{:S(2)}, u32[]{:S(2)}) collective-permute-start(bf16[48,2048]{1,0:T(8,128)(2,1)S(1)} %get-tuple-element.92), channel_id=1, source_target_pairs={{0,32},{32,64},{64,96},{96,0},{1,33},{33,65},{65,97},{97,1},{2,34}... | collective-permute-start | bytes 589832 | tf_op jit(solution)/shard_map/ppermute | solution.py:36
  116.1 5.8 %collective-permute-start.22 = (bf16[48,2048]{1,0:T(8,128)(2,1)S(1)}, bf16[48,2048]{1,0:T(8,128)(2,1)S(1)}, u32[]{:S(2)}, u32[]{:S(2)}) collective-permute-start(bf16[48,2048]{1,0:T(8,128)(2,1)S(1)} %get-tuple-element.93), channel_id=1, source_target_pairs={{0,96},{32,0},{64,32},{96,64},{1,97},{33,1},{65,33},{97,65},{2,98}... | collective-permute-start | bytes 589832 | tf_op jit(solution)/shard_map/ppermute | solution.py:36
  118.8 6.4 %collective-permute-start.27 = (bf16[48,2048]{1,0:T(8,128)(2,1)S(1)}, bf16[48,2048]{1,0:T(8,128)(2,1)S(1)}, u32[]{:S(2)}, u32[]{:S(2)}) collective-permute-start(bf16[48,2048]{1,0:T(8,128)(2,1)S(1)} %get-tuple-element.98), channel_id=1, source_target_pairs={{0,8},{8,16},{16,24},{24,0},{1,9},{9,17},{17,25},{25,1},{2,10},{10... | collective-permute-start | bytes 589832 | tf_op jit(solution)/shard_map/ppermute | solution.py:36
  119.3 5.9 %collective-permute-start.29 = (bf16[48,2048]{1,0:T(8,128)(2,1)S(1)}, bf16[48,2048]{1,0:T(8,128)(2,1)S(1)}, u32[]{:S(2)}, u32[]{:S(2)}) collective-permute-start(bf16[48,2048]{1,0:T(8,128)(2,1)S(1)} %get-tuple-element.99), channel_id=1, source_target_pairs={{0,24},{8,0},{16,8},{24,16},{1,25},{9,1},{17,9},{25,17},{2,26},{10... | collective-permute-start | bytes 589832 | tf_op jit(solution)/shard_map/ppermute | solution.py:36
  122.1 7.8 %collective-permute-start.23 = (bf16[96,2048]{1,0:T(8,128)(2,1)S(1)}, bf16[96,2048]{1,0:T(8,128)(2,1)S(1)}, u32[]{:S(2)}, u32[]{:S(2)}) collective-permute-start(bf16[96,2048]{1,0:T(8,128)(2,1)S(1)} %pad_maximum_fusion.6), channel_id=1, source_target_pairs={{0,96},{32,0},{64,32},{96,64},{1,97},{33,1},{65,33},{97,65},{2,98}... | collective-permute-start | bytes 1179656 | tf_op jit(solution)/shard_map/ppermute | solution.py:36
  124.7 7.9 %collective-permute-start.21 = (bf16[96,2048]{1,0:T(8,128)(2,1)S(1)}, bf16[96,2048]{1,0:T(8,128)(2,1)S(1)}, u32[]{:S(2)}, u32[]{:S(2)}) collective-permute-start(bf16[96,2048]{1,0:T(8,128)(2,1)S(1)} %pad_maximum_fusion.5), channel_id=1, source_target_pairs={{0,32},{32,64},{64,96},{96,0},{1,33},{33,65},{65,97},{97,1},{2,34}... | collective-permute-start | bytes 1179656 | tf_op jit(solution)/shard_map/ppermute | solution.py:36
  125.3 11.7 %collective-permute-start.30 = (bf16[96,2048]{1,0:T(8,128)(2,1)S(1)}, bf16[96,2048]{1,0:T(8,128)(2,1)S(1)}, u32[]{:S(2)}, u32[]{:S(2)}) collective-permute-start(bf16[96,2048]{1,0:T(8,128)(2,1)S(1)} %pad_maximum_fusion.8), channel_id=1, source_target_pairs={{0,24},{8,0},{16,8},{24,16},{1,25},{9,1},{17,9},{25,17},{2,26},{10... | collective-permute-start | bytes 1179656 | tf_op jit(solution)/shard_map/ppermute | solution.py:36
  128.2 8.8 %collective-permute-start.28 = (bf16[96,2048]{1,0:T(8,128)(2,1)S(1)}, bf16[96,2048]{1,0:T(8,128)(2,1)S(1)}, u32[]{:S(2)}, u32[]{:S(2)}) collective-permute-start(bf16[96,2048]{1,0:T(8,128)(2,1)S(1)} %pad_maximum_fusion.7), channel_id=1, source_target_pairs={{0,8},{8,16},{16,24},{24,0},{1,9},{9,17},{17,25},{25,1},{2,10},{10... | collective-permute-start | bytes 1179656 | tf_op jit(solution)/shard_map/ppermute | solution.py:36
  132.8 7.1 %collective-permute-start.24 = (bf16[24,2048]{1,0:T(8,128)(2,1)S(1)}, bf16[24,2048]{1,0:T(8,128)(2,1)S(1)}, u32[]{:S(2)}, u32[]{:S(2)}) collective-permute-start(bf16[24,2048]{1,0:T(8,128)(2,1)S(1)} %get-tuple-element.102), channel_id=1, source_target_pairs={{0,8},{8,16},{16,24},{24,0},{1,9},{9,17},{17,25},{25,1},{2,10},{10... | collective-permute-start | bytes 294920 | tf_op jit(solution)/shard_map/ppermute | solution.py:36
  133.3 6.9 %collective-permute-start.26 = (bf16[24,2048]{1,0:T(8,128)(2,1)S(1)}, bf16[24,2048]{1,0:T(8,128)(2,1)S(1)}, u32[]{:S(2)}, u32[]{:S(2)}) collective-permute-start(bf16[24,2048]{1,0:T(8,128)(2,1)S(1)} %get-tuple-element.103), channel_id=1, source_target_pairs={{0,24},{8,0},{16,8},{24,16},{1,25},{9,1},{17,9},{25,17},{2,26},{10... | collective-permute-start | bytes 294920 | tf_op jit(solution)/shard_map/ppermute | solution.py:36
  135.9 6.0 %collective-permute-start.25 = (bf16[24,2048]{1,0:T(8,128)(2,1)S(1)}, bf16[24,2048]{1,0:T(8,128)(2,1)S(1)}, u32[]{:S(2)}, u32[]{:S(2)}) collective-permute-start(bf16[24,2048]{1,0:T(8,128)(2,1)S(1)} %get-tuple-element.104), channel_id=1, source_target_pairs={{0,16},{8,24},{16,0},{24,8},{1,17},{9,25},{17,1},{25,9},{2,18},{10... | collective-permute-start | bytes 294920 | tf_op jit(solution)/shard_map/ppermute | solution.py:36
  137.2 5.0 %collective-permute-start.31 = (bf16[24,2048]{1,0:T(8,128)(2,1)S(1)}, bf16[24,2048]{1,0:T(8,128)(2,1)S(1)}, u32[]{:S(2)}, u32[]{:S(2)}) collective-permute-start(bf16[24,2048]{1,0:T(8,128)(2,1)S(1)} %get-tuple-element.105), channel_id=1, source_target_pairs={{0,32},{32,64},{64,96},{96,0},{1,33},{33,65},{65,97},{97,1},{2,34}... | collective-permute-start | bytes 294920 | tf_op jit(solution)/shard_map/ppermute | solution.py:36
  137.3 5.0 %collective-permute-start.33 = (bf16[24,2048]{1,0:T(8,128)(2,1)S(1)}, bf16[24,2048]{1,0:T(8,128)(2,1)S(1)}, u32[]{:S(2)}, u32[]{:S(2)}) collective-permute-start(bf16[24,2048]{1,0:T(8,128)(2,1)S(1)} %get-tuple-element.106), channel_id=1, source_target_pairs={{0,96},{32,0},{64,32},{96,64},{1,97},{33,1},{65,33},{97,65},{2,98}... | collective-permute-start | bytes 294920 | tf_op jit(solution)/shard_map/ppermute | solution.py:36
  139.9 5.0 %collective-permute-start.32 = (bf16[24,2048]{1,0:T(8,128)(2,1)S(1)}, bf16[24,2048]{1,0:T(8,128)(2,1)S(1)}, u32[]{:S(2)}, u32[]{:S(2)}) collective-permute-start(bf16[24,2048]{1,0:T(8,128)(2,1)S(1)} %get-tuple-element.107), channel_id=1, source_target_pairs={{0,64},{32,96},{64,0},{96,32},{1,65},{33,97},{65,1},{97,33},{2,66}... | collective-permute-start | bytes 294920 | tf_op jit(solution)/shard_map/ppermute | solution.py:36
  145.4 6.1 %collective-permute-start.36 = (bf16[24,4096]{1,0:T(8,128)(2,1)S(1)}, bf16[24,4096]{1,0:T(8,128)(2,1)S(1)}, u32[]{:S(2)}, u32[]{:S(2)}) collective-permute-start(bf16[24,4096]{1,0:T(8,128)(2,1)S(1)} %divide_convert_fusion), channel_id=1, source_target_pairs={{0,1},{1,2},{2,3},{3,0},{4,5},{5,6},{6,7},{7,4},{8,9},{9,10},{10,1... | collective-permute-start | bytes 589832 | tf_op jit(solution)/shard_map/ppermute | solution.py:36
  145.5 9.1 %collective-permute-start.35 = (bf16[24,4096]{1,0:T(8,128)(2,1)S(1)}, bf16[24,4096]{1,0:T(8,128)(2,1)S(1)}, u32[]{:S(2)}, u32[]{:S(2)}) collective-permute-start(bf16[24,4096]{1,0:T(8,128)(2,1)S(1)} %divide_convert_fusion), channel_id=1, source_target_pairs={{0,2},{1,3},{2,0},{3,1},{4,6},{5,7},{6,4},{7,5},{8,10},{9,11},{10,... | collective-permute-start | bytes 589832 | tf_op jit(solution)/shard_map/ppermute | solution.py:36
  149.1 5.5 %collective-permute-start.34 = (bf16[24,4096]{1,0:T(8,128)(2,1)S(1)}, bf16[24,4096]{1,0:T(8,128)(2,1)S(1)}, u32[]{:S(2)}, u32[]{:S(2)}) collective-permute-start(bf16[24,4096]{1,0:T(8,128)(2,1)S(1)} %divide_convert_fusion), channel_id=1, source_target_pairs={{0,3},{1,0},{2,1},{3,2},{4,7},{5,4},{6,5},{7,6},{8,11},{9,8},{10,9... | collective-permute-start | bytes 589832 | tf_op jit(solution)/shard_map/ppermute | solution.py:36
  189.9 12.8 %all-to-all-start.3 = ((bf16[32,32,128]{2,1,0:T(8,128)(2,1)}), bf16[32,32,128]{2,1,0:T(8,128)(2,1)S(1)}, u32[]{:S(2)}, u32[]{:S(2)}) async-start(bf16[32,32,128]{2,1,0:T(8,128)(2,1)} %leave.1), calls=%async_computation.3 | async-start | bytes 524288 | tf_op jit(solution)/shard_map/all_to_all | solution.py:727
  213.6 9.5 %collective-permute-start.37 = (bf16[128,1024]{1,0:T(8,128)(2,1)}, bf16[128,1024]{1,0:T(8,128)(2,1)S(1)}, u32[]{:S(2)}, u32[]{:S(2)}) collective-permute-start(bf16[128,1024]{1,0:T(8,128)(2,1)} %get-tuple-element.80), channel_id=1, source_target_pairs={{0,2},{1,3},{2,0},{3,1},{4,6},{5,7},{6,4},{7,5},{8,10},{9,11},{10,... | collective-permute-start | bytes 786440 | tf_op jit(solution)/shard_map/ppermute | solution.py:36
  215.4 13.8 %collective-permute-start.38 = (bf16[128,1024]{1,0:T(8,128)(2,1)}, bf16[128,1024]{1,0:T(8,128)(2,1)S(1)}, u32[]{:S(2)}, u32[]{:S(2)}) collective-permute-start(bf16[128,1024]{1,0:T(8,128)(2,1)} %get-tuple-element.81), channel_id=1, source_target_pairs={{0,1},{1,2},{2,3},{3,0},{4,5},{5,6},{6,7},{7,4},{8,9},{9,10},{10,1... | collective-permute-start | bytes 786440 | tf_op jit(solution)/shard_map/ppermute | solution.py:36
  216.3 12.9 %collective-permute-start.39 = (bf16[128,1024]{1,0:T(8,128)(2,1)}, bf16[128,1024]{1,0:T(8,128)(2,1)S(1)}, u32[]{:S(2)}, u32[]{:S(2)}) collective-permute-start(bf16[128,1024]{1,0:T(8,128)(2,1)} %get-tuple-element.82), channel_id=1, source_target_pairs={{0,3},{1,0},{2,1},{3,2},{4,7},{5,4},{6,5},{7,6},{8,11},{9,8},{10,9... | collective-permute-start | bytes 786440 | tf_op jit(solution)/shard_map/ppermute | solution.py:36
  (2 other events, 1.4 us)

commit v6 on v5

--- a/solution.py
+++ b/solution.py
@@ -116,16 +116,19 @@
     )(*args)
 
 
-def gather_around(value, axis):
-    count = lax.axis_size(axis)
+def gather_around(near, far):
+    count = lax.axis_size("x")
     if count != 4:
-        return [value] + [shift(value, axis, count - k) for k in range(1, count)]
-    left, right = shift(value, axis, 1), shift(value, axis, 3)
-    cut = value.shape[0] // 2
-    across = jnp.concatenate(
-        [shift(left[:cut], axis, 1), shift(right[cut:], axis, 3)], axis=0
-    )
-    return [value, right, across, left]
+        return gather_direct(near, "x"), gather_direct(far, "z")
+    cut = near.shape[0] // 2
+    sides = (shift(near, "x", 1), shift(near, "x", 3), shift(far, "z", 1), shift(far, "z", 3))
+    near_l, near_r, far_l, far_r = lax.optimization_barrier(sides)
+    near_a = [shift(near_l[:cut], "x", 1), shift(near_r[cut:], "x", 3)]
+    far_a = [shift(far_l[:cut], "z", 1), shift(far_r[cut:], "z", 3)]
+    return (
+        [near, near_r, jnp.concatenate(near_a, axis=0), near_l],
+        [far, far_r, jnp.concatenate(far_a, axis=0), far_l],
+    )
 
 
 def gather_direct(value, axis):
@@ -140,20 +143,32 @@
     return total
 
 
-def scatter_around(pieces, axis):
-    if len(pieces) != 4:
-        return scatter_direct(pieces, axis)
-    own, right, across, left = pieces
-    cut = across.shape[0] // 2
-    top = shift(across[:cut], axis, 1)
-    bottom = shift(across[cut:], axis, 3)
-    right = jnp.concatenate(
-        [(right[:cut].astype(F32) + top.astype(F32)).astype(BF), right[cut:]], axis=0
-    )
-    left = jnp.concatenate(
-        [left[:cut], (left[cut:].astype(F32) + bottom.astype(F32)).astype(BF)], axis=0
-    )
-    return own.astype(F32) + shift(right, axis, 1).astype(F32) + shift(left, axis, 3).astype(F32)
+def scatter_around(near, far):
+    if len(near) != 4:
+        return scatter_direct(near, "x"), scatter_direct(far, "z")
+    cut = near[2].shape[0] // 2
+    crossed = (
+        shift(near[2][:cut], "x", 1), shift(near[2][cut:], "x", 3),
+        shift(far[2][:cut], "z", 1), shift(far[2][cut:], "z", 3),
+    )
+    crossed = lax.optimization_barrier(crossed)
+
+    def added(pieces, top, bottom):
+        _, right, _, left = pieces
+        right = jnp.concatenate(
+            [(right[:cut].astype(F32) + top.astype(F32)).astype(BF), right[cut:]], axis=0
+        )
+        left = jnp.concatenate(
+            [left[:cut], (left[cut:].astype(F32) + bottom.astype(F32)).astype(BF)], axis=0
+        )
+        return right, left
+
+    near_r, near_l = added(near, crossed[0], crossed[1])
+    far_r, far_l = added(far, crossed[2], crossed[3])
+    near_r, near_l, far_r, far_l = lax.optimization_barrier((near_r, near_l, far_r, far_l))
+    sums = (shift(near_r, "x", 1), shift(near_l, "x", 3), shift(far_r, "z", 1), shift(far_l, "z", 3))
+    sums = [v.astype(F32) for v in lax.optimization_barrier(sums)]
+    return near[0].astype(F32) + sums[0] + sums[1], far[0].astype(F32) + sums[2] + sums[3]
 
 
 def split_rows(value, count):
@@ -694,13 +709,14 @@
 
     side = lax.axis_size("x")
     cut = width // 2
+    routed, head_vec = lax.optimization_barrier((routed, head_vec))
     near_own = jnp.concatenate(gather_direct(routed[:, :cut], "z"), axis=0)
     far_own = jnp.concatenate(gather_direct(routed[:, cut:], "x"), axis=0)
-    near_rows = gather_around(near_own, "x")
-    far_rows = gather_around(far_own, "z")
+    near_own, far_own = lax.optimization_barrier((near_own, far_own))
+    near_rows, far_rows = gather_around(near_own, far_own)
     out_near, out_far = expert_rows(near_rows, far_rows, wg0, wg1, wu0, wu1, head_vec)
-    near_sum = scatter_around(split_rows(out_near, side), "x").astype(BF)
-    far_sum = scatter_around(split_rows(out_far, side), "z").astype(BF)
+    near_sum, far_sum = scatter_around(split_rows(out_near, side), split_rows(out_far, side))
+    near_sum, far_sum = near_sum.astype(BF), far_sum.astype(BF)
     slot_grad = jnp.concatenate(
         [
             scatter_direct(split_rows(near_sum, side), "z"),

time: 232 us -> 231 us (level)
  starting transfers between devices: 63.3 us -> 54 us
  blocking collectives: 43.9 us -> 48.9 us
  waiting for transfers between devices: 56.5 us -> 61 us
    ppermute x40, starting transfers between devices: 56 us -> 46.7 us  [shift(): lax.ppermute(value, axis, [(i, (i + by) % count) for i in range(count)])]
    all_to_all x1, blocking collectives: 25 us -> 30 us  [shards(): lax.all_to_all(local_grad.reshape(n_seq, slice_rows, nstate), SEQ, 0, 0,...]
    ppermute x40, waiting for transfers between devices: 45.9 us -> 50.3 us  [shift(): lax.ppermute(value, axis, [(i, (i + by) % count) for i in range(count)])]
  transfers between devices with their start and end apart: 42 -> 42, of which waited for: 21 -> 28; matrix products, arithmetic and copies ran while one was open for 2% -> 2% of each run, Pallas kernels for 8% -> 8%
where the time goes in v6:
time: 231 us
  waiting for transfers between devices  61 us (26%)
  Pallas kernels  54.9 us (24%)
  starting transfers between devices  54 us (23%)
  blocking collectives  48.9 us (21%)
  other arithmetic  7.64 us (3%)
  local copies, waits for them, and re-layouts  3.61 us (2%)
    ppermute x40, waiting for transfers between devices, shift(): lax.ppermute(value, axis, [(i, (i + by) % count) for i in range(count)])  50.3 us
    ppermute x40, starting transfers between devices, shift(): lax.ppermute(value, axis, [(i, (i + by) % count) for i in range(count)])  46.7 us
    all_to_all x1, blocking collectives, shards(): lax.all_to_all(local_grad.reshape(n_seq, slice_rows, nstate), SEQ, 0, 0,...  30 us
    all_to_all x1, blocking collectives, shards(): got = lax.all_to_all(payload, SEQ, 0, 0, tiled=True)  18.9 us
    pallas_call x5, Pallas kernels, single(): pl.pallas_call(kernel, grid=(1,), out_shape=out_shape, in_specs=whole(arg...  12.3 us
    pallas_call x2, Pallas kernels, back_columns(): pl.pallas_call(functools.partial(back_kernel, heads, per), grid_spec=pltp...  11 us
    pallas_call x1, Pallas kernels, expert_rows(): pl.pallas_call(functools.partial(expert_kernel, side), out_shape=(out, ou...  9.18 us
    pallas_call x1, Pallas kernels, project(): pl.pallas_call(functools.partial(proj_kernel, heads, slice_rows), grid=(w...  8.04 us
  transfers between devices with their start and end apart: 42, of which 28 were waited for; matrix products, arithmetic and copies ran while one was open for 2% of the time, Pallas kernels for 8%

profile of v6, /device:TPU:1, one launch (start us, length us, event | category | flops | bytes accessed | tf_op | source)
XLA Modules:
  0.0 230.5 jit_solution(11052202349644235349)
XLA Ops:
  0.0 1.4 collective-permute-start
  4.5 8.0 %project.1 = (bf16[128,1024]{1,0:T(8,128)(2,1)}, bf16[128,256]{1,0:T(8,128)(2,1)}, f32[128,128]{1,0:T(8,128)}, f32[128,128]{1,0:T(8,128)}, f32[128,128]{1,0:T(8,...) custom-call(bf16[128,4096]{1,0:T(8,128)(2,1)} %cand.3, bf16[4096,1024]{1,0:T(8,128)(2,1)} %w_in.5, ...), custom_call_target="tpu_custom_call" | custom-call | flops 1342177280 | bytes 12582912 | tf_op jit(solution)/shard_map/project/pallas_call | solution.py:277
  12.6 18.9 %all_to_all.20.got = bf16[32,48,128]{2,1,0:T(8,128)(2,1)} all-to-all(bf16[32,48,128]{2,1,0:T(8,128)(2,1)} %get-tuple-element.72), channel_id=1, replica_groups=mesh['x'=4,'z'=4,'c'=2,'e'=4] {'x','z','c'}, dimensions={0} | all-to-all | bytes 786432 | tf_op jit(solution)/shard_map/all_to_all | solution.py:691
  31.6 1.8 enter.1
  33.4 3.7 %all-to-all-start.1 = ((bf16[32,32,128]{2,1,0:T(8,128)(2,1)}), bf16[32,32,128]{2,1,0:T(8,128)(2,1)S(1)}, u32[]{:S(2)}, u32[]{:S(2)}) async-start(bf16[32,32,128]{2,1,0:T(8,128)(2,1)} %get-tuple-element.74), calls=%async_computation.1 | async-start | bytes 524288 | tf_op jit(solution)/shard_map/all_to_all | solution.py:698
  37.7 2.2 mix_within.1.within
  39.9 6.0 %all-to-all-done.1 = bf16[32,32,128]{2,1,0:T(8,128)(2,1)S(1)} async-done(((bf16[32,32,128]{2,1,0:T(8,128)(2,1)}), bf16[32,32,128]{2,1,0:T(8,128)(2,1)S(1)}, u32[]{:S(2)}, u32[]{:S(2)}) %all-to-all-start.1) | async-done | bytes 262176 | tf_op jit(solution)/shard_map/all_to_all | solution.py:698
  46.6 6.7 %mix_slots.1 = (f32[24,4096]{1,0:T(8,128)}, bf16[24,4096]{1,0:T(8,128)(2,1)}, bf16[24,4096]{1,0:T(8,128)(2,1)}, bf16[24,4096]{1,0:T(8,128)(2,1)}, f32[128,1024]{1,0:T(8,128)}) custom-call(f32[128,1024]{1,0:T(8,128)} %mix_within.1.within, bf16[128,256]{1,0:T(8,128)(2,1)} %get-tuple-element.68.bc_ref, f32[128,128]{1,0:T(8,128)} %get-tuple-element.69.cum_ref, ...), custom_call_target="tpu_custom_call" | custom-call | flops 805306368 | bytes 8388608 | tf_op jit(solution)/shard_map/mix_slots/pallas_call | solution.py:417
  53.4 1.4 collective-permute-start.2
  54.7 2.6 %collective-permute-start.3 = (bf16[24,4096]{1,0:T(8,128)(2,1)}, bf16[24,4096]{1,0:T(8,128)(2,1)S(1)}, u32[]{:S(2)}, u32[]{:S(2)}) collective-permute-start(bf16[24,4096]{1,0:T(8,128)(2,1)} %get-tuple-element.78), channel_id=1, source_target_pairs={{0,2},{1,3},{2,0},{3,1},{4,6},{5,7},{6,4},{7,5},{8,10},{9,11},{10,... | collective-permute-start | bytes 589832 | tf_op jit(solution)/shard_map/ppermute | solution.py:36
  61.3 5.3 %collective-permute-done.3 = bf16[24,4096]{1,0:T(8,128)(2,1)S(1)} collective-permute-done((bf16[24,4096]{1,0:T(8,128)(2,1)}, bf16[24,4096]{1,0:T(8,128)(2,1)S(1)}, u32[]{:S(2)}, u32[]{:S(2)}) %collective-permute-start.3) | collective-permute-done | bytes 196640 | tf_op jit(solution)/shard_map/ppermute | solution.py:36
  67.3 1.7 collective-permute-start.10
  70.7 1.6 collective-permute-start.7
  78.5 2.0 collective-permute-start.15
  80.4 3.8 %collective-permute-done.13.refs_1_ = bf16[96,2048]{1,0:T(8,128)(2,1)S(1)} collective-permute-done((bf16[96,2048]{1,0:T(8,128)(2,1)S(1)}, bf16[96,2048]{1,0:T(8,128)(2,1)S(1)}, u32[]{:S(2)}, u32[]{:S(2)}) %collective-permute-start.13) | collective-permute-done | bytes 393248 | tf_op jit(solution)/shard_map/ppermute | solution.py:36
  84.3 1.7 collective-permute-done.12.refs_3_
  86.0 2.6 %collective-permute-done.14.refs_7_ = bf16[96,2048]{1,0:T(8,128)(2,1)S(1)} collective-permute-done((bf16[96,2048]{1,0:T(8,128)(2,1)S(1)}, bf16[96,2048]{1,0:T(8,128)(2,1)S(1)}, u32[]{:S(2)}, u32[]{:S(2)}) %collective-permute-start.14) | collective-permute-done | bytes 393248 | tf_op jit(solution)/shard_map/ppermute | solution.py:36
  88.7 2.7 %collective-permute-start.19 = (bf16[48,2048]{1,0:T(8,128)(2,1)S(1)}, bf16[48,2048]{1,0:T(8,128)(2,1)S(1)}, u32[]{:S(2)}, u32[]{:S(2)}) collective-permute-start(bf16[48,2048]{1,0:T(8,128)(2,1)S(1)} %slice.107), channel_id=1, source_target_pairs={{0,24},{8,0},{16,8},{24,16},{1,25},{9,1},{17,9},{25,17},{2,26},{10... | collective-permute-start | bytes 589832 | tf_op jit(solution)/shard_map/ppermute | solution.py:36
  91.5 2.6 %collective-permute-start.17 = (bf16[48,2048]{1,0:T(8,128)(2,1)S(1)}, bf16[48,2048]{1,0:T(8,128)(2,1)S(1)}, u32[]{:S(2)}, u32[]{:S(2)}) collective-permute-start(bf16[48,2048]{1,0:T(8,128)(2,1)S(1)} %slice.105), channel_id=1, source_target_pairs={{0,96},{32,0},{64,32},{96,64},{1,97},{33,1},{65,33},{97,65},{2,98}... | collective-permute-start | bytes 589832 | tf_op jit(solution)/shard_map/ppermute | solution.py:36
  95.5 1.7 collective-permute-done.16
  97.3 9.2 %experts.1 = (bf16[384,2048]{1,0:T(8,128)(2,1)S(1)}, bf16[384,2048]{1,0:T(8,128)(2,1)S(1)}) custom-call(bf16[96,2048]{1,0:T(8,128)(2,1)S(1)} %pad_maximum_fusion.1.refs_0_, bf16[96,2048]{1,0:T(8,128)(2,1)S(1)} %collective-permute-done.13.refs_1_, bf16[96,2048]{1,0:T(8,128)(2,1)S(1)} %pad_maximum_fusion.3.refs_2_, ...), custom_call_target="tpu_custom_call" | custom-call | flops 6442450944 | bytes 14680064 | tf_op jit(solution)/shard_map/experts/pallas_call | solution.py:107
  106.5 2.7 %collective-permute-start.21 = (bf16[48,2048]{1,0:T(8,128)(2,1)S(1)}, bf16[48,2048]{1,0:T(8,128)(2,1)S(1)}, u32[]{:S(2)}, u32[]{:S(2)}) collective-permute-start(bf16[48,2048]{1,0:T(8,128)(2,1)S(1)} %get-tuple-element.138), channel_id=1, source_target_pairs={{0,96},{32,0},{64,32},{96,64},{1,97},{33,1},{65,33},{97,65},{2,98}... | collective-permute-start | bytes 589832 | tf_op jit(solution)/shard_map/ppermute | solution.py:36
  109.4 1.5 collective-permute-start.22
  111.9 3.1 %collective-permute-done.20 = bf16[48,2048]{1,0:T(8,128)(2,1)S(1)} collective-permute-done((bf16[48,2048]{1,0:T(8,128)(2,1)S(1)}, bf16[48,2048]{1,0:T(8,128)(2,1)S(1)}, u32[]{:S(2)}, u32[]{:S(2)}) %collective-permute-start.20) | collective-permute-done | bytes 196640 | tf_op jit(solution)/shard_map/ppermute | solution.py:36
  115.7 2.7 %collective-permute-start.25 = (bf16[96,2048]{1,0:T(8,128)(2,1)S(1)}, bf16[96,2048]{1,0:T(8,128)(2,1)S(1)}, u32[]{:S(2)}, u32[]{:S(2)}) collective-permute-start(bf16[96,2048]{1,0:T(8,128)(2,1)S(1)} %pad_maximum_fusion.6), channel_id=1, source_target_pairs={{0,96},{32,0},{64,32},{96,64},{1,97},{33,1},{65,33},{97,65},{2,98}... | collective-permute-start | bytes 1179656 | tf_op jit(solution)/shard_map/ppermute | solution.py:36
  118.6 2.5 %collective-permute-start.27 = (bf16[96,2048]{1,0:T(8,128)(2,1)S(1)}, bf16[96,2048]{1,0:T(8,128)(2,1)S(1)}, u32[]{:S(2)}, u32[]{:S(2)}) collective-permute-start(bf16[96,2048]{1,0:T(8,128)(2,1)S(1)} %pad_maximum_fusion.8), channel_id=1, source_target_pairs={{0,24},{8,0},{16,8},{24,16},{1,25},{9,1},{17,9},{25,17},{2,26},{10... | collective-permute-start | bytes 1179656 | tf_op jit(solution)/shard_map/ppermute | solution.py:36
  121.1 4.1 %collective-permute-done.24 = bf16[96,2048]{1,0:T(8,128)(2,1)S(1)} collective-permute-done((bf16[96,2048]{1,0:T(8,128)(2,1)S(1)}, bf16[96,2048]{1,0:T(8,128)(2,1)S(1)}, u32[]{:S(2)}, u32[]{:S(2)}) %collective-permute-start.24) | collective-permute-done | bytes 393248 | tf_op jit(solution)/shard_map/ppermute | solution.py:36
  125.2 3.1 %collective-permute-done.26 = bf16[96,2048]{1,0:T(8,128)(2,1)S(1)} collective-permute-done((bf16[96,2048]{1,0:T(8,128)(2,1)S(1)}, bf16[96,2048]{1,0:T(8,128)(2,1)S(1)}, u32[]{:S(2)}, u32[]{:S(2)}) %collective-permute-start.26) | collective-permute-done | bytes 393248 | tf_op jit(solution)/shard_map/ppermute | solution.py:36
  128.6 2.7 %collective-permute-start.30 = (bf16[24,2048]{1,0:T(8,128)(2,1)S(1)}, bf16[24,2048]{1,0:T(8,128)(2,1)S(1)}, u32[]{:S(2)}, u32[]{:S(2)}) collective-permute-start(bf16[24,2048]{1,0:T(8,128)(2,1)S(1)} %get-tuple-element.143), channel_id=1, source_target_pairs={{0,24},{8,0},{16,8},{24,16},{1,25},{9,1},{17,9},{25,17},{2,26},{10... | collective-permute-start | bytes 294920 | tf_op jit(solution)/shard_map/ppermute | solution.py:36
  131.6 2.7 %collective-permute-start.33 = (bf16[24,2048]{1,0:T(8,128)(2,1)S(1)}, bf16[24,2048]{1,0:T(8,128)(2,1)S(1)}, u32[]{:S(2)}, u32[]{:S(2)}) collective-permute-start(bf16[24,2048]{1,0:T(8,128)(2,1)S(1)} %get-tuple-element.146), channel_id=1, source_target_pairs={{0,96},{32,0},{64,32},{96,64},{1,97},{33,1},{65,33},{97,65},{2,98}... | collective-permute-start | bytes 294920 | tf_op jit(solution)/shard_map/ppermute | solution.py:36
  134.4 3.0 %collective-permute-done.29 = bf16[24,2048]{1,0:T(8,128)(2,1)S(1)} collective-permute-done((bf16[24,2048]{1,0:T(8,128)(2,1)S(1)}, bf16[24,2048]{1,0:T(8,128)(2,1)S(1)}, u32[]{:S(2)}, u32[]{:S(2)}) %collective-permute-start.29) | collective-permute-done | bytes 98336 | tf_op jit(solution)/shard_map/ppermute | solution.py:36
  137.8 1.7 collective-permute-done.32
  140.4 2.7 %collective-permute-start.35 = (bf16[24,4096]{1,0:T(8,128)(2,1)S(1)}, bf16[24,4096]{1,0:T(8,128)(2,1)S(1)}, u32[]{:S(2)}, u32[]{:S(2)}) collective-permute-start(bf16[24,4096]{1,0:T(8,128)(2,1)S(1)} %divide_convert_fusion), channel_id=1, source_target_pairs={{0,2},{1,3},{2,0},{3,1},{4,6},{5,7},{6,4},{7,5},{8,10},{9,11},{10,... | collective-permute-start | bytes 589832 | tf_op jit(solution)/shard_map/ppermute | solution.py:36
  144.1 2.0 collective-permute-done.36
  146.1 2.1 collective-permute-done.35
  149.7 7.6 %out_gradient.1 = (f32[128,4096]{1,0:T(8,128)}, f32[128,1024]{1,0:T(8,128)}, bf16[1024,128]{1,0:T(8,128)(2,1)}) custom-call(bf16[96,128]{1,0:T(8,128)(2,1)} %pad_maximum_fusion.10.table, bf16[96,4096]{1,0:T(8,128)(2,1)} %pad_maximum_fusion.terms, f32[1,4096]{1,0:T(1,128)} %bitcast.33, bf16[1024,4096]{1,0:T(8,128)(2,1)} %w_out.3, ...), custom_call_target="tpu_custom_call" | custom-call | flops 1073741824 | bytes 8388608 | tf_op jit(solution)/shard_map/out_gradient/pallas_call | solution.py:467
  157.4 30.0 %all_to_all.21.got = bf16[32,32,128]{2,1,0:T(8,128)(2,1)} all-to-all(bf16[32,32,128]{2,1,0:T(8,128)(2,1)} %bitcast.32), channel_id=1, replica_groups=mesh['x'=4,'z'=4,'c'=2,'e'=4] {'x','z','c'}, dimensions={0} | all-to-all | bytes 524288 | tf_op jit(solution)/shard_map/all_to_all | solution.py:736
  187.3 1.7 leave.1
  189.1 3.7 %all-to-all-start.3 = ((bf16[32,32,128]{2,1,0:T(8,128)(2,1)}), bf16[32,32,128]{2,1,0:T(8,128)(2,1)S(1)}, u32[]{:S(2)}, u32[]{:S(2)}) async-start(bf16[32,32,128]{2,1,0:T(8,128)(2,1)} %leave.1), calls=%async_computation.3 | async-start | bytes 524288 | tf_op jit(solution)/shard_map/all_to_all | solution.py:743
  193.4 3.7 %near_gradient.1 = (f32[128,1024]{1,0:T(8,128)}, f32[128,128]{1,0:T(8,128)}, f32[128,128]{1,0:T(8,128)}, f32[128,128]{1,0:T(8,128)}, f32[128,128]{1,0:T(8,128)}) custom-call(f32[128,1024]{1,0:T(8,128)} %get-tuple-element.110.grad_ref, bf16[128,1024]{1,0:T(8,128)(2,1)} %get-tuple-element.67.inner_ref, bf16[128,256]{1,0:T(8,128)(2,1)} %get-tuple-element.68.bc_ref, ...), custom_call_target="tpu_custom_call" | custom-call | flops 268435456 | bytes 2621440 | tf_op jit(solution)/shard_map/near_gradient/pallas_call | solution.py:195
  197.1 4.8 %all-to-all-done.3 = bf16[32,32,128]{2,1,0:T(8,128)(2,1)S(1)} async-done(((bf16[32,32,128]{2,1,0:T(8,128)(2,1)}), bf16[32,32,128]{2,1,0:T(8,128)(2,1)S(1)}, u32[]{:S(2)}, u32[]{:S(2)}) %all-to-all-start.3) | async-done | bytes 262176 | tf_op jit(solution)/shard_map/all_to_all | solution.py:743
  202.6 2.8 %far_gradient.1 = (bf16[128,1024]{1,0:T(8,128)(2,1)}, bf16[128,256]{1,0:T(8,128)(2,1)}, bf16[128,128]{1,0:T(8,128)(2,1)}) custom-call(bf16[1024,128]{1,0:T(8,128)(2,1)} %bitcast.28, bf16[1024,128]{1,0:T(8,128)(2,1)} %bitcast.26, bf16[128,1024]{1,0:T(8,128)(2,1)} %get-tuple-element.67.inner_ref, bf16[128,256]{1,0:T(8,128)(2,1)} %get-tuple-element.68.bc_ref, ...), custom_call_target="tpu_custom_call" | custom-call | flops 134217728 | bytes 2621440 | tf_op jit(solution)/shard_map/far_gradient/pallas_call | solution.py:195
  205.4 7.4 %back_columns.3 = (bf16[128,1024]{1,0:T(8,128)(2,1)}, bf16[128,1024]{1,0:T(8,128)(2,1)}, bf16[128,1024]{1,0:T(8,128)(2,1)}) custom-call(s32[3]{0:T(128)} %pad_add_fusion.which, bf16[128,1024]{1,0:T(8,128)(2,1)} %get-tuple-element.117.g_ref, bf16[128,256]{1,0:T(8,128)(2,1)} %get-tuple-element.118.gbc, bf16[128,128]{1,0:T(8,128)(2,1)} %get-tuple-element.119.gpre, ...), custom_call_target="tpu_custom_call" | custom-call | flops 1006632960 | bytes 7864320 | tf_op jit(solution)/shard_map/back_columns/pallas_call | solution.py:620
  212.8 1.9 collective-permute-start.37
  215.7 1.7 collective-permute-start.39
  217.4 3.7 %back_columns.2 = f32[128,1024]{1,0:T(8,128)} custom-call(s32[1]{0:T(128)} %bitcast.12.which, bf16[128,1024]{1,0:T(8,128)(2,1)} %get-tuple-element.117.g_ref, bf16[128,256]{1,0:T(8,128)(2,1)} %get-tuple-element.118.gbc, bf16[128,128]{1,0:T(8,128)(2,1)} %get-tuple-element.119.gpre, bf16[4096,1024]{1,0:T(8,128)(2,1)} %w_in.5, bf16[4096,256]{1,0:T(8,128)(2,1)} %w_bc.5, ...), custom_call_target="tpu_custom_call" | custom-call | flops 335544320 | bytes 2621440 | tf_op jit(solution)/shard_map/back_columns/pallas_call | solution.py:620
  222.3 6.1 %collective-permute-done.38 = bf16[128,1024]{1,0:T(8,128)(2,1)S(1)} collective-permute-done((bf16[128,1024]{1,0:T(8,128)(2,1)}, bf16[128,1024]{1,0:T(8,128)(2,1)S(1)}, u32[]{:S(2)}, u32[]{:S(2)}) %collective-permute-start.38) | collective-permute-done | bytes 262176 | tf_op jit(solution)/shard_map/ppermute | solution.py:36
  228.4 2.2 subtract_convert_fusion
  (112 shorter events, 28.6 us)
Async XLA Ops:
  0.0 12.6 %collective-permute-start = (bf16[4096,256]{1,0:T(8,128)(2,1)}, bf16[4096,256]{1,0:T(8,128)(2,1)S(1)}, u32[]{:S(2)}, u32[]{:S(2)}) collective-permute-start(bf16[4096,256]{1,0:T(8,128)(2,1)} %bitcast.20), channel_id=1, source_target_pairs={{0,4},{4,0},{1,5},{5,1},{2,6},{6,2},{3,7},{7,3},{8,12},{12,8},{9,1... | collective-permute-start | bytes 6291464 | tf_op jit(solution)/shard_map/ppermute | solution.py:36
  1.4 11.2 %collective-permute-start.1 = (bf16[4096,256]{1,0:T(8,128)(2,1)}, bf16[4096,256]{1,0:T(8,128)(2,1)}, u32[]{:S(2)}, u32[]{:S(2)}) collective-permute-start(bf16[4096,256]{1,0:T(8,128)(2,1)} %bitcast.22), channel_id=1, source_target_pairs={{0,4},{4,0},{1,5},{5,1},{2,6},{6,2},{3,7},{7,3},{8,12},{12,8},{9,1... | collective-permute-start | bytes 6291464 | tf_op jit(solution)/shard_map/ppermute | solution.py:36
  12.6 24.5 %copy-start.8 = (f32[8]{0:T(128)S(1)}, f32[8]{0:T(128)}, u32[]{:S(2)}) copy-start(f32[8]{0:T(128)} %param.20) | copy-start | bytes 100
  33.4 12.5 %all-to-all-start.1 = ((bf16[32,32,128]{2,1,0:T(8,128)(2,1)}), bf16[32,32,128]{2,1,0:T(8,128)(2,1)S(1)}, u32[]{:S(2)}, u32[]{:S(2)}) async-start(bf16[32,32,128]{2,1,0:T(8,128)(2,1)} %get-tuple-element.74), calls=%async_computation.1 | async-start | bytes 524288 | tf_op jit(solution)/shard_map/all_to_all | solution.py:698
  46.6 11.8 %copy-start.3 = (bf16[1,256,4096]{2,1,0:T(8,128)(2,1)S(1)}, bf16[1,256,4096]{2,1,0:T(8,128)(2,1)}, u32[]{:S(2)}) copy-start(bf16[1,256,4096]{2,1,0:T(8,128)(2,1)} %param.26) | copy-start | bytes 6291460
  46.6 11.8 %copy-start.6 = (f32[4096]{0:T(1024)S(1)}, f32[4096]{0:T(1024)}, u32[]{:S(2)}) copy-start(f32[4096]{0:T(1024)} %param.27) | copy-start | bytes 49156
  53.4 13.3 %copy-start.5 = (f32[24,4096]{1,0:T(8,128)S(1)}, f32[24,4096]{1,0:T(8,128)}, u32[]{:S(2)}) copy-start(f32[24,4096]{1,0:T(8,128)} %get-tuple-element.76) | copy-start | bytes 1179652
  53.4 7.9 %collective-permute-start.2 = (bf16[24,4096]{1,0:T(8,128)(2,1)}, bf16[24,4096]{1,0:T(8,128)(2,1)S(1)}, u32[]{:S(2)}, u32[]{:S(2)}) collective-permute-start(bf16[24,4096]{1,0:T(8,128)(2,1)} %get-tuple-element.77), channel_id=1, source_target_pairs={{0,1},{1,2},{2,3},{3,0},{4,5},{5,6},{6,7},{7,4},{8,9},{9,10},{10,1... | collective-permute-start | bytes 589832 | tf_op jit(solution)/shard_map/ppermute | solution.py:36
  54.7 11.9 %collective-permute-start.3 = (bf16[24,4096]{1,0:T(8,128)(2,1)}, bf16[24,4096]{1,0:T(8,128)(2,1)S(1)}, u32[]{:S(2)}, u32[]{:S(2)}) collective-permute-start(bf16[24,4096]{1,0:T(8,128)(2,1)} %get-tuple-element.78), channel_id=1, source_target_pairs={{0,2},{1,3},{2,0},{3,1},{4,6},{5,7},{6,4},{7,5},{8,10},{9,11},{10,... | collective-permute-start | bytes 589832 | tf_op jit(solution)/shard_map/ppermute | solution.py:36
  57.4 9.3 %collective-permute-start.4 = (bf16[24,4096]{1,0:T(8,128)(2,1)}, bf16[24,4096]{1,0:T(8,128)(2,1)S(1)}, u32[]{:S(2)}, u32[]{:S(2)}) collective-permute-start(bf16[24,4096]{1,0:T(8,128)(2,1)} %get-tuple-element.79), channel_id=1, source_target_pairs={{0,3},{1,0},{2,1},{3,2},{4,7},{5,4},{6,5},{7,6},{8,11},{9,8},{10,9... | collective-permute-start | bytes 589832 | tf_op jit(solution)/shard_map/ppermute | solution.py:36
  58.9 1.9 collective-permute-start.5
  67.0 6.1 %collective-permute-start.11 = (bf16[24,2048]{1,0:T(8,128)(2,1)S(1)}, bf16[24,2048]{1,0:T(8,128)(2,1)S(1)}, u32[]{:S(2)}, u32[]{:S(2)}) collective-permute-start(bf16[24,2048]{1,0:T(8,128)(2,1)S(1)} %get-tuple-element.148), channel_id=1, source_target_pairs={{0,32},{32,64},{64,96},{96,0},{1,33},{33,65},{65,97},{97,1},{2,34}... | collective-permute-start | bytes 294920 | tf_op jit(solution)/shard_map/ppermute | solution.py:36
  67.3 6.6 %collective-permute-start.10 = (bf16[24,2048]{1,0:T(8,128)(2,1)S(1)}, bf16[24,2048]{1,0:T(8,128)(2,1)S(1)}, u32[]{:S(2)}, u32[]{:S(2)}) collective-permute-start(bf16[24,2048]{1,0:T(8,128)(2,1)S(1)} %get-tuple-element.148), channel_id=1, source_target_pairs={{0,64},{32,96},{64,0},{96,32},{1,65},{33,97},{65,1},{97,33},{2,66}... | collective-permute-start | bytes 294920 | tf_op jit(solution)/shard_map/ppermute | solution.py:36
  69.0 5.0 %collective-permute-start.9 = (bf16[24,2048]{1,0:T(8,128)(2,1)S(1)}, bf16[24,2048]{1,0:T(8,128)(2,1)S(1)}, u32[]{:S(2)}, u32[]{:S(2)}) collective-permute-start(bf16[24,2048]{1,0:T(8,128)(2,1)S(1)} %get-tuple-element.148), channel_id=1, source_target_pairs={{0,96},{32,0},{64,32},{96,64},{1,97},{33,1},{65,33},{97,65},{2,98}... | collective-permute-start | bytes 294920 | tf_op jit(solution)/shard_map/ppermute | solution.py:36
  70.2 5.2 %collective-permute-start.8 = (bf16[24,2048]{1,0:T(8,128)(2,1)S(1)}, bf16[24,2048]{1,0:T(8,128)(2,1)S(1)}, u32[]{:S(2)}, u32[]{:S(2)}) collective-permute-start(bf16[24,2048]{1,0:T(8,128)(2,1)S(1)} %get-tuple-element.149), channel_id=1, source_target_pairs={{0,8},{8,16},{16,24},{24,0},{1,9},{9,17},{17,25},{25,1},{2,10},{10... | collective-permute-start | bytes 294920 | tf_op jit(solution)/shard_map/ppermute | solution.py:36
  70.7 5.7 %collective-permute-start.7 = (bf16[24,2048]{1,0:T(8,128)(2,1)S(1)}, bf16[24,2048]{1,0:T(8,128)(2,1)S(1)}, u32[]{:S(2)}, u32[]{:S(2)}) collective-permute-start(bf16[24,2048]{1,0:T(8,128)(2,1)S(1)} %get-tuple-element.149), channel_id=1, source_target_pairs={{0,16},{8,24},{16,0},{24,8},{1,17},{9,25},{17,1},{25,9},{2,18},{10... | collective-permute-start | bytes 294920 | tf_op jit(solution)/shard_map/ppermute | solution.py:36
  73.1 3.8 %collective-permute-start.6 = (bf16[24,2048]{1,0:T(8,128)(2,1)S(1)}, bf16[24,2048]{1,0:T(8,128)(2,1)S(1)}, u32[]{:S(2)}, u32[]{:S(2)}) collective-permute-start(bf16[24,2048]{1,0:T(8,128)(2,1)S(1)} %get-tuple-element.149), channel_id=1, source_target_pairs={{0,24},{8,0},{16,8},{24,16},{1,25},{9,1},{17,9},{25,17},{2,26},{10... | collective-permute-start | bytes 294920 | tf_op jit(solution)/shard_map/ppermute | solution.py:36
  74.0 23.2 %copy-start.1 = (bf16[1,4096,256]{2,1,0:T(8,128)(2,1)S(1)}, bf16[1,4096,256]{2,1,0:T(8,128)(2,1)}, u32[]{:S(2)}) copy-start(bf16[1,4096,256]{2,1,0:T(8,128)(2,1)} %param.25) | copy-start | bytes 6291460
  76.9 20.3 %copy-start = (bf16[1,4096,256]{2,1,0:T(8,128)(2,1)S(1)}, bf16[1,4096,256]{2,1,0:T(8,128)(2,1)}, u32[]{:S(2)}) copy-start(bf16[1,4096,256]{2,1,0:T(8,128)(2,1)} %param.24) | copy-start | bytes 6291460
  76.9 7.3 %collective-permute-start.13 = (bf16[96,2048]{1,0:T(8,128)(2,1)S(1)}, bf16[96,2048]{1,0:T(8,128)(2,1)S(1)}, u32[]{:S(2)}, u32[]{:S(2)}) collective-permute-start(bf16[96,2048]{1,0:T(8,128)(2,1)S(1)} %pad_maximum_fusion.1.refs_0_), channel_id=1, source_target_pairs={{0,96},{32,0},{64,32},{96,64},{1,97},{33,1},{65,33},{97,65},{2,98}... | collective-permute-start | bytes 1179656 | tf_op jit(solution)/shard_map/ppermute | solution.py:36
  77.4 8.6 %collective-permute-start.12 = (bf16[96,2048]{1,0:T(8,128)(2,1)S(1)}, bf16[96,2048]{1,0:T(8,128)(2,1)S(1)}, u32[]{:S(2)}, u32[]{:S(2)}) collective-permute-start(bf16[96,2048]{1,0:T(8,128)(2,1)S(1)} %pad_maximum_fusion.1.refs_0_), channel_id=1, source_target_pairs={{0,32},{32,64},{64,96},{96,0},{1,33},{33,65},{65,97},{97,1},{2,34}... | collective-permute-start | bytes 1179656 | tf_op jit(solution)/shard_map/ppermute | solution.py:36
  78.5 7.5 %collective-permute-start.15 = (bf16[96,2048]{1,0:T(8,128)(2,1)S(1)}, bf16[96,2048]{1,0:T(8,128)(2,1)S(1)}, u32[]{:S(2)}, u32[]{:S(2)}) collective-permute-start(bf16[96,2048]{1,0:T(8,128)(2,1)S(1)} %pad_maximum_fusion.2.refs_4_), channel_id=1, source_target_pairs={{0,24},{8,0},{16,8},{24,16},{1,25},{9,1},{17,9},{25,17},{2,26},{10... | collective-permute-start | bytes 1179656 | tf_op jit(solution)/shard_map/ppermute | solution.py:36
  80.4 8.1 %collective-permute-start.14 = (bf16[96,2048]{1,0:T(8,128)(2,1)S(1)}, bf16[96,2048]{1,0:T(8,128)(2,1)S(1)}, u32[]{:S(2)}, u32[]{:S(2)}) collective-permute-start(bf16[96,2048]{1,0:T(8,128)(2,1)S(1)} %pad_maximum_fusion.2.refs_4_), channel_id=1, source_target_pairs={{0,8},{8,16},{16,24},{24,0},{1,9},{9,17},{17,25},{25,1},{2,10},{10... | collective-permute-start | bytes 1179656 | tf_op jit(solution)/shard_map/ppermute | solution.py:36
  88.6 6.8 %collective-permute-start.18 = (bf16[48,2048]{1,0:T(8,128)(2,1)S(1)}, bf16[48,2048]{1,0:T(8,128)(2,1)S(1)}, u32[]{:S(2)}, u32[]{:S(2)}) collective-permute-start(bf16[48,2048]{1,0:T(8,128)(2,1)S(1)} %slice.106), channel_id=1, source_target_pairs={{0,8},{8,16},{16,24},{24,0},{1,9},{9,17},{17,25},{25,1},{2,10},{10... | collective-permute-start | bytes 589832 | tf_op jit(solution)/shard_map/ppermute | solution.py:36
  88.7 6.7 %collective-permute-start.19 = (bf16[48,2048]{1,0:T(8,128)(2,1)S(1)}, bf16[48,2048]{1,0:T(8,128)(2,1)S(1)}, u32[]{:S(2)}, u32[]{:S(2)}) collective-permute-start(bf16[48,2048]{1,0:T(8,128)(2,1)S(1)} %slice.107), channel_id=1, source_target_pairs={{0,24},{8,0},{16,8},{24,16},{1,25},{9,1},{17,9},{25,17},{2,26},{10... | collective-permute-start | bytes 589832 | tf_op jit(solution)/shard_map/ppermute | solution.py:36
  91.4 5.8 %collective-permute-start.16 = (bf16[48,2048]{1,0:T(8,128)(2,1)S(1)}, bf16[48,2048]{1,0:T(8,128)(2,1)S(1)}, u32[]{:S(2)}, u32[]{:S(2)}) collective-permute-start(bf16[48,2048]{1,0:T(8,128)(2,1)S(1)} %slice.104), channel_id=1, source_target_pairs={{0,32},{32,64},{64,96},{96,0},{1,33},{33,65},{65,97},{97,1},{2,34}... | collective-permute-start | bytes 589832 | tf_op jit(solution)/shard_map/ppermute | solution.py:36
  91.5 5.7 %collective-permute-start.17 = (bf16[48,2048]{1,0:T(8,128)(2,1)S(1)}, bf16[48,2048]{1,0:T(8,128)(2,1)S(1)}, u32[]{:S(2)}, u32[]{:S(2)}) collective-permute-start(bf16[48,2048]{1,0:T(8,128)(2,1)S(1)} %slice.105), channel_id=1, source_target_pairs={{0,96},{32,0},{64,32},{96,64},{1,97},{33,1},{65,33},{97,65},{2,98}... | collective-permute-start | bytes 589832 | tf_op jit(solution)/shard_map/ppermute | solution.py:36
  106.5 5.4 %collective-permute-start.21 = (bf16[48,2048]{1,0:T(8,128)(2,1)S(1)}, bf16[48,2048]{1,0:T(8,128)(2,1)S(1)}, u32[]{:S(2)}, u32[]{:S(2)}) collective-permute-start(bf16[48,2048]{1,0:T(8,128)(2,1)S(1)} %get-tuple-element.138), channel_id=1, source_target_pairs={{0,96},{32,0},{64,32},{96,64},{1,97},{33,1},{65,33},{97,65},{2,98}... | collective-permute-start | bytes 589832 | tf_op jit(solution)/shard_map/ppermute | solution.py:36
  109.3 5.7 %collective-permute-start.20 = (bf16[48,2048]{1,0:T(8,128)(2,1)S(1)}, bf16[48,2048]{1,0:T(8,128)(2,1)S(1)}, u32[]{:S(2)}, u32[]{:S(2)}) collective-permute-start(bf16[48,2048]{1,0:T(8,128)(2,1)S(1)} %get-tuple-element.139), channel_id=1, source_target_pairs={{0,32},{32,64},{64,96},{96,0},{1,33},{33,65},{65,97},{97,1},{2,34}... | collective-permute-start | bytes 589832 | tf_op jit(solution)/shard_map/ppermute | solution.py:36
  109.3 5.7 %collective-permute-start.23 = (bf16[48,2048]{1,0:T(8,128)(2,1)S(1)}, bf16[48,2048]{1,0:T(8,128)(2,1)S(1)}, u32[]{:S(2)}, u32[]{:S(2)}) collective-permute-start(bf16[48,2048]{1,0:T(8,128)(2,1)S(1)} %get-tuple-element.132), channel_id=1, source_target_pairs={{0,24},{8,0},{16,8},{24,16},{1,25},{9,1},{17,9},{25,17},{2,26},{10... | collective-permute-start | bytes 589832 | tf_op jit(solution)/shard_map/ppermute | solution.py:36
  109.4 5.8 %collective-permute-start.22 = (bf16[48,2048]{1,0:T(8,128)(2,1)S(1)}, bf16[48,2048]{1,0:T(8,128)(2,1)S(1)}, u32[]{:S(2)}, u32[]{:S(2)}) collective-permute-start(bf16[48,2048]{1,0:T(8,128)(2,1)S(1)} %get-tuple-element.133), channel_id=1, source_target_pairs={{0,8},{8,16},{16,24},{24,0},{1,9},{9,17},{17,25},{25,1},{2,10},{10... | collective-permute-start | bytes 589832 | tf_op jit(solution)/shard_map/ppermute | solution.py:36
  115.6 9.6 %collective-permute-start.24 = (bf16[96,2048]{1,0:T(8,128)(2,1)S(1)}, bf16[96,2048]{1,0:T(8,128)(2,1)S(1)}, u32[]{:S(2)}, u32[]{:S(2)}) collective-permute-start(bf16[96,2048]{1,0:T(8,128)(2,1)S(1)} %pad_maximum_fusion.5), channel_id=1, source_target_pairs={{0,32},{32,64},{64,96},{96,0},{1,33},{33,65},{65,97},{97,1},{2,34}... | collective-permute-start | bytes 1179656 | tf_op jit(solution)/shard_map/ppermute | solution.py:36
  115.7 9.6 %collective-permute-start.25 = (bf16[96,2048]{1,0:T(8,128)(2,1)S(1)}, bf16[96,2048]{1,0:T(8,128)(2,1)S(1)}, u32[]{:S(2)}, u32[]{:S(2)}) collective-permute-start(bf16[96,2048]{1,0:T(8,128)(2,1)S(1)} %pad_maximum_fusion.6), channel_id=1, source_target_pairs={{0,96},{32,0},{64,32},{96,64},{1,97},{33,1},{65,33},{97,65},{2,98}... | collective-permute-start | bytes 1179656 | tf_op jit(solution)/shard_map/ppermute | solution.py:36
  118.4 9.9 %collective-permute-start.26 = (bf16[96,2048]{1,0:T(8,128)(2,1)S(1)}, bf16[96,2048]{1,0:T(8,128)(2,1)S(1)}, u32[]{:S(2)}, u32[]{:S(2)}) collective-permute-start(bf16[96,2048]{1,0:T(8,128)(2,1)S(1)} %pad_maximum_fusion.7), channel_id=1, source_target_pairs={{0,8},{8,16},{16,24},{24,0},{1,9},{9,17},{17,25},{25,1},{2,10},{10... | collective-permute-start | bytes 1179656 | tf_op jit(solution)/shard_map/ppermute | solution.py:36
  118.6 9.8 %collective-permute-start.27 = (bf16[96,2048]{1,0:T(8,128)(2,1)S(1)}, bf16[96,2048]{1,0:T(8,128)(2,1)S(1)}, u32[]{:S(2)}, u32[]{:S(2)}) collective-permute-start(bf16[96,2048]{1,0:T(8,128)(2,1)S(1)} %pad_maximum_fusion.8), channel_id=1, source_target_pairs={{0,24},{8,0},{16,8},{24,16},{1,25},{9,1},{17,9},{25,17},{2,26},{10... | collective-permute-start | bytes 1179656 | tf_op jit(solution)/shard_map/ppermute | solution.py:36
  128.5 5.7 %collective-permute-start.28 = (bf16[24,2048]{1,0:T(8,128)(2,1)S(1)}, bf16[24,2048]{1,0:T(8,128)(2,1)S(1)}, u32[]{:S(2)}, u32[]{:S(2)}) collective-permute-start(bf16[24,2048]{1,0:T(8,128)(2,1)S(1)} %get-tuple-element.142), channel_id=1, source_target_pairs={{0,8},{8,16},{16,24},{24,0},{1,9},{9,17},{17,25},{25,1},{2,10},{10... | collective-permute-start | bytes 294920 | tf_op jit(solution)/shard_map/ppermute | solution.py:36
  128.6 5.8 %collective-permute-start.30 = (bf16[24,2048]{1,0:T(8,128)(2,1)S(1)}, bf16[24,2048]{1,0:T(8,128)(2,1)S(1)}, u32[]{:S(2)}, u32[]{:S(2)}) collective-permute-start(bf16[24,2048]{1,0:T(8,128)(2,1)S(1)} %get-tuple-element.143), channel_id=1, source_target_pairs={{0,24},{8,0},{16,8},{24,16},{1,25},{9,1},{17,9},{25,17},{2,26},{10... | collective-permute-start | bytes 294920 | tf_op jit(solution)/shard_map/ppermute | solution.py:36
  131.3 6.1 %collective-permute-start.29 = (bf16[24,2048]{1,0:T(8,128)(2,1)S(1)}, bf16[24,2048]{1,0:T(8,128)(2,1)S(1)}, u32[]{:S(2)}, u32[]{:S(2)}) collective-permute-start(bf16[24,2048]{1,0:T(8,128)(2,1)S(1)} %get-tuple-element.144), channel_id=1, source_target_pairs={{0,16},{8,24},{16,0},{24,8},{1,17},{9,25},{17,1},{25,9},{2,18},{10... | collective-permute-start | bytes 294920 | tf_op jit(solution)/shard_map/ppermute | solution.py:36
  131.5 6.0 %collective-permute-start.31 = (bf16[24,2048]{1,0:T(8,128)(2,1)S(1)}, bf16[24,2048]{1,0:T(8,128)(2,1)S(1)}, u32[]{:S(2)}, u32[]{:S(2)}) collective-permute-start(bf16[24,2048]{1,0:T(8,128)(2,1)S(1)} %get-tuple-element.145), channel_id=1, source_target_pairs={{0,32},{32,64},{64,96},{96,0},{1,33},{33,65},{65,97},{97,1},{2,34}... | collective-permute-start | bytes 294920 | tf_op jit(solution)/shard_map/ppermute | solution.py:36
  131.6 6.2 %collective-permute-start.33 = (bf16[24,2048]{1,0:T(8,128)(2,1)S(1)}, bf16[24,2048]{1,0:T(8,128)(2,1)S(1)}, u32[]{:S(2)}, u32[]{:S(2)}) collective-permute-start(bf16[24,2048]{1,0:T(8,128)(2,1)S(1)} %get-tuple-element.146), channel_id=1, source_target_pairs={{0,96},{32,0},{64,32},{96,64},{1,97},{33,1},{65,33},{97,65},{2,98}... | collective-permute-start | bytes 294920 | tf_op jit(solution)/shard_map/ppermute | solution.py:36
  134.2 5.3 %collective-permute-start.32 = (bf16[24,2048]{1,0:T(8,128)(2,1)S(1)}, bf16[24,2048]{1,0:T(8,128)(2,1)S(1)}, u32[]{:S(2)}, u32[]{:S(2)}) collective-permute-start(bf16[24,2048]{1,0:T(8,128)(2,1)S(1)} %get-tuple-element.147), channel_id=1, source_target_pairs={{0,64},{32,96},{64,0},{96,32},{1,65},{33,97},{65,1},{97,33},{2,66}... | collective-permute-start | bytes 294920 | tf_op jit(solution)/shard_map/ppermute | solution.py:36
  140.0 6.1 %collective-permute-start.36 = (bf16[24,4096]{1,0:T(8,128)(2,1)S(1)}, bf16[24,4096]{1,0:T(8,128)(2,1)S(1)}, u32[]{:S(2)}, u32[]{:S(2)}) collective-permute-start(bf16[24,4096]{1,0:T(8,128)(2,1)S(1)} %divide_convert_fusion), channel_id=1, source_target_pairs={{0,1},{1,2},{2,3},{3,0},{4,5},{5,6},{6,7},{7,4},{8,9},{9,10},{10,1... | collective-permute-start | bytes 589832 | tf_op jit(solution)/shard_map/ppermute | solution.py:36
  140.4 7.8 %collective-permute-start.35 = (bf16[24,4096]{1,0:T(8,128)(2,1)S(1)}, bf16[24,4096]{1,0:T(8,128)(2,1)S(1)}, u32[]{:S(2)}, u32[]{:S(2)}) collective-permute-start(bf16[24,4096]{1,0:T(8,128)(2,1)S(1)} %divide_convert_fusion), channel_id=1, source_target_pairs={{0,2},{1,3},{2,0},{3,1},{4,6},{5,7},{6,4},{7,5},{8,10},{9,11},{10,... | collective-permute-start | bytes 589832 | tf_op jit(solution)/shard_map/ppermute | solution.py:36
  143.1 5.7 %collective-permute-start.34 = (bf16[24,4096]{1,0:T(8,128)(2,1)S(1)}, bf16[24,4096]{1,0:T(8,128)(2,1)S(1)}, u32[]{:S(2)}, u32[]{:S(2)}) collective-permute-start(bf16[24,4096]{1,0:T(8,128)(2,1)S(1)} %divide_convert_fusion), channel_id=1, source_target_pairs={{0,3},{1,0},{2,1},{3,2},{4,7},{5,4},{6,5},{7,6},{8,11},{9,8},{10,9... | collective-permute-start | bytes 589832 | tf_op jit(solution)/shard_map/ppermute | solution.py:36
  189.1 12.8 %all-to-all-start.3 = ((bf16[32,32,128]{2,1,0:T(8,128)(2,1)}), bf16[32,32,128]{2,1,0:T(8,128)(2,1)S(1)}, u32[]{:S(2)}, u32[]{:S(2)}) async-start(bf16[32,32,128]{2,1,0:T(8,128)(2,1)} %leave.1), calls=%async_computation.3 | async-start | bytes 524288 | tf_op jit(solution)/shard_map/all_to_all | solution.py:743
  212.8 9.5 %collective-permute-start.37 = (bf16[128,1024]{1,0:T(8,128)(2,1)}, bf16[128,1024]{1,0:T(8,128)(2,1)S(1)}, u32[]{:S(2)}, u32[]{:S(2)}) collective-permute-start(bf16[128,1024]{1,0:T(8,128)(2,1)} %get-tuple-element.120), channel_id=1, source_target_pairs={{0,2},{1,3},{2,0},{3,1},{4,6},{5,7},{6,4},{7,5},{8,10},{9,11},{10,... | collective-permute-start | bytes 786440 | tf_op jit(solution)/shard_map/ppermute | solution.py:36
  214.7 13.6 %collective-permute-start.38 = (bf16[128,1024]{1,0:T(8,128)(2,1)}, bf16[128,1024]{1,0:T(8,128)(2,1)S(1)}, u32[]{:S(2)}, u32[]{:S(2)}) collective-permute-start(bf16[128,1024]{1,0:T(8,128)(2,1)} %get-tuple-element.121), channel_id=1, source_target_pairs={{0,1},{1,2},{2,3},{3,0},{4,5},{5,6},{6,7},{7,4},{8,9},{9,10},{10,1... | collective-permute-start | bytes 786440 | tf_op jit(solution)/shard_map/ppermute | solution.py:36
  215.7 12.6 %collective-permute-start.39 = (bf16[128,1024]{1,0:T(8,128)(2,1)}, bf16[128,1024]{1,0:T(8,128)(2,1)S(1)}, u32[]{:S(2)}, u32[]{:S(2)}) collective-permute-start(bf16[128,1024]{1,0:T(8,128)(2,1)} %get-tuple-element.122), channel_id=1, source_target_pairs={{0,3},{1,0},{2,1},{3,2},{4,7},{5,4},{6,5},{7,6},{8,11},{9,8},{10,9... | collective-permute-start | bytes 786440 | tf_op jit(solution)/shard_map/ppermute | solution.py:36
  (3 other events, 10.2 us)

commit v7 on v5

--- a/solution.py
+++ b/solution.py
@@ -694,6 +694,7 @@
 
     side = lax.axis_size("x")
     cut = width // 2
+    routed, head_vec = lax.optimization_barrier((routed, head_vec))
     near_own = jnp.concatenate(gather_direct(routed[:, :cut], "z"), axis=0)
     far_own = jnp.concatenate(gather_direct(routed[:, cut:], "x"), axis=0)
     near_rows = gather_around(near_own, "x")

time: 232 us -> 220 us (0.948)
  waiting for transfers between devices: 56.5 us -> 46 us
    ppermute x40, waiting for transfers between devices: 45.9 us -> 35.3 us  [shift(): lax.ppermute(value, axis, [(i, (i + by) % count) for i in range(count)])]
  transfers between devices with their start and end apart: 42 -> 42, of which waited for: 21 -> 21; matrix products, arithmetic and copies ran while one was open for 2% -> 3% of each run, Pallas kernels for 8% -> 8%
where the time goes in v7:
time: 220 us; the launch traced here: 219 us
  starting transfers between devices  63.7 us (29%)
  Pallas kernels  54.9 us (25%)
  waiting for transfers between devices  46 us (21%)
  blocking collectives  42.7 us (19%)
  other arithmetic  7.64 us (3%)
  local copies, waits for them, and re-layouts  3.61 us (2%)
    ppermute x40, starting transfers between devices, shift(): lax.ppermute(value, axis, [(i, (i + by) % count) for i in range(count)])  56.4 us
    ppermute x40, waiting for transfers between devices, shift(): lax.ppermute(value, axis, [(i, (i + by) % count) for i in range(count)])  35.3 us
    all_to_all x1, blocking collectives, shards(): lax.all_to_all(local_grad.reshape(n_seq, slice_rows, nstate), SEQ, 0, 0,...  23.7 us
    all_to_all x1, blocking collectives, shards(): got = lax.all_to_all(payload, SEQ, 0, 0, tiled=True)  18.9 us
    pallas_call x5, Pallas kernels, single(): pl.pallas_call(kernel, grid=(1,), out_shape=out_shape, in_specs=whole(arg...  12.3 us
    pallas_call x2, Pallas kernels, back_columns(): pl.pallas_call(functools.partial(back_kernel, heads, per), grid_spec=pltp...  11 us
    pallas_call x1, Pallas kernels, expert_rows(): pl.pallas_call(functools.partial(expert_kernel, side), out_shape=(out, ou...  9.18 us
    pallas_call x1, Pallas kernels, project(): pl.pallas_call(functools.partial(proj_kernel, heads, slice_rows), grid=(w...  8.04 us
  transfers between devices with their start and end apart: 42, of which 21 were waited for; matrix products, arithmetic and copies ran while one was open for 3% of the time, Pallas kernels for 8%

profile of v7, /device:TPU:1, one launch (start us, length us, event | category | flops | bytes accessed | tf_op | source)
XLA Modules:
  0.0 219.0 jit_solution(16014293857401493203)
XLA Ops:
  0.0 1.4 collective-permute-start
  4.5 8.0 %project.1 = (bf16[128,1024]{1,0:T(8,128)(2,1)}, bf16[128,256]{1,0:T(8,128)(2,1)}, f32[128,128]{1,0:T(8,128)}, f32[128,128]{1,0:T(8,128)}, f32[128,128]{1,0:T(8,...) custom-call(bf16[128,4096]{1,0:T(8,128)(2,1)} %cand.3, bf16[4096,1024]{1,0:T(8,128)(2,1)} %w_in.5, ...), custom_call_target="tpu_custom_call" | custom-call | flops 1342177280 | bytes 12582912 | tf_op jit(solution)/shard_map/project/pallas_call | solution.py:262
  12.6 18.9 %all_to_all.20.got = bf16[32,48,128]{2,1,0:T(8,128)(2,1)} all-to-all(bf16[32,48,128]{2,1,0:T(8,128)(2,1)} %get-tuple-element.54), channel_id=1, replica_groups=mesh['x'=4,'z'=4,'c'=2,'e'=4] {'x','z','c'}, dimensions={0} | all-to-all | bytes 786432 | tf_op jit(solution)/shard_map/all_to_all | solution.py:676
  31.6 1.8 enter.1
  33.4 3.7 %all-to-all-start.1 = ((bf16[32,32,128]{2,1,0:T(8,128)(2,1)}), bf16[32,32,128]{2,1,0:T(8,128)(2,1)S(1)}, u32[]{:S(2)}, u32[]{:S(2)}) async-start(bf16[32,32,128]{2,1,0:T(8,128)(2,1)} %get-tuple-element.56), calls=%async_computation.1 | async-start | bytes 524288 | tf_op jit(solution)/shard_map/all_to_all | solution.py:683
  37.7 2.2 %mix_within.1.within = f32[128,1024]{1,0:T(8,128)} custom-call(bf16[128,1024]{1,0:T(8,128)(2,1)} %get-tuple-element.49.inner_ref, bf16[128,256]{1,0:T(8,128)(2,1)} %get-tuple-element.50.bc_ref, f32[128,128]{1,0:T(8,128)} %get-tuple-element.51.cum_ref, f32[128,128]{1,0:T(8,128)} %get-tuple-element.52.cum_t_ref, f32[128,128]{1,0:T(8,128)} %get-tuple-element.53.step_t_ref, ...), custom_call_target="tpu_custom_call" | custom-call | flops 134217728 | bytes 1048576 | tf_op jit(solution)/shard_map/mix_within/pallas_call | solution.py:180
  39.9 6.0 %all-to-all-done.1 = bf16[32,32,128]{2,1,0:T(8,128)(2,1)S(1)} async-done(((bf16[32,32,128]{2,1,0:T(8,128)(2,1)}), bf16[32,32,128]{2,1,0:T(8,128)(2,1)S(1)}, u32[]{:S(2)}, u32[]{:S(2)}) %all-to-all-start.1) | async-done | bytes 262176 | tf_op jit(solution)/shard_map/all_to_all | solution.py:683
  46.6 6.7 %mix_slots.1 = (f32[24,4096]{1,0:T(8,128)}, bf16[24,4096]{1,0:T(8,128)(2,1)}, bf16[24,4096]{1,0:T(8,128)(2,1)}, bf16[24,4096]{1,0:T(8,128)(2,1)}, f32[128,1024]{1,0:T(8,128)}) custom-call(f32[128,1024]{1,0:T(8,128)} %mix_within.1.within, bf16[128,256]{1,0:T(8,128)(2,1)} %get-tuple-element.50.bc_ref, f32[128,128]{1,0:T(8,128)} %get-tuple-element.51.cum_ref, ...), custom_call_target="tpu_custom_call" | custom-call | flops 805306368 | bytes 8388608 | tf_op jit(solution)/shard_map/mix_slots/pallas_call | solution.py:402
  54.7 2.6 %collective-permute-start.3 = (bf16[24,4096]{1,0:T(8,128)(2,1)}, bf16[24,4096]{1,0:T(8,128)(2,1)S(1)}, u32[]{:S(2)}, u32[]{:S(2)}) collective-permute-start(bf16[24,4096]{1,0:T(8,128)(2,1)} %get-tuple-element.60), channel_id=1, source_target_pairs={{0,2},{1,3},{2,0},{3,1},{4,6},{5,7},{6,4},{7,5},{8,10},{9,11},{10,... | collective-permute-start | bytes 589832 | tf_op jit(solution)/shard_map/ppermute | solution.py:36
  61.3 5.3 %collective-permute-done.3 = bf16[24,4096]{1,0:T(8,128)(2,1)S(1)} collective-permute-done((bf16[24,4096]{1,0:T(8,128)(2,1)}, bf16[24,4096]{1,0:T(8,128)(2,1)S(1)}, u32[]{:S(2)}, u32[]{:S(2)}) %collective-permute-start.3) | collective-permute-done | bytes 196640 | tf_op jit(solution)/shard_map/ppermute | solution.py:36
  67.6 1.8 collective-permute-start.7
  70.6 1.7 collective-permute-start.14
  74.5 2.3 %collective-permute-start.9 = (bf16[96,2048]{1,0:T(8,128)(2,1)S(1)}, bf16[96,2048]{1,0:T(8,128)(2,1)S(1)}, u32[]{:S(2)}, u32[]{:S(2)}) collective-permute-start(bf16[96,2048]{1,0:T(8,128)(2,1)S(1)} %pad_maximum_fusion.1.refs_0_), channel_id=1, source_target_pairs={{0,96},{32,0},{64,32},{96,64},{1,97},{33,1},{65,33},{97,65},{2,98}... | collective-permute-start | bytes 1179656 | tf_op jit(solution)/shard_map/ppermute | solution.py:36
  77.8 2.7 %collective-permute-start.16 = (bf16[96,2048]{1,0:T(8,128)(2,1)S(1)}, bf16[96,2048]{1,0:T(8,128)(2,1)S(1)}, u32[]{:S(2)}, u32[]{:S(2)}) collective-permute-start(bf16[96,2048]{1,0:T(8,128)(2,1)S(1)} %pad_maximum_fusion.3.refs_4_), channel_id=1, source_target_pairs={{0,24},{8,0},{16,8},{24,16},{1,25},{9,1},{17,9},{25,17},{2,26},{10... | collective-permute-start | bytes 1179656 | tf_op jit(solution)/shard_map/ppermute | solution.py:36
  80.6 3.0 %collective-permute-done.10.refs_3_ = bf16[96,2048]{1,0:T(8,128)(2,1)S(1)} collective-permute-done((bf16[96,2048]{1,0:T(8,128)(2,1)S(1)}, bf16[96,2048]{1,0:T(8,128)(2,1)S(1)}, u32[]{:S(2)}, u32[]{:S(2)}) %collective-permute-start.10) | collective-permute-done | bytes 393248 | tf_op jit(solution)/shard_map/ppermute | solution.py:36
  85.1 2.6 %collective-permute-start.12 = (bf16[48,2048]{1,0:T(8,128)(2,1)S(1)}, bf16[48,2048]{1,0:T(8,128)(2,1)S(1)}, u32[]{:S(2)}, u32[]{:S(2)}) collective-permute-start(bf16[48,2048]{1,0:T(8,128)(2,1)S(1)} %slice.131), channel_id=1, source_target_pairs={{0,96},{32,0},{64,32},{96,64},{1,97},{33,1},{65,33},{97,65},{2,98}... | collective-permute-start | bytes 589832 | tf_op jit(solution)/shard_map/ppermute | solution.py:36
  88.6 3.1 %collective-permute-start.19 = (bf16[48,2048]{1,0:T(8,128)(2,1)S(1)}, bf16[48,2048]{1,0:T(8,128)(2,1)S(1)}, u32[]{:S(2)}, u32[]{:S(2)}) collective-permute-start(bf16[48,2048]{1,0:T(8,128)(2,1)S(1)} %slice.133), channel_id=1, source_target_pairs={{0,24},{8,0},{16,8},{24,16},{1,25},{9,1},{17,9},{25,17},{2,26},{10... | collective-permute-start | bytes 589832 | tf_op jit(solution)/shard_map/ppermute | solution.py:36
  91.7 2.7 %collective-permute-done.18 = bf16[48,2048]{1,0:T(8,128)(2,1)S(1)} collective-permute-done((bf16[48,2048]{1,0:T(8,128)(2,1)S(1)}, bf16[48,2048]{1,0:T(8,128)(2,1)S(1)}, u32[]{:S(2)}, u32[]{:S(2)}) %collective-permute-start.18) | collective-permute-done | bytes 196640 | tf_op jit(solution)/shard_map/ppermute | solution.py:36
  94.5 9.2 %experts.1 = (bf16[384,2048]{1,0:T(8,128)(2,1)S(1)}, bf16[384,2048]{1,0:T(8,128)(2,1)S(1)}) custom-call(bf16[96,2048]{1,0:T(8,128)(2,1)S(1)} %pad_maximum_fusion.1.refs_0_, bf16[96,2048]{1,0:T(8,128)(2,1)S(1)} %collective-permute-done.9.refs_1_, bf16[96,2048]{1,0:T(8,128)(2,1)S(1)} %pad_maximum_fusion.2.refs_2_, ...), custom_call_target="tpu_custom_call" | custom-call | flops 6442450944 | bytes 14680064 | tf_op jit(solution)/shard_map/experts/pallas_call | solution.py:107
  103.9 2.7 %collective-permute-start.22 = (bf16[48,2048]{1,0:T(8,128)(2,1)S(1)}, bf16[48,2048]{1,0:T(8,128)(2,1)S(1)}, u32[]{:S(2)}, u32[]{:S(2)}) collective-permute-start(bf16[48,2048]{1,0:T(8,128)(2,1)S(1)} %get-tuple-element.97), channel_id=1, source_target_pairs={{0,96},{32,0},{64,32},{96,64},{1,97},{33,1},{65,33},{97,65},{2,98}... | collective-permute-start | bytes 589832 | tf_op jit(solution)/shard_map/ppermute | solution.py:36
  106.6 1.5 collective-permute-start.27
  108.1 1.6 collective-permute-start.29
  109.9 2.6 %collective-permute-start.23 = (bf16[96,2048]{1,0:T(8,128)(2,1)S(1)}, bf16[96,2048]{1,0:T(8,128)(2,1)S(1)}, u32[]{:S(2)}, u32[]{:S(2)}) collective-permute-start(bf16[96,2048]{1,0:T(8,128)(2,1)S(1)} %pad_maximum_fusion.6), channel_id=1, source_target_pairs={{0,96},{32,0},{64,32},{96,64},{1,97},{33,1},{65,33},{97,65},{2,98}... | collective-permute-start | bytes 1179656 | tf_op jit(solution)/shard_map/ppermute | solution.py:36
  113.1 2.8 %collective-permute-start.30 = (bf16[96,2048]{1,0:T(8,128)(2,1)S(1)}, bf16[96,2048]{1,0:T(8,128)(2,1)S(1)}, u32[]{:S(2)}, u32[]{:S(2)}) collective-permute-start(bf16[96,2048]{1,0:T(8,128)(2,1)S(1)} %pad_maximum_fusion.8), channel_id=1, source_target_pairs={{0,24},{8,0},{16,8},{24,16},{1,25},{9,1},{17,9},{25,17},{2,26},{10... | collective-permute-start | bytes 1179656 | tf_op jit(solution)/shard_map/ppermute | solution.py:36
  116.1 1.5 collective-permute-done.23
  117.6 2.8 %collective-permute-done.21 = bf16[96,2048]{1,0:T(8,128)(2,1)S(1)} collective-permute-done((bf16[96,2048]{1,0:T(8,128)(2,1)S(1)}, bf16[96,2048]{1,0:T(8,128)(2,1)S(1)}, u32[]{:S(2)}, u32[]{:S(2)}) %collective-permute-start.21) | collective-permute-done | bytes 393248 | tf_op jit(solution)/shard_map/ppermute | solution.py:36
  120.6 1.5 collective-permute-start.24
  122.1 1.6 collective-permute-start.26
  123.7 1.6 collective-permute-start.25
  125.6 2.7 %collective-permute-start.33 = (bf16[24,2048]{1,0:T(8,128)(2,1)S(1)}, bf16[24,2048]{1,0:T(8,128)(2,1)S(1)}, u32[]{:S(2)}, u32[]{:S(2)}) collective-permute-start(bf16[24,2048]{1,0:T(8,128)(2,1)S(1)} %get-tuple-element.110), channel_id=1, source_target_pairs={{0,96},{32,0},{64,32},{96,64},{1,97},{33,1},{65,33},{97,65},{2,98}... | collective-permute-start | bytes 294920 | tf_op jit(solution)/shard_map/ppermute | solution.py:36
  128.3 1.4 collective-permute-done.25
  130.9 2.4 %collective-permute-done.32 = bf16[24,2048]{1,0:T(8,128)(2,1)S(1)} collective-permute-done((bf16[24,2048]{1,0:T(8,128)(2,1)S(1)}, bf16[24,2048]{1,0:T(8,128)(2,1)S(1)}, u32[]{:S(2)}, u32[]{:S(2)}) %collective-permute-start.32) | collective-permute-done | bytes 98336 | tf_op jit(solution)/shard_map/ppermute | solution.py:36
  133.8 3.7 %collective-permute-start.35 = (bf16[24,4096]{1,0:T(8,128)(2,1)S(1)}, bf16[24,4096]{1,0:T(8,128)(2,1)S(1)}, u32[]{:S(2)}, u32[]{:S(2)}) collective-permute-start(bf16[24,4096]{1,0:T(8,128)(2,1)S(1)} %divide_convert_fusion), channel_id=1, source_target_pairs={{0,2},{1,3},{2,0},{3,1},{4,6},{5,7},{6,4},{7,5},{8,10},{9,11},{10,... | collective-permute-start | bytes 589832 | tf_op jit(solution)/shard_map/ppermute | solution.py:36
  137.6 2.0 collective-permute-done.36
  139.5 3.2 %collective-permute-done.35 = bf16[24,4096]{1,0:T(8,128)(2,1)S(1)} collective-permute-done((bf16[24,4096]{1,0:T(8,128)(2,1)S(1)}, bf16[24,4096]{1,0:T(8,128)(2,1)S(1)}, u32[]{:S(2)}, u32[]{:S(2)}) %collective-permute-start.35) | collective-permute-done | bytes 196640 | tf_op jit(solution)/shard_map/ppermute | solution.py:36
  143.7 7.6 %out_gradient.1 = (f32[128,4096]{1,0:T(8,128)}, f32[128,1024]{1,0:T(8,128)}, bf16[1024,128]{1,0:T(8,128)(2,1)}) custom-call(bf16[96,128]{1,0:T(8,128)(2,1)} %pad_maximum_fusion.10.table, bf16[96,4096]{1,0:T(8,128)(2,1)} %pad_maximum_fusion.terms, f32[1,4096]{1,0:T(1,128)} %bitcast.33, bf16[1024,4096]{1,0:T(8,128)(2,1)} %w_out.3, ...), custom_call_target="tpu_custom_call" | custom-call | flops 1073741824 | bytes 8388608 | tf_op jit(solution)/shard_map/out_gradient/pallas_call | solution.py:452
  151.3 23.7 %all_to_all.21.got = bf16[32,32,128]{2,1,0:T(8,128)(2,1)} all-to-all(bf16[32,32,128]{2,1,0:T(8,128)(2,1)} %bitcast.32), channel_id=1, replica_groups=mesh['x'=4,'z'=4,'c'=2,'e'=4] {'x','z','c'}, dimensions={0} | all-to-all | bytes 524288 | tf_op jit(solution)/shard_map/all_to_all | solution.py:721
  175.1 1.7 leave.1
  176.8 3.7 %all-to-all-start.3 = ((bf16[32,32,128]{2,1,0:T(8,128)(2,1)}), bf16[32,32,128]{2,1,0:T(8,128)(2,1)S(1)}, u32[]{:S(2)}, u32[]{:S(2)}) async-start(bf16[32,32,128]{2,1,0:T(8,128)(2,1)} %leave.1), calls=%async_computation.3 | async-start | bytes 524288 | tf_op jit(solution)/shard_map/all_to_all | solution.py:728
  181.1 3.7 %near_gradient.1 = (f32[128,1024]{1,0:T(8,128)}, f32[128,128]{1,0:T(8,128)}, f32[128,128]{1,0:T(8,128)}, f32[128,128]{1,0:T(8,128)}, f32[128,128]{1,0:T(8,128)}) custom-call(f32[128,1024]{1,0:T(8,128)} %get-tuple-element.74.grad_ref, bf16[128,1024]{1,0:T(8,128)(2,1)} %get-tuple-element.49.inner_ref, bf16[128,256]{1,0:T(8,128)(2,1)} %get-tuple-element.50.bc_ref, ...), custom_call_target="tpu_custom_call" | custom-call | flops 268435456 | bytes 2621440 | tf_op jit(solution)/shard_map/near_gradient/pallas_call | solution.py:180
  184.8 4.8 %all-to-all-done.3 = bf16[32,32,128]{2,1,0:T(8,128)(2,1)S(1)} async-done(((bf16[32,32,128]{2,1,0:T(8,128)(2,1)}), bf16[32,32,128]{2,1,0:T(8,128)(2,1)S(1)}, u32[]{:S(2)}, u32[]{:S(2)}) %all-to-all-start.3) | async-done | bytes 262176 | tf_op jit(solution)/shard_map/all_to_all | solution.py:728
  190.3 2.8 %far_gradient.1 = (bf16[128,1024]{1,0:T(8,128)(2,1)}, bf16[128,256]{1,0:T(8,128)(2,1)}, bf16[128,128]{1,0:T(8,128)(2,1)}) custom-call(bf16[1024,128]{1,0:T(8,128)(2,1)} %bitcast.28, bf16[1024,128]{1,0:T(8,128)(2,1)} %bitcast.26, bf16[128,1024]{1,0:T(8,128)(2,1)} %get-tuple-element.49.inner_ref, bf16[128,256]{1,0:T(8,128)(2,1)} %get-tuple-element.50.bc_ref, ...), custom_call_target="tpu_custom_call" | custom-call | flops 134217728 | bytes 2621440 | tf_op jit(solution)/shard_map/far_gradient/pallas_call | solution.py:180
  193.1 7.4 %back_columns.3 = (bf16[128,1024]{1,0:T(8,128)(2,1)}, bf16[128,1024]{1,0:T(8,128)(2,1)}, bf16[128,1024]{1,0:T(8,128)(2,1)}) custom-call(s32[3]{0:T(128)} %pad_add_fusion.which, bf16[128,1024]{1,0:T(8,128)(2,1)} %get-tuple-element.81.g_ref, bf16[128,256]{1,0:T(8,128)(2,1)} %get-tuple-element.82.gbc, bf16[128,128]{1,0:T(8,128)(2,1)} %get-tuple-element.83.gpre, ...), custom_call_target="tpu_custom_call" | custom-call | flops 1006632960 | bytes 7864320 | tf_op jit(solution)/shard_map/back_columns/pallas_call | solution.py:605
  200.5 3.7 %collective-permute-start.37 = (bf16[128,1024]{1,0:T(8,128)(2,1)}, bf16[128,1024]{1,0:T(8,128)(2,1)S(1)}, u32[]{:S(2)}, u32[]{:S(2)}) collective-permute-start(bf16[128,1024]{1,0:T(8,128)(2,1)} %get-tuple-element.84), channel_id=1, source_target_pairs={{0,2},{1,3},{2,0},{3,1},{4,6},{5,7},{6,4},{7,5},{8,10},{9,11},{10,... | collective-permute-start | bytes 786440 | tf_op jit(solution)/shard_map/ppermute | solution.py:36
  204.4 2.4 %collective-permute-start.39 = (bf16[128,1024]{1,0:T(8,128)(2,1)}, bf16[128,1024]{1,0:T(8,128)(2,1)S(1)}, u32[]{:S(2)}, u32[]{:S(2)}) collective-permute-start(bf16[128,1024]{1,0:T(8,128)(2,1)} %get-tuple-element.86), channel_id=1, source_target_pairs={{0,3},{1,0},{2,1},{3,2},{4,7},{5,4},{6,5},{7,6},{8,11},{9,8},{10,9... | collective-permute-start | bytes 786440 | tf_op jit(solution)/shard_map/ppermute | solution.py:36
  206.9 3.7 %back_columns.2 = f32[128,1024]{1,0:T(8,128)} custom-call(s32[1]{0:T(128)} %bitcast.12.which, bf16[128,1024]{1,0:T(8,128)(2,1)} %get-tuple-element.81.g_ref, bf16[128,256]{1,0:T(8,128)(2,1)} %get-tuple-element.82.gbc, bf16[128,128]{1,0:T(8,128)(2,1)} %get-tuple-element.83.gpre, bf16[4096,1024]{1,0:T(8,128)(2,1)} %w_in.5, bf16[4096,256]{1,0:T(8,128)(2,1)} %w_bc.5, ...), custom_call_target="tpu_custom_call" | custom-call | flops 335544320 | bytes 2621440 | tf_op jit(solution)/shard_map/back_columns/pallas_call | solution.py:605
  211.1 5.8 %collective-permute-done.38 = bf16[128,1024]{1,0:T(8,128)(2,1)S(1)} collective-permute-done((bf16[128,1024]{1,0:T(8,128)(2,1)}, bf16[128,1024]{1,0:T(8,128)(2,1)S(1)}, u32[]{:S(2)}, u32[]{:S(2)}) %collective-permute-start.38) | collective-permute-done | bytes 262176 | tf_op jit(solution)/shard_map/ppermute | solution.py:36
  216.8 2.2 subtract_convert_fusion
  (112 shorter events, 23.9 us)
Async XLA Ops:
  0.0 12.6 %collective-permute-start = (bf16[4096,256]{1,0:T(8,128)(2,1)}, bf16[4096,256]{1,0:T(8,128)(2,1)S(1)}, u32[]{:S(2)}, u32[]{:S(2)}) collective-permute-start(bf16[4096,256]{1,0:T(8,128)(2,1)} %bitcast.20), channel_id=1, source_target_pairs={{0,4},{4,0},{1,5},{5,1},{2,6},{6,2},{3,7},{7,3},{8,12},{12,8},{9,1... | collective-permute-start | bytes 6291464 | tf_op jit(solution)/shard_map/ppermute | solution.py:36
  1.4 11.2 %collective-permute-start.1 = (bf16[4096,256]{1,0:T(8,128)(2,1)}, bf16[4096,256]{1,0:T(8,128)(2,1)}, u32[]{:S(2)}, u32[]{:S(2)}) collective-permute-start(bf16[4096,256]{1,0:T(8,128)(2,1)} %bitcast.22), channel_id=1, source_target_pairs={{0,4},{4,0},{1,5},{5,1},{2,6},{6,2},{3,7},{7,3},{8,12},{12,8},{9,1... | collective-permute-start | bytes 6291464 | tf_op jit(solution)/shard_map/ppermute | solution.py:36
  12.6 24.5 %copy-start.8 = (f32[8]{0:T(128)S(1)}, f32[8]{0:T(128)}, u32[]{:S(2)}) copy-start(f32[8]{0:T(128)} %param.20) | copy-start | bytes 100
  33.4 12.5 %all-to-all-start.1 = ((bf16[32,32,128]{2,1,0:T(8,128)(2,1)}), bf16[32,32,128]{2,1,0:T(8,128)(2,1)S(1)}, u32[]{:S(2)}, u32[]{:S(2)}) async-start(bf16[32,32,128]{2,1,0:T(8,128)(2,1)} %get-tuple-element.56), calls=%async_computation.1 | async-start | bytes 524288 | tf_op jit(solution)/shard_map/all_to_all | solution.py:683
  46.6 11.8 %copy-start.3 = (bf16[1,256,4096]{2,1,0:T(8,128)(2,1)S(1)}, bf16[1,256,4096]{2,1,0:T(8,128)(2,1)}, u32[]{:S(2)}) copy-start(bf16[1,256,4096]{2,1,0:T(8,128)(2,1)} %param.26) | copy-start | bytes 6291460
  46.6 11.8 %copy-start.6 = (f32[4096]{0:T(1024)S(1)}, f32[4096]{0:T(1024)}, u32[]{:S(2)}) copy-start(f32[4096]{0:T(1024)} %param.27) | copy-start | bytes 49156
  53.4 13.3 %copy-start.5 = (f32[24,4096]{1,0:T(8,128)S(1)}, f32[24,4096]{1,0:T(8,128)}, u32[]{:S(2)}) copy-start(f32[24,4096]{1,0:T(8,128)} %get-tuple-element.58) | copy-start | bytes 1179652
  53.4 7.9 %collective-permute-start.2 = (bf16[24,4096]{1,0:T(8,128)(2,1)}, bf16[24,4096]{1,0:T(8,128)(2,1)S(1)}, u32[]{:S(2)}, u32[]{:S(2)}) collective-permute-start(bf16[24,4096]{1,0:T(8,128)(2,1)} %get-tuple-element.59), channel_id=1, source_target_pairs={{0,1},{1,2},{2,3},{3,0},{4,5},{5,6},{6,7},{7,4},{8,9},{9,10},{10,1... | collective-permute-start | bytes 589832 | tf_op jit(solution)/shard_map/ppermute | solution.py:36
  54.7 11.9 %collective-permute-start.3 = (bf16[24,4096]{1,0:T(8,128)(2,1)}, bf16[24,4096]{1,0:T(8,128)(2,1)S(1)}, u32[]{:S(2)}, u32[]{:S(2)}) collective-permute-start(bf16[24,4096]{1,0:T(8,128)(2,1)} %get-tuple-element.60), channel_id=1, source_target_pairs={{0,2},{1,3},{2,0},{3,1},{4,6},{5,7},{6,4},{7,5},{8,10},{9,11},{10,... | collective-permute-start | bytes 589832 | tf_op jit(solution)/shard_map/ppermute | solution.py:36
  57.4 9.3 %collective-permute-start.4 = (bf16[24,4096]{1,0:T(8,128)(2,1)}, bf16[24,4096]{1,0:T(8,128)(2,1)S(1)}, u32[]{:S(2)}, u32[]{:S(2)}) collective-permute-start(bf16[24,4096]{1,0:T(8,128)(2,1)} %get-tuple-element.61), channel_id=1, source_target_pairs={{0,3},{1,0},{2,1},{3,2},{4,7},{5,4},{6,5},{7,6},{8,11},{9,8},{10,9... | collective-permute-start | bytes 589832 | tf_op jit(solution)/shard_map/ppermute | solution.py:36
  58.9 1.9 collective-permute-start.5
  67.0 5.3 %collective-permute-start.8 = (bf16[24,2048]{1,0:T(8,128)(2,1)S(1)}, bf16[24,2048]{1,0:T(8,128)(2,1)S(1)}, u32[]{:S(2)}, u32[]{:S(2)}) collective-permute-start(bf16[24,2048]{1,0:T(8,128)(2,1)S(1)} %get-tuple-element.113), channel_id=1, source_target_pairs={{0,8},{8,16},{16,24},{24,0},{1,9},{9,17},{17,25},{25,1},{2,10},{10... | collective-permute-start | bytes 294920 | tf_op jit(solution)/shard_map/ppermute | solution.py:36
  67.6 5.9 %collective-permute-start.7 = (bf16[24,2048]{1,0:T(8,128)(2,1)S(1)}, bf16[24,2048]{1,0:T(8,128)(2,1)S(1)}, u32[]{:S(2)}, u32[]{:S(2)}) collective-permute-start(bf16[24,2048]{1,0:T(8,128)(2,1)S(1)} %get-tuple-element.113), channel_id=1, source_target_pairs={{0,16},{8,24},{16,0},{24,8},{1,17},{9,25},{17,1},{25,9},{2,18},{10... | collective-permute-start | bytes 294920 | tf_op jit(solution)/shard_map/ppermute | solution.py:36
  69.4 4.6 %collective-permute-start.6 = (bf16[24,2048]{1,0:T(8,128)(2,1)S(1)}, bf16[24,2048]{1,0:T(8,128)(2,1)S(1)}, u32[]{:S(2)}, u32[]{:S(2)}) collective-permute-start(bf16[24,2048]{1,0:T(8,128)(2,1)S(1)} %get-tuple-element.113), channel_id=1, source_target_pairs={{0,24},{8,0},{16,8},{24,16},{1,25},{9,1},{17,9},{25,17},{2,26},{10... | collective-permute-start | bytes 294920 | tf_op jit(solution)/shard_map/ppermute | solution.py:36
  70.1 6.7 %collective-permute-start.15 = (bf16[24,2048]{1,0:T(8,128)(2,1)S(1)}, bf16[24,2048]{1,0:T(8,128)(2,1)S(1)}, u32[]{:S(2)}, u32[]{:S(2)}) collective-permute-start(bf16[24,2048]{1,0:T(8,128)(2,1)S(1)} %get-tuple-element.112), channel_id=1, source_target_pairs={{0,32},{32,64},{64,96},{96,0},{1,33},{33,65},{65,97},{97,1},{2,34}... | collective-permute-start | bytes 294920 | tf_op jit(solution)/shard_map/ppermute | solution.py:36
  70.6 6.2 %collective-permute-start.14 = (bf16[24,2048]{1,0:T(8,128)(2,1)S(1)}, bf16[24,2048]{1,0:T(8,128)(2,1)S(1)}, u32[]{:S(2)}, u32[]{:S(2)}) collective-permute-start(bf16[24,2048]{1,0:T(8,128)(2,1)S(1)} %get-tuple-element.112), channel_id=1, source_target_pairs={{0,64},{32,96},{64,0},{96,32},{1,65},{33,97},{65,1},{97,33},{2,66}... | collective-permute-start | bytes 294920 | tf_op jit(solution)/shard_map/ppermute | solution.py:36
  72.3 4.5 %collective-permute-start.13 = (bf16[24,2048]{1,0:T(8,128)(2,1)S(1)}, bf16[24,2048]{1,0:T(8,128)(2,1)S(1)}, u32[]{:S(2)}, u32[]{:S(2)}) collective-permute-start(bf16[24,2048]{1,0:T(8,128)(2,1)S(1)} %get-tuple-element.112), channel_id=1, source_target_pairs={{0,96},{32,0},{64,32},{96,64},{1,97},{33,1},{65,33},{97,65},{2,98}... | collective-permute-start | bytes 294920 | tf_op jit(solution)/shard_map/ppermute | solution.py:36
  74.0 20.5 %copy-start.1 = (bf16[1,4096,256]{2,1,0:T(8,128)(2,1)S(1)}, bf16[1,4096,256]{2,1,0:T(8,128)(2,1)}, u32[]{:S(2)}) copy-start(bf16[1,4096,256]{2,1,0:T(8,128)(2,1)} %param.25) | copy-start | bytes 6291460
  74.0 9.5 %collective-permute-start.10 = (bf16[96,2048]{1,0:T(8,128)(2,1)S(1)}, bf16[96,2048]{1,0:T(8,128)(2,1)S(1)}, u32[]{:S(2)}, u32[]{:S(2)}) collective-permute-start(bf16[96,2048]{1,0:T(8,128)(2,1)S(1)} %pad_maximum_fusion.1.refs_0_), channel_id=1, source_target_pairs={{0,32},{32,64},{64,96},{96,0},{1,33},{33,65},{65,97},{97,1},{2,34}... | collective-permute-start | bytes 1179656 | tf_op jit(solution)/shard_map/ppermute | solution.py:36
  74.5 10.6 %collective-permute-start.9 = (bf16[96,2048]{1,0:T(8,128)(2,1)S(1)}, bf16[96,2048]{1,0:T(8,128)(2,1)S(1)}, u32[]{:S(2)}, u32[]{:S(2)}) collective-permute-start(bf16[96,2048]{1,0:T(8,128)(2,1)S(1)} %pad_maximum_fusion.1.refs_0_), channel_id=1, source_target_pairs={{0,96},{32,0},{64,32},{96,64},{1,97},{33,1},{65,33},{97,65},{2,98}... | collective-permute-start | bytes 1179656 | tf_op jit(solution)/shard_map/ppermute | solution.py:36
  76.8 17.7 %copy-start = (bf16[1,4096,256]{2,1,0:T(8,128)(2,1)S(1)}, bf16[1,4096,256]{2,1,0:T(8,128)(2,1)}, u32[]{:S(2)}) copy-start(bf16[1,4096,256]{2,1,0:T(8,128)(2,1)} %param.24) | copy-start | bytes 6291460
  76.9 10.9 %collective-permute-start.17 = (bf16[96,2048]{1,0:T(8,128)(2,1)S(1)}, bf16[96,2048]{1,0:T(8,128)(2,1)S(1)}, u32[]{:S(2)}, u32[]{:S(2)}) collective-permute-start(bf16[96,2048]{1,0:T(8,128)(2,1)S(1)} %pad_maximum_fusion.3.refs_4_), channel_id=1, source_target_pairs={{0,8},{8,16},{16,24},{24,0},{1,9},{9,17},{17,25},{25,1},{2,10},{10... | collective-permute-start | bytes 1179656 | tf_op jit(solution)/shard_map/ppermute | solution.py:36
  77.8 10.8 %collective-permute-start.16 = (bf16[96,2048]{1,0:T(8,128)(2,1)S(1)}, bf16[96,2048]{1,0:T(8,128)(2,1)S(1)}, u32[]{:S(2)}, u32[]{:S(2)}) collective-permute-start(bf16[96,2048]{1,0:T(8,128)(2,1)S(1)} %pad_maximum_fusion.3.refs_4_), channel_id=1, source_target_pairs={{0,24},{8,0},{16,8},{24,16},{1,25},{9,1},{17,9},{25,17},{2,26},{10... | collective-permute-start | bytes 1179656 | tf_op jit(solution)/shard_map/ppermute | solution.py:36
  83.6 8.1 %collective-permute-start.11 = (bf16[48,2048]{1,0:T(8,128)(2,1)S(1)}, bf16[48,2048]{1,0:T(8,128)(2,1)S(1)}, u32[]{:S(2)}, u32[]{:S(2)}) collective-permute-start(bf16[48,2048]{1,0:T(8,128)(2,1)S(1)} %slice.130), channel_id=1, source_target_pairs={{0,32},{32,64},{64,96},{96,0},{1,33},{33,65},{65,97},{97,1},{2,34}... | collective-permute-start | bytes 589832 | tf_op jit(solution)/shard_map/ppermute | solution.py:36
  85.1 6.6 %collective-permute-start.12 = (bf16[48,2048]{1,0:T(8,128)(2,1)S(1)}, bf16[48,2048]{1,0:T(8,128)(2,1)S(1)}, u32[]{:S(2)}, u32[]{:S(2)}) collective-permute-start(bf16[48,2048]{1,0:T(8,128)(2,1)S(1)} %slice.131), channel_id=1, source_target_pairs={{0,96},{32,0},{64,32},{96,64},{1,97},{33,1},{65,33},{97,65},{2,98}... | collective-permute-start | bytes 589832 | tf_op jit(solution)/shard_map/ppermute | solution.py:36
  87.7 6.7 %collective-permute-start.18 = (bf16[48,2048]{1,0:T(8,128)(2,1)S(1)}, bf16[48,2048]{1,0:T(8,128)(2,1)S(1)}, u32[]{:S(2)}, u32[]{:S(2)}) collective-permute-start(bf16[48,2048]{1,0:T(8,128)(2,1)S(1)} %slice.132), channel_id=1, source_target_pairs={{0,8},{8,16},{16,24},{24,0},{1,9},{9,17},{17,25},{25,1},{2,10},{10... | collective-permute-start | bytes 589832 | tf_op jit(solution)/shard_map/ppermute | solution.py:36
  88.6 5.8 %collective-permute-start.19 = (bf16[48,2048]{1,0:T(8,128)(2,1)S(1)}, bf16[48,2048]{1,0:T(8,128)(2,1)S(1)}, u32[]{:S(2)}, u32[]{:S(2)}) collective-permute-start(bf16[48,2048]{1,0:T(8,128)(2,1)S(1)} %slice.133), channel_id=1, source_target_pairs={{0,24},{8,0},{16,8},{24,16},{1,25},{9,1},{17,9},{25,17},{2,26},{10... | collective-permute-start | bytes 589832 | tf_op jit(solution)/shard_map/ppermute | solution.py:36
  103.8 5.9 %collective-permute-start.20 = (bf16[48,2048]{1,0:T(8,128)(2,1)S(1)}, bf16[48,2048]{1,0:T(8,128)(2,1)S(1)}, u32[]{:S(2)}, u32[]{:S(2)}) collective-permute-start(bf16[48,2048]{1,0:T(8,128)(2,1)S(1)} %get-tuple-element.96), channel_id=1, source_target_pairs={{0,32},{32,64},{64,96},{96,0},{1,33},{33,65},{65,97},{97,1},{2,34}... | collective-permute-start | bytes 589832 | tf_op jit(solution)/shard_map/ppermute | solution.py:36
  103.9 5.9 %collective-permute-start.22 = (bf16[48,2048]{1,0:T(8,128)(2,1)S(1)}, bf16[48,2048]{1,0:T(8,128)(2,1)S(1)}, u32[]{:S(2)}, u32[]{:S(2)}) collective-permute-start(bf16[48,2048]{1,0:T(8,128)(2,1)S(1)} %get-tuple-element.97), channel_id=1, source_target_pairs={{0,96},{32,0},{64,32},{96,64},{1,97},{33,1},{65,33},{97,65},{2,98}... | collective-permute-start | bytes 589832 | tf_op jit(solution)/shard_map/ppermute | solution.py:36
  106.6 6.4 %collective-permute-start.27 = (bf16[48,2048]{1,0:T(8,128)(2,1)S(1)}, bf16[48,2048]{1,0:T(8,128)(2,1)S(1)}, u32[]{:S(2)}, u32[]{:S(2)}) collective-permute-start(bf16[48,2048]{1,0:T(8,128)(2,1)S(1)} %get-tuple-element.102), channel_id=1, source_target_pairs={{0,8},{8,16},{16,24},{24,0},{1,9},{9,17},{17,25},{25,1},{2,10},{10... | collective-permute-start | bytes 589832 | tf_op jit(solution)/shard_map/ppermute | solution.py:36
  108.1 4.9 %collective-permute-start.29 = (bf16[48,2048]{1,0:T(8,128)(2,1)S(1)}, bf16[48,2048]{1,0:T(8,128)(2,1)S(1)}, u32[]{:S(2)}, u32[]{:S(2)}) collective-permute-start(bf16[48,2048]{1,0:T(8,128)(2,1)S(1)} %get-tuple-element.103), channel_id=1, source_target_pairs={{0,24},{8,0},{16,8},{24,16},{1,25},{9,1},{17,9},{25,17},{2,26},{10... | collective-permute-start | bytes 589832 | tf_op jit(solution)/shard_map/ppermute | solution.py:36
  109.9 7.7 %collective-permute-start.23 = (bf16[96,2048]{1,0:T(8,128)(2,1)S(1)}, bf16[96,2048]{1,0:T(8,128)(2,1)S(1)}, u32[]{:S(2)}, u32[]{:S(2)}) collective-permute-start(bf16[96,2048]{1,0:T(8,128)(2,1)S(1)} %pad_maximum_fusion.6), channel_id=1, source_target_pairs={{0,96},{32,0},{64,32},{96,64},{1,97},{33,1},{65,33},{97,65},{2,98}... | collective-permute-start | bytes 1179656 | tf_op jit(solution)/shard_map/ppermute | solution.py:36
  112.5 7.9 %collective-permute-start.21 = (bf16[96,2048]{1,0:T(8,128)(2,1)S(1)}, bf16[96,2048]{1,0:T(8,128)(2,1)S(1)}, u32[]{:S(2)}, u32[]{:S(2)}) collective-permute-start(bf16[96,2048]{1,0:T(8,128)(2,1)S(1)} %pad_maximum_fusion.5), channel_id=1, source_target_pairs={{0,32},{32,64},{64,96},{96,0},{1,33},{33,65},{65,97},{97,1},{2,34}... | collective-permute-start | bytes 1179656 | tf_op jit(solution)/shard_map/ppermute | solution.py:36
  113.1 12.2 %collective-permute-start.30 = (bf16[96,2048]{1,0:T(8,128)(2,1)S(1)}, bf16[96,2048]{1,0:T(8,128)(2,1)S(1)}, u32[]{:S(2)}, u32[]{:S(2)}) collective-permute-start(bf16[96,2048]{1,0:T(8,128)(2,1)S(1)} %pad_maximum_fusion.8), channel_id=1, source_target_pairs={{0,24},{8,0},{16,8},{24,16},{1,25},{9,1},{17,9},{25,17},{2,26},{10... | collective-permute-start | bytes 1179656 | tf_op jit(solution)/shard_map/ppermute | solution.py:36
  116.0 9.4 %collective-permute-start.28 = (bf16[96,2048]{1,0:T(8,128)(2,1)S(1)}, bf16[96,2048]{1,0:T(8,128)(2,1)S(1)}, u32[]{:S(2)}, u32[]{:S(2)}) collective-permute-start(bf16[96,2048]{1,0:T(8,128)(2,1)S(1)} %pad_maximum_fusion.7), channel_id=1, source_target_pairs={{0,8},{8,16},{16,24},{24,0},{1,9},{9,17},{17,25},{25,1},{2,10},{10... | collective-permute-start | bytes 1179656 | tf_op jit(solution)/shard_map/ppermute | solution.py:36
  120.6 7.7 %collective-permute-start.24 = (bf16[24,2048]{1,0:T(8,128)(2,1)S(1)}, bf16[24,2048]{1,0:T(8,128)(2,1)S(1)}, u32[]{:S(2)}, u32[]{:S(2)}) collective-permute-start(bf16[24,2048]{1,0:T(8,128)(2,1)S(1)} %get-tuple-element.106), channel_id=1, source_target_pairs={{0,8},{8,16},{16,24},{24,0},{1,9},{9,17},{17,25},{25,1},{2,10},{10... | collective-permute-start | bytes 294920 | tf_op jit(solution)/shard_map/ppermute | solution.py:36
  122.1 6.2 %collective-permute-start.26 = (bf16[24,2048]{1,0:T(8,128)(2,1)S(1)}, bf16[24,2048]{1,0:T(8,128)(2,1)S(1)}, u32[]{:S(2)}, u32[]{:S(2)}) collective-permute-start(bf16[24,2048]{1,0:T(8,128)(2,1)S(1)} %get-tuple-element.107), channel_id=1, source_target_pairs={{0,24},{8,0},{16,8},{24,16},{1,25},{9,1},{17,9},{25,17},{2,26},{10... | collective-permute-start | bytes 294920 | tf_op jit(solution)/shard_map/ppermute | solution.py:36
  123.7 6.0 %collective-permute-start.25 = (bf16[24,2048]{1,0:T(8,128)(2,1)S(1)}, bf16[24,2048]{1,0:T(8,128)(2,1)S(1)}, u32[]{:S(2)}, u32[]{:S(2)}) collective-permute-start(bf16[24,2048]{1,0:T(8,128)(2,1)S(1)} %get-tuple-element.108), channel_id=1, source_target_pairs={{0,16},{8,24},{16,0},{24,8},{1,17},{9,25},{17,1},{25,9},{2,18},{10... | collective-permute-start | bytes 294920 | tf_op jit(solution)/shard_map/ppermute | solution.py:36
  125.5 5.0 %collective-permute-start.31 = (bf16[24,2048]{1,0:T(8,128)(2,1)S(1)}, bf16[24,2048]{1,0:T(8,128)(2,1)S(1)}, u32[]{:S(2)}, u32[]{:S(2)}) collective-permute-start(bf16[24,2048]{1,0:T(8,128)(2,1)S(1)} %get-tuple-element.109), channel_id=1, source_target_pairs={{0,32},{32,64},{64,96},{96,0},{1,33},{33,65},{65,97},{97,1},{2,34}... | collective-permute-start | bytes 294920 | tf_op jit(solution)/shard_map/ppermute | solution.py:36
  125.6 5.3 %collective-permute-start.33 = (bf16[24,2048]{1,0:T(8,128)(2,1)S(1)}, bf16[24,2048]{1,0:T(8,128)(2,1)S(1)}, u32[]{:S(2)}, u32[]{:S(2)}) collective-permute-start(bf16[24,2048]{1,0:T(8,128)(2,1)S(1)} %get-tuple-element.110), channel_id=1, source_target_pairs={{0,96},{32,0},{64,32},{96,64},{1,97},{33,1},{65,33},{97,65},{2,98}... | collective-permute-start | bytes 294920 | tf_op jit(solution)/shard_map/ppermute | solution.py:36
  128.3 5.0 %collective-permute-start.32 = (bf16[24,2048]{1,0:T(8,128)(2,1)S(1)}, bf16[24,2048]{1,0:T(8,128)(2,1)S(1)}, u32[]{:S(2)}, u32[]{:S(2)}) collective-permute-start(bf16[24,2048]{1,0:T(8,128)(2,1)S(1)} %get-tuple-element.111), channel_id=1, source_target_pairs={{0,64},{32,96},{64,0},{96,32},{1,65},{33,97},{65,1},{97,33},{2,66}... | collective-permute-start | bytes 294920 | tf_op jit(solution)/shard_map/ppermute | solution.py:36
  133.7 5.8 %collective-permute-start.36 = (bf16[24,4096]{1,0:T(8,128)(2,1)S(1)}, bf16[24,4096]{1,0:T(8,128)(2,1)S(1)}, u32[]{:S(2)}, u32[]{:S(2)}) collective-permute-start(bf16[24,4096]{1,0:T(8,128)(2,1)S(1)} %divide_convert_fusion), channel_id=1, source_target_pairs={{0,1},{1,2},{2,3},{3,0},{4,5},{5,6},{6,7},{7,4},{8,9},{9,10},{10,1... | collective-permute-start | bytes 589832 | tf_op jit(solution)/shard_map/ppermute | solution.py:36
  133.8 8.9 %collective-permute-start.35 = (bf16[24,4096]{1,0:T(8,128)(2,1)S(1)}, bf16[24,4096]{1,0:T(8,128)(2,1)S(1)}, u32[]{:S(2)}, u32[]{:S(2)}) collective-permute-start(bf16[24,4096]{1,0:T(8,128)(2,1)S(1)} %divide_convert_fusion), channel_id=1, source_target_pairs={{0,2},{1,3},{2,0},{3,1},{4,6},{5,7},{6,4},{7,5},{8,10},{9,11},{10,... | collective-permute-start | bytes 589832 | tf_op jit(solution)/shard_map/ppermute | solution.py:36
  137.6 5.2 %collective-permute-start.34 = (bf16[24,4096]{1,0:T(8,128)(2,1)S(1)}, bf16[24,4096]{1,0:T(8,128)(2,1)S(1)}, u32[]{:S(2)}, u32[]{:S(2)}) collective-permute-start(bf16[24,4096]{1,0:T(8,128)(2,1)S(1)} %divide_convert_fusion), channel_id=1, source_target_pairs={{0,3},{1,0},{2,1},{3,2},{4,7},{5,4},{6,5},{7,6},{8,11},{9,8},{10,9... | collective-permute-start | bytes 589832 | tf_op jit(solution)/shard_map/ppermute | solution.py:36
  176.8 12.8 %all-to-all-start.3 = ((bf16[32,32,128]{2,1,0:T(8,128)(2,1)}), bf16[32,32,128]{2,1,0:T(8,128)(2,1)S(1)}, u32[]{:S(2)}, u32[]{:S(2)}) async-start(bf16[32,32,128]{2,1,0:T(8,128)(2,1)} %leave.1), calls=%async_computation.3 | async-start | bytes 524288 | tf_op jit(solution)/shard_map/all_to_all | solution.py:728
  200.5 10.5 %collective-permute-start.37 = (bf16[128,1024]{1,0:T(8,128)(2,1)}, bf16[128,1024]{1,0:T(8,128)(2,1)S(1)}, u32[]{:S(2)}, u32[]{:S(2)}) collective-permute-start(bf16[128,1024]{1,0:T(8,128)(2,1)} %get-tuple-element.84), channel_id=1, source_target_pairs={{0,2},{1,3},{2,0},{3,1},{4,6},{5,7},{6,4},{7,5},{8,10},{9,11},{10,... | collective-permute-start | bytes 786440 | tf_op jit(solution)/shard_map/ppermute | solution.py:36
  204.2 12.6 %collective-permute-start.38 = (bf16[128,1024]{1,0:T(8,128)(2,1)}, bf16[128,1024]{1,0:T(8,128)(2,1)S(1)}, u32[]{:S(2)}, u32[]{:S(2)}) collective-permute-start(bf16[128,1024]{1,0:T(8,128)(2,1)} %get-tuple-element.85), channel_id=1, source_target_pairs={{0,1},{1,2},{2,3},{3,0},{4,5},{5,6},{6,7},{7,4},{8,9},{9,10},{10,1... | collective-permute-start | bytes 786440 | tf_op jit(solution)/shard_map/ppermute | solution.py:36
  204.4 12.4 %collective-permute-start.39 = (bf16[128,1024]{1,0:T(8,128)(2,1)}, bf16[128,1024]{1,0:T(8,128)(2,1)S(1)}, u32[]{:S(2)}, u32[]{:S(2)}) collective-permute-start(bf16[128,1024]{1,0:T(8,128)(2,1)} %get-tuple-element.86), channel_id=1, source_target_pairs={{0,3},{1,0},{2,1},{3,2},{4,7},{5,4},{6,5},{7,6},{8,11},{9,8},{10,9... | collective-permute-start | bytes 786440 | tf_op jit(solution)/shard_map/ppermute | solution.py:36
  (3 other events, 10.2 us)
